TPU v7x, 512 devices: a whole 4x8x8 slice. The times are simulated.
512 devices in a mesh: dp: 16 (over y, core), section: 8 (over z), tensor: 4 (over x).
Axes of the slice: x: 4, y: 8, z: 8, core: 2. Of those that a mesh axis runs over, the one named last changes fastest.
Arguments:
- sent_queries: bfloat16 [8, 32, 128, 2048], P('section', 'dp', None, 'tensor'), may hold values from -96 to 96
- mem_keys: bfloat16 [8, 128, 64, 2048], P('section', 'dp', None, 'tensor'), may hold values from -4 to 4
- mem_values: bfloat16 [8, 128, 64, 2048], P('section', 'dp', None, 'tensor'), may hold values from -24 to 24
- out_weight: bfloat16 [8, 2048, 4096], P('section', 'tensor', 'dp'), may hold values from -0.5 to 0.5
- sent_grads: bfloat16 [8, 32, 128, 4096], P('section', 'dp', None, 'tensor'), may hold values from -24 to 24
- counts: int32 [32], P('dp'), may hold values from 1 to 4, 80 in all
- neg_ids: int32 [32, 4], P('dp'), may hold values from 0 to 127, as said below
Outputs:
- mixed: bfloat16 [8, 32, 128, 4096], P('section', 'dp', None, 'tensor')
- query_grads: bfloat16 [8, 32, 128, 2048], P('section', 'dp', None, 'tensor')
- key_grads: bfloat16 [8, 128, 64, 2048], P('section', 'dp', None, 'tensor')
- value_grads: bfloat16 [8, 128, 64, 2048], P('section', 'dp', None, 'tensor')
Inputs may be any that keep to these rules, and one draw needn't show every extreme that they name: `neg_ids`: an id names a memory block, blocks numbered replica by replica with 8 to a replica (replica r holds documents r * 2 .. (r + 1) * 2 - 1); every entry names a block of another replica than its document's; the entries of one replica's documents name at most 1 entries held by any one other replica, and exactly 1 for some other replica; two entries may name the same block.
All inputs are finite; a program needn't handle non-finite values. No bound on the sum of `counts` on one device may be relied on, other than what follows from the above.
Results may differ from a plain program's by a relative error of at most 0.04.
Values may be sent and summed in bfloat16 or wider, within the bound.
No kernel may reach another device: no remote copies, remote signals or barrier semaphores. Data moves between devices by JAX's collectives and lax.ppermute only.
A program may use at most 64 MiB of HBM per device.

v0:
```python
import jax
import jax.numpy as jnp
from jax import lax
from jax.sharding import PartitionSpec as P

HD = 128


def passed_along(block, axis, distance):
    devices = range(lax.axis_size(axis))
    route = [((i - distance) % len(devices), i) for i in devices]
    return lax.ppermute(block, axis, route)


def on_device(sent_queries, mem_keys, mem_values, out_weight, sent_grads, counts, neg_ids):
    queries = passed_along(sent_queries, "section", 1)[0]
    grads = passed_along(sent_grads, "section", -1)[0]
    docs_dev, query_count, features = queries.shape
    heads_dev = features // HD
    memory_keys = mem_keys[0]
    memory_values = mem_values[0]
    mem_count, block_rows = (memory_keys.shape[0], memory_keys.shape[1])
    own_count = mem_count // docs_dev
    neg_count = neg_ids.shape[1]
    entries = docs_dev * neg_count
    groups = lax.axis_size("dp")
    capacity = (entries + groups - 2) // (groups - 1)
    slot_count = groups * capacity
    flat_ids = neg_ids.reshape(entries)
    holder = flat_ids // mem_count
    block_spot = flat_ids - holder * mem_count
    entry_order = jnp.arange(entries, dtype=jnp.int32)
    earlier = (holder[:, None] == holder[None, :]) & (entry_order[None, :] < entry_order[:, None])
    rank_within = jnp.sum(earlier.astype(jnp.int32), axis=1)
    slot_index = holder * capacity + rank_within
    picked = slot_index[None, :] == jnp.arange(slot_count, dtype=jnp.int32)[:, None]
    request = jnp.sum(jnp.where(picked, block_spot[None, :], 0), axis=1).reshape(groups, capacity)
    asked = lax.all_to_all(request, "dp", split_axis=0, concat_axis=0, tiled=True).reshape(
        slot_count
    )
    send_keys = jnp.take(memory_keys, asked, axis=0).reshape(groups, capacity, block_rows, features)
    send_values = jnp.take(memory_values, asked, axis=0).reshape(
        groups, capacity, block_rows, features
    )
    recv_keys, recv_values = (
        lax.all_to_all(send_keys, "dp", split_axis=0, concat_axis=0, tiled=True),
        lax.all_to_all(send_values, "dp", split_axis=0, concat_axis=0, tiled=True),
    )
    neg_keys = jnp.take(recv_keys.reshape(slot_count, block_rows, features), slot_index, axis=0)
    neg_values = jnp.take(recv_values.reshape(slot_count, block_rows, features), slot_index, axis=0)
    own_rows = own_count * block_rows
    key_rows = jnp.concatenate(
        [
            memory_keys.reshape(docs_dev, own_rows, features),
            neg_keys.reshape(docs_dev, neg_count * block_rows, features),
        ],
        axis=1,
    )
    value_rows = jnp.concatenate(
        [
            memory_values.reshape(docs_dev, own_rows, features),
            neg_values.reshape(docs_dev, neg_count * block_rows, features),
        ],
        axis=1,
    )
    key_total = key_rows.shape[1]
    position = jnp.arange(key_total, dtype=jnp.int32)
    valid = (position[None, :] < counts[:, None] * block_rows) | (position[None, :] >= own_rows)
    scale_value = HD ** (-0.5)
    query_heads = queries.reshape(docs_dev, query_count, heads_dev, HD)
    key_heads = key_rows.reshape(docs_dev, key_total, heads_dev, HD)
    value_heads = value_rows.reshape(docs_dev, key_total, heads_dev, HD)
    scores = (
        jnp.einsum("dqhe,dkhe->dhqk", query_heads, key_heads, preferred_element_type=jnp.float32)
        * scale_value
    )
    scores = jnp.where(valid[:, None, None, :], scores, -jnp.inf)
    row_max = jnp.max(scores, axis=-1, keepdims=True)
    expo_terms = jnp.exp(scores - row_max)
    probabilities = expo_terms / jnp.sum(expo_terms, axis=-1, keepdims=True)
    prob_round = probabilities.astype(jnp.bfloat16)
    attended = jnp.einsum(
        "dhqk,dkhe->dqhe", prob_round, value_heads, preferred_element_type=jnp.float32
    ).astype(jnp.bfloat16)
    attended_rows = attended.reshape(docs_dev * query_count, features)
    weight = out_weight[0]
    partial_terms = jnp.dot(
        attended_rows,
        lax.all_gather(weight, "dp", axis=1, tiled=True),
        preferred_element_type=jnp.float32,
    )
    mixed = lax.psum_scatter(
        partial_terms.astype(jnp.bfloat16), "tensor", scatter_dimension=1, tiled=True
    )
    mixed = mixed.reshape(1, docs_dev, query_count, mixed.shape[1])
    back_weight = lax.all_gather(weight, "dp", axis=1, tiled=True)
    grad_rows = grads.reshape(docs_dev * query_count, grads.shape[2])
    grad_attended = lax.dot_general(
        lax.all_gather(grad_rows, "tensor", axis=1, tiled=True),
        back_weight,
        (((1,), (1,)), ((), ())),
        preferred_element_type=jnp.float32,
    ).astype(jnp.bfloat16)
    grad_heads = grad_attended.reshape(docs_dev, query_count, heads_dev, HD)
    row_delta = jnp.einsum(
        "dqhe,dqhe->dhq", grad_heads, attended, preferred_element_type=jnp.float32
    )
    grad_values = jnp.einsum(
        "dhqk,dqhe->dkhe", prob_round, grad_heads, preferred_element_type=jnp.float32
    )
    grad_probs = jnp.einsum(
        "dqhe,dkhe->dhqk", grad_heads, value_heads, preferred_element_type=jnp.float32
    )
    grad_scores = (probabilities * (grad_probs - row_delta[..., None])).astype(jnp.bfloat16)
    grad_query = (
        jnp.einsum("dhqk,dkhe->dqhe", grad_scores, key_heads, preferred_element_type=jnp.float32)
        * scale_value
    )
    query_grads = grad_query.astype(jnp.bfloat16).reshape(1, docs_dev, query_count, features)
    grad_keys = (
        jnp.einsum("dhqk,dqhe->dkhe", grad_scores, query_heads, preferred_element_type=jnp.float32)
        * scale_value
    )
    grad_keys = grad_keys.reshape(docs_dev, key_total, features)
    grad_values = grad_values.reshape(docs_dev, key_total, features)
    row_width = block_rows * features
    own_keys = grad_keys[:, :own_rows].reshape(mem_count, row_width)
    own_values = grad_values[:, :own_rows].reshape(mem_count, row_width)
    neg_key_rows = grad_keys[:, own_rows:].reshape(entries, row_width).astype(jnp.bfloat16)
    neg_value_rows = grad_values[:, own_rows:].reshape(entries, row_width).astype(jnp.bfloat16)
    slot_fill = picked.astype(jnp.bfloat16)
    slot_keys = jnp.dot(slot_fill, neg_key_rows, preferred_element_type=jnp.float32).astype(
        jnp.bfloat16
    )
    slot_values = jnp.dot(slot_fill, neg_value_rows, preferred_element_type=jnp.float32).astype(
        jnp.bfloat16
    )
    slot_keys = slot_keys.reshape(groups, capacity, block_rows, features)
    slot_values = slot_values.reshape(groups, capacity, block_rows, features)
    back_keys, back_values = (
        lax.all_to_all(slot_keys, "dp", split_axis=0, concat_axis=0, tiled=True),
        lax.all_to_all(slot_values, "dp", split_axis=0, concat_axis=0, tiled=True),
    )
    owned = (asked[None, :] == jnp.arange(mem_count, dtype=jnp.int32)[:, None]).astype(jnp.bfloat16)
    total_keys = own_keys + jnp.dot(
        owned, back_keys.reshape(slot_count, row_width), preferred_element_type=jnp.float32
    )
    total_values = own_values + jnp.dot(
        owned, back_values.reshape(slot_count, row_width), preferred_element_type=jnp.float32
    )
    key_grads = total_keys.astype(jnp.bfloat16).reshape(1, mem_count, block_rows, features)
    value_grads = total_values.astype(jnp.bfloat16).reshape(1, mem_count, block_rows, features)
    return (mixed, query_grads, key_grads, value_grads)


def solution(mesh):
    placed = (
        P("section", "dp", None, "tensor"),
        P("section", "dp", None, "tensor"),
        P("section", "dp", None, "tensor"),
        P("section", "tensor", "dp"),
        P("section", "dp", None, "tensor"),
        P("dp"),
        P("dp", None),
    )
    return jax.shard_map(
        on_device,
        mesh=mesh,
        in_specs=placed,
        out_specs=(
            P("section", "dp", None, "tensor"),
            P("section", "dp", None, "tensor"),
            P("section", "dp", None, "tensor"),
            P("section", "dp", None, "tensor"),
        ),
        check_vma=False,
    )
```

profile of v0, /device:TPU:1, one launch (start us, length us, event | category | flops | bytes accessed | tf_op | source)
XLA Modules:
  0.0 224.3 jit_solution(13579695742543437191)
XLA Ops:
  7.2 11.6 %collective-permute-start.1 = (bf16[1,2,128,1024]{3,2,1,0:T(8,128)(2,1)}, bf16[1,2,128,1024]{3,2,1,0:T(8,128)(2,1)S(1)}, u32[]{:S(2)}, u32[]{:S(2)}) collective-permute-start(bf16[1,2,128,1024]{3,2,1,0:T(8,128)(2,1)} %param.15), channel_id=1, source_target_pairs={{4,0},{8,4},{12,8},{16,12},{20,16},{24,20},{28,24},{0,28},{5,1},{9... | collective-permute-start | bytes 1572872 | tf_op jit(solution)/shard_map/ppermute | solution.py:12
  18.9 10.9 %collective-permute-done.1 = bf16[1,2,128,1024]{3,2,1,0:T(8,128)(2,1)S(1)} collective-permute-done((bf16[1,2,128,1024]{3,2,1,0:T(8,128)(2,1)}, bf16[1,2,128,1024]{3,2,1,0:T(8,128)(2,1)S(1)}, u32[]{:S(2)}, u32[]{:S(2)}) %collective-permute-start.1) | collective-permute-done | bytes 524320 | tf_op jit(solution)/shard_map/ppermute | solution.py:12
  32.5 15.5 %all_to_all.29 = s32[16,1,1]{2,1,0:T(1,128)S(1)} all-to-all(s32[16,1,1]{2,1,0:T(1,128)S(1)} %copy.131), channel_id=1, replica_groups=mesh['dp'=16,'section'=8,'tensor'=4] {'dp'}, dimensions={0} | all-to-all | bytes 128 | tf_op jit(solution)/shard_map/all_to_all | solution.py:38
  48.3 1.7 gather_fusion.2
  51.9 31.8 %all_to_all.30 = bf16[16,1,64,512]{3,2,1,0:T(8,128)(2,1)S(1)} all-to-all(bf16[16,1,64,512]{3,2,1,0:T(8,128)(2,1)S(1)} %get-tuple-element.36), channel_id=1, replica_groups=mesh['dp'=16,'section'=8,'tensor'=4] {'dp'}, dimensions={0} | all-to-all | bytes 2097152 | tf_op jit(solution)/shard_map/all_to_all | solution.py:46
  83.7 3.6 %all-to-all-start.1 = ((bf16[16,1,64,512]{3,2,1,0:T(8,128)(2,1)}), bf16[16,1,64,512]{3,2,1,0:T(8,128)(2,1)S(1)}, u32[]{:S(2)}, u32[]{:S(2)}) async-start(bf16[16,1,64,512]{3,2,1,0:T(8,128)(2,1)} %get-tuple-element.37), calls=%async_computation.1 | async-start | bytes 2097152 | tf_op jit(solution)/shard_map/all_to_all | solution.py:47
  88.1 1.9 collective-permute-start
  93.3 1.4 gather_fusion.3
  94.7 25.4 %all-to-all-done.1 = bf16[16,1,64,512]{3,2,1,0:T(8,128)(2,1)S(1)} async-done(((bf16[16,1,64,512]{3,2,1,0:T(8,128)(2,1)}), bf16[16,1,64,512]{3,2,1,0:T(8,128)(2,1)S(1)}, u32[]{:S(2)}, u32[]{:S(2)}) %all-to-all-start.1) | async-done | bytes 1048608 | tf_op jit(solution)/shard_map/all_to_all | solution.py:47
  123.4 2.2 fusion.34
  125.6 12.9 %all-gather.6.cloned.1.call-done = bf16[1,512,4096]{2,1,0:T(8,128)(2,1)} async-done(((bf16[1,512,256]{2,1,0:T(8,128)(2,1)}), bf16[1,512,4096]{2,1,0:T(8,128)(2,1)}) %all-gather.6.cloned.1.call-update) | async-done | bytes 4194320 | tf_op jit(solution)/shard_map/all_gather | solution.py:89
  138.5 4.1 %fusion.11 = bf16[256,512]{1,0:T(8,128)(2,1)S(1)} fusion(bf16[256,4096]{1,0:T(8,128)(2,1)} %all-gather.4.cloned.1.call-done, bf16[1,512,4096]{2,1,0:T(8,128)(2,1)} %all-gather.6.cloned.1.call-done), kind=kOutput, calls=%fused_computation.25 | convolution fusion | flops 1073872896 | bytes 6553600 | tf_op jit(solution)/shard_map/dot_general | solution.py:98
  143.9 2.2 fusion.31
  150.4 4.6 %all-to-all-start.4 = ((bf16[16,1,64,512]{3,2,1,0:T(8,128)(2,1)}), bf16[16,1,64,512]{3,2,1,0:T(8,128)(2,1)S(1)}, u32[]{:S(2)}, u32[]{:S(2)}) async-start(bf16[16,1,64,512]{3,2,1,0:T(8,128)(2,1)} %bitcast.25), calls=%async_computation.5 | async-start | bytes 2097152 | tf_op jit(solution)/shard_map/all_to_all | solution.py:142
  155.3 4.8 %convolution_convert_fusion.2 = bf16[256,4096]{1,0:T(8,128)(2,1)} fusion(bf16[1,512,4096]{2,1,0:T(8,128)(2,1)} %all-gather.6.cloned.1.call-done, bf16[32,8,4,128]{3,2,1,0:T(4,128)(2,1)S(1)} %bitcast.107), kind=kOutput, calls=%fused_computation.11 | convolution fusion | flops 1074790400 | bytes 6553600 | tf_op jit(solution)/shard_map/dot_general | solution.py:87
  161.3 2.2 multiply_convert_fusion
  165.0 1.8 copy.147
  170.4 12.6 %all-to-all-done.4 = bf16[16,1,64,512]{3,2,1,0:T(8,128)(2,1)S(1)} async-done(((bf16[16,1,64,512]{3,2,1,0:T(8,128)(2,1)}), bf16[16,1,64,512]{3,2,1,0:T(8,128)(2,1)S(1)}, u32[]{:S(2)}, u32[]{:S(2)}) %all-to-all-start.4) | async-done | bytes 1048608 | tf_op jit(solution)/shard_map/all_to_all | solution.py:142
  183.0 4.4 %all-to-all-start.3 = ((bf16[16,1,64,512]{3,2,1,0:T(8,128)(2,1)}), bf16[16,1,64,512]{3,2,1,0:T(8,128)(2,1)}, u32[]{:S(2)}, u32[]{:S(2)}) async-start(bf16[16,1,64,512]{3,2,1,0:T(8,128)(2,1)} %bitcast.94), calls=%async_computation.4 | async-start | bytes 2097152 | tf_op jit(solution)/shard_map/all_to_all | solution.py:141
  187.4 2.5 %slice.28 = f32[2,256,512]{1,2,0:T(8,128)} slice(f32[2,512,512]{1,2,0:T(8,128)} %bitcast.104), slice={[0:2], [0:256], [0:512]} | slice | bytes 2097152 | tf_op jit(solution)/shard_map/slice | solution.py:128
  193.6 1.4 reshape.237
  196.4 1.4 reshape.232
  199.6 15.1 %all-to-all-done.3 = bf16[16,1,64,512]{3,2,1,0:T(8,128)(2,1)} async-done(((bf16[16,1,64,512]{3,2,1,0:T(8,128)(2,1)}), bf16[16,1,64,512]{3,2,1,0:T(8,128)(2,1)}, u32[]{:S(2)}, u32[]{:S(2)}) %all-to-all-start.3) | async-done | bytes 1048608 | tf_op jit(solution)/shard_map/all_to_all | solution.py:141
  214.7 1.8 copy.177
  (108 shorter events, 32.6 us)
Async XLA Ops:
  7.2 42.8 %copy-start.2 = (bf16[1,8,64,512]{3,2,1,0:T(8,128)(2,1)S(1)}, bf16[1,8,64,512]{3,2,1,0:T(8,128)(2,1)}, u32[]{:S(2)}) copy-start(bf16[1,8,64,512]{3,2,1,0:T(8,128)(2,1)} %param.13) | copy-start | bytes 1572868
  7.2 118.4 %all-gather.4.cloned.1.call-start = ((), (), s32[]{:S(2)}) async-start(), calls=%async_computation.7 | async-start | bytes 2621440 | tf_op jit(solution)/shard_map/all_gather | solution.py:99
  7.2 22.5 %collective-permute-start.1 = (bf16[1,2,128,1024]{3,2,1,0:T(8,128)(2,1)}, bf16[1,2,128,1024]{3,2,1,0:T(8,128)(2,1)S(1)}, u32[]{:S(2)}, u32[]{:S(2)}) collective-permute-start(bf16[1,2,128,1024]{3,2,1,0:T(8,128)(2,1)} %param.15), channel_id=1, source_target_pairs={{4,0},{8,4},{12,8},{16,12},{20,16},{24,20},{28,24},{0,28},{5,1},{9... | collective-permute-start | bytes 1572872 | tf_op jit(solution)/shard_map/ppermute | solution.py:12
  30.6 107.9 %all-gather.6.cloned.1.call-start = ((), (), s32[]{:S(2)}) async-start(), calls=%async_computation.8 | async-start | bytes 4456448 | tf_op jit(solution)/shard_map/all_gather | solution.py:89
  51.9 35.4 %copy-start.16 = (bf16[1,2,128,512]{3,2,1,0:T(8,128)(2,1)S(1)}, bf16[1,2,128,512]{3,2,1,0:T(8,128)(2,1)}, u32[]{:S(2)}) copy-start(bf16[1,2,128,512]{3,2,1,0:T(8,128)(2,1)} %param.11) | copy-start | bytes 786436
  51.9 38.1 %copy-start.1 = (bf16[1,8,64,512]{3,2,1,0:T(8,128)(2,1)S(1)}, bf16[1,8,64,512]{3,2,1,0:T(8,128)(2,1)}, u32[]{:S(2)}) copy-start(bf16[1,8,64,512]{3,2,1,0:T(8,128)(2,1)} %param.12) | copy-start | bytes 1572868
  83.7 36.4 %all-to-all-start.1 = ((bf16[16,1,64,512]{3,2,1,0:T(8,128)(2,1)}), bf16[16,1,64,512]{3,2,1,0:T(8,128)(2,1)S(1)}, u32[]{:S(2)}, u32[]{:S(2)}) async-start(bf16[16,1,64,512]{3,2,1,0:T(8,128)(2,1)} %get-tuple-element.37), calls=%async_computation.1 | async-start | bytes 2097152 | tf_op jit(solution)/shard_map/all_to_all | solution.py:47
  87.2 4.9 %copy-start.20 = (s32[2]{0:T(128)S(1)}, s32[2]{0:T(128)}, u32[]{:S(2)}) copy-start(s32[2]{0:T(128)} %param.16) | copy-start | bytes 28
  88.1 35.3 %collective-permute-start = (bf16[1,2,128,512]{2,3,1,0:T(8,128)(2,1)}, bf16[1,2,128,512]{2,3,1,0:T(8,128)(2,1)S(1)}, u32[]{:S(2)}, u32[]{:S(2)}) collective-permute-start(bf16[1,2,128,512]{2,3,1,0:T(8,128)(2,1)} %copy.136), channel_id=1, source_target_pairs={{28,0},{0,4},{4,8},{8,12},{12,16},{16,20},{20,24},{24,28},{29,1},{... | collective-permute-start | bytes 786440 | tf_op jit(solution)/shard_map/ppermute | solution.py:12
  123.3 2.2 copy-start.7
  123.4 2.2 copy-start.18
  143.9 2.2 copy-start.11
  143.9 2.2 copy-start.13
  143.9 2.2 copy-start.15
  143.9 2.7 %copy-start.21 = (f32[2,4,128,512]{2,3,1,0:T(8,128)S(1)}, f32[2,4,128,512]{2,3,1,0:T(8,128)}, u32[]{:S(2)}) copy-start(f32[2,4,128,512]{2,3,1,0:T(8,128)} %get-tuple-element.39) | copy-start | bytes 6291460
  149.1 6.2 %copy-start.17 = (bf16[2,128,4,128]{3,2,1,0:T(4,128)(2,1)S(1)}, bf16[2,128,4,128]{3,2,1,0:T(4,128)(2,1)}, u32[]{:S(2)}) copy-start(bf16[2,128,4,128]{3,2,1,0:T(4,128)(2,1)} %copy.139) | copy-start | bytes 786436
  150.4 32.5 %all-to-all-start.4 = ((bf16[16,1,64,512]{3,2,1,0:T(8,128)(2,1)}), bf16[16,1,64,512]{3,2,1,0:T(8,128)(2,1)S(1)}, u32[]{:S(2)}, u32[]{:S(2)}) async-start(bf16[16,1,64,512]{3,2,1,0:T(8,128)(2,1)} %bitcast.25), calls=%async_computation.5 | async-start | bytes 2097152 | tf_op jit(solution)/shard_map/all_to_all | solution.py:142
  155.1 62.7 %reduce-scatter.2.cloned.1.call-start = ((), (), s32[]{:S(2)}) async-start(), calls=%async_computation.6 | async-start | bytes 2621440 | tf_op jit(solution)/shard_map/reduce_scatter | solution.py:92
  161.3 3.3 %copy-start.19 = (bf16[1,2,128,512]{2,3,1,0:T(8,128)(2,1)S(1)}, bf16[1,2,128,512]{2,3,1,0:T(8,128)(2,1)}, u32[]{:S(2)}) copy-start(bf16[1,2,128,512]{2,3,1,0:T(8,128)(2,1)} %copy-done.18) | copy-start | bytes 786436
  183.0 6.9 %copy-start = (f32[2,512,4,128]{1,3,2,0:T(8,128)S(1)}, f32[2,512,4,128]{1,3,2,0:T(8,128)}, u32[]{:S(2)}) copy-start(f32[2,512,4,128]{1,3,2,0:T(8,128)} %copy.147) | copy-start | bytes 6291460
  183.0 31.7 %all-to-all-start.3 = ((bf16[16,1,64,512]{3,2,1,0:T(8,128)(2,1)}), bf16[16,1,64,512]{3,2,1,0:T(8,128)(2,1)}, u32[]{:S(2)}, u32[]{:S(2)}) async-start(bf16[16,1,64,512]{3,2,1,0:T(8,128)(2,1)} %bitcast.94), calls=%async_computation.4 | async-start | bytes 2097152 | tf_op jit(solution)/shard_map/all_to_all | solution.py:141
  187.4 3.6 %copy-start.4 = (bf16[2,4,128,512]{2,3,1,0:T(8,128)(2,1)S(1)}, bf16[2,4,128,512]{2,3,1,0:T(8,128)(2,1)}, u32[]{:S(2)}) copy-start(bf16[2,4,128,512]{2,3,1,0:T(8,128)(2,1)} %copy-done.3) | copy-start | bytes 3145732
  187.4 3.6 %copy-start.8 = (bf16[2,512,4,128]{3,1,2,0:T(8,128)(2,1)S(1)}, bf16[2,512,4,128]{3,1,2,0:T(8,128)(2,1)}, u32[]{:S(2)}) copy-start(bf16[2,512,4,128]{3,1,2,0:T(8,128)(2,1)} %copy-done.7) | copy-start | bytes 3145732
  192.3 2.7 %copy-start.5 = (f32[2,256,512]{1,2,0:T(8,128)S(1)}, f32[2,256,512]{1,2,0:T(8,128)}, u32[]{:S(2)}) copy-start(f32[2,256,512]{1,2,0:T(8,128)} %slice.26) | copy-start | bytes 3145732
  (6 other events, 6.8 us)
Sparse Core Ops, SparseCore 0:
  30.7 36.2 all-gather.3
  69.0 69.4 all-gather.5
  160.2 37.4 reduce-scatter.1
where the time goes:
time: 225 us; the launch traced here: 224 us
  waiting for transfers between devices  77.6 us (34%)
  blocking collectives  47.3 us (21%)
  local copies, waits for them, and re-layouts  37.2 us (17%)
  starting transfers between devices  26.4 us (12%)
  matrix products  18.5 us (8%)
  between operations  14.2 us (6%)
  other arithmetic  3.25 us (1%)
    all_to_all x1, blocking collectives, on_device(): lax.all_to_all(send_keys, 'dp', split_axis=0, concat_axis=0, tiled=True)  31.8 us
    all_to_all x1, waiting for transfers between devices, on_device(): lax.all_to_all(send_values, 'dp', split_axis=0, concat_axis=0, tiled=True)  25.4 us
    all_to_all x1, blocking collectives, on_device(): lax.all_to_all(request, 'dp', split_axis=0, concat_axis=0, tiled=True)  15.5 us
    all_to_all x1, waiting for transfers between devices, on_device(): lax.all_to_all(slot_keys, 'dp', split_axis=0, concat_axis=0, tiled=True)  15.1 us
    unnamed x55, local copies, waits for them, and re-layouts  14.5 us
    ppermute x2, starting transfers between devices, passed_along(): return lax.ppermute(block, axis, route)  13.5 us
    all_gather x1, waiting for transfers between devices, on_device(): lax.all_gather(weight, 'dp', axis=1, tiled=True)  12.9 us
    all_to_all x1, waiting for transfers between devices, on_device(): lax.all_to_all(slot_values, 'dp', split_axis=0, concat_axis=0, tiled=True)  12.6 us
  transfers between devices with their start and end apart: 8, of which 5 were waited for; matrix products, arithmetic and copies ran while one was open for 20% of the time, Pallas kernels for 0%

commit v1 on v0

v1 whole, which is shorter than its diff:
```python
import functools

import jax
import jax.numpy as jnp
from jax import lax
from jax.experimental import pallas as pl
from jax.experimental.pallas import tpu as pltpu
from jax.sharding import PartitionSpec as P

HD = 128
PARTS = 2
F32 = jnp.float32
BF16 = jnp.bfloat16
NT = (((1,), (1,)), ((), ()))
TN = (((0,), (0,)), ((), ()))
VMEM = pl.BlockSpec(memory_space=pltpu.VMEM)
SMEM = pl.BlockSpec(memory_space=pltpu.SMEM)
PARAMS = pltpu.CompilerParams(vmem_limit_bytes=40 * 1024 * 1024)


def passed_along(block, axis, distance):
    count = lax.axis_size(axis)
    return lax.ppermute(block, axis, [(i, (i + distance) % count) for i in range(count)])


def exchanged(slots):
    return lax.all_to_all(slots, "dp", split_axis=0, concat_axis=0, tiled=True)


def cost(flops, nbytes):
    return pl.CostEstimate(flops=int(flops), bytes_accessed=int(nbytes), transcendentals=0)


def pick_kernel(asked, keys, values, *slots):
    rows = keys.shape[1]
    wide = slots[0].shape[2]
    for slot in range(slots[0].shape[0]):
        spot = jnp.maximum(asked[slot], 0)
        for part, out in enumerate(slots):
            lanes = slice(part * wide, (part + 1) * wide)
            out[slot, :rows, :] = keys[spot, :, lanes]
            out[slot, rows:, :] = values[spot, :, lanes]


def picked_slots(asked, keys, values):
    slot_count = asked.shape[0]
    _, rows, features = keys.shape
    shape = jax.ShapeDtypeStruct((slot_count, 2 * rows, features // PARTS), BF16)
    return pl.pallas_call(
        pick_kernel,
        out_shape=[shape] * PARTS,
        in_specs=[SMEM, VMEM, VMEM],
        out_specs=[VMEM] * PARTS,
        compiler_params=PARAMS,
        cost_estimate=cost(0, 3 * 2**20),
        name="pick_blocks",
    )(asked, keys, values)


def attend_kernel(part, counts, holder, queries, keys, values, recv, grads, attended, grad_query, own_keys, own_values, slots):
    docs, _, _ = queries.shape
    mem_count, rows, _ = keys.shape
    own = mem_count // docs
    neg = holder.shape[0] // docs
    wide = recv.shape[2]
    scale = HD**-0.5
    total = (own + neg) * rows
    position = lax.broadcasted_iota(jnp.int32, (total, 1), 0)
    for doc in range(docs):
        valid = (position < counts[doc] * rows) | (position >= own * rows)
        for head in range(wide // HD):
            at = slice(head * HD, (head + 1) * HD)
            lanes = slice(part * wide + head * HD, part * wide + (head + 1) * HD)
            query = queries[doc, :, lanes]
            grad = grads[doc, :, lanes]
            key_rows = [keys[doc * own + m, :, lanes] for m in range(own)]
            value_rows = [values[doc * own + m, :, lanes] for m in range(own)]
            for m in range(neg):
                slot = holder[doc * neg + m]
                key_rows.append(recv[slot, :rows, at])
                value_rows.append(recv[slot, rows:, at])
            key = jnp.concatenate(key_rows, axis=0)
            value = jnp.concatenate(value_rows, axis=0)
            scores = lax.dot_general(key, query, NT, preferred_element_type=F32) * scale
            scores = jnp.where(valid, scores, -jnp.inf)
            expo = jnp.exp(scores - jnp.max(scores, axis=0, keepdims=True))
            prob = expo / jnp.sum(expo, axis=0, keepdims=True)
            prob_round = prob.astype(BF16)
            attended[doc, :, at] = lax.dot_general(prob_round, value, TN, preferred_element_type=F32).astype(BF16)
            grad_prob = lax.dot_general(value, grad, NT, preferred_element_type=F32)
            delta = jnp.sum(prob * grad_prob, axis=0, keepdims=True)
            grad_score = (prob * (grad_prob - delta)).astype(BF16)
            grad_query[doc, :, at] = (
                lax.dot_general(grad_score, key, TN, preferred_element_type=F32) * scale
            ).astype(BF16)
            grad_key = jnp.dot(grad_score, query, preferred_element_type=F32) * scale
            grad_value = jnp.dot(prob_round, grad, preferred_element_type=F32)
            for m in range(own):
                here = slice(m * rows, (m + 1) * rows)
                own_keys[doc * own + m, :, at] = grad_key[here]
                own_values[doc * own + m, :, at] = grad_value[here]
            for m in range(neg):
                here = slice((own + m) * rows, (own + m + 1) * rows)
                slot = holder[doc * neg + m]
                slots[slot, :rows, at] = grad_key[here].astype(BF16)
                slots[slot, rows:, at] = grad_value[here].astype(BF16)


def attend_part(part, counts, holder, queries, keys, values, recv, grads):
    docs, query_count, _ = queries.shape
    mem_count, rows, _ = keys.shape
    wide = recv.shape[2]
    query_shape = jax.ShapeDtypeStruct((docs, query_count, wide), BF16)
    own_shape = jax.ShapeDtypeStruct((mem_count, rows, wide), F32)
    return pl.pallas_call(
        functools.partial(attend_kernel, part),
        out_shape=[query_shape, query_shape, own_shape, own_shape, jax.ShapeDtypeStruct(recv.shape, BF16)],
        in_specs=[SMEM, SMEM] + [VMEM] * 5,
        out_specs=[VMEM] * 5,
        compiler_params=PARAMS,
        cost_estimate=cost(4 * 2**30, 8 * 2**20),
        name=f"attend_part{part}",
    )(counts, holder, queries, keys, values, recv, grads)


def back_kernel(spot, weight, grad0, grad1, grad2, grad3, out):
    block = weight.shape[2]
    held = (grad0, grad1, grad2, grad3)
    per = weight.shape[0] // len(held)
    total = None
    for j, grad in enumerate(held):
        first = lax.rem(spot[0] + j, len(held)) * per
        for c in range(per):
            term = lax.dot_general(
                grad[:, c * block : (c + 1) * block], weight[first + c], NT, preferred_element_type=F32
            )
            total = term if total is None else total + term
    out[...] = total.astype(BF16)


def back_projected(weight, held):
    rows = held[0].shape[0]
    return pl.pallas_call(
        back_kernel,
        out_shape=jax.ShapeDtypeStruct((rows, weight.shape[1]), BF16),
        in_specs=[SMEM] + [VMEM] * (1 + len(held)),
        out_specs=VMEM,
        compiler_params=PARAMS,
        cost_estimate=cost(2 * 2**30, 8 * 2**20),
        name="back_projection",
    )(lax.axis_index("tensor").astype(jnp.int32).reshape(1), weight, *held)


def project_kernel(weight, *refs):
    *parts, out = refs
    block = weight.shape[2]
    per = weight.shape[0] // out.shape[0]
    wide = parts[0].shape[1]
    for b in range(weight.shape[0]):
        total = None
        for p, part in enumerate(parts):
            term = jnp.dot(part[...], weight[b, p * wide : (p + 1) * wide, :], preferred_element_type=F32)
            total = term if total is None else total + term
        out[b // per, :, (b % per) * block : (b % per + 1) * block] = total.astype(BF16)


def projected(weight, parts, groups):
    columns = weight.shape[0] * weight.shape[2] // groups
    return pl.pallas_call(
        project_kernel,
        out_shape=jax.ShapeDtypeStruct((groups, parts[0].shape[0], columns), BF16),
        in_specs=[VMEM] * (1 + len(parts)),
        out_specs=VMEM,
        compiler_params=PARAMS,
        cost_estimate=cost(2 * 2**30, 8 * 2**20),
        name="projection",
    )(weight, *parts)


def combine_kernel(part, asked, own_keys, own_values, back, *refs):
    key_grads, value_grads, key_total, value_total = refs[-4:]
    rows = own_keys.shape[1]
    key_total[...] = own_keys[...]
    value_total[...] = own_values[...]
    for slot in range(back.shape[0]):
        spot = asked[slot]

        @pl.when(spot >= 0)
        def _(slot=slot, spot=spot):
            key_total[spot] += back[slot, :rows, :].astype(F32)
            value_total[spot] += back[slot, rows:, :].astype(F32)

    key_grads[...] = key_total[...].astype(BF16)
    value_grads[...] = value_total[...].astype(BF16)


def combined(part, asked, own_keys, own_values, back, earlier):
    mem_count, rows, wide = own_keys.shape
    shape = jax.ShapeDtypeStruct((mem_count, rows, wide * PARTS), BF16)
    block = pl.BlockSpec((mem_count, rows, wide), lambda i: (0, 0, part))
    return pl.pallas_call(
        functools.partial(combine_kernel, part),
        grid=(1,),
        out_shape=[shape, shape],
        in_specs=[SMEM, VMEM, VMEM, VMEM] + [pl.BlockSpec(memory_space=pl.ANY)] * len(earlier),
        out_specs=[block, block],
        scratch_shapes=[pltpu.VMEM(own_keys.shape, F32)] * 2,
        input_output_aliases={4 + i: i for i in range(len(earlier))},
        compiler_params=PARAMS,
        cost_estimate=cost(0, 4 * 2**20),
        name=f"combine_part{part}",
    )(asked, own_keys, own_values, back, *earlier)


def on_device(sent_queries, mem_keys, mem_values, out_weight, sent_grads, counts, neg_ids):
    keys, values = mem_keys[0], mem_values[0]
    mem_count = keys.shape[0]
    groups = lax.axis_size("dp")
    tensor = lax.axis_size("tensor")

    flat_ids = neg_ids.reshape(-1)
    holder = flat_ids // mem_count
    spot = flat_ids - holder * mem_count
    named = holder[None, :] == jnp.arange(groups, dtype=jnp.int32)[:, None]
    request = jnp.sum(jnp.where(named, spot[None, :] + 1, 0), axis=1) - 1
    asked = exchanged(request.reshape(groups, 1)).reshape(groups)

    queries = passed_along(sent_queries, "section", 1)[0]
    grads = passed_along(sent_grads, "section", -1)[0]
    docs, query_count, features = queries.shape
    weight = lax.all_gather(out_weight[0], "dp")

    recv = [exchanged(part) for part in picked_slots(asked, keys, values)]

    grad_rows = grads.reshape(docs * query_count, grads.shape[2])
    held = [grad_rows] + [passed_along(grad_rows, "tensor", -j) for j in range(1, tensor)]
    grad_attended = back_projected(weight, held).reshape(docs, query_count, features)

    attended, query_grads, own, back = [], [], [], []
    for part in range(PARTS):
        out, grad_query, own_keys, own_values, slots = attend_part(
            part, counts, holder, queries, keys, values, recv[part], grad_attended
        )
        attended.append(out.reshape(docs * query_count, -1))
        query_grads.append(grad_query)
        own.append((own_keys, own_values))
        back.append(exchanged(slots))

    mixed = lax.psum_scatter(projected(weight, attended, tensor), "tensor", scatter_dimension=0)
    mixed = mixed.reshape(1, docs, query_count, -1)

    grads_out = []
    for part in range(PARTS):
        grads_out = combined(part, asked, *own[part], back[part], grads_out)
    key_grads, value_grads = grads_out
    return mixed, jnp.concatenate(query_grads, axis=-1)[None], key_grads[None], value_grads[None]


def solution(mesh):
    rows = P("section", "dp", None, "tensor")
    return jax.shard_map(
        on_device,
        mesh=mesh,
        in_specs=(rows, rows, rows, P("section", "tensor", "dp"), rows, P("dp"), P("dp", None)),
        out_specs=(rows, rows, rows, rows),
        check_vma=False,
    )
```

time: 225 us -> 233 us (1.036)
  blocking collectives: 47.3 us -> 93.7 us
  waiting for transfers between devices: 77.6 us -> 56.3 us
  matrix products: 18.5 us -> 0 us
  Pallas kernels: 0 us -> 16.9 us
  local copies, waits for them, and re-layouts: 37.2 us -> 20.9 us
    all_to_all x2 -> x3, blocking collectives: 47.3 us -> 93.7 us  [exchanged(): return lax.all_to_all(slots, 'dp', split_axis=0, concat_axis=0, tiled=True)]
    all_to_all x3 -> x2, waiting for transfers between devices: 53 us -> 22.8 us  [exchanged(): return lax.all_to_all(slots, 'dp', split_axis=0, concat_axis=0, tiled=True)]
    ppermute x2 -> x5, waiting for transfers between devices: 10.9 us -> 32.7 us  [passed_along(): lax.ppermute(block, axis, [(i, (i + distance) % count) for i in range(cou...]
    pallas_call x0 -> x7, Pallas kernels: none -> 16.9 us  [the longest x2 6.81 us: attend_part(): pl.pallas_call(functools.partial(attend_kernel, part), out_shape=[query_s...]
    dot_general x11 -> x0, matrix products: 16.3 us -> none  [the longest x1 4.78 us: on_device(): jnp.dot(attended_rows, lax.all_gather(weight, 'dp', axis=1, tiled=True),...]
    all_gather x2 -> x1, waiting for transfers between devices: 12.9 us -> 0.01 us  [on_device(): weight = lax.all_gather(out_weight[0], 'dp')]
    slice x7 -> x0, local copies, waits for them, and re-layouts: 7.77 us -> none  [the longest x2 3.79 us: on_device(): own_values = grad_values[:, :own_rows].reshape(mem_count, row_width)]
    ppermute x2 -> x5, starting transfers between devices: 13.5 us -> 21 us  [passed_along(): lax.ppermute(block, axis, [(i, (i + distance) % count) for i in range(cou...]
  transfers between devices with their start and end apart: 8 -> 9, of which waited for: 5 -> 5; matrix products, arithmetic and copies ran while one was open for 20% -> 1% of each run, Pallas kernels for 0% -> 4%
where the time goes in v1:
time: 233 us; the launch traced here: 232 us
  blocking collectives  93.7 us (40%)
  waiting for transfers between devices  56.3 us (24%)
  starting transfers between devices  28.5 us (12%)
  local copies, waits for them, and re-layouts  20.9 us (9%)
  Pallas kernels  16.9 us (7%)
  between operations  14.2 us (6%)
    all_to_all x3, blocking collectives, exchanged(): return lax.all_to_all(slots, 'dp', split_axis=0, concat_axis=0, tiled=True)  93.7 us
    ppermute x5, waiting for transfers between devices, passed_along(): lax.ppermute(block, axis, [(i, (i + distance) % count) for i in range(cou...  32.7 us
    all_to_all x2, waiting for transfers between devices, exchanged(): return lax.all_to_all(slots, 'dp', split_axis=0, concat_axis=0, tiled=True)  22.8 us
    ppermute x5, starting transfers between devices, passed_along(): lax.ppermute(block, axis, [(i, (i + distance) % count) for i in range(cou...  21 us
    unnamed x46, local copies, waits for them, and re-layouts  20 us
    all_to_all x2, starting transfers between devices, exchanged(): return lax.all_to_all(slots, 'dp', split_axis=0, concat_axis=0, tiled=True)  7.4 us
    pallas_call x2, Pallas kernels, attend_part(): pl.pallas_call(functools.partial(attend_kernel, part), out_shape=[query_s...  6.81 us
  transfers between devices with their start and end apart: 9, of which 5 were waited for; matrix products, arithmetic and copies ran while one was open for 1% of the time, Pallas kernels for 4%

profile of v1, /device:TPU:1, one launch (start us, length us, event | category | flops | bytes accessed | tf_op | source)
XLA Modules:
  0.0 231.6 jit_solution(13182766281860140424)
XLA Ops:
  8.9 16.3 %all_to_all.26 = s32[16,1,1]{2,1,0:T(1,128)S(1)} all-to-all(s32[16,1,1]{2,1,0:T(1,128)S(1)} %copy.15), channel_id=1, replica_groups=mesh['dp'=16,'section'=8,'tensor'=4] {'dp'}, dimensions={0} | all-to-all | bytes 128 | tf_op jit(solution)/shard_map/all_to_all | solution.py:27
  25.6 1.0 copy-done.4
  27.6 1.7 pick_blocks.1
  29.4 41.8 %all_to_all.27.recv = bf16[16,128,256]{2,1,0:T(8,128)(2,1)S(1)} all-to-all(bf16[16,128,256]{2,1,0:T(8,128)(2,1)S(1)} %get-tuple-element.20), channel_id=1, replica_groups=mesh['dp'=16,'section'=8,'tensor'=4] {'dp'}, dimensions={0} | all-to-all | bytes 2097152 | tf_op jit(solution)/shard_map/all_to_all | solution.py:27
  71.2 3.9 %all-to-all-start.2 = ((bf16[16,128,256]{2,1,0:T(8,128)(2,1)}), bf16[16,128,256]{2,1,0:T(8,128)(2,1)S(1)}, u32[]{:S(2)}, u32[]{:S(2)}) async-start(bf16[16,128,256]{2,1,0:T(8,128)(2,1)} %get-tuple-element.22), calls=%async_computation.2 | async-start | bytes 2097152 | tf_op jit(solution)/shard_map/all_to_all | solution.py:27
  75.1 9.6 %collective-permute-start.1 = (bf16[1,2,128,1024]{3,2,1,0:T(8,128)(2,1)S(1)}, bf16[1,2,128,1024]{3,2,1,0:T(8,128)(2,1)S(1)}, u32[]{:S(2)}, u32[]{:S(2)}) collective-permute-start(bf16[1,2,128,1024]{3,2,1,0:T(8,128)(2,1)S(1)} %copy-done.22), channel_id=1, source_target_pairs={{0,28},{4,0},{8,4},{12,8},{16,12},{20,16},{24,20},{28,24},{1,29},{... | collective-permute-start | bytes 1572872 | tf_op jit(solution)/shard_map/ppermute | solution.py:23
  84.7 11.1 %collective-permute-done.1 = bf16[1,2,128,1024]{3,2,1,0:T(8,128)(2,1)S(1)} collective-permute-done((bf16[1,2,128,1024]{3,2,1,0:T(8,128)(2,1)S(1)}, bf16[1,2,128,1024]{3,2,1,0:T(8,128)(2,1)S(1)}, u32[]{:S(2)}, u32[]{:S(2)}) %collective-permute-start.1) | collective-permute-done | bytes 524320 | tf_op jit(solution)/shard_map/ppermute | solution.py:23
  95.8 4.5 %collective-permute-start.2 = (bf16[256,1024]{1,0:T(8,128)(2,1)S(1)}, bf16[256,1024]{1,0:T(8,128)(2,1)S(1)}, u32[]{:S(2)}, u32[]{:S(2)}) collective-permute-start(bf16[256,1024]{1,0:T(8,128)(2,1)S(1)} %bitcast.21), channel_id=1, source_target_pairs={{0,3},{1,0},{2,1},{3,2},{4,7},{5,4},{6,5},{7,6},{8,11},{9,8},{10,9... | collective-permute-start | bytes 1572872 | tf_op jit(solution)/shard_map/ppermute | solution.py:23
  100.3 2.4 %collective-permute-start.3 = (bf16[256,1024]{1,0:T(8,128)(2,1)S(1)}, bf16[256,1024]{1,0:T(8,128)(2,1)}, u32[]{:S(2)}, u32[]{:S(2)}) collective-permute-start(bf16[256,1024]{1,0:T(8,128)(2,1)S(1)} %bitcast.22), channel_id=1, source_target_pairs={{0,2},{1,3},{2,0},{3,1},{4,6},{5,7},{6,4},{7,5},{8,10},{9,11},{10,... | collective-permute-start | bytes 1572872 | tf_op jit(solution)/shard_map/ppermute | solution.py:23
  102.6 2.6 %collective-permute-start.4 = (bf16[256,1024]{1,0:T(8,128)(2,1)S(1)}, bf16[256,1024]{1,0:T(8,128)(2,1)}, u32[]{:S(2)}, u32[]{:S(2)}) collective-permute-start(bf16[256,1024]{1,0:T(8,128)(2,1)S(1)} %bitcast.23), channel_id=1, source_target_pairs={{0,1},{1,2},{2,3},{3,0},{4,5},{5,6},{6,7},{7,4},{8,9},{9,10},{10,1... | collective-permute-start | bytes 1572872 | tf_op jit(solution)/shard_map/ppermute | solution.py:23
  105.3 1.9 collective-permute-start
  107.2 4.1 %collective-permute-done.2.grad1 = bf16[256,1024]{1,0:T(8,128)(2,1)S(1)} collective-permute-done((bf16[256,1024]{1,0:T(8,128)(2,1)S(1)}, bf16[256,1024]{1,0:T(8,128)(2,1)S(1)}, u32[]{:S(2)}, u32[]{:S(2)}) %collective-permute-start.2) | collective-permute-done | bytes 524320 | tf_op jit(solution)/shard_map/ppermute | solution.py:23
  111.3 4.6 %collective-permute-done.3.grad2 = bf16[256,1024]{1,0:T(8,128)(2,1)} collective-permute-done((bf16[256,1024]{1,0:T(8,128)(2,1)S(1)}, bf16[256,1024]{1,0:T(8,128)(2,1)}, u32[]{:S(2)}, u32[]{:S(2)}) %collective-permute-start.3) | collective-permute-done | bytes 524320 | tf_op jit(solution)/shard_map/ppermute | solution.py:23
  115.9 12.9 %collective-permute-done.4.grad3 = bf16[256,1024]{1,0:T(8,128)(2,1)} collective-permute-done((bf16[256,1024]{1,0:T(8,128)(2,1)S(1)}, bf16[256,1024]{1,0:T(8,128)(2,1)}, u32[]{:S(2)}, u32[]{:S(2)}) %collective-permute-start.4) | collective-permute-done | bytes 524320 | tf_op jit(solution)/shard_map/ppermute | solution.py:23
  128.8 2.2 copy-done.14
  131.0 2.5 %back_projection.1 = bf16[256,512]{1,0:T(8,128)(2,1)S(1)} custom-call(s32[1]{0:T(128)} %bitcast.4.spot, bf16[16,512,256]{2,1,0:T(8,128)(2,1)S(1)} %copy-done.14, bf16[256,1024]{1,0:T(8,128)(2,1)S(1)} %bitcast.24, bf16[256,1024]{1,0:T(8,128)(2,1)S(1)} %collective-permute-done.2.grad1, bf16[256,1024]{1,0:T(8,128)(2,1)} %collective-permute-done.3.grad2, ...), custom_call_target="tpu_custom_call" | custom-call | flops 2147483648 | bytes 8388608 | tf_op jit(solution)/shard_map/back_projection/pallas_call | solution.py:143
  137.3 2.9 %attend_part0.1 = (bf16[2,128,256]{2,1,0:T(8,128)(2,1)S(1)}, bf16[2,128,256]{2,1,0:T(8,128)(2,1)S(1)}, f32[8,64,256]{2,1,0:T(8,128)S(1)}, f32[8,64,256]{2,1,0:T(8,128)S(1)}, bf16[16,128,256]{2,1,0:T(8,128)(2,1)S(1)}) custom-call(s32[2]{0:T(128)S(1)} %copy-done.19, s32[8]{0:T(128)S(1)} %get-tuple-element.37.holder, bf16[2,128,512]{2,1,0:T(8,128)(2,1)S(1)} %bitcast.25, ...), custom_call_target="tpu_custom_call" | custom-call | flops 4294967296 | bytes 8388608 | tf_op jit(solution)/shard_map/attend_part0/pallas_call | solution.py:115
  146.5 3.9 %attend_part1.1 = (bf16[2,128,256]{2,1,0:T(8,128)(2,1)S(1)}, bf16[2,128,256]{2,1,0:T(8,128)(2,1)S(1)}, f32[8,64,256]{2,1,0:T(8,128)S(1)}, f32[8,64,256]{2,1,0:T(8,128)S(1)}, bf16[16,128,256]{2,1,0:T(8,128)(2,1)}) custom-call(s32[2]{0:T(128)S(1)} %copy-done.19, s32[8]{0:T(128)S(1)} %get-tuple-element.37.holder, bf16[2,128,512]{2,1,0:T(8,128)(2,1)S(1)} %bitcast.26, ...), custom_call_target="tpu_custom_call" | custom-call | flops 4294967296 | bytes 8388608 | tf_op jit(solution)/shard_map/attend_part1/pallas_call | solution.py:115
  152.0 2.6 %projection.1 = bf16[4,256,1024]{2,1,0:T(8,128)(2,1)} custom-call(bf16[16,512,256]{2,1,0:T(8,128)(2,1)S(1)} %copy-done.15, bf16[256,256]{1,0:T(8,128)(2,1)S(1)} %bitcast.29, bf16[256,256]{1,0:T(8,128)(2,1)S(1)} %bitcast.30), custom_call_target="tpu_custom_call" | custom-call | flops 2147483648 | bytes 8388608 | tf_op jit(solution)/shard_map/projection/pallas_call | solution.py:169
  154.6 35.6 %all_to_all.28.back = bf16[16,128,256]{2,1,0:T(8,128)(2,1)S(1)} all-to-all(bf16[16,128,256]{2,1,0:T(8,128)(2,1)S(1)} %get-tuple-element.31), channel_id=1, replica_groups=mesh['dp'=16,'section'=8,'tensor'=4] {'dp'}, dimensions={0} | all-to-all | bytes 2097152 | tf_op jit(solution)/shard_map/all_to_all | solution.py:27
  190.2 3.6 %all-to-all-start.3 = ((bf16[16,128,256]{2,1,0:T(8,128)(2,1)}), bf16[16,128,256]{2,1,0:T(8,128)(2,1)S(1)}, u32[]{:S(2)}, u32[]{:S(2)}) async-start(bf16[16,128,256]{2,1,0:T(8,128)(2,1)} %get-tuple-element.28), calls=%async_computation.4 | async-start | bytes 2097152 | tf_op jit(solution)/shard_map/all_to_all | solution.py:27
  196.6 1.6 combine_part0.1
  198.2 22.8 %all-to-all-done.3.back = bf16[16,128,256]{2,1,0:T(8,128)(2,1)S(1)} async-done(((bf16[16,128,256]{2,1,0:T(8,128)(2,1)}), bf16[16,128,256]{2,1,0:T(8,128)(2,1)S(1)}, u32[]{:S(2)}, u32[]{:S(2)}) %all-to-all-start.3) | async-done | bytes 1048608 | tf_op jit(solution)/shard_map/all_to_all | solution.py:27
  223.1 1.6 combine_part1.1
  (59 shorter events, 19.6 us)
Async XLA Ops:
  7.2 121.7 %all-gather.2.cloned.1.call-start = ((), (), s32[]{:S(2)}) async-start(), calls=%async_computation.6 | async-start | bytes 4456448 | tf_op jit(solution)/shard_map/all_gather | solution.py:231
  25.5 1.1 copy-start.4
  26.6 1.0 copy-start.7
  27.6 47.4 %copy-start.22 = (bf16[1,2,128,1024]{3,2,1,0:T(8,128)(2,1)S(1)}, bf16[1,2,128,1024]{3,2,1,0:T(8,128)(2,1)}, u32[]{:S(2)}) copy-start(bf16[1,2,128,1024]{3,2,1,0:T(8,128)(2,1)} %param.11) | copy-start | bytes 1572868
  71.2 71.3 %all-to-all-start.2 = ((bf16[16,128,256]{2,1,0:T(8,128)(2,1)}), bf16[16,128,256]{2,1,0:T(8,128)(2,1)S(1)}, u32[]{:S(2)}, u32[]{:S(2)}) async-start(bf16[16,128,256]{2,1,0:T(8,128)(2,1)} %get-tuple-element.22), calls=%async_computation.2 | async-start | bytes 2097152 | tf_op jit(solution)/shard_map/all_to_all | solution.py:27
  75.0 59.2 %copy-start.19 = (s32[2]{0:T(128)S(1)}, s32[2]{0:T(128)}, u32[]{:S(2)}) copy-start(s32[2]{0:T(128)} %counts.3) | copy-start | bytes 28
  75.0 149.7 %reduce-scatter.2.cloned.1.call-start = ((), (), s32[]{:S(2)}) async-start(), calls=%async_computation.7 | async-start | bytes 2621440 | tf_op jit(solution)/shard_map/reduce_scatter | solution.py:249
  75.1 20.7 %collective-permute-start.1 = (bf16[1,2,128,1024]{3,2,1,0:T(8,128)(2,1)S(1)}, bf16[1,2,128,1024]{3,2,1,0:T(8,128)(2,1)S(1)}, u32[]{:S(2)}, u32[]{:S(2)}) collective-permute-start(bf16[1,2,128,1024]{3,2,1,0:T(8,128)(2,1)S(1)} %copy-done.22), channel_id=1, source_target_pairs={{0,28},{4,0},{8,4},{12,8},{16,12},{20,16},{24,20},{28,24},{1,29},{... | collective-permute-start | bytes 1572872 | tf_op jit(solution)/shard_map/ppermute | solution.py:23
  95.8 15.5 %collective-permute-start.2 = (bf16[256,1024]{1,0:T(8,128)(2,1)S(1)}, bf16[256,1024]{1,0:T(8,128)(2,1)S(1)}, u32[]{:S(2)}, u32[]{:S(2)}) collective-permute-start(bf16[256,1024]{1,0:T(8,128)(2,1)S(1)} %bitcast.21), channel_id=1, source_target_pairs={{0,3},{1,0},{2,1},{3,2},{4,7},{5,4},{6,5},{7,6},{8,11},{9,8},{10,9... | collective-permute-start | bytes 1572872 | tf_op jit(solution)/shard_map/ppermute | solution.py:23
  100.3 15.6 %collective-permute-start.3 = (bf16[256,1024]{1,0:T(8,128)(2,1)S(1)}, bf16[256,1024]{1,0:T(8,128)(2,1)}, u32[]{:S(2)}, u32[]{:S(2)}) collective-permute-start(bf16[256,1024]{1,0:T(8,128)(2,1)S(1)} %bitcast.22), channel_id=1, source_target_pairs={{0,2},{1,3},{2,0},{3,1},{4,6},{5,7},{6,4},{7,5},{8,10},{9,11},{10,... | collective-permute-start | bytes 1572872 | tf_op jit(solution)/shard_map/ppermute | solution.py:23
  102.6 26.2 %collective-permute-start.4 = (bf16[256,1024]{1,0:T(8,128)(2,1)S(1)}, bf16[256,1024]{1,0:T(8,128)(2,1)}, u32[]{:S(2)}, u32[]{:S(2)}) collective-permute-start(bf16[256,1024]{1,0:T(8,128)(2,1)S(1)} %bitcast.23), channel_id=1, source_target_pairs={{0,1},{1,2},{2,3},{3,0},{4,5},{5,6},{6,7},{7,4},{8,9},{9,10},{10,1... | collective-permute-start | bytes 1572872 | tf_op jit(solution)/shard_map/ppermute | solution.py:23
  105.3 28.3 %collective-permute-start = (bf16[1,2,128,512]{3,2,1,0:T(8,128)(2,1)}, bf16[1,2,128,512]{3,2,1,0:T(8,128)(2,1)S(1)}, u32[]{:S(2)}, u32[]{:S(2)}) collective-permute-start(bf16[1,2,128,512]{3,2,1,0:T(8,128)(2,1)} %param.7), channel_id=1, source_target_pairs={{0,4},{4,8},{8,12},{12,16},{16,20},{20,24},{24,28},{28,0},{1,5},{5... | collective-permute-start | bytes 786440 | tf_op jit(solution)/shard_map/ppermute | solution.py:23
  128.8 2.2 copy-start.14
  134.2 1.0 copy-start.5
  135.3 1.0 copy-start.8
  136.3 0.9 copy-start.17
  142.5 1.0 copy-start.6
  143.5 1.0 copy-start.9
  146.5 5.5 %copy-start.15 = (bf16[16,512,256]{2,1,0:T(8,128)(2,1)S(1)}, bf16[16,512,256]{2,1,0:T(8,128)(2,1)}, u32[]{:S(2)}) copy-start(bf16[16,512,256]{2,1,0:T(8,128)(2,1)} %all-gather.2.cloned.1.call-done.weight) | copy-start | bytes 12582916
  190.2 30.8 %all-to-all-start.3 = ((bf16[16,128,256]{2,1,0:T(8,128)(2,1)}), bf16[16,128,256]{2,1,0:T(8,128)(2,1)S(1)}, u32[]{:S(2)}, u32[]{:S(2)}) async-start(bf16[16,128,256]{2,1,0:T(8,128)(2,1)} %get-tuple-element.28), calls=%async_computation.4 | async-start | bytes 2097152 | tf_op jit(solution)/shard_map/all_to_all | solution.py:27
  194.5 1.0 copy-start.1
  195.5 1.0 copy-start.3
  221.0 1.0 copy-start.11
  222.1 1.0 copy-start.13
  (8 other events, 6.5 us)
Sparse Core Ops, SparseCore 0:
  10.1 69.6 all-gather.1
  154.7 31.5 reduce-scatter.1

commit v2 on v1

--- a/solution.py
+++ b/solution.py
@@ -8,7 +8,7 @@
 from jax.sharding import PartitionSpec as P
 
 HD = 128
-PARTS = 2
+PARTS = 1
 F32 = jnp.float32
 BF16 = jnp.bfloat16
 NT = (((1,), (1,)), ((), ()))

time: 233 us -> 186 us (0.80)
  blocking collectives: 93.7 us -> 71.7 us
  waiting for transfers between devices: 56.3 us -> 44.7 us
  local copies, waits for them, and re-layouts: 20.9 us -> 14.1 us
  Pallas kernels: 16.9 us -> 13.1 us
    all_to_all x2 -> x1, waiting for transfers between devices: 22.8 us -> 0.01 us  [exchanged(): return lax.all_to_all(slots, 'dp', split_axis=0, concat_axis=0, tiled=True)]
    all_to_all x3 -> x2, blocking collectives: 93.7 us -> 71.7 us  [exchanged(): return lax.all_to_all(slots, 'dp', split_axis=0, concat_axis=0, tiled=True)]
    all_gather x1, waiting for transfers between devices: 0.01 us -> 15.8 us  [on_device(): weight = lax.all_gather(out_weight[0], 'dp')]
    unnamed x46 -> x30, local copies, waits for them, and re-layouts: 20 us -> 13.2 us
    ppermute x5, waiting for transfers between devices: 32.7 us -> 28.2 us  [passed_along(): lax.ppermute(block, axis, [(i, (i + distance) % count) for i in range(cou...]
    all_to_all x2 -> x1, starting transfers between devices: 7.4 us -> 4.3 us  [exchanged(): return lax.all_to_all(slots, 'dp', split_axis=0, concat_axis=0, tiled=True)]
    pallas_call x2 -> x1, Pallas kernels: 6.81 us -> 5.44 us  [attend_part(): pl.pallas_call(functools.partial(attend_kernel, part), out_shape=[query_s...]
  transfers between devices with their start and end apart: 9 -> 8, of which waited for: 5 -> 5; matrix products, arithmetic and copies ran while one was open for 1% -> 1% of each run, Pallas kernels for 4% -> 3%
where the time goes in v2:
time: 186 us; the launch traced here: 185 us
  blocking collectives  71.7 us (39%)
  waiting for transfers between devices  44.7 us (24%)
  starting transfers between devices  26.6 us (14%)
  between operations  14.2 us (8%)
  local copies, waits for them, and re-layouts  14.1 us (8%)
  Pallas kernels  13.1 us (7%)
    all_to_all x2, blocking collectives, exchanged(): return lax.all_to_all(slots, 'dp', split_axis=0, concat_axis=0, tiled=True)  71.7 us
    ppermute x5, waiting for transfers between devices, passed_along(): lax.ppermute(block, axis, [(i, (i + distance) % count) for i in range(cou...  28.2 us
    ppermute x5, starting transfers between devices, passed_along(): lax.ppermute(block, axis, [(i, (i + distance) % count) for i in range(cou...  22.2 us
    all_gather x1, waiting for transfers between devices, on_device(): weight = lax.all_gather(out_weight[0], 'dp')  15.8 us
    unnamed x30, local copies, waits for them, and re-layouts  13.2 us
    pallas_call x1, Pallas kernels, attend_part(): pl.pallas_call(functools.partial(attend_kernel, part), out_shape=[query_s...  5.44 us
    all_to_all x1, starting transfers between devices, exchanged(): return lax.all_to_all(slots, 'dp', split_axis=0, concat_axis=0, tiled=True)  4.3 us
  transfers between devices with their start and end apart: 8, of which 5 were waited for; matrix products, arithmetic and copies ran while one was open for 1% of the time, Pallas kernels for 3%

profile of v2, /device:TPU:1, one launch (start us, length us, event | category | flops | bytes accessed | tf_op | source)
XLA Modules:
  0.0 184.8 jit_solution(6765007839977671619)
XLA Ops:
  8.9 16.3 %all_to_all.16 = s32[16,1,1]{2,1,0:T(1,128)S(1)} all-to-all(s32[16,1,1]{2,1,0:T(1,128)S(1)} %copy.13), channel_id=1, replica_groups=mesh['dp'=16,'section'=8,'tensor'=4] {'dp'}, dimensions={0} | all-to-all | bytes 128 | tf_op jit(solution)/shard_map/all_to_all | solution.py:27
  25.6 1.0 copy-done.5
  26.6 1.0 copy-done.7
  27.6 2.0 %pick_blocks.1 = bf16[16,128,512]{2,1,0:T(8,128)(2,1)} custom-call(s32[16]{0:T(128)S(1)} %reduce.asked, bf16[8,64,512]{2,1,0:T(8,128)(2,1)S(1)} %bitcast.13, bf16[8,64,512]{2,1,0:T(8,128)(2,1)S(1)} %bitcast.15), custom_call_target="tpu_custom_call" | custom-call | bytes 3145728 | tf_op jit(solution)/shard_map/pick_blocks/pallas_call | solution.py:49
  29.7 4.3 %all-to-all-start.1 = ((bf16[16,128,512]{2,1,0:T(8,128)(2,1)}), bf16[16,128,512]{2,1,0:T(8,128)(2,1)S(1)}, u32[]{:S(2)}, u32[]{:S(2)}) async-start(bf16[16,128,512]{2,1,0:T(8,128)(2,1)} %pick_blocks.1), calls=%async_computation.1 | async-start | bytes 4194304 | tf_op jit(solution)/shard_map/all_to_all | solution.py:27
  34.0 9.8 %collective-permute-start.1 = (bf16[1,2,128,1024]{3,2,1,0:T(8,128)(2,1)S(1)}, bf16[1,2,128,1024]{3,2,1,0:T(8,128)(2,1)S(1)}, u32[]{:S(2)}, u32[]{:S(2)}) collective-permute-start(bf16[1,2,128,1024]{3,2,1,0:T(8,128)(2,1)S(1)} %copy-done.14), channel_id=1, source_target_pairs={{0,28},{4,0},{8,4},{12,8},{16,12},{20,16},{24,20},{28,24},{1,29},{... | collective-permute-start | bytes 1572872 | tf_op jit(solution)/shard_map/ppermute | solution.py:23
  43.8 11.1 %collective-permute-done.1 = bf16[1,2,128,1024]{3,2,1,0:T(8,128)(2,1)S(1)} collective-permute-done((bf16[1,2,128,1024]{3,2,1,0:T(8,128)(2,1)S(1)}, bf16[1,2,128,1024]{3,2,1,0:T(8,128)(2,1)S(1)}, u32[]{:S(2)}, u32[]{:S(2)}) %collective-permute-start.1) | collective-permute-done | bytes 524320 | tf_op jit(solution)/shard_map/ppermute | solution.py:23
  54.9 3.1 %collective-permute-start.4 = (bf16[256,1024]{1,0:T(8,128)(2,1)S(1)}, bf16[256,1024]{1,0:T(8,128)(2,1)S(1)}, u32[]{:S(2)}, u32[]{:S(2)}) collective-permute-start(bf16[256,1024]{1,0:T(8,128)(2,1)S(1)} %bitcast.17), channel_id=1, source_target_pairs={{0,1},{1,2},{2,3},{3,0},{4,5},{5,6},{6,7},{7,4},{8,9},{9,10},{10,1... | collective-permute-start | bytes 1572872 | tf_op jit(solution)/shard_map/ppermute | solution.py:23
  58.0 4.4 %collective-permute-start.3 = (bf16[256,1024]{1,0:T(8,128)(2,1)S(1)}, bf16[256,1024]{1,0:T(8,128)(2,1)}, u32[]{:S(2)}, u32[]{:S(2)}) collective-permute-start(bf16[256,1024]{1,0:T(8,128)(2,1)S(1)} %bitcast.18), channel_id=1, source_target_pairs={{0,2},{1,3},{2,0},{3,1},{4,6},{5,7},{6,4},{7,5},{8,10},{9,11},{10,... | collective-permute-start | bytes 1572872 | tf_op jit(solution)/shard_map/ppermute | solution.py:23
  62.4 3.1 %collective-permute-start.2 = (bf16[256,1024]{1,0:T(8,128)(2,1)S(1)}, bf16[256,1024]{1,0:T(8,128)(2,1)}, u32[]{:S(2)}, u32[]{:S(2)}) collective-permute-start(bf16[256,1024]{1,0:T(8,128)(2,1)S(1)} %bitcast.19), channel_id=1, source_target_pairs={{0,3},{1,0},{2,1},{3,2},{4,7},{5,4},{6,5},{7,6},{8,11},{9,8},{10,9... | collective-permute-start | bytes 1572872 | tf_op jit(solution)/shard_map/ppermute | solution.py:23
  65.4 1.9 %collective-permute-start = (bf16[1,2,128,512]{3,2,1,0:T(8,128)(2,1)}, bf16[1,2,128,512]{3,2,1,0:T(8,128)(2,1)S(1)}, u32[]{:S(2)}, u32[]{:S(2)}) collective-permute-start(bf16[1,2,128,512]{3,2,1,0:T(8,128)(2,1)} %param.7), channel_id=1, source_target_pairs={{0,4},{4,8},{8,12},{12,16},{16,20},{20,24},{24,28},{28,0},{1,5},{5... | collective-permute-start | bytes 786440 | tf_op jit(solution)/shard_map/ppermute | solution.py:23
  67.4 3.1 %collective-permute-done.4.grad3 = bf16[256,1024]{1,0:T(8,128)(2,1)S(1)} collective-permute-done((bf16[256,1024]{1,0:T(8,128)(2,1)S(1)}, bf16[256,1024]{1,0:T(8,128)(2,1)S(1)}, u32[]{:S(2)}, u32[]{:S(2)}) %collective-permute-start.4) | collective-permute-done | bytes 524320 | tf_op jit(solution)/shard_map/ppermute | solution.py:23
  70.5 12.2 %collective-permute-done.3.grad2 = bf16[256,1024]{1,0:T(8,128)(2,1)} collective-permute-done((bf16[256,1024]{1,0:T(8,128)(2,1)S(1)}, bf16[256,1024]{1,0:T(8,128)(2,1)}, u32[]{:S(2)}, u32[]{:S(2)}) %collective-permute-start.3) | collective-permute-done | bytes 524320 | tf_op jit(solution)/shard_map/ppermute | solution.py:23
  82.7 1.9 %collective-permute-done.2.grad1 = bf16[256,1024]{1,0:T(8,128)(2,1)} collective-permute-done((bf16[256,1024]{1,0:T(8,128)(2,1)S(1)}, bf16[256,1024]{1,0:T(8,128)(2,1)}, u32[]{:S(2)}, u32[]{:S(2)}) %collective-permute-start.2) | collective-permute-done | bytes 524320 | tf_op jit(solution)/shard_map/ppermute | solution.py:23
  84.5 15.8 %all-gather.2.cloned.1.call-done.weight = bf16[16,512,256]{2,1,0:T(8,128)(2,1)} async-done(((bf16[1,512,256]{2,1,0:T(8,128)(2,1)}), bf16[16,512,256]{2,1,0:T(8,128)(2,1)}) %all-gather.2.cloned.1.call-update) | async-done | bytes 4194320 | tf_op jit(solution)/shard_map/all_gather | solution.py:231
  100.3 2.2 %copy-done.9 = bf16[16,512,256]{2,1,0:T(8,128)(2,1)S(1)} copy-done((bf16[16,512,256]{2,1,0:T(8,128)(2,1)S(1)}, bf16[16,512,256]{2,1,0:T(8,128)(2,1)}, u32[]{:S(2)}) %copy-start.9) | copy-done | bytes 4194328
  102.5 2.5 %back_projection.1 = bf16[256,512]{1,0:T(8,128)(2,1)S(1)} custom-call(s32[1]{0:T(128)} %bitcast.4.spot, bf16[16,512,256]{2,1,0:T(8,128)(2,1)S(1)} %copy-done.9, bf16[256,1024]{1,0:T(8,128)(2,1)S(1)} %bitcast.20, bf16[256,1024]{1,0:T(8,128)(2,1)} %collective-permute-done.2.grad1, bf16[256,1024]{1,0:T(8,128)(2,1)} %collective-permute-done.3.grad2, ...), custom_call_target="tpu_custom_call" | custom-call | flops 2147483648 | bytes 8388608 | tf_op jit(solution)/shard_map/back_projection/pallas_call | solution.py:143
  108.7 5.4 %attend_part0.1 = (bf16[2,128,512]{2,1,0:T(8,128)(2,1)S(1)}, bf16[2,128,512]{2,1,0:T(8,128)(2,1)}, f32[8,64,512]{2,1,0:T(8,128)S(1)}, f32[8,64,512]{2,1,0:T(8,128)S(1)}, bf16[16,128,512]{2,1,0:T(8,128)(2,1)S(1)}) custom-call(s32[2]{0:T(128)S(1)} %copy-done.11, s32[8]{0:T(128)S(1)} %get-tuple-element.19.holder, bf16[2,128,512]{2,1,0:T(8,128)(2,1)S(1)} %bitcast.21, ...), custom_call_target="tpu_custom_call" | custom-call | flops 4294967296 | bytes 8388608 | tf_op jit(solution)/shard_map/attend_part0/pallas_call | solution.py:115
  114.2 1.3 copy-done
  116.5 1.3 projection.1
  117.8 1.3 copy-done.2
  119.1 1.6 copy-done.1
  120.7 55.4 %all_to_all.17.back = bf16[16,128,512]{2,1,0:T(8,128)(2,1)S(1)} all-to-all(bf16[16,128,512]{2,1,0:T(8,128)(2,1)S(1)} %copy-done.1), channel_id=1, replica_groups=mesh['dp'=16,'section'=8,'tensor'=4] {'dp'}, dimensions={0} | all-to-all | bytes 4194304 | tf_op jit(solution)/shard_map/all_to_all | solution.py:27
  176.1 1.9 %combine_part0.1 = (bf16[8,64,512]{2,1,0:T(8,128)(2,1)}, bf16[8,64,512]{2,1,0:T(8,128)(2,1)}) custom-call(s32[16]{0:T(128)S(1)} %reduce.asked, f32[8,64,512]{2,1,0:T(8,128)S(1)} %get-tuple-element.13.own_keys, f32[8,64,512]{2,1,0:T(8,128)S(1)} %copy-done.4, bf16[16,128,512]{2,1,0:T(8,128)(2,1)S(1)} %all_to_all.17.back), custom_call_target="tpu_custom_call" | custom-call | bytes 4194304 | tf_op jit(solution)/shard_map/combine_part0/pallas_call | solution.py:201
  (37 shorter events, 6.8 us)
Async XLA Ops:
  7.2 93.1 %all-gather.2.cloned.1.call-start = ((), (), s32[]{:S(2)}) async-start(), calls=%async_computation.4 | async-start | bytes 4456448 | tf_op jit(solution)/shard_map/all_gather | solution.py:231
  25.5 1.1 copy-start.5
  26.6 1.0 copy-start.7
  29.7 4.4 %copy-start.14 = (bf16[1,2,128,1024]{3,2,1,0:T(8,128)(2,1)S(1)}, bf16[1,2,128,1024]{3,2,1,0:T(8,128)(2,1)}, u32[]{:S(2)}) copy-start(bf16[1,2,128,1024]{3,2,1,0:T(8,128)(2,1)} %param.11) | copy-start | bytes 1572868
  29.7 76.0 %all-to-all-start.1 = ((bf16[16,128,512]{2,1,0:T(8,128)(2,1)}), bf16[16,128,512]{2,1,0:T(8,128)(2,1)S(1)}, u32[]{:S(2)}, u32[]{:S(2)}) async-start(bf16[16,128,512]{2,1,0:T(8,128)(2,1)} %pick_blocks.1), calls=%async_computation.1 | async-start | bytes 4194304 | tf_op jit(solution)/shard_map/all_to_all | solution.py:27
  34.0 144.0 %reduce-scatter.2.cloned.1.call-start = ((), (), s32[]{:S(2)}) async-start(), calls=%async_computation.5 | async-start | bytes 2621440 | tf_op jit(solution)/shard_map/reduce_scatter | solution.py:249
  34.0 20.9 %collective-permute-start.1 = (bf16[1,2,128,1024]{3,2,1,0:T(8,128)(2,1)S(1)}, bf16[1,2,128,1024]{3,2,1,0:T(8,128)(2,1)S(1)}, u32[]{:S(2)}, u32[]{:S(2)}) collective-permute-start(bf16[1,2,128,1024]{3,2,1,0:T(8,128)(2,1)S(1)} %copy-done.14), channel_id=1, source_target_pairs={{0,28},{4,0},{8,4},{12,8},{16,12},{20,16},{24,20},{28,24},{1,29},{... | collective-permute-start | bytes 1572872 | tf_op jit(solution)/shard_map/ppermute | solution.py:23
  54.9 15.6 %collective-permute-start.4 = (bf16[256,1024]{1,0:T(8,128)(2,1)S(1)}, bf16[256,1024]{1,0:T(8,128)(2,1)S(1)}, u32[]{:S(2)}, u32[]{:S(2)}) collective-permute-start(bf16[256,1024]{1,0:T(8,128)(2,1)S(1)} %bitcast.17), channel_id=1, source_target_pairs={{0,1},{1,2},{2,3},{3,0},{4,5},{5,6},{6,7},{7,4},{8,9},{9,10},{10,1... | collective-permute-start | bytes 1572872 | tf_op jit(solution)/shard_map/ppermute | solution.py:23
  58.0 24.7 %collective-permute-start.3 = (bf16[256,1024]{1,0:T(8,128)(2,1)S(1)}, bf16[256,1024]{1,0:T(8,128)(2,1)}, u32[]{:S(2)}, u32[]{:S(2)}) collective-permute-start(bf16[256,1024]{1,0:T(8,128)(2,1)S(1)} %bitcast.18), channel_id=1, source_target_pairs={{0,2},{1,3},{2,0},{3,1},{4,6},{5,7},{6,4},{7,5},{8,10},{9,11},{10,... | collective-permute-start | bytes 1572872 | tf_op jit(solution)/shard_map/ppermute | solution.py:23
  62.4 22.2 %collective-permute-start.2 = (bf16[256,1024]{1,0:T(8,128)(2,1)S(1)}, bf16[256,1024]{1,0:T(8,128)(2,1)}, u32[]{:S(2)}, u32[]{:S(2)}) collective-permute-start(bf16[256,1024]{1,0:T(8,128)(2,1)S(1)} %bitcast.19), channel_id=1, source_target_pairs={{0,3},{1,0},{2,1},{3,2},{4,7},{5,4},{6,5},{7,6},{8,11},{9,8},{10,9... | collective-permute-start | bytes 1572872 | tf_op jit(solution)/shard_map/ppermute | solution.py:23
  65.4 40.3 %collective-permute-start = (bf16[1,2,128,512]{3,2,1,0:T(8,128)(2,1)}, bf16[1,2,128,512]{3,2,1,0:T(8,128)(2,1)S(1)}, u32[]{:S(2)}, u32[]{:S(2)}) collective-permute-start(bf16[1,2,128,512]{3,2,1,0:T(8,128)(2,1)} %param.7), channel_id=1, source_target_pairs={{0,4},{4,8},{8,12},{12,16},{16,20},{20,24},{24,28},{28,0},{1,5},{5... | collective-permute-start | bytes 786440 | tf_op jit(solution)/shard_map/ppermute | solution.py:23
  100.3 2.2 %copy-start.9 = (bf16[16,512,256]{2,1,0:T(8,128)(2,1)S(1)}, bf16[16,512,256]{2,1,0:T(8,128)(2,1)}, u32[]{:S(2)}) copy-start(bf16[16,512,256]{2,1,0:T(8,128)(2,1)} %all-gather.2.cloned.1.call-done.weight) | copy-start | bytes 12582916
  102.5 3.2 %copy-start.11 = (s32[2]{0:T(128)S(1)}, s32[2]{0:T(128)}, u32[]{:S(2)}) copy-start(s32[2]{0:T(128)} %counts.1) | copy-start | bytes 28
  105.0 0.7 copy-start.12
  105.7 1.0 copy-start.6
  106.7 1.0 copy-start.8
  107.8 0.9 copy-start.13
  108.7 7.8 %copy-start.10 = (bf16[16,512,256]{2,1,0:T(8,128)(2,1)S(1)}, bf16[16,512,256]{2,1,0:T(8,128)(2,1)}, u32[]{:S(2)}) copy-start(bf16[16,512,256]{2,1,0:T(8,128)(2,1)} %all-gather.2.cloned.1.call-done.weight) | copy-start | bytes 12582916
  114.2 1.3 copy-start
  115.5 1.0 copy-start.3
  117.8 1.3 copy-start.2
  119.1 1.6 copy-start.1
  120.7 55.4 %copy-start.4 = (f32[8,64,512]{2,1,0:T(8,128)S(1)}, f32[8,64,512]{2,1,0:T(8,128)}, u32[]{:S(2)}) copy-start(f32[8,64,512]{2,1,0:T(8,128)} %copy-done.3) | copy-start | bytes 3145732
Sparse Core Ops, SparseCore 0:
  10.1 90.1 all-gather.1
  119.2 32.0 reduce-scatter.1

commit v3 on v2

v3 whole, which is shorter than its diff:
```python
import jax
import jax.numpy as jnp
from jax import lax
from jax.experimental import pallas as pl
from jax.experimental.pallas import tpu as pltpu
from jax.sharding import PartitionSpec as P

HD = 128
F32 = jnp.float32
BF16 = jnp.bfloat16
NT = (((1,), (1,)), ((), ()))
TN = (((0,), (0,)), ((), ()))
VMEM = pl.BlockSpec(memory_space=pltpu.VMEM)
HBM = pl.BlockSpec(memory_space=pltpu.HBM)
SMEM = pl.BlockSpec(memory_space=pltpu.SMEM)
PARAMS = pltpu.CompilerParams(vmem_limit_bytes=60 * 1024 * 1024)


def passed_along(block, axis, distance):
    count = lax.axis_size(axis)
    return lax.ppermute(block, axis, [(i, (i + distance) % count) for i in range(count)])


def exchanged(slots):
    return lax.all_to_all(slots, "dp", split_axis=0, concat_axis=0, tiled=True)


def cost(flops, nbytes):
    return pl.CostEstimate(flops=int(flops), bytes_accessed=int(nbytes), transcendentals=0)


def pick_kernel(asked, keys, values, slots, sem):
    rows = keys.shape[1]
    copies = []
    for slot in range(slots.shape[0]):
        spot = jnp.maximum(asked[slot], 0)
        copies.append(pltpu.make_async_copy(keys.at[spot], slots.at[slot, pl.ds(0, rows)], sem.at[slot, 0]))
        copies.append(pltpu.make_async_copy(values.at[spot], slots.at[slot, pl.ds(rows, rows)], sem.at[slot, 1]))
    for copy in copies:
        copy.start()
    for copy in copies:
        copy.wait()


def picked_slots(asked, keys, values):
    slot_count = asked.shape[0]
    _, rows, features = keys.shape
    return pl.pallas_call(
        pick_kernel,
        out_shape=jax.ShapeDtypeStruct((slot_count, 2 * rows, features), BF16),
        in_specs=[SMEM, HBM, HBM],
        out_specs=HBM,
        scratch_shapes=[pltpu.SemaphoreType.DMA((slot_count, 2))],
        compiler_params=PARAMS,
        cost_estimate=cost(0, 4 * 2**20),
        name="pick_blocks",
    )(asked, keys, values)


def layer_kernel(
    counts, holder, spot, queries_hbm, keys_hbm, values_hbm, recv_hbm, weight_hbm, grad0, grad1, grad2, grad3,
    terms_hbm, grad_query_hbm, own_keys_hbm, own_values_hbm, slots_hbm,
    queries, keys, values, recv, weight, held, grads, attended, terms, grad_query, own_keys, own_values, slots,
    weight_sem, held_sem, in_sem, recv_sem, own_sem, slot_sem, term_sem, query_sem,
):
    docs = queries.shape[0]
    mem_count, rows, features = keys.shape
    own = mem_count // docs
    neg = holder.shape[0] // docs
    groups, per, _, block = weight.shape
    scale = HD**-0.5
    total = (own + neg) * rows

    group_of = [lax.rem(spot[0] + j, groups) for j in range(groups)]
    in_weight = [
        pltpu.make_async_copy(weight_hbm.at[pl.ds(group_of[j] * per, per)], weight.at[j], weight_sem.at[j])
        for j in range(groups)
    ]
    in_held = [
        pltpu.make_async_copy(ref, held.at[j], held_sem.at[j]) for j, ref in enumerate((grad0, grad1, grad2, grad3))
    ]
    in_rest = [
        pltpu.make_async_copy(source, target, in_sem.at[i])
        for i, (source, target) in enumerate(((queries_hbm, queries), (keys_hbm, keys), (values_hbm, values)))
    ]
    in_recv = [
        pltpu.make_async_copy(recv_hbm.at[holder[e]], recv.at[e], recv_sem.at[e]) for e in range(docs * neg)
    ]
    for j in range(groups):
        in_weight[j].start()
        in_held[j].start()
    for copy in in_rest + in_recv:
        copy.start()

    grad_rows = None
    for j in range(groups):
        in_weight[j].wait()
        in_held[j].wait()
        for c in range(per):
            term = lax.dot_general(
                held[j, :, c * block : (c + 1) * block], weight[j, c], NT, preferred_element_type=F32
            )
            grad_rows = term if grad_rows is None else grad_rows + term
    grads[...] = grad_rows.astype(BF16)

    for copy in in_rest + in_recv:
        copy.wait()
    position = lax.broadcasted_iota(jnp.int32, (total, 1), 0)
    outgoing = []
    for doc in range(docs):
        valid = (position < counts[doc] * rows) | (position >= own * rows)
        query_rows = slice(doc * queries.shape[1], (doc + 1) * queries.shape[1])
        entries = range(doc * neg, (doc + 1) * neg)
        blocks = range(doc * own, (doc + 1) * own)
        for head in range(features // HD):
            at = slice(head * HD, (head + 1) * HD)
            query = queries[doc, :, at]
            grad = grads[query_rows, at]
            key = jnp.concatenate([keys[m, :, at] for m in blocks] + [recv[e, :rows, at] for e in entries], axis=0)
            value = jnp.concatenate([values[m, :, at] for m in blocks] + [recv[e, rows:, at] for e in entries], axis=0)
            scores = lax.dot_general(key, query, NT, preferred_element_type=F32) * scale
            scores = jnp.where(valid, scores, -jnp.inf)
            expo = jnp.exp(scores - jnp.max(scores, axis=0, keepdims=True))
            prob = expo * (1.0 / jnp.sum(expo, axis=0, keepdims=True))
            prob_round = prob.astype(BF16)
            attended[query_rows, at] = lax.dot_general(
                prob_round, value, TN, preferred_element_type=F32
            ).astype(BF16)
            grad_prob = lax.dot_general(value, grad, NT, preferred_element_type=F32)
            delta = jnp.sum(prob * grad_prob, axis=0, keepdims=True)
            grad_score = (prob * (grad_prob - delta)).astype(BF16)
            grad_query[doc, :, at] = (
                lax.dot_general(grad_score, key, TN, preferred_element_type=F32) * scale
            ).astype(BF16)
            grad_key = jnp.dot(grad_score, query, preferred_element_type=F32) * scale
            grad_value = jnp.dot(prob_round, grad, preferred_element_type=F32)
            for m, place in enumerate(blocks):
                here = slice(m * rows, (m + 1) * rows)
                own_keys[place, :, at] = grad_key[here]
                own_values[place, :, at] = grad_value[here]
            for m, entry in enumerate(entries):
                here = slice((own + m) * rows, (own + m + 1) * rows)
                slots[entry, :rows, at] = grad_key[here].astype(BF16)
                slots[entry, rows:, at] = grad_value[here].astype(BF16)
        for e in entries:
            outgoing.append(pltpu.make_async_copy(slots.at[e], slots_hbm.at[holder[e]], slot_sem.at[e]))
        span = pl.ds(doc * own, own)
        outgoing.append(pltpu.make_async_copy(own_keys.at[span], own_keys_hbm.at[span], own_sem.at[doc, 0]))
        outgoing.append(pltpu.make_async_copy(own_values.at[span], own_values_hbm.at[span], own_sem.at[doc, 1]))
        outgoing.append(pltpu.make_async_copy(grad_query.at[doc], grad_query_hbm.at[doc], query_sem.at[doc]))
        for copy in outgoing[-(neg + 3) :]:
            copy.start()

    for j in range(groups):
        for c in range(per):
            term = jnp.dot(attended[...], weight[j, c], preferred_element_type=F32)
            terms[j, :, c * block : (c + 1) * block] = term.astype(BF16)
        outgoing.append(pltpu.make_async_copy(terms.at[j], terms_hbm.at[group_of[j]], term_sem.at[j]))
        outgoing[-1].start()
    for copy in outgoing:
        copy.wait()


def layer(counts, holder, spot, queries, keys, values, recv, weight, held):
    docs, query_count, features = queries.shape
    entries, groups = holder.shape[0], len(held)
    rows, columns = held[0].shape
    dma = pltpu.SemaphoreType.DMA
    return pl.pallas_call(
        layer_kernel,
        out_shape=[
            jax.ShapeDtypeStruct((groups, rows, columns), BF16),
            jax.ShapeDtypeStruct(queries.shape, BF16),
            jax.ShapeDtypeStruct(keys.shape, F32),
            jax.ShapeDtypeStruct(values.shape, F32),
            jax.ShapeDtypeStruct(recv.shape, BF16),
        ],
        in_specs=[SMEM] * 3 + [HBM] * (5 + groups),
        out_specs=[HBM] * 5,
        scratch_shapes=[
            pltpu.VMEM(queries.shape, BF16),
            pltpu.VMEM(keys.shape, BF16),
            pltpu.VMEM(values.shape, BF16),
            pltpu.VMEM((entries, *recv.shape[1:]), BF16),
            pltpu.VMEM((groups, weight.shape[0] // groups, *weight.shape[1:]), BF16),
            pltpu.VMEM((groups, rows, columns), BF16),
            pltpu.VMEM((rows, features), BF16),
            pltpu.VMEM((rows, features), BF16),
            pltpu.VMEM((groups, rows, columns), BF16),
            pltpu.VMEM(queries.shape, BF16),
            pltpu.VMEM(keys.shape, F32),
            pltpu.VMEM(values.shape, F32),
            pltpu.VMEM((entries, *recv.shape[1:]), BF16),
            dma((groups,)),
            dma((groups,)),
            dma((3,)),
            dma((entries,)),
            dma((docs, 2)),
            dma((entries,)),
            dma((groups,)),
            dma((docs,)),
        ],
        compiler_params=PARAMS,
        cost_estimate=cost(5 * 2**30, 16 * 2**20),
        name="layer",
    )(counts, holder, spot, queries, keys, values, recv, weight, *held)


def combine_kernel(asked, own_keys, own_values, back, key_grads, value_grads, key_total, value_total):
    rows = own_keys.shape[1]
    key_total[...] = own_keys[...]
    value_total[...] = own_values[...]
    for slot in range(back.shape[0]):
        spot = asked[slot]

        @pl.when(spot >= 0)
        def _(slot=slot, spot=spot):
            key_total[spot] += back[slot, :rows, :].astype(F32)
            value_total[spot] += back[slot, rows:, :].astype(F32)

    key_grads[...] = key_total[...].astype(BF16)
    value_grads[...] = value_total[...].astype(BF16)


def combined(asked, own_keys, own_values, back):
    shape = jax.ShapeDtypeStruct(own_keys.shape, BF16)
    return pl.pallas_call(
        combine_kernel,
        out_shape=[shape, shape],
        in_specs=[SMEM, VMEM, VMEM, VMEM],
        out_specs=[VMEM, VMEM],
        scratch_shapes=[pltpu.VMEM(own_keys.shape, F32)] * 2,
        compiler_params=PARAMS,
        cost_estimate=cost(0, 4 * 2**20),
        name="combine",
    )(asked, own_keys, own_values, back)


def on_device(sent_queries, mem_keys, mem_values, out_weight, sent_grads, counts, neg_ids):
    keys, values = mem_keys[0], mem_values[0]
    mem_count = keys.shape[0]
    groups = lax.axis_size("dp")
    tensor = lax.axis_size("tensor")
    tensor_spot = lax.axis_index("tensor").astype(jnp.int32).reshape(1)

    flat_ids = neg_ids.reshape(-1)
    holder = flat_ids // mem_count
    spot = flat_ids - holder * mem_count
    named = holder[None, :] == jnp.arange(groups, dtype=jnp.int32)[:, None]
    request = jnp.sum(jnp.where(named, spot[None, :] + 1, 0), axis=1) - 1
    asked = exchanged(request.reshape(groups, 1)).reshape(groups)

    queries = passed_along(sent_queries, "section", 1)[0]
    grads = passed_along(sent_grads, "section", -1)[0]
    docs, query_count, features = queries.shape
    weight = lax.all_gather(out_weight[0], "dp")

    recv = exchanged(picked_slots(asked, keys, values))

    grad_rows = grads.reshape(docs * query_count, grads.shape[2])
    held = [grad_rows] + [passed_along(grad_rows, "tensor", -j) for j in range(1, tensor)]
    terms, query_grads, own_keys, own_values, slots = layer(
        counts, holder, tensor_spot, queries, keys, values, recv, weight, held
    )
    back = exchanged(slots)
    mixed = lax.psum_scatter(terms, "tensor", scatter_dimension=0).reshape(1, docs, query_count, -1)

    key_grads, value_grads = combined(asked, own_keys, own_values, back)
    return mixed, query_grads[None], key_grads[None], value_grads[None]


def solution(mesh):
    rows = P("section", "dp", None, "tensor")
    return jax.shard_map(
        on_device,
        mesh=mesh,
        in_specs=(rows, rows, rows, P("section", "tensor", "dp"), rows, P("dp"), P("dp", None)),
        out_specs=(rows, rows, rows, rows),
        check_vma=False,
    )
```

time: 186 us -> 237 us (1.27)
  Pallas kernels: 13.1 us -> 80.4 us
  waiting for transfers between devices: 44.7 us -> 28.9 us
  local copies, waits for them, and re-layouts: 14.1 us -> 3.76 us
  starting transfers between devices: 26.6 us -> 32.9 us
  blocking collectives: 71.7 us -> 75.4 us
    pallas_call x5 -> x3, Pallas kernels: 13.1 us -> 80.4 us  [the longest x1 65.6 us: picked_slots(): pl.pallas_call(pick_kernel, out_shape=jax.ShapeDtypeStruct((slot_count, 2...]
    all_gather x1, waiting for transfers between devices: 15.8 us -> 0.01 us  [on_device(): weight = lax.all_gather(out_weight[0], 'dp')]
    unnamed x30 -> x14, local copies, waits for them, and re-layouts: 13.2 us -> 2.91 us
    ppermute x5, starting transfers between devices: 22.2 us -> 28.5 us  [passed_along(): lax.ppermute(block, axis, [(i, (i + distance) % count) for i in range(cou...]
    all_to_all x2, blocking collectives: 71.7 us -> 75.4 us  [exchanged(): return lax.all_to_all(slots, 'dp', split_axis=0, concat_axis=0, tiled=True)]
  transfers between devices with their start and end apart: 8 -> 8, of which waited for: 5 -> 4; matrix products, arithmetic and copies ran while one was open for 1% -> 1% of each run, Pallas kernels for 3% -> 29%
where the time goes in v3:
time: 237 us
  Pallas kernels  80.4 us (34%)
  blocking collectives  75.4 us (32%)
  starting transfers between devices  32.9 us (14%)
  waiting for transfers between devices  28.9 us (12%)
  between operations  14.2 us (6%)
  local copies, waits for them, and re-layouts  3.76 us (2%)
    all_to_all x2, blocking collectives, exchanged(): return lax.all_to_all(slots, 'dp', split_axis=0, concat_axis=0, tiled=True)  75.4 us
    pallas_call x1, Pallas kernels, picked_slots(): pl.pallas_call(pick_kernel, out_shape=jax.ShapeDtypeStruct((slot_count, 2...  65.6 us
    ppermute x5, starting transfers between devices, passed_along(): lax.ppermute(block, axis, [(i, (i + distance) % count) for i in range(cou...  28.5 us
    ppermute x5, waiting for transfers between devices, passed_along(): lax.ppermute(block, axis, [(i, (i + distance) % count) for i in range(cou...  28.2 us
    pallas_call x1, Pallas kernels, layer(): pl.pallas_call(layer_kernel, out_shape=[jax.ShapeDtypeStruct((groups, row...  11.1 us
  transfers between devices with their start and end apart: 8, of which 4 were waited for; matrix products, arithmetic and copies ran while one was open for 1% of the time, Pallas kernels for 29%

profile of v3, /device:TPU:1, one launch (start us, length us, event | category | flops | bytes accessed | tf_op | source)
XLA Modules:
  0.0 236.5 jit_solution(14519999829814451936)
XLA Ops:
  7.2 0.0 all-gather.2.cloned.1.call-start
  7.2 0.7 all-gather.2.cloned.1.call-update
  7.9 0.8 reshape.75
  8.7 0.1 select_reduce_fusion
  8.8 0.1 copy.13
  8.9 16.3 %all_to_all.16 = s32[16,1,1]{2,1,0:T(1,128)S(1)} all-to-all(s32[16,1,1]{2,1,0:T(1,128)S(1)} %copy.13), channel_id=1, replica_groups=mesh['dp'=16,'section'=8,'tensor'=4] {'dp'}, dimensions={0} | all-to-all | bytes 128 | tf_op jit(solution)/shard_map/all_to_all | solution.py:25
  25.2 0.9 reduce.asked
  26.0 65.6 %pick_blocks.1 = bf16[16,128,512]{2,1,0:T(8,128)(2,1)} custom-call(s32[16]{0:T(128)} %reduce.asked, bf16[8,64,512]{2,1,0:T(8,128)(2,1)} %bitcast.11, bf16[8,64,512]{2,1,0:T(8,128)(2,1)} %bitcast.13), custom_call_target="tpu_custom_call" | custom-call | bytes 4194304 | tf_op jit(solution)/shard_map/pick_blocks/pallas_call | solution.py:48
  91.7 4.3 %all-to-all-start.1 = ((bf16[16,128,512]{2,1,0:T(8,128)(2,1)}), bf16[16,128,512]{2,1,0:T(8,128)(2,1)S(1)}, u32[]{:S(2)}, u32[]{:S(2)}) async-start(bf16[16,128,512]{2,1,0:T(8,128)(2,1)} %pick_blocks.1), calls=%async_computation.1 | async-start | bytes 4194304 | tf_op jit(solution)/shard_map/all_to_all | solution.py:25
  96.0 0.0 reduce-scatter.2.cloned.1.call-start
  96.0 15.7 %collective-permute-start.1 = (bf16[1,2,128,1024]{3,2,1,0:T(8,128)(2,1)S(1)}, bf16[1,2,128,1024]{3,2,1,0:T(8,128)(2,1)S(1)}, u32[]{:S(2)}, u32[]{:S(2)}) collective-permute-start(bf16[1,2,128,1024]{3,2,1,0:T(8,128)(2,1)S(1)} %copy-done.2), channel_id=1, source_target_pairs={{0,28},{4,0},{8,4},{12,8},{16,12},{20,16},{24,20},{28,24},{1,29},{... | collective-permute-start | bytes 1572872 | tf_op jit(solution)/shard_map/ppermute | solution.py:21
  111.8 11.2 %collective-permute-done.1 = bf16[1,2,128,1024]{3,2,1,0:T(8,128)(2,1)S(1)} collective-permute-done((bf16[1,2,128,1024]{3,2,1,0:T(8,128)(2,1)S(1)}, bf16[1,2,128,1024]{3,2,1,0:T(8,128)(2,1)S(1)}, u32[]{:S(2)}, u32[]{:S(2)}) %collective-permute-start.1) | collective-permute-done | bytes 524320 | tf_op jit(solution)/shard_map/ppermute | solution.py:21
  123.0 3.5 %collective-permute-start.4 = (bf16[256,1024]{1,0:T(8,128)(2,1)S(1)}, bf16[256,1024]{1,0:T(8,128)(2,1)S(1)}, u32[]{:S(2)}, u32[]{:S(2)}) collective-permute-start(bf16[256,1024]{1,0:T(8,128)(2,1)S(1)} %bitcast.15), channel_id=1, source_target_pairs={{0,1},{1,2},{2,3},{3,0},{4,5},{5,6},{6,7},{7,4},{8,9},{9,10},{10,1... | collective-permute-start | bytes 1572872 | tf_op jit(solution)/shard_map/ppermute | solution.py:21
  126.5 4.3 %collective-permute-start.3 = (bf16[256,1024]{1,0:T(8,128)(2,1)S(1)}, bf16[256,1024]{1,0:T(8,128)(2,1)}, u32[]{:S(2)}, u32[]{:S(2)}) collective-permute-start(bf16[256,1024]{1,0:T(8,128)(2,1)S(1)} %bitcast.16), channel_id=1, source_target_pairs={{0,2},{1,3},{2,0},{3,1},{4,6},{5,7},{6,4},{7,5},{8,10},{9,11},{10,... | collective-permute-start | bytes 1572872 | tf_op jit(solution)/shard_map/ppermute | solution.py:21
  130.8 3.1 %collective-permute-start.2 = (bf16[256,1024]{1,0:T(8,128)(2,1)S(1)}, bf16[256,1024]{1,0:T(8,128)(2,1)}, u32[]{:S(2)}, u32[]{:S(2)}) collective-permute-start(bf16[256,1024]{1,0:T(8,128)(2,1)S(1)} %bitcast.17), channel_id=1, source_target_pairs={{0,3},{1,0},{2,1},{3,2},{4,7},{5,4},{6,5},{7,6},{8,11},{9,8},{10,9... | collective-permute-start | bytes 1572872 | tf_op jit(solution)/shard_map/ppermute | solution.py:21
  133.9 1.9 collective-permute-start
  135.9 8.4 %collective-permute-done = bf16[1,2,128,512]{3,2,1,0:T(8,128)(2,1)} collective-permute-done((bf16[1,2,128,512]{3,2,1,0:T(8,128)(2,1)S(1)}, bf16[1,2,128,512]{3,2,1,0:T(8,128)(2,1)}, u32[]{:S(2)}, u32[]{:S(2)}) %collective-permute-start) | collective-permute-done | bytes 262176 | tf_op jit(solution)/shard_map/ppermute | solution.py:21
  144.3 7.1 %collective-permute-done.3.grad2 = bf16[256,1024]{1,0:T(8,128)(2,1)} collective-permute-done((bf16[256,1024]{1,0:T(8,128)(2,1)S(1)}, bf16[256,1024]{1,0:T(8,128)(2,1)}, u32[]{:S(2)}, u32[]{:S(2)}) %collective-permute-start.3) | collective-permute-done | bytes 524320 | tf_op jit(solution)/shard_map/ppermute | solution.py:21
  151.3 1.5 collective-permute-done.2.grad1
  152.8 1.3 copy-done
  154.2 11.1 %layer.1 = (bf16[4,256,1024]{2,1,0:T(8,128)(2,1)}, bf16[2,128,512]{2,1,0:T(8,128)(2,1)}, f32[8,64,512]{2,1,0:T(8,128)}, f32[8,64,512]{2,1,0:T(8,128)}, bf16[16,128,512]{2,1,0:T(8,128)(2,1)}) custom-call(s32[2]{0:T(128)} %counts.1, s32[8]{0:T(128)} %copy-done.6, s32[1]{0:T(128)} %bitcast.spot, bf16[2,128,512]{2,1,0:T(8,128)(2,1)} %bitcast.1.queries_hbm, ...), custom_call_target="tpu_custom_call" | custom-call | flops 5368709120 | bytes 16777216 | tf_op jit(solution)/shard_map/layer/pallas_call | solution.py:169
  165.3 1.6 copy-done.1
  166.9 59.1 %all_to_all.17.back = bf16[16,128,512]{2,1,0:T(8,128)(2,1)} all-to-all(bf16[16,128,512]{2,1,0:T(8,128)(2,1)S(1)} %copy-done.1), channel_id=1, replica_groups=mesh['dp'=16,'section'=8,'tensor'=4] {'dp'}, dimensions={0} | all-to-all | bytes 4194304 | tf_op jit(solution)/shard_map/all_to_all | solution.py:25
  226.0 3.7 %combine.1 = (bf16[8,64,512]{2,1,0:T(8,128)(2,1)}, bf16[8,64,512]{2,1,0:T(8,128)(2,1)}) custom-call(s32[16]{0:T(128)} %reduce.asked, f32[8,64,512]{2,1,0:T(8,128)} %get-tuple-element.13.own_keys, f32[8,64,512]{2,1,0:T(8,128)} %get-tuple-element.14.own_values, bf16[16,128,512]{2,1,0:T(8,128)(2,1)} %all_to_all.17.back), custom_call_target="tpu_custom_call" | custom-call | bytes 4194304 | tf_op jit(solution)/shard_map/combine/pallas_call | solution.py:227
  (19 shorter events, 0.1 us)
Async XLA Ops:
  7.2 145.7 %all-gather.2.cloned.1.call-start = ((), (), s32[]{:S(2)}) async-start(), calls=%async_computation.4 | async-start | bytes 4456448 | tf_op jit(solution)/shard_map/all_gather | solution.py:256
  8.7 83.0 %copy-start.6 = (s32[8]{0:T(128)}, s32[8]{0:T(128)S(1)}, u32[]{:S(2)}) copy-start(s32[8]{0:T(128)S(1)} %get-tuple-element.19.holder) | copy-start | bytes 100
  91.6 4.4 %copy-start.2 = (bf16[1,2,128,1024]{3,2,1,0:T(8,128)(2,1)S(1)}, bf16[1,2,128,1024]{3,2,1,0:T(8,128)(2,1)}, u32[]{:S(2)}) copy-start(bf16[1,2,128,1024]{3,2,1,0:T(8,128)(2,1)} %param.11) | copy-start | bytes 1572868
  91.6 42.3 %copy-start.5 = (bf16[1,2,128,512]{3,2,1,0:T(8,128)(2,1)S(1)}, bf16[1,2,128,512]{3,2,1,0:T(8,128)(2,1)}, u32[]{:S(2)}) copy-start(bf16[1,2,128,512]{3,2,1,0:T(8,128)(2,1)} %param.7) | copy-start | bytes 786436
  91.7 61.2 %all-to-all-start.1 = ((bf16[16,128,512]{2,1,0:T(8,128)(2,1)}), bf16[16,128,512]{2,1,0:T(8,128)(2,1)S(1)}, u32[]{:S(2)}, u32[]{:S(2)}) async-start(bf16[16,128,512]{2,1,0:T(8,128)(2,1)} %pick_blocks.1), calls=%async_computation.1 | async-start | bytes 4194304 | tf_op jit(solution)/shard_map/all_to_all | solution.py:25
  96.0 133.7 %reduce-scatter.2.cloned.1.call-start = ((), (), s32[]{:S(2)}) async-start(), calls=%async_computation.5 | async-start | bytes 2621440 | tf_op jit(solution)/shard_map/reduce_scatter | solution.py:266
  96.0 27.0 %collective-permute-start.1 = (bf16[1,2,128,1024]{3,2,1,0:T(8,128)(2,1)S(1)}, bf16[1,2,128,1024]{3,2,1,0:T(8,128)(2,1)S(1)}, u32[]{:S(2)}, u32[]{:S(2)}) collective-permute-start(bf16[1,2,128,1024]{3,2,1,0:T(8,128)(2,1)S(1)} %copy-done.2), channel_id=1, source_target_pairs={{0,28},{4,0},{8,4},{12,8},{16,12},{20,16},{24,20},{28,24},{1,29},{... | collective-permute-start | bytes 1572872 | tf_op jit(solution)/shard_map/ppermute | solution.py:21
  123.0 29.8 %copy-start.3 = (bf16[1,2,128,1024]{3,2,1,0:T(8,128)(2,1)}, bf16[1,2,128,1024]{3,2,1,0:T(8,128)(2,1)S(1)}, u32[]{:S(2)}) copy-start(bf16[1,2,128,1024]{3,2,1,0:T(8,128)(2,1)S(1)} %collective-permute-done.1) | copy-start | bytes 1572868
  123.0 21.3 %collective-permute-start.4 = (bf16[256,1024]{1,0:T(8,128)(2,1)S(1)}, bf16[256,1024]{1,0:T(8,128)(2,1)S(1)}, u32[]{:S(2)}, u32[]{:S(2)}) collective-permute-start(bf16[256,1024]{1,0:T(8,128)(2,1)S(1)} %bitcast.15), channel_id=1, source_target_pairs={{0,1},{1,2},{2,3},{3,0},{4,5},{5,6},{6,7},{7,4},{8,9},{9,10},{10,1... | collective-permute-start | bytes 1572872 | tf_op jit(solution)/shard_map/ppermute | solution.py:21
  126.5 24.9 %collective-permute-start.3 = (bf16[256,1024]{1,0:T(8,128)(2,1)S(1)}, bf16[256,1024]{1,0:T(8,128)(2,1)}, u32[]{:S(2)}, u32[]{:S(2)}) collective-permute-start(bf16[256,1024]{1,0:T(8,128)(2,1)S(1)} %bitcast.16), channel_id=1, source_target_pairs={{0,2},{1,3},{2,0},{3,1},{4,6},{5,7},{6,4},{7,5},{8,10},{9,11},{10,... | collective-permute-start | bytes 1572872 | tf_op jit(solution)/shard_map/ppermute | solution.py:21
  130.8 22.0 %collective-permute-start.2 = (bf16[256,1024]{1,0:T(8,128)(2,1)S(1)}, bf16[256,1024]{1,0:T(8,128)(2,1)}, u32[]{:S(2)}, u32[]{:S(2)}) collective-permute-start(bf16[256,1024]{1,0:T(8,128)(2,1)S(1)} %bitcast.17), channel_id=1, source_target_pairs={{0,3},{1,0},{2,1},{3,2},{4,7},{5,4},{6,5},{7,6},{8,11},{9,8},{10,9... | collective-permute-start | bytes 1572872 | tf_op jit(solution)/shard_map/ppermute | solution.py:21
  133.9 10.3 %collective-permute-start = (bf16[1,2,128,512]{3,2,1,0:T(8,128)(2,1)S(1)}, bf16[1,2,128,512]{3,2,1,0:T(8,128)(2,1)}, u32[]{:S(2)}, u32[]{:S(2)}) collective-permute-start(bf16[1,2,128,512]{3,2,1,0:T(8,128)(2,1)S(1)} %copy-done.5), channel_id=1, source_target_pairs={{0,4},{4,8},{8,12},{12,16},{16,20},{20,24},{24,28},{28,0},{1,5},{5... | collective-permute-start | bytes 786440 | tf_op jit(solution)/shard_map/ppermute | solution.py:21
  144.3 8.6 %copy-start.4 = (bf16[256,1024]{1,0:T(8,128)(2,1)}, bf16[256,1024]{1,0:T(8,128)(2,1)S(1)}, u32[]{:S(2)}) copy-start(bf16[256,1024]{1,0:T(8,128)(2,1)S(1)} %collective-permute-done.4.grad3) | copy-start | bytes 1572868
  152.8 1.3 copy-start
  165.3 1.6 copy-start.1
Sparse Core Ops, SparseCore 0:
  10.1 89.4 all-gather.1
  165.4 35.9 reduce-scatter.1

commit v4 on v3

v4 whole, which is shorter than its diff:
```python
import jax
import jax.numpy as jnp
from jax import lax
from jax.experimental import pallas as pl
from jax.experimental.pallas import tpu as pltpu
from jax.sharding import PartitionSpec as P

HD = 128
F32 = jnp.float32
BF16 = jnp.bfloat16
NT = (((1,), (1,)), ((), ()))
TN = (((0,), (0,)), ((), ()))
VMEM = pl.BlockSpec(memory_space=pltpu.VMEM)
HBM = pl.BlockSpec(memory_space=pltpu.HBM)
ANY = pl.BlockSpec(memory_space=pl.ANY)
SMEM = pl.BlockSpec(memory_space=pltpu.SMEM)
PARAMS = pltpu.CompilerParams(vmem_limit_bytes=24 * 1024 * 1024)


def passed_along(block, axis, distance):
    count = lax.axis_size(axis)
    return lax.ppermute(block, axis, [(i, (i + distance) % count) for i in range(count)])


def exchanged(slots):
    return lax.all_to_all(slots, "dp", split_axis=0, concat_axis=0, tiled=True)


def in_hbm(array):
    return pltpu.with_memory_space_constraint(array, pltpu.HBM)


def cost(flops, nbytes):
    return pl.CostEstimate(flops=int(flops), bytes_accessed=int(nbytes), transcendentals=0)


def pick_kernel(asked, keys_hbm, values_hbm, slots, keys, values, in_sem, out_sem):
    rows = keys.shape[1]
    in_key = pltpu.make_async_copy(keys_hbm, keys, in_sem.at[0])
    in_value = pltpu.make_async_copy(values_hbm, values, in_sem.at[1])
    in_key.start()
    in_value.start()
    outgoing = []
    for which, (arriving, source) in enumerate(((in_key, keys), (in_value, values))):
        arriving.wait()
        for slot in range(slots.shape[0]):
            spot = jnp.maximum(asked[slot, 0], 0)
            target = slots.at[slot, pl.ds(which * rows, rows)]
            outgoing.append(pltpu.make_async_copy(source.at[spot], target, out_sem.at[slot, which]))
            outgoing[-1].start()
    for copy in outgoing:
        copy.wait()


def picked_slots(asked, keys, values):
    slot_count = asked.shape[0]
    _, rows, features = keys.shape
    return pl.pallas_call(
        pick_kernel,
        out_shape=pltpu.HBM((slot_count, 2 * rows, features), BF16),
        in_specs=[SMEM, HBM, HBM],
        out_specs=HBM,
        scratch_shapes=[
            pltpu.VMEM(keys.shape, BF16),
            pltpu.VMEM(values.shape, BF16),
            pltpu.SemaphoreType.DMA((2,)),
            pltpu.SemaphoreType.DMA((slot_count, 2)),
        ],
        compiler_params=PARAMS,
        cost_estimate=cost(0, 4 * 2**20),
        name="pick_blocks",
    )(asked, in_hbm(keys), in_hbm(values))


def layer_kernel(
    counts, holder, spot, queries_hbm, keys_hbm, values_hbm, recv_hbm, weight_hbm, grad0, grad1, grad2, grad3,
    attended, grad_query_hbm, own_rows_hbm, slots_hbm,
    queries, keys, values, recv, weight, held, grads, grad_query, own_rows, slots,
    weight_sem, held_sem, in_sem, recv_sem, own_sem, slot_sem, query_sem,
):
    docs = queries.shape[0]
    mem_count, rows, features = keys.shape
    own = mem_count // docs
    neg = holder.shape[1]
    groups, per, _, block = weight.shape
    scale = HD**-0.5
    total = (own + neg) * rows

    group_of = [lax.rem(spot[0] + j, groups) for j in range(groups)]
    in_weight = [
        pltpu.make_async_copy(weight_hbm.at[pl.ds(group_of[j] * per, per)], weight.at[j], weight_sem.at[j])
        for j in range(groups)
    ]
    in_held = [
        pltpu.make_async_copy(ref, held.at[j], held_sem.at[j]) for j, ref in enumerate((grad0, grad1, grad2, grad3))
    ]
    in_rest = [
        pltpu.make_async_copy(source, target, in_sem.at[i])
        for i, (source, target) in enumerate(((queries_hbm, queries), (keys_hbm, keys), (values_hbm, values)))
    ]
    in_recv = [
        pltpu.make_async_copy(recv_hbm.at[holder[e // neg, e % neg]], recv.at[e], recv_sem.at[e])
        for e in range(docs * neg)
    ]
    for j in range(groups):
        in_weight[j].start()
        in_held[j].start()
    for copy in in_rest + in_recv:
        copy.start()

    grad_rows = None
    for j in range(groups):
        in_weight[j].wait()
        in_held[j].wait()
        for c in range(per):
            term = lax.dot_general(
                held[j, :, c * block : (c + 1) * block], weight[j, c], NT, preferred_element_type=F32
            )
            grad_rows = term if grad_rows is None else grad_rows + term
    grads[...] = grad_rows.astype(BF16)

    for copy in in_rest + in_recv:
        copy.wait()
    position = lax.broadcasted_iota(jnp.int32, (total, 1), 0)
    outgoing = []
    for doc in range(docs):
        valid = (position < counts[doc] * rows) | (position >= own * rows)
        query_rows = slice(doc * queries.shape[1], (doc + 1) * queries.shape[1])
        entries = range(doc * neg, (doc + 1) * neg)
        blocks = range(doc * own, (doc + 1) * own)
        for head in range(features // HD):
            at = slice(head * HD, (head + 1) * HD)
            query = queries[doc, :, at]
            grad = grads[query_rows, at]
            key = jnp.concatenate([keys[m, :, at] for m in blocks] + [recv[e, :rows, at] for e in entries], axis=0)
            value = jnp.concatenate([values[m, :, at] for m in blocks] + [recv[e, rows:, at] for e in entries], axis=0)
            scores = lax.dot_general(key, query, NT, preferred_element_type=F32) * scale
            scores = jnp.where(valid, scores, -jnp.inf)
            expo = jnp.exp(scores - jnp.max(scores, axis=0, keepdims=True))
            prob = expo * (1.0 / jnp.sum(expo, axis=0, keepdims=True))
            prob_round = prob.astype(BF16)
            attended[query_rows, at] = lax.dot_general(
                prob_round, value, TN, preferred_element_type=F32
            ).astype(BF16)
            grad_prob = lax.dot_general(value, grad, NT, preferred_element_type=F32)
            delta = jnp.sum(prob * grad_prob, axis=0, keepdims=True)
            grad_score = (prob * (grad_prob - delta)).astype(BF16)
            grad_query[doc, :, at] = (
                lax.dot_general(grad_score, key, TN, preferred_element_type=F32) * scale
            ).astype(BF16)
            grad_key = jnp.dot(grad_score, query, preferred_element_type=F32) * scale
            grad_value = jnp.dot(prob_round, grad, preferred_element_type=F32)
            for m, place in enumerate(blocks):
                here = slice(m * rows, (m + 1) * rows)
                own_rows[0, place, :, at] = grad_key[here]
                own_rows[1, place, :, at] = grad_value[here]
            for m in range(neg):
                here = slice((own + m) * rows, (own + m + 1) * rows)
                slots[doc * neg + m, :rows, at] = grad_key[here].astype(BF16)
                slots[doc * neg + m, rows:, at] = grad_value[here].astype(BF16)
        for m in range(neg):
            entry = doc * neg + m
            outgoing.append(pltpu.make_async_copy(slots.at[entry], slots_hbm.at[holder[doc, m]], slot_sem.at[entry]))
        span = pl.ds(doc * own, own)
        outgoing.append(pltpu.make_async_copy(own_rows.at[:, span], own_rows_hbm.at[:, span], own_sem.at[doc]))
        outgoing.append(pltpu.make_async_copy(grad_query.at[doc], grad_query_hbm.at[doc], query_sem.at[doc]))
        for copy in outgoing[-(neg + 2) :]:
            copy.start()

    for copy in outgoing:
        copy.wait()


def layer(counts, holder, spot, queries, keys, values, recv, weight, held):
    docs, query_count, features = queries.shape
    entries, groups = holder.shape[0] * holder.shape[1], len(held)
    rows, columns = held[0].shape
    dma = pltpu.SemaphoreType.DMA
    return pl.pallas_call(
        layer_kernel,
        out_shape=[
            jax.ShapeDtypeStruct((rows, features), BF16),
            pltpu.HBM(queries.shape, BF16),
            pltpu.HBM((2, *keys.shape), F32),
            pltpu.HBM(recv.shape, BF16),
        ],
        in_specs=[SMEM] * 3 + [HBM, HBM, HBM, ANY, HBM] + [HBM] * groups,
        out_specs=[VMEM] + [HBM] * 3,
        scratch_shapes=[
            pltpu.VMEM(queries.shape, BF16),
            pltpu.VMEM(keys.shape, BF16),
            pltpu.VMEM(values.shape, BF16),
            pltpu.VMEM((entries, *recv.shape[1:]), BF16),
            pltpu.VMEM((groups, weight.shape[0] // groups, *weight.shape[1:]), BF16),
            pltpu.VMEM((groups, rows, columns), BF16),
            pltpu.VMEM((rows, features), BF16),
            pltpu.VMEM(queries.shape, BF16),
            pltpu.VMEM((2, *keys.shape), F32),
            pltpu.VMEM((entries, *recv.shape[1:]), BF16),
            dma((groups,)),
            dma((groups,)),
            dma((3,)),
            dma((entries,)),
            dma((docs,)),
            dma((entries,)),
            dma((docs,)),
        ],
        compiler_params=PARAMS,
        cost_estimate=cost(5 * 2**30, 16 * 2**20),
        name="layer",
    )(counts, holder, spot, in_hbm(queries), in_hbm(keys), in_hbm(values), recv, in_hbm(weight), *map(in_hbm, held))


def project_kernel(spot, weight_hbm, attended, out0, out1, out2, out3, weight, sem):
    groups, per, _, block = weight.shape
    outs = (out0, out1, out2, out3)
    copies = []
    for j in range(groups):
        first = lax.rem(spot[0] + j, groups) * per
        copies.append(pltpu.make_async_copy(weight_hbm.at[pl.ds(first, per)], weight.at[j], sem.at[j]))
        copies[j].start()
    for j, out in enumerate(outs):
        copies[j].wait()
        for c in range(per):
            term = jnp.dot(attended[...], weight[j, c], preferred_element_type=F32)
            out[:, c * block : (c + 1) * block] = term.astype(BF16)


def projected(spot, weight, attended, groups):
    per = weight.shape[0] // groups
    shape = jax.ShapeDtypeStruct((attended.shape[0], per * weight.shape[2]), BF16)
    return pl.pallas_call(
        project_kernel,
        out_shape=[shape] * groups,
        in_specs=[SMEM, HBM, VMEM],
        out_specs=[VMEM] * groups,
        scratch_shapes=[
            pltpu.VMEM((groups, per, *weight.shape[1:]), BF16),
            pltpu.SemaphoreType.DMA((groups,)),
        ],
        compiler_params=PARAMS,
        cost_estimate=cost(2 * 2**30, 8 * 2**20),
        name="projection",
    )(spot, in_hbm(weight), attended)


def combine_kernel(asked, own_rows, back, key_grads, value_grads, total):
    rows = own_rows.shape[2]
    total[...] = own_rows[...]
    for slot in range(back.shape[0]):
        spot = asked[slot, 0]

        @pl.when(spot >= 0)
        def _(slot=slot, spot=spot):
            total[0, spot] += back[slot, :rows, :].astype(F32)
            total[1, spot] += back[slot, rows:, :].astype(F32)

    key_grads[...] = total[0].astype(BF16)
    value_grads[...] = total[1].astype(BF16)


def combined(asked, own_rows, back):
    shape = jax.ShapeDtypeStruct(own_rows.shape[1:], BF16)
    return pl.pallas_call(
        combine_kernel,
        out_shape=[shape, shape],
        in_specs=[SMEM, VMEM, VMEM],
        out_specs=[VMEM, VMEM],
        scratch_shapes=[pltpu.VMEM(own_rows.shape, F32)],
        compiler_params=PARAMS,
        cost_estimate=cost(0, 4 * 2**20),
        name="combine",
    )(asked, own_rows, back)


def on_device(sent_queries, mem_keys, mem_values, out_weight, sent_grads, counts, neg_ids):
    keys, values = mem_keys[0], mem_values[0]
    mem_count = keys.shape[0]
    groups = lax.axis_size("dp")
    tensor = lax.axis_size("tensor")
    tensor_spot = lax.axis_index("tensor").astype(jnp.int32).reshape(1)

    holder = neg_ids // mem_count
    spot = neg_ids - holder * mem_count
    named = holder[None] == jnp.arange(groups, dtype=jnp.int32)[:, None, None]
    request = jnp.sum(jnp.where(named, spot[None] + 1, 0), axis=(1, 2)) - 1
    asked = exchanged(request.reshape(groups, 1))

    queries = passed_along(sent_queries, "section", 1)[0]
    grads = passed_along(sent_grads, "section", -1)[0]
    docs, query_count, features = queries.shape
    weight = lax.all_gather(out_weight[0], "dp")

    recv = exchanged(picked_slots(asked, keys, values))

    grad_rows = grads.reshape(docs * query_count, grads.shape[2])
    held = [grad_rows] + [passed_along(grad_rows, "tensor", -j) for j in range(1, tensor)]
    attended, query_grads, own_rows, slots = layer(
        counts, holder, tensor_spot, queries, keys, values, recv, weight, held
    )
    back = exchanged(slots)
    terms = projected(tensor_spot, weight, attended, tensor)
    arrived = [terms[0]] + [passed_along(terms[j], "tensor", j) for j in range(1, tensor)]
    mixed = sum(term.astype(F32) for term in arrived).astype(BF16).reshape(1, docs, query_count, -1)

    key_grads, value_grads = combined(asked, own_rows, back)
    return mixed, query_grads[None], key_grads[None], value_grads[None]


def solution(mesh):
    rows = P("section", "dp", None, "tensor")
    return jax.shard_map(
        on_device,
        mesh=mesh,
        in_specs=(rows, rows, rows, P("section", "tensor", "dp"), rows, P("dp"), P("dp", None)),
        out_specs=(rows, rows, rows, rows),
        check_vma=False,
    )
```

time: 237 us -> 174 us (0.73)
  Pallas kernels: 80.4 us -> 17.9 us
  blocking collectives: 75.4 us -> 16.3 us
  waiting for transfers between devices: 28.9 us -> 80.3 us
  starting transfers between devices: 32.9 us -> 41.1 us
    pallas_call x2 -> x3, Pallas kernels: 76.7 us -> 15.8 us  [the longest x1 9.4 us: layer(): pl.pallas_call(layer_kernel, out_shape=[jax.ShapeDtypeStruct((rows, featu...]
    all_to_all x2 -> x1, blocking collectives: 75.4 us -> 16.3 us  [exchanged(): return lax.all_to_all(slots, 'dp', split_axis=0, concat_axis=0, tiled=True)]
    all_to_all x1 -> x2, waiting for transfers between devices: 0.01 us -> 29.5 us  [exchanged(): return lax.all_to_all(slots, 'dp', split_axis=0, concat_axis=0, tiled=True)]
    ppermute x5 -> x8, waiting for transfers between devices: 28.2 us -> 48.1 us  [passed_along(): lax.ppermute(block, axis, [(i, (i + distance) % count) for i in range(cou...]
    all_to_all x1 -> x2, starting transfers between devices: 4.32 us -> 8.73 us  [exchanged(): return lax.all_to_all(slots, 'dp', split_axis=0, concat_axis=0, tiled=True)]
    ppermute x5 -> x8, starting transfers between devices: 28.5 us -> 32.4 us  [passed_along(): lax.ppermute(block, axis, [(i, (i + distance) % count) for i in range(cou...]
  transfers between devices with their start and end apart: 8 -> 11, of which waited for: 4 -> 10; matrix products, arithmetic and copies ran while one was open for 1% -> 1% of each run, Pallas kernels for 29% -> 4%
where the time goes in v4:
time: 174 us
  waiting for transfers between devices  80.3 us (46%)
  starting transfers between devices  41.1 us (24%)
  Pallas kernels  17.9 us (10%)
  blocking collectives  16.3 us (9%)
  between operations  14.2 us (8%)
  other arithmetic  1.95 us (1%)
    ppermute x8, waiting for transfers between devices, passed_along(): lax.ppermute(block, axis, [(i, (i + distance) % count) for i in range(cou...  48.1 us
    ppermute x8, starting transfers between devices, passed_along(): lax.ppermute(block, axis, [(i, (i + distance) % count) for i in range(cou...  32.4 us
    all_to_all x2, waiting for transfers between devices, exchanged(): return lax.all_to_all(slots, 'dp', split_axis=0, concat_axis=0, tiled=True)  29.5 us
    all_to_all x1, blocking collectives, exchanged(): return lax.all_to_all(slots, 'dp', split_axis=0, concat_axis=0, tiled=True)  16.3 us
    pallas_call x1, Pallas kernels, layer(): pl.pallas_call(layer_kernel, out_shape=[jax.ShapeDtypeStruct((rows, featu...  9.4 us
    all_to_all x2, starting transfers between devices, exchanged(): return lax.all_to_all(slots, 'dp', split_axis=0, concat_axis=0, tiled=True)  8.73 us
  transfers between devices with their start and end apart: 11, of which 10 were waited for; matrix products, arithmetic and copies ran while one was open for 1% of the time, Pallas kernels for 4%

profile of v4, /device:TPU:1, one launch (start us, length us, event | category | flops | bytes accessed | tf_op | source)
XLA Modules:
  0.0 173.5 jit_solution(16826273138633284353)
XLA Ops:
  8.8 16.3 %all_to_all.18 = s32[16,1,1]{2,1,0:T(1,128)S(1)} all-to-all(s32[16,1,1]{2,1,0:T(1,128)S(1)} %copy.19), channel_id=1, replica_groups=mesh['dp'=16,'section'=8,'tensor'=4] {'dp'}, dimensions={0} | all-to-all | bytes 128 | tf_op jit(solution)/shard_map/all_to_all | solution.py:26
  25.1 3.4 %pick_blocks.1 = bf16[16,128,512]{2,1,0:T(8,128)(2,1)} custom-call(s32[16,1]{1,0:T(8,128)S(1)} %bitcast.12, bf16[8,64,512]{2,1,0:T(8,128)(2,1)} %bitcast.15, bf16[8,64,512]{2,1,0:T(8,128)(2,1)} %bitcast.17), custom_call_target="tpu_custom_call" | custom-call | bytes 4194304 | tf_op jit(solution)/shard_map/pick_blocks/pallas_call | solution.py:58
  28.5 4.3 %all-to-all-start.1 = ((bf16[16,128,512]{2,1,0:T(8,128)(2,1)}), bf16[16,128,512]{2,1,0:T(8,128)(2,1)S(1)}, u32[]{:S(2)}, u32[]{:S(2)}) async-start(bf16[16,128,512]{2,1,0:T(8,128)(2,1)} %pick_blocks.1), calls=%async_computation.1 | async-start | bytes 4194304 | tf_op jit(solution)/shard_map/all_to_all | solution.py:26
  32.8 9.8 %collective-permute-start.1 = (bf16[1,2,128,1024]{3,2,1,0:T(8,128)(2,1)S(1)}, bf16[1,2,128,1024]{3,2,1,0:T(8,128)(2,1)S(1)}, u32[]{:S(2)}, u32[]{:S(2)}) collective-permute-start(bf16[1,2,128,1024]{3,2,1,0:T(8,128)(2,1)S(1)} %copy-done.2), channel_id=1, source_target_pairs={{0,28},{4,0},{8,4},{12,8},{16,12},{20,16},{24,20},{28,24},{1,29},{... | collective-permute-start | bytes 1572872 | tf_op jit(solution)/shard_map/ppermute | solution.py:22
  42.6 11.1 %collective-permute-done.1 = bf16[1,2,128,1024]{3,2,1,0:T(8,128)(2,1)S(1)} collective-permute-done((bf16[1,2,128,1024]{3,2,1,0:T(8,128)(2,1)S(1)}, bf16[1,2,128,1024]{3,2,1,0:T(8,128)(2,1)S(1)}, u32[]{:S(2)}, u32[]{:S(2)}) %collective-permute-start.1) | collective-permute-done | bytes 524320 | tf_op jit(solution)/shard_map/ppermute | solution.py:22
  53.7 3.1 %collective-permute-start.4 = (bf16[256,1024]{1,0:T(8,128)(2,1)S(1)}, bf16[256,1024]{1,0:T(8,128)(2,1)S(1)}, u32[]{:S(2)}, u32[]{:S(2)}) collective-permute-start(bf16[256,1024]{1,0:T(8,128)(2,1)S(1)} %bitcast.19), channel_id=1, source_target_pairs={{0,1},{1,2},{2,3},{3,0},{4,5},{5,6},{6,7},{7,4},{8,9},{9,10},{10,1... | collective-permute-start | bytes 1572872 | tf_op jit(solution)/shard_map/ppermute | solution.py:22
  56.8 4.4 %collective-permute-start.3 = (bf16[256,1024]{1,0:T(8,128)(2,1)S(1)}, bf16[256,1024]{1,0:T(8,128)(2,1)}, u32[]{:S(2)}, u32[]{:S(2)}) collective-permute-start(bf16[256,1024]{1,0:T(8,128)(2,1)S(1)} %bitcast.20), channel_id=1, source_target_pairs={{0,2},{1,3},{2,0},{3,1},{4,6},{5,7},{6,4},{7,5},{8,10},{9,11},{10,... | collective-permute-start | bytes 1572872 | tf_op jit(solution)/shard_map/ppermute | solution.py:22
  61.2 3.1 %collective-permute-start.2 = (bf16[256,1024]{1,0:T(8,128)(2,1)S(1)}, bf16[256,1024]{1,0:T(8,128)(2,1)}, u32[]{:S(2)}, u32[]{:S(2)}) collective-permute-start(bf16[256,1024]{1,0:T(8,128)(2,1)S(1)} %bitcast.21), channel_id=1, source_target_pairs={{0,3},{1,0},{2,1},{3,2},{4,7},{5,4},{6,5},{7,6},{8,11},{9,8},{10,9... | collective-permute-start | bytes 1572872 | tf_op jit(solution)/shard_map/ppermute | solution.py:22
  64.3 1.9 %collective-permute-start = (bf16[1,2,128,512]{3,2,1,0:T(8,128)(2,1)S(1)}, bf16[1,2,128,512]{3,2,1,0:T(8,128)(2,1)}, u32[]{:S(2)}, u32[]{:S(2)}) collective-permute-start(bf16[1,2,128,512]{3,2,1,0:T(8,128)(2,1)S(1)} %copy-done.5), channel_id=1, source_target_pairs={{0,4},{4,8},{8,12},{12,16},{16,20},{20,24},{24,28},{28,0},{1,5},{5... | collective-permute-start | bytes 786440 | tf_op jit(solution)/shard_map/ppermute | solution.py:22
  66.2 8.4 %collective-permute-done = bf16[1,2,128,512]{3,2,1,0:T(8,128)(2,1)} collective-permute-done((bf16[1,2,128,512]{3,2,1,0:T(8,128)(2,1)S(1)}, bf16[1,2,128,512]{3,2,1,0:T(8,128)(2,1)}, u32[]{:S(2)}, u32[]{:S(2)}) %collective-permute-start) | collective-permute-done | bytes 262176 | tf_op jit(solution)/shard_map/ppermute | solution.py:22
  74.6 6.9 %collective-permute-done.3.grad2 = bf16[256,1024]{1,0:T(8,128)(2,1)} collective-permute-done((bf16[256,1024]{1,0:T(8,128)(2,1)S(1)}, bf16[256,1024]{1,0:T(8,128)(2,1)}, u32[]{:S(2)}, u32[]{:S(2)}) %collective-permute-start.3) | collective-permute-done | bytes 524320 | tf_op jit(solution)/shard_map/ppermute | solution.py:22
  81.5 1.9 %collective-permute-done.2.grad1 = bf16[256,1024]{1,0:T(8,128)(2,1)} collective-permute-done((bf16[256,1024]{1,0:T(8,128)(2,1)S(1)}, bf16[256,1024]{1,0:T(8,128)(2,1)}, u32[]{:S(2)}, u32[]{:S(2)}) %collective-permute-start.2) | collective-permute-done | bytes 524320 | tf_op jit(solution)/shard_map/ppermute | solution.py:22
  83.3 14.8 %all-to-all-done.1.recv_hbm = bf16[16,128,512]{2,1,0:T(8,128)(2,1)S(1)} async-done(((bf16[16,128,512]{2,1,0:T(8,128)(2,1)}), bf16[16,128,512]{2,1,0:T(8,128)(2,1)S(1)}, u32[]{:S(2)}, u32[]{:S(2)}) %all-to-all-start.1) | async-done | bytes 2097184 | tf_op jit(solution)/shard_map/all_to_all | solution.py:26
  98.1 2.0 %all-gather.2.cloned.1.call-done.weight_hbm = bf16[16,512,256]{2,1,0:T(8,128)(2,1)} async-done(((bf16[1,512,256]{2,1,0:T(8,128)(2,1)}), bf16[16,512,256]{2,1,0:T(8,128)(2,1)}) %all-gather.2.cloned.1.call-update) | async-done | bytes 4194320 | tf_op jit(solution)/shard_map/all_gather | solution.py:292
  100.2 9.4 %layer.1 = (bf16[256,512]{1,0:T(8,128)(2,1)S(1)}, bf16[2,128,512]{2,1,0:T(8,128)(2,1)}, f32[2,8,64,512]{3,2,1,0:T(8,128)}, bf16[16,128,512]{2,1,0:T(8,128)(2,1)}) custom-call(s32[2]{0:T(128)S(1)} %copy-done.1, s32[2,4]{1,0:T(2,128)S(1)} %get-tuple-element.25.holder, s32[1]{0:T(128)} %bitcast.spot, bf16[2,128,512]{2,1,0:T(8,128)(2,1)} %bitcast.1.queries_hbm, ...), custom_call_target="tpu_custom_call" | custom-call | flops 5368709120 | bytes 16777216 | tf_op jit(solution)/shard_map/layer/pallas_call | solution.py:179
  109.6 4.4 %all-to-all-start.2 = ((bf16[16,128,512]{2,1,0:T(8,128)(2,1)}), bf16[16,128,512]{2,1,0:T(8,128)(2,1)S(1)}, u32[]{:S(2)}, u32[]{:S(2)}) async-start(bf16[16,128,512]{2,1,0:T(8,128)(2,1)} %get-tuple-element.21), calls=%async_computation.2 | async-start | bytes 4194304 | tf_op jit(solution)/shard_map/all_to_all | solution.py:26
  114.0 3.0 %projection.1 = (bf16[256,1024]{1,0:T(8,128)(2,1)S(1)}, bf16[256,1024]{1,0:T(8,128)(2,1)S(1)}, bf16[256,1024]{1,0:T(8,128)(2,1)S(1)}, bf16[256,1024]{1,0:T(8,128)(2,1)S(1)}) custom-call(s32[1]{0:T(128)} %bitcast.spot, bf16[16,512,256]{2,1,0:T(8,128)(2,1)} %all-gather.2.cloned.1.call-done.weight_hbm, bf16[256,512]{1,0:T(8,128)(2,1)S(1)} %get-tuple-element.14.attended), custom_call_target="tpu_custom_call" | custom-call | flops 2147483648 | bytes 8388608 | tf_op jit(solution)/shard_map/projection/pallas_call | solution.py:232
  117.0 2.7 %collective-permute-start.5 = (bf16[256,1024]{1,0:T(8,128)(2,1)S(1)}, bf16[256,1024]{1,0:T(8,128)(2,1)S(1)}, u32[]{:S(2)}, u32[]{:S(2)}) collective-permute-start(bf16[256,1024]{1,0:T(8,128)(2,1)S(1)} %get-tuple-element.16), channel_id=1, source_target_pairs={{0,1},{1,2},{2,3},{3,0},{4,5},{5,6},{6,7},{7,4},{8,9},{9,10},{10,1... | collective-permute-start | bytes 1572872 | tf_op jit(solution)/shard_map/ppermute | solution.py:22
  119.8 4.3 %collective-permute-start.6 = (bf16[256,1024]{1,0:T(8,128)(2,1)S(1)}, bf16[256,1024]{1,0:T(8,128)(2,1)S(1)}, u32[]{:S(2)}, u32[]{:S(2)}) collective-permute-start(bf16[256,1024]{1,0:T(8,128)(2,1)S(1)} %get-tuple-element.17), channel_id=1, source_target_pairs={{0,2},{1,3},{2,0},{3,1},{4,6},{5,7},{6,4},{7,5},{8,10},{9,11},{10,... | collective-permute-start | bytes 1572872 | tf_op jit(solution)/shard_map/ppermute | solution.py:22
  124.1 3.1 %collective-permute-start.7 = (bf16[256,1024]{1,0:T(8,128)(2,1)S(1)}, bf16[256,1024]{1,0:T(8,128)(2,1)S(1)}, u32[]{:S(2)}, u32[]{:S(2)}) collective-permute-start(bf16[256,1024]{1,0:T(8,128)(2,1)S(1)} %get-tuple-element.18), channel_id=1, source_target_pairs={{0,3},{1,0},{2,1},{3,2},{4,7},{5,4},{6,5},{7,6},{8,11},{9,8},{10,9... | collective-permute-start | bytes 1572872 | tf_op jit(solution)/shard_map/ppermute | solution.py:22
  127.2 6.4 %collective-permute-done.5 = bf16[256,1024]{1,0:T(8,128)(2,1)S(1)} collective-permute-done((bf16[256,1024]{1,0:T(8,128)(2,1)S(1)}, bf16[256,1024]{1,0:T(8,128)(2,1)S(1)}, u32[]{:S(2)}, u32[]{:S(2)}) %collective-permute-start.5) | collective-permute-done | bytes 524320 | tf_op jit(solution)/shard_map/ppermute | solution.py:22
  133.6 11.8 %collective-permute-done.6 = bf16[256,1024]{1,0:T(8,128)(2,1)S(1)} collective-permute-done((bf16[256,1024]{1,0:T(8,128)(2,1)S(1)}, bf16[256,1024]{1,0:T(8,128)(2,1)S(1)}, u32[]{:S(2)}, u32[]{:S(2)}) %collective-permute-start.6) | collective-permute-done | bytes 524320 | tf_op jit(solution)/shard_map/ppermute | solution.py:22
  148.2 14.7 %all-to-all-done.2.back = bf16[16,128,512]{2,1,0:T(8,128)(2,1)S(1)} async-done(((bf16[16,128,512]{2,1,0:T(8,128)(2,1)}), bf16[16,128,512]{2,1,0:T(8,128)(2,1)S(1)}, u32[]{:S(2)}, u32[]{:S(2)}) %all-to-all-start.2) | async-done | bytes 2097184 | tf_op jit(solution)/shard_map/all_to_all | solution.py:26
  164.5 2.1 %combine.1 = (bf16[8,64,512]{2,1,0:T(8,128)(2,1)}, bf16[8,64,512]{2,1,0:T(8,128)(2,1)}) custom-call(s32[16,1]{1,0:T(8,128)S(1)} %bitcast.13, f32[2,8,64,512]{3,2,1,0:T(8,128)S(1)} %copy-done, bf16[16,128,512]{2,1,0:T(8,128)(2,1)S(1)} %all-to-all-done.2.back), custom_call_target="tpu_custom_call" | custom-call | bytes 4194304 | tf_op jit(solution)/shard_map/combine/pallas_call | solution.py:264
  (21 shorter events, 6.0 us)
Async XLA Ops:
  7.2 93.0 %all-gather.2.cloned.1.call-start = ((), (), s32[]{:S(2)}) async-start(), calls=%async_computation.3 | async-start | bytes 4456448 | tf_op jit(solution)/shard_map/all_gather | solution.py:292
  28.5 4.4 %copy-start.2 = (bf16[1,2,128,1024]{3,2,1,0:T(8,128)(2,1)S(1)}, bf16[1,2,128,1024]{3,2,1,0:T(8,128)(2,1)}, u32[]{:S(2)}) copy-start(bf16[1,2,128,1024]{3,2,1,0:T(8,128)(2,1)} %param.11) | copy-start | bytes 1572868
  28.5 35.8 %copy-start.5 = (bf16[1,2,128,512]{3,2,1,0:T(8,128)(2,1)S(1)}, bf16[1,2,128,512]{3,2,1,0:T(8,128)(2,1)}, u32[]{:S(2)}) copy-start(bf16[1,2,128,512]{3,2,1,0:T(8,128)(2,1)} %param.7) | copy-start | bytes 786436
  28.5 71.7 %copy-start.1 = (s32[2]{0:T(128)S(1)}, s32[2]{0:T(128)}, u32[]{:S(2)}) copy-start(s32[2]{0:T(128)} %counts.1) | copy-start | bytes 28
  28.5 69.6 %all-to-all-start.1 = ((bf16[16,128,512]{2,1,0:T(8,128)(2,1)}), bf16[16,128,512]{2,1,0:T(8,128)(2,1)S(1)}, u32[]{:S(2)}, u32[]{:S(2)}) async-start(bf16[16,128,512]{2,1,0:T(8,128)(2,1)} %pick_blocks.1), calls=%async_computation.1 | async-start | bytes 4194304 | tf_op jit(solution)/shard_map/all_to_all | solution.py:26
  32.8 20.8 %collective-permute-start.1 = (bf16[1,2,128,1024]{3,2,1,0:T(8,128)(2,1)S(1)}, bf16[1,2,128,1024]{3,2,1,0:T(8,128)(2,1)S(1)}, u32[]{:S(2)}, u32[]{:S(2)}) collective-permute-start(bf16[1,2,128,1024]{3,2,1,0:T(8,128)(2,1)S(1)} %copy-done.2), channel_id=1, source_target_pairs={{0,28},{4,0},{8,4},{12,8},{16,12},{20,16},{24,20},{28,24},{1,29},{... | collective-permute-start | bytes 1572872 | tf_op jit(solution)/shard_map/ppermute | solution.py:22
  53.7 46.5 %copy-start.3 = (bf16[1,2,128,1024]{3,2,1,0:T(8,128)(2,1)}, bf16[1,2,128,1024]{3,2,1,0:T(8,128)(2,1)S(1)}, u32[]{:S(2)}) copy-start(bf16[1,2,128,1024]{3,2,1,0:T(8,128)(2,1)S(1)} %collective-permute-done.1) | copy-start | bytes 1572868
  53.7 20.9 %collective-permute-start.4 = (bf16[256,1024]{1,0:T(8,128)(2,1)S(1)}, bf16[256,1024]{1,0:T(8,128)(2,1)S(1)}, u32[]{:S(2)}, u32[]{:S(2)}) collective-permute-start(bf16[256,1024]{1,0:T(8,128)(2,1)S(1)} %bitcast.19), channel_id=1, source_target_pairs={{0,1},{1,2},{2,3},{3,0},{4,5},{5,6},{6,7},{7,4},{8,9},{9,10},{10,1... | collective-permute-start | bytes 1572872 | tf_op jit(solution)/shard_map/ppermute | solution.py:22
  56.8 24.7 %collective-permute-start.3 = (bf16[256,1024]{1,0:T(8,128)(2,1)S(1)}, bf16[256,1024]{1,0:T(8,128)(2,1)}, u32[]{:S(2)}, u32[]{:S(2)}) collective-permute-start(bf16[256,1024]{1,0:T(8,128)(2,1)S(1)} %bitcast.20), channel_id=1, source_target_pairs={{0,2},{1,3},{2,0},{3,1},{4,6},{5,7},{6,4},{7,5},{8,10},{9,11},{10,... | collective-permute-start | bytes 1572872 | tf_op jit(solution)/shard_map/ppermute | solution.py:22
  61.2 22.2 %collective-permute-start.2 = (bf16[256,1024]{1,0:T(8,128)(2,1)S(1)}, bf16[256,1024]{1,0:T(8,128)(2,1)}, u32[]{:S(2)}, u32[]{:S(2)}) collective-permute-start(bf16[256,1024]{1,0:T(8,128)(2,1)S(1)} %bitcast.21), channel_id=1, source_target_pairs={{0,3},{1,0},{2,1},{3,2},{4,7},{5,4},{6,5},{7,6},{8,11},{9,8},{10,9... | collective-permute-start | bytes 1572872 | tf_op jit(solution)/shard_map/ppermute | solution.py:22
  64.3 10.4 %collective-permute-start = (bf16[1,2,128,512]{3,2,1,0:T(8,128)(2,1)S(1)}, bf16[1,2,128,512]{3,2,1,0:T(8,128)(2,1)}, u32[]{:S(2)}, u32[]{:S(2)}) collective-permute-start(bf16[1,2,128,512]{3,2,1,0:T(8,128)(2,1)S(1)} %copy-done.5), channel_id=1, source_target_pairs={{0,4},{4,8},{8,12},{12,16},{16,20},{20,24},{24,28},{28,0},{1,5},{5... | collective-permute-start | bytes 786440 | tf_op jit(solution)/shard_map/ppermute | solution.py:22
  74.6 25.6 %copy-start.4 = (bf16[256,1024]{1,0:T(8,128)(2,1)}, bf16[256,1024]{1,0:T(8,128)(2,1)S(1)}, u32[]{:S(2)}) copy-start(bf16[256,1024]{1,0:T(8,128)(2,1)S(1)} %collective-permute-done.4.grad3) | copy-start | bytes 1572868
  109.6 53.4 %all-to-all-start.2 = ((bf16[16,128,512]{2,1,0:T(8,128)(2,1)}), bf16[16,128,512]{2,1,0:T(8,128)(2,1)S(1)}, u32[]{:S(2)}, u32[]{:S(2)}) async-start(bf16[16,128,512]{2,1,0:T(8,128)(2,1)} %get-tuple-element.21), calls=%async_computation.2 | async-start | bytes 4194304 | tf_op jit(solution)/shard_map/all_to_all | solution.py:26
  117.0 16.6 %collective-permute-start.5 = (bf16[256,1024]{1,0:T(8,128)(2,1)S(1)}, bf16[256,1024]{1,0:T(8,128)(2,1)S(1)}, u32[]{:S(2)}, u32[]{:S(2)}) collective-permute-start(bf16[256,1024]{1,0:T(8,128)(2,1)S(1)} %get-tuple-element.16), channel_id=1, source_target_pairs={{0,1},{1,2},{2,3},{3,0},{4,5},{5,6},{6,7},{7,4},{8,9},{9,10},{10,1... | collective-permute-start | bytes 1572872 | tf_op jit(solution)/shard_map/ppermute | solution.py:22
  119.8 25.6 %collective-permute-start.6 = (bf16[256,1024]{1,0:T(8,128)(2,1)S(1)}, bf16[256,1024]{1,0:T(8,128)(2,1)S(1)}, u32[]{:S(2)}, u32[]{:S(2)}) collective-permute-start(bf16[256,1024]{1,0:T(8,128)(2,1)S(1)} %get-tuple-element.17), channel_id=1, source_target_pairs={{0,2},{1,3},{2,0},{3,1},{4,6},{5,7},{6,4},{7,5},{8,10},{9,11},{10,... | collective-permute-start | bytes 1572872 | tf_op jit(solution)/shard_map/ppermute | solution.py:22
  124.1 23.0 %collective-permute-start.7 = (bf16[256,1024]{1,0:T(8,128)(2,1)S(1)}, bf16[256,1024]{1,0:T(8,128)(2,1)S(1)}, u32[]{:S(2)}, u32[]{:S(2)}) collective-permute-start(bf16[256,1024]{1,0:T(8,128)(2,1)S(1)} %get-tuple-element.18), channel_id=1, source_target_pairs={{0,3},{1,0},{2,1},{3,2},{4,7},{5,4},{6,5},{7,6},{8,11},{9,8},{10,9... | collective-permute-start | bytes 1572872 | tf_op jit(solution)/shard_map/ppermute | solution.py:22
  163.0 1.6 copy-start
Sparse Core Ops, SparseCore 0:
  10.1 90.0 all-gather.1

commit v5 on v4

v5 whole, which is shorter than its diff:
```python
import jax
import jax.numpy as jnp
from jax import lax
from jax.experimental import pallas as pl
from jax.experimental.pallas import tpu as pltpu
from jax.sharding import PartitionSpec as P

HD = 128
F32 = jnp.float32
BF16 = jnp.bfloat16
NT = (((1,), (1,)), ((), ()))
TN = (((0,), (0,)), ((), ()))
VMEM = pl.BlockSpec(memory_space=pltpu.VMEM)
HBM = pl.BlockSpec(memory_space=pltpu.HBM)
ANY = pl.BlockSpec(memory_space=pl.ANY)
SMEM = pl.BlockSpec(memory_space=pltpu.SMEM)
PARAMS = pltpu.CompilerParams(vmem_limit_bytes=16 * 1024 * 1024)


def passed_along(block, axis, distance):
    count = lax.axis_size(axis)
    return lax.ppermute(block, axis, [(i, (i + distance) % count) for i in range(count)])


def exchanged(slots):
    return lax.all_to_all(slots, "dp", split_axis=0, concat_axis=0, tiled=True)


def in_hbm(array):
    return pltpu.with_memory_space_constraint(array, pltpu.HBM)


def cost(flops, nbytes):
    return pl.CostEstimate(flops=int(flops), bytes_accessed=int(nbytes), transcendentals=0)


def pick_kernel(asked, keys_hbm, values_hbm, slots, keys, values, in_sem, out_sem):
    rows = keys.shape[1]
    in_key = pltpu.make_async_copy(keys_hbm, keys, in_sem.at[0])
    in_value = pltpu.make_async_copy(values_hbm, values, in_sem.at[1])
    in_key.start()
    in_value.start()
    outgoing = []
    for which, (arriving, source) in enumerate(((in_key, keys), (in_value, values))):
        arriving.wait()
        for slot in range(slots.shape[0]):
            spot = asked[slot, 0]
            target = slots.at[slot, pl.ds(which * rows, rows)]
            copy = pltpu.make_async_copy(source.at[jnp.maximum(spot, 0)], target, out_sem.at[slot, which])
            pl.when(spot >= 0)(copy.start)
            outgoing.append((spot, copy))
    for spot, copy in outgoing:
        pl.when(spot >= 0)(copy.wait)


def picked_slots(asked, keys, values):
    slot_count = asked.shape[0]
    _, rows, features = keys.shape
    return pl.pallas_call(
        pick_kernel,
        out_shape=pltpu.HBM((slot_count, 2 * rows, features), BF16),
        in_specs=[SMEM, HBM, HBM],
        out_specs=HBM,
        scratch_shapes=[
            pltpu.VMEM(keys.shape, BF16),
            pltpu.VMEM(values.shape, BF16),
            pltpu.SemaphoreType.DMA((2,)),
            pltpu.SemaphoreType.DMA((slot_count, 2)),
        ],
        compiler_params=PARAMS,
        cost_estimate=cost(0, 4 * 2**20),
        name="pick_blocks",
    )(asked, in_hbm(keys), in_hbm(values))


def layer_kernel(
    counts, holder, spot, queries, keys, values, recv, weight_hbm, grad0, grad1, grad2, grad3,
    attended_hbm, grad_query, own_rows_hbm, slots_hbm,
    weight, held, grads, probs, attended, own_rows, slots, weight_sem, held_sem, out_sem, own_sem, slot_sem,
):
    docs, query_count, _ = queries.shape
    mem_count, rows, features = keys.shape
    own = mem_count // docs
    neg = holder.shape[1]
    groups, per, _, block = weight.shape
    heads = features // HD
    scale = HD**-0.5
    total = (own + neg) * rows

    arriving = []
    for j, grad in enumerate((grad0, grad1, grad2, grad3)):
        first = lax.rem(spot[0] + j, groups) * per
        in_weight = pltpu.make_async_copy(weight_hbm.at[pl.ds(first, per)], weight.at[j], weight_sem.at[j])
        in_held = pltpu.make_async_copy(grad, held.at[j], held_sem.at[j])
        in_held.start()
        in_weight.start()
        arriving.append((in_held, in_weight))

    def listed(doc, head):
        at = slice(head * HD, (head + 1) * HD)
        blocks = range(doc * own, (doc + 1) * own)
        senders = [holder[doc, m] for m in range(neg)]
        key = jnp.concatenate([keys[m, :, at] for m in blocks] + [recv[e, :rows, at] for e in senders], axis=0)
        value = jnp.concatenate([values[m, :, at] for m in blocks] + [recv[e, rows:, at] for e in senders], axis=0)
        return at, slice(doc * query_count, (doc + 1) * query_count), key, value

    position = lax.broadcasted_iota(jnp.int32, (total, 1), 0)
    for doc in range(docs):
        valid = (position < counts[doc] * rows) | (position >= own * rows)
        for head in range(heads):
            at, query_rows, key, value = listed(doc, head)
            scores = lax.dot_general(key, queries[doc, :, at], NT, preferred_element_type=F32) * scale
            scores = jnp.where(valid, scores, -jnp.inf)
            expo = jnp.exp(scores - jnp.max(scores, axis=0, keepdims=True))
            prob = expo * (1.0 / jnp.sum(expo, axis=0, keepdims=True))
            probs[doc * heads + head] = prob
            attended[query_rows, at] = lax.dot_general(
                prob.astype(BF16), value, TN, preferred_element_type=F32
            ).astype(BF16)

    outgoing = [pltpu.make_async_copy(attended, attended_hbm, out_sem)]
    outgoing[0].start()

    grad_rows = None
    for j, copies in enumerate(arriving):
        for copy in copies:
            copy.wait()
        for c in range(per):
            term = lax.dot_general(
                held[j, :, c * block : (c + 1) * block], weight[j, c], NT, preferred_element_type=F32
            )
            grad_rows = term if grad_rows is None else grad_rows + term
    grads[...] = grad_rows.astype(BF16)

    for doc in range(docs):
        for head in range(heads):
            at, query_rows, key, value = listed(doc, head)
            grad = grads[query_rows, at]
            prob = probs[doc * heads + head]
            grad_prob = lax.dot_general(value, grad, NT, preferred_element_type=F32)
            delta = jnp.sum(prob * grad_prob, axis=0, keepdims=True)
            grad_score = (prob * (grad_prob - delta)).astype(BF16)
            grad_value = jnp.dot(prob.astype(BF16), grad, preferred_element_type=F32)
            grad_key = jnp.dot(grad_score, queries[doc, :, at], preferred_element_type=F32) * scale
            grad_query[doc, :, at] = (
                lax.dot_general(grad_score, key, TN, preferred_element_type=F32) * scale
            ).astype(BF16)
            for m in range(own):
                here = slice(m * rows, (m + 1) * rows)
                own_rows[0, doc * own + m, :, at] = grad_key[here]
                own_rows[1, doc * own + m, :, at] = grad_value[here]
            for m in range(neg):
                here = slice((own + m) * rows, (own + m + 1) * rows)
                slots[doc * neg + m, :rows, at] = grad_key[here].astype(BF16)
                slots[doc * neg + m, rows:, at] = grad_value[here].astype(BF16)
        for m in range(neg):
            entry = doc * neg + m
            outgoing.append(pltpu.make_async_copy(slots.at[entry], slots_hbm.at[holder[doc, m]], slot_sem.at[entry]))
        span = pl.ds(doc * own, own)
        outgoing.append(pltpu.make_async_copy(own_rows.at[:, span], own_rows_hbm.at[:, span], own_sem.at[doc]))
        for copy in outgoing[-(neg + 1) :]:
            copy.start()
    for copy in outgoing:
        copy.wait()


def layer(counts, holder, spot, queries, keys, values, recv, weight, held):
    docs, query_count, features = queries.shape
    entries, groups = holder.shape[0] * holder.shape[1], len(held)
    rows, columns = held[0].shape
    dma = pltpu.SemaphoreType.DMA
    return pl.pallas_call(
        layer_kernel,
        out_shape=[
            pltpu.HBM((rows, features), BF16),
            jax.ShapeDtypeStruct(queries.shape, BF16),
            pltpu.HBM((2, *keys.shape), F32),
            pltpu.HBM(recv.shape, BF16),
        ],
        in_specs=[SMEM] * 3 + [VMEM] * 4 + [HBM] * (1 + groups),
        out_specs=[HBM, VMEM, HBM, HBM],
        scratch_shapes=[
            pltpu.VMEM((groups, weight.shape[0] // groups, *weight.shape[1:]), BF16),
            pltpu.VMEM((groups, rows, columns), BF16),
            pltpu.VMEM((rows, features), BF16),
            pltpu.VMEM((docs * features // HD, (keys.shape[0] // docs + holder.shape[1]) * keys.shape[1], query_count), F32),
            pltpu.VMEM((rows, features), BF16),
            pltpu.VMEM((2, *keys.shape), F32),
            pltpu.VMEM((entries, *recv.shape[1:]), BF16),
            dma((groups,)),
            dma((groups,)),
            dma,
            dma((docs,)),
            dma((entries,)),
        ],
        compiler_params=PARAMS,
        cost_estimate=cost(5 * 2**30, 16 * 2**20),
        name="layer",
    )(counts, holder, spot, queries, keys, values, recv, in_hbm(weight), *map(in_hbm, held))


def project_kernel(spot, weight_hbm, attended_hbm, out0, out1, out2, out3, weight, attended, sem, in_sem):
    groups, per, _, block = weight.shape
    outs = (out0, out1, out2, out3)
    in_attended = pltpu.make_async_copy(attended_hbm, attended, in_sem)
    in_attended.start()
    copies = []
    for j in range(groups):
        first = lax.rem(spot[0] + j, groups) * per
        copies.append(pltpu.make_async_copy(weight_hbm.at[pl.ds(first, per)], weight.at[j], sem.at[j]))
        copies[j].start()
    in_attended.wait()
    for j, out in enumerate(outs):
        copies[j].wait()
        for c in range(per):
            term = jnp.dot(attended[...], weight[j, c], preferred_element_type=F32)
            out[:, c * block : (c + 1) * block] = term.astype(BF16)


def projected(spot, weight, attended, groups):
    per = weight.shape[0] // groups
    shape = jax.ShapeDtypeStruct((attended.shape[0], per * weight.shape[2]), BF16)
    return pl.pallas_call(
        project_kernel,
        out_shape=[shape] * groups,
        in_specs=[SMEM, HBM, HBM],
        out_specs=[VMEM] * groups,
        scratch_shapes=[
            pltpu.VMEM((groups, per, *weight.shape[1:]), BF16),
            pltpu.VMEM(attended.shape, BF16),
            pltpu.SemaphoreType.DMA((groups,)),
            pltpu.SemaphoreType.DMA,
        ],
        compiler_params=PARAMS,
        cost_estimate=cost(2 * 2**30, 8 * 2**20),
        name="projection",
    )(spot, in_hbm(weight), in_hbm(attended))


def combine_kernel(asked, own_rows_hbm, back, key_grads_hbm, value_grads_hbm, own_rows, total, grads, in_sem, out_sem):
    rows = own_rows.shape[2]
    arriving = [pltpu.make_async_copy(own_rows_hbm.at[i], own_rows.at[i], in_sem.at[i]) for i in range(2)]
    for copy in arriving:
        copy.start()
    total[...] = jnp.zeros_like(total)
    for slot in range(back.shape[0]):
        spot = asked[slot, 0]

        @pl.when(spot >= 0)
        def _(slot=slot, spot=spot):
            total[0, spot] += back[slot, :rows, :].astype(F32)
            total[1, spot] += back[slot, rows:, :].astype(F32)

    outgoing = []
    for i, target in enumerate((key_grads_hbm, value_grads_hbm)):
        arriving[i].wait()
        grads[i] = (own_rows[i] + total[i]).astype(BF16)
        outgoing.append(pltpu.make_async_copy(grads.at[i], target, out_sem.at[i]))
        outgoing[i].start()
    for copy in outgoing:
        copy.wait()


def combined(asked, own_rows, back):
    shape = pltpu.HBM(own_rows.shape[1:], BF16)
    return pl.pallas_call(
        combine_kernel,
        out_shape=[shape, shape],
        in_specs=[SMEM, HBM, VMEM],
        out_specs=[HBM, HBM],
        scratch_shapes=[
            pltpu.VMEM(own_rows.shape, F32),
            pltpu.VMEM(own_rows.shape, F32),
            pltpu.VMEM(own_rows.shape, BF16),
            pltpu.SemaphoreType.DMA((2,)),
            pltpu.SemaphoreType.DMA((2,)),
        ],
        compiler_params=PARAMS,
        cost_estimate=cost(0, 4 * 2**20),
        name="combine",
    )(asked, in_hbm(own_rows), back)


def on_device(sent_queries, mem_keys, mem_values, out_weight, sent_grads, counts, neg_ids):
    keys, values = mem_keys[0], mem_values[0]
    mem_count = keys.shape[0]
    groups = lax.axis_size("dp")
    tensor = lax.axis_size("tensor")
    tensor_spot = lax.axis_index("tensor").astype(jnp.int32).reshape(1)

    holder = neg_ids // mem_count
    spot = neg_ids - holder * mem_count
    named = holder[None] == jnp.arange(groups, dtype=jnp.int32)[:, None, None]
    request = jnp.sum(jnp.where(named, spot[None] + 1, 0), axis=(1, 2)) - 1
    asked = exchanged(request.reshape(groups, 1))

    queries = passed_along(sent_queries, "section", 1)[0]
    grads = passed_along(sent_grads, "section", -1)[0]
    docs, query_count, features = queries.shape
    weight = lax.all_gather(out_weight[0], "dp")

    recv = exchanged(picked_slots(asked, keys, values))

    grad_rows = grads.reshape(docs * query_count, grads.shape[2])
    held = [grad_rows] + [passed_along(grad_rows, "tensor", -j) for j in range(1, tensor)]
    attended, query_grads, own_rows, slots = layer(
        counts, holder, tensor_spot, queries, keys, values, recv, weight, held
    )
    back = exchanged(slots)
    terms = projected(tensor_spot, weight, attended, tensor)
    arrived = [terms[0]] + [passed_along(terms[j], "tensor", j) for j in range(1, tensor)]
    mixed = sum(term.astype(F32) for term in arrived).astype(BF16).reshape(1, docs, query_count, -1)

    key_grads, value_grads = combined(asked, own_rows, back)
    return mixed, query_grads[None], key_grads[None], value_grads[None]


def solution(mesh):
    rows = P("section", "dp", None, "tensor")
    return jax.shard_map(
        on_device,
        mesh=mesh,
        in_specs=(rows, rows, rows, P("section", "tensor", "dp"), rows, P("dp"), P("dp", None)),
        out_specs=(rows, rows, rows, rows),
        check_vma=False,
    )
```

time: 174 us -> 174 us (level)
  Pallas kernels: 17.9 us -> 19.7 us
where the time goes in v5:
time: 174 us; the launch traced here: 173 us
  waiting for transfers between devices  79.5 us (46%)
  starting transfers between devices  41.4 us (24%)
  Pallas kernels  19.7 us (11%)
  blocking collectives  16.3 us (9%)
  between operations  14.2 us (8%)
  other arithmetic  1.95 us (1%)
    ppermute x8, waiting for transfers between devices, passed_along(): lax.ppermute(block, axis, [(i, (i + distance) % count) for i in range(cou...  48.5 us
    ppermute x8, starting transfers between devices, passed_along(): lax.ppermute(block, axis, [(i, (i + distance) % count) for i in range(cou...  32.6 us
    all_to_all x2, waiting for transfers between devices, exchanged(): return lax.all_to_all(slots, 'dp', split_axis=0, concat_axis=0, tiled=True)  27.9 us
    all_to_all x1, blocking collectives, exchanged(): return lax.all_to_all(slots, 'dp', split_axis=0, concat_axis=0, tiled=True)  16.3 us
    pallas_call x1, Pallas kernels, layer(): pl.pallas_call(layer_kernel, out_shape=[pltpu.HBM((rows, features), BF16)...  9.69 us
    all_to_all x2, starting transfers between devices, exchanged(): return lax.all_to_all(slots, 'dp', split_axis=0, concat_axis=0, tiled=True)  8.78 us
    pallas_call x1, Pallas kernels, projected(): pl.pallas_call(project_kernel, out_shape=[shape] * groups, in_specs=[SMEM...  3.71 us
  transfers between devices with their start and end apart: 11, of which 10 were waited for; matrix products, arithmetic and copies ran while one was open for 1% of the time, Pallas kernels for 4%

profile of v5, /device:TPU:1, one launch (start us, length us, event | category | flops | bytes accessed | tf_op | source)
XLA Modules:
  0.0 173.0 jit_solution(5957782682255257025)
XLA Ops:
  8.8 16.3 %all_to_all.18 = s32[16,1,1]{2,1,0:T(1,128)S(1)} all-to-all(s32[16,1,1]{2,1,0:T(1,128)S(1)} %copy.19), channel_id=1, replica_groups=mesh['dp'=16,'section'=8,'tensor'=4] {'dp'}, dimensions={0} | all-to-all | bytes 128 | tf_op jit(solution)/shard_map/all_to_all | solution.py:26
  25.1 3.1 %pick_blocks.1 = bf16[16,128,512]{2,1,0:T(8,128)(2,1)} custom-call(s32[16,1]{1,0:T(8,128)S(1)} %bitcast.16, bf16[8,64,512]{2,1,0:T(8,128)(2,1)} %bitcast.12, bf16[8,64,512]{2,1,0:T(8,128)(2,1)} %bitcast.14), custom_call_target="tpu_custom_call" | custom-call | bytes 4194304 | tf_op jit(solution)/shard_map/pick_blocks/pallas_call | solution.py:59
  28.3 4.3 %all-to-all-start.1 = ((bf16[16,128,512]{2,1,0:T(8,128)(2,1)}), bf16[16,128,512]{2,1,0:T(8,128)(2,1)S(1)}, u32[]{:S(2)}, u32[]{:S(2)}) async-start(bf16[16,128,512]{2,1,0:T(8,128)(2,1)} %pick_blocks.1), calls=%async_computation.1 | async-start | bytes 4194304 | tf_op jit(solution)/shard_map/all_to_all | solution.py:26
  32.5 9.7 %collective-permute-start.1 = (bf16[1,2,128,1024]{3,2,1,0:T(8,128)(2,1)}, bf16[1,2,128,1024]{3,2,1,0:T(8,128)(2,1)}, u32[]{:S(2)}, u32[]{:S(2)}) collective-permute-start(bf16[1,2,128,1024]{3,2,1,0:T(8,128)(2,1)} %param.11), channel_id=1, source_target_pairs={{0,28},{4,0},{8,4},{12,8},{16,12},{20,16},{24,20},{28,24},{1,29},{... | collective-permute-start | bytes 1572872 | tf_op jit(solution)/shard_map/ppermute | solution.py:22
  42.3 11.4 %collective-permute-done.1 = bf16[1,2,128,1024]{3,2,1,0:T(8,128)(2,1)} collective-permute-done((bf16[1,2,128,1024]{3,2,1,0:T(8,128)(2,1)}, bf16[1,2,128,1024]{3,2,1,0:T(8,128)(2,1)}, u32[]{:S(2)}, u32[]{:S(2)}) %collective-permute-start.1) | collective-permute-done | bytes 524320 | tf_op jit(solution)/shard_map/ppermute | solution.py:22
  53.7 3.1 %collective-permute-start.4 = (bf16[256,1024]{1,0:T(8,128)(2,1)}, bf16[256,1024]{1,0:T(8,128)(2,1)}, u32[]{:S(2)}, u32[]{:S(2)}) collective-permute-start(bf16[256,1024]{1,0:T(8,128)(2,1)} %bitcast.6.grad0), channel_id=1, source_target_pairs={{0,1},{1,2},{2,3},{3,0},{4,5},{5,6},{6,7},{7,4},{8,9},{9,10},{10,1... | collective-permute-start | bytes 1572872 | tf_op jit(solution)/shard_map/ppermute | solution.py:22
  56.8 4.4 %collective-permute-start.3 = (bf16[256,1024]{1,0:T(8,128)(2,1)}, bf16[256,1024]{1,0:T(8,128)(2,1)}, u32[]{:S(2)}, u32[]{:S(2)}) collective-permute-start(bf16[256,1024]{1,0:T(8,128)(2,1)} %bitcast.6.grad0), channel_id=1, source_target_pairs={{0,2},{1,3},{2,0},{3,1},{4,6},{5,7},{6,4},{7,5},{8,10},{9,11},{10,... | collective-permute-start | bytes 1572872 | tf_op jit(solution)/shard_map/ppermute | solution.py:22
  61.1 3.1 %collective-permute-start.2 = (bf16[256,1024]{1,0:T(8,128)(2,1)}, bf16[256,1024]{1,0:T(8,128)(2,1)}, u32[]{:S(2)}, u32[]{:S(2)}) collective-permute-start(bf16[256,1024]{1,0:T(8,128)(2,1)} %bitcast.6.grad0), channel_id=1, source_target_pairs={{0,3},{1,0},{2,1},{3,2},{4,7},{5,4},{6,5},{7,6},{8,11},{9,8},{10,9... | collective-permute-start | bytes 1572872 | tf_op jit(solution)/shard_map/ppermute | solution.py:22
  64.2 1.9 %collective-permute-start = (bf16[1,2,128,512]{3,2,1,0:T(8,128)(2,1)}, bf16[1,2,128,512]{3,2,1,0:T(8,128)(2,1)S(1)}, u32[]{:S(2)}, u32[]{:S(2)}) collective-permute-start(bf16[1,2,128,512]{3,2,1,0:T(8,128)(2,1)} %param.7), channel_id=1, source_target_pairs={{0,4},{4,8},{8,12},{12,16},{16,20},{20,24},{24,28},{28,0},{1,5},{5... | collective-permute-start | bytes 786440 | tf_op jit(solution)/shard_map/ppermute | solution.py:22
  66.1 8.4 %collective-permute-done = bf16[1,2,128,512]{3,2,1,0:T(8,128)(2,1)S(1)} collective-permute-done((bf16[1,2,128,512]{3,2,1,0:T(8,128)(2,1)}, bf16[1,2,128,512]{3,2,1,0:T(8,128)(2,1)S(1)}, u32[]{:S(2)}, u32[]{:S(2)}) %collective-permute-start) | collective-permute-done | bytes 262176 | tf_op jit(solution)/shard_map/ppermute | solution.py:22
  74.6 7.1 %collective-permute-done.3.grad2 = bf16[256,1024]{1,0:T(8,128)(2,1)} collective-permute-done((bf16[256,1024]{1,0:T(8,128)(2,1)}, bf16[256,1024]{1,0:T(8,128)(2,1)}, u32[]{:S(2)}, u32[]{:S(2)}) %collective-permute-start.3) | collective-permute-done | bytes 524320 | tf_op jit(solution)/shard_map/ppermute | solution.py:22
  81.7 2.0 %collective-permute-done.2.grad1 = bf16[256,1024]{1,0:T(8,128)(2,1)} collective-permute-done((bf16[256,1024]{1,0:T(8,128)(2,1)}, bf16[256,1024]{1,0:T(8,128)(2,1)}, u32[]{:S(2)}, u32[]{:S(2)}) %collective-permute-start.2) | collective-permute-done | bytes 524320 | tf_op jit(solution)/shard_map/ppermute | solution.py:22
  83.6 13.9 %all-to-all-done.1.recv = bf16[16,128,512]{2,1,0:T(8,128)(2,1)S(1)} async-done(((bf16[16,128,512]{2,1,0:T(8,128)(2,1)}), bf16[16,128,512]{2,1,0:T(8,128)(2,1)S(1)}, u32[]{:S(2)}, u32[]{:S(2)}) %all-to-all-start.1) | async-done | bytes 2097184 | tf_op jit(solution)/shard_map/all_to_all | solution.py:26
  97.5 2.4 %all-gather.2.cloned.1.call-done.weight_hbm = bf16[16,512,256]{2,1,0:T(8,128)(2,1)} async-done(((bf16[1,512,256]{2,1,0:T(8,128)(2,1)}), bf16[16,512,256]{2,1,0:T(8,128)(2,1)}) %all-gather.2.cloned.1.call-update) | async-done | bytes 4194320 | tf_op jit(solution)/shard_map/all_gather | solution.py:300
  99.9 9.7 %layer.1 = (bf16[256,512]{1,0:T(8,128)(2,1)}, bf16[2,128,512]{2,1,0:T(8,128)(2,1)}, f32[2,8,64,512]{3,2,1,0:T(8,128)}, bf16[16,128,512]{2,1,0:T(8,128)(2,1)}) custom-call(s32[2]{0:T(128)S(1)} %copy-done.2, s32[2,4]{1,0:T(2,128)S(1)} %get-tuple-element.25.holder, s32[1]{0:T(128)} %bitcast.spot, bf16[2,128,512]{2,1,0:T(8,128)(2,1)S(1)} %bitcast.18, ...), custom_call_target="tpu_custom_call" | custom-call | flops 5368709120 | bytes 16777216 | tf_op jit(solution)/shard_map/layer/pallas_call | solution.py:172
  109.6 4.5 %all-to-all-start.2 = ((bf16[16,128,512]{2,1,0:T(8,128)(2,1)}), bf16[16,128,512]{2,1,0:T(8,128)(2,1)S(1)}, u32[]{:S(2)}, u32[]{:S(2)}) async-start(bf16[16,128,512]{2,1,0:T(8,128)(2,1)} %get-tuple-element.21), calls=%async_computation.2 | async-start | bytes 4194304 | tf_op jit(solution)/shard_map/all_to_all | solution.py:26
  114.1 3.7 %projection.1 = (bf16[256,1024]{1,0:T(8,128)(2,1)S(1)}, bf16[256,1024]{1,0:T(8,128)(2,1)S(1)}, bf16[256,1024]{1,0:T(8,128)(2,1)S(1)}, bf16[256,1024]{1,0:T(8,128)(2,1)S(1)}) custom-call(s32[1]{0:T(128)} %bitcast.spot, bf16[16,512,256]{2,1,0:T(8,128)(2,1)} %all-gather.2.cloned.1.call-done.weight_hbm, bf16[256,512]{1,0:T(8,128)(2,1)} %get-tuple-element.14.attended_hbm), custom_call_target="tpu_custom_call" | custom-call | flops 2147483648 | bytes 8388608 | tf_op jit(solution)/shard_map/projection/pallas_call | solution.py:223
  117.8 3.0 %collective-permute-start.5 = (bf16[256,1024]{1,0:T(8,128)(2,1)S(1)}, bf16[256,1024]{1,0:T(8,128)(2,1)S(1)}, u32[]{:S(2)}, u32[]{:S(2)}) collective-permute-start(bf16[256,1024]{1,0:T(8,128)(2,1)S(1)} %get-tuple-element.16), channel_id=1, source_target_pairs={{0,1},{1,2},{2,3},{3,0},{4,5},{5,6},{6,7},{7,4},{8,9},{9,10},{10,1... | collective-permute-start | bytes 1572872 | tf_op jit(solution)/shard_map/ppermute | solution.py:22
  120.8 4.3 %collective-permute-start.6 = (bf16[256,1024]{1,0:T(8,128)(2,1)S(1)}, bf16[256,1024]{1,0:T(8,128)(2,1)S(1)}, u32[]{:S(2)}, u32[]{:S(2)}) collective-permute-start(bf16[256,1024]{1,0:T(8,128)(2,1)S(1)} %get-tuple-element.17), channel_id=1, source_target_pairs={{0,2},{1,3},{2,0},{3,1},{4,6},{5,7},{6,4},{7,5},{8,10},{9,11},{10,... | collective-permute-start | bytes 1572872 | tf_op jit(solution)/shard_map/ppermute | solution.py:22
  125.1 3.1 %collective-permute-start.7 = (bf16[256,1024]{1,0:T(8,128)(2,1)S(1)}, bf16[256,1024]{1,0:T(8,128)(2,1)S(1)}, u32[]{:S(2)}, u32[]{:S(2)}) collective-permute-start(bf16[256,1024]{1,0:T(8,128)(2,1)S(1)} %get-tuple-element.18), channel_id=1, source_target_pairs={{0,3},{1,0},{2,1},{3,2},{4,7},{5,4},{6,5},{7,6},{8,11},{9,8},{10,9... | collective-permute-start | bytes 1572872 | tf_op jit(solution)/shard_map/ppermute | solution.py:22
  128.2 6.2 %collective-permute-done.5 = bf16[256,1024]{1,0:T(8,128)(2,1)S(1)} collective-permute-done((bf16[256,1024]{1,0:T(8,128)(2,1)S(1)}, bf16[256,1024]{1,0:T(8,128)(2,1)S(1)}, u32[]{:S(2)}, u32[]{:S(2)}) %collective-permute-start.5) | collective-permute-done | bytes 524320 | tf_op jit(solution)/shard_map/ppermute | solution.py:22
  134.4 12.0 %collective-permute-done.6 = bf16[256,1024]{1,0:T(8,128)(2,1)S(1)} collective-permute-done((bf16[256,1024]{1,0:T(8,128)(2,1)S(1)}, bf16[256,1024]{1,0:T(8,128)(2,1)S(1)}, u32[]{:S(2)}, u32[]{:S(2)}) %collective-permute-start.6) | collective-permute-done | bytes 524320 | tf_op jit(solution)/shard_map/ppermute | solution.py:22
  149.0 14.0 %all-to-all-done.2.back = bf16[16,128,512]{2,1,0:T(8,128)(2,1)S(1)} async-done(((bf16[16,128,512]{2,1,0:T(8,128)(2,1)}), bf16[16,128,512]{2,1,0:T(8,128)(2,1)S(1)}, u32[]{:S(2)}, u32[]{:S(2)}) %all-to-all-start.2) | async-done | bytes 2097184 | tf_op jit(solution)/shard_map/all_to_all | solution.py:26
  163.0 3.1 %combine.1 = (bf16[8,64,512]{2,1,0:T(8,128)(2,1)}, bf16[8,64,512]{2,1,0:T(8,128)(2,1)}) custom-call(s32[16,1]{1,0:T(8,128)S(1)} %bitcast.17, f32[2,8,64,512]{3,2,1,0:T(8,128)} %get-tuple-element.20.own_rows_hbm, bf16[16,128,512]{2,1,0:T(8,128)(2,1)S(1)} %all-to-all-done.2.back), custom_call_target="tpu_custom_call" | custom-call | bytes 4194304 | tf_op jit(solution)/shard_map/combine/pallas_call | solution.py:266
  (15 shorter events, 4.2 us)
Async XLA Ops:
  7.2 92.7 %all-gather.2.cloned.1.call-start = ((), (), s32[]{:S(2)}) async-start(), calls=%async_computation.3 | async-start | bytes 4456448 | tf_op jit(solution)/shard_map/all_gather | solution.py:300
  28.2 71.7 %copy-start = (bf16[1,8,64,512]{3,2,1,0:T(8,128)(2,1)S(1)}, bf16[1,8,64,512]{3,2,1,0:T(8,128)(2,1)}, u32[]{:S(2)}) copy-start(bf16[1,8,64,512]{3,2,1,0:T(8,128)(2,1)} %param.8) | copy-start | bytes 1572868
  28.2 71.6 %copy-start.1 = (bf16[1,8,64,512]{3,2,1,0:T(8,128)(2,1)S(1)}, bf16[1,8,64,512]{3,2,1,0:T(8,128)(2,1)}, u32[]{:S(2)}) copy-start(bf16[1,8,64,512]{3,2,1,0:T(8,128)(2,1)} %param.9) | copy-start | bytes 1572868
  28.2 71.6 %copy-start.2 = (s32[2]{0:T(128)S(1)}, s32[2]{0:T(128)}, u32[]{:S(2)}) copy-start(s32[2]{0:T(128)} %counts.1) | copy-start | bytes 28
  28.3 69.3 %all-to-all-start.1 = ((bf16[16,128,512]{2,1,0:T(8,128)(2,1)}), bf16[16,128,512]{2,1,0:T(8,128)(2,1)S(1)}, u32[]{:S(2)}, u32[]{:S(2)}) async-start(bf16[16,128,512]{2,1,0:T(8,128)(2,1)} %pick_blocks.1), calls=%async_computation.1 | async-start | bytes 4194304 | tf_op jit(solution)/shard_map/all_to_all | solution.py:26
  32.5 21.1 %collective-permute-start.1 = (bf16[1,2,128,1024]{3,2,1,0:T(8,128)(2,1)}, bf16[1,2,128,1024]{3,2,1,0:T(8,128)(2,1)}, u32[]{:S(2)}, u32[]{:S(2)}) collective-permute-start(bf16[1,2,128,1024]{3,2,1,0:T(8,128)(2,1)} %param.11), channel_id=1, source_target_pairs={{0,28},{4,0},{8,4},{12,8},{16,12},{20,16},{24,20},{28,24},{1,29},{... | collective-permute-start | bytes 1572872 | tf_op jit(solution)/shard_map/ppermute | solution.py:22
  53.7 20.9 %collective-permute-start.4 = (bf16[256,1024]{1,0:T(8,128)(2,1)}, bf16[256,1024]{1,0:T(8,128)(2,1)}, u32[]{:S(2)}, u32[]{:S(2)}) collective-permute-start(bf16[256,1024]{1,0:T(8,128)(2,1)} %bitcast.6.grad0), channel_id=1, source_target_pairs={{0,1},{1,2},{2,3},{3,0},{4,5},{5,6},{6,7},{7,4},{8,9},{9,10},{10,1... | collective-permute-start | bytes 1572872 | tf_op jit(solution)/shard_map/ppermute | solution.py:22
  56.8 24.9 %collective-permute-start.3 = (bf16[256,1024]{1,0:T(8,128)(2,1)}, bf16[256,1024]{1,0:T(8,128)(2,1)}, u32[]{:S(2)}, u32[]{:S(2)}) collective-permute-start(bf16[256,1024]{1,0:T(8,128)(2,1)} %bitcast.6.grad0), channel_id=1, source_target_pairs={{0,2},{1,3},{2,0},{3,1},{4,6},{5,7},{6,4},{7,5},{8,10},{9,11},{10,... | collective-permute-start | bytes 1572872 | tf_op jit(solution)/shard_map/ppermute | solution.py:22
  61.1 22.5 %collective-permute-start.2 = (bf16[256,1024]{1,0:T(8,128)(2,1)}, bf16[256,1024]{1,0:T(8,128)(2,1)}, u32[]{:S(2)}, u32[]{:S(2)}) collective-permute-start(bf16[256,1024]{1,0:T(8,128)(2,1)} %bitcast.6.grad0), channel_id=1, source_target_pairs={{0,3},{1,0},{2,1},{3,2},{4,7},{5,4},{6,5},{7,6},{8,11},{9,8},{10,9... | collective-permute-start | bytes 1572872 | tf_op jit(solution)/shard_map/ppermute | solution.py:22
  64.2 10.4 %collective-permute-start = (bf16[1,2,128,512]{3,2,1,0:T(8,128)(2,1)}, bf16[1,2,128,512]{3,2,1,0:T(8,128)(2,1)S(1)}, u32[]{:S(2)}, u32[]{:S(2)}) collective-permute-start(bf16[1,2,128,512]{3,2,1,0:T(8,128)(2,1)} %param.7), channel_id=1, source_target_pairs={{0,4},{4,8},{8,12},{12,16},{16,20},{20,24},{24,28},{28,0},{1,5},{5... | collective-permute-start | bytes 786440 | tf_op jit(solution)/shard_map/ppermute | solution.py:22
  109.6 53.5 %all-to-all-start.2 = ((bf16[16,128,512]{2,1,0:T(8,128)(2,1)}), bf16[16,128,512]{2,1,0:T(8,128)(2,1)S(1)}, u32[]{:S(2)}, u32[]{:S(2)}) async-start(bf16[16,128,512]{2,1,0:T(8,128)(2,1)} %get-tuple-element.21), calls=%async_computation.2 | async-start | bytes 4194304 | tf_op jit(solution)/shard_map/all_to_all | solution.py:26
  117.8 16.6 %collective-permute-start.5 = (bf16[256,1024]{1,0:T(8,128)(2,1)S(1)}, bf16[256,1024]{1,0:T(8,128)(2,1)S(1)}, u32[]{:S(2)}, u32[]{:S(2)}) collective-permute-start(bf16[256,1024]{1,0:T(8,128)(2,1)S(1)} %get-tuple-element.16), channel_id=1, source_target_pairs={{0,1},{1,2},{2,3},{3,0},{4,5},{5,6},{6,7},{7,4},{8,9},{9,10},{10,1... | collective-permute-start | bytes 1572872 | tf_op jit(solution)/shard_map/ppermute | solution.py:22
  120.8 25.6 %collective-permute-start.6 = (bf16[256,1024]{1,0:T(8,128)(2,1)S(1)}, bf16[256,1024]{1,0:T(8,128)(2,1)S(1)}, u32[]{:S(2)}, u32[]{:S(2)}) collective-permute-start(bf16[256,1024]{1,0:T(8,128)(2,1)S(1)} %get-tuple-element.17), channel_id=1, source_target_pairs={{0,2},{1,3},{2,0},{3,1},{4,6},{5,7},{6,4},{7,5},{8,10},{9,11},{10,... | collective-permute-start | bytes 1572872 | tf_op jit(solution)/shard_map/ppermute | solution.py:22
  125.1 22.7 %collective-permute-start.7 = (bf16[256,1024]{1,0:T(8,128)(2,1)S(1)}, bf16[256,1024]{1,0:T(8,128)(2,1)S(1)}, u32[]{:S(2)}, u32[]{:S(2)}) collective-permute-start(bf16[256,1024]{1,0:T(8,128)(2,1)S(1)} %get-tuple-element.18), channel_id=1, source_target_pairs={{0,3},{1,0},{2,1},{3,2},{4,7},{5,4},{6,5},{7,6},{8,11},{9,8},{10,9... | collective-permute-start | bytes 1572872 | tf_op jit(solution)/shard_map/ppermute | solution.py:22
Sparse Core Ops, SparseCore 0:
  10.1 89.7 all-gather.1

commit v6 on v5

--- a/solution.py
+++ b/solution.py
@@ -40,17 +40,23 @@
     in_value = pltpu.make_async_copy(values_hbm, values, in_sem.at[1])
     in_key.start()
     in_value.start()
-    outgoing = []
+
+    def sent(slot, which, source):
+        target = slots.at[slot, pl.ds(which * rows, rows)]
+        return pltpu.make_async_copy(source.at[jnp.maximum(asked[slot, 0], 0)], target, out_sem.at[slot, which])
+
     for which, (arriving, source) in enumerate(((in_key, keys), (in_value, values))):
         arriving.wait()
-        for slot in range(slots.shape[0]):
-            spot = asked[slot, 0]
-            target = slots.at[slot, pl.ds(which * rows, rows)]
-            copy = pltpu.make_async_copy(source.at[jnp.maximum(spot, 0)], target, out_sem.at[slot, which])
-            pl.when(spot >= 0)(copy.start)
-            outgoing.append((spot, copy))
-    for spot, copy in outgoing:
-        pl.when(spot >= 0)(copy.wait)
+
+        @pl.loop(0, slots.shape[0])
+        def _(slot, which=which, source=source):
+            copy = sent(slot, which, source)
+            pl.when(asked[slot, 0] >= 0)(copy.start)
+
+    @pl.loop(0, slots.shape[0])
+    def _(slot):
+        for which, source in enumerate((keys, values)):
+            pl.when(asked[slot, 0] >= 0)(sent(slot, which, source).wait)
 
 
 def picked_slots(asked, keys, values):
@@ -75,8 +81,8 @@
 
 def layer_kernel(
     counts, holder, spot, queries, keys, values, recv, weight_hbm, grad0, grad1, grad2, grad3,
-    attended_hbm, grad_query, own_rows_hbm, slots_hbm,
-    weight, held, grads, probs, attended, own_rows, slots, weight_sem, held_sem, out_sem, own_sem, slot_sem,
+    attended_hbm, grad_query_hbm, own_rows_hbm, slots_hbm,
+    weight, held, grads, probs, attended, grad_query, own_rows, slots, weight_sem, held_sem, out_sem, own_sem, slot_sem,
 ):
     docs, query_count, _ = queries.shape
     mem_count, rows, features = keys.shape
@@ -96,72 +102,85 @@
         in_weight.start()
         arriving.append((in_held, in_weight))
 
-    def listed(doc, head):
-        at = slice(head * HD, (head + 1) * HD)
-        blocks = range(doc * own, (doc + 1) * own)
+    def place(step):
+        doc, head = step // heads, lax.rem(step, heads)
+        at = pl.ds(pl.multiple_of(head * HD, HD), HD)
+        query_rows = pl.ds(pl.multiple_of(doc * query_count, query_count), query_count)
         senders = [holder[doc, m] for m in range(neg)]
-        key = jnp.concatenate([keys[m, :, at] for m in blocks] + [recv[e, :rows, at] for e in senders], axis=0)
-        value = jnp.concatenate([values[m, :, at] for m in blocks] + [recv[e, rows:, at] for e in senders], axis=0)
-        return at, slice(doc * query_count, (doc + 1) * query_count), key, value
+        key = jnp.concatenate(
+            [keys[doc * own + m, :, at] for m in range(own)] + [recv[e, :rows, at] for e in senders], axis=0
+        )
+        value = jnp.concatenate(
+            [values[doc * own + m, :, at] for m in range(own)] + [recv[e, rows:, at] for e in senders], axis=0
+        )
+        return doc, at, query_rows, key, value
 
     position = lax.broadcasted_iota(jnp.int32, (total, 1), 0)
-    for doc in range(docs):
+
+    @pl.loop(0, docs * heads, unroll=4)
+    def _(step):
+        doc, at, query_rows, key, value = place(step)
         valid = (position < counts[doc] * rows) | (position >= own * rows)
-        for head in range(heads):
-            at, query_rows, key, value = listed(doc, head)
-            scores = lax.dot_general(key, queries[doc, :, at], NT, preferred_element_type=F32) * scale
-            scores = jnp.where(valid, scores, -jnp.inf)
-            expo = jnp.exp(scores - jnp.max(scores, axis=0, keepdims=True))
-            prob = expo * (1.0 / jnp.sum(expo, axis=0, keepdims=True))
-            probs[doc * heads + head] = prob
-            attended[query_rows, at] = lax.dot_general(
-                prob.astype(BF16), value, TN, preferred_element_type=F32
-            ).astype(BF16)
-
-    outgoing = [pltpu.make_async_copy(attended, attended_hbm, out_sem)]
-    outgoing[0].start()
-
-    grad_rows = None
+        scores = lax.dot_general(key, queries[doc, :, at], NT, preferred_element_type=F32) * scale
+        scores = jnp.where(valid, scores, -jnp.inf)
+        expo = jnp.exp(scores - jnp.max(scores, axis=0, keepdims=True))
+        prob = expo * (1.0 / jnp.sum(expo, axis=0, keepdims=True))
+        probs[step] = prob
+        attended[query_rows, at] = lax.dot_general(prob.astype(BF16), value, TN, preferred_element_type=F32).astype(BF16)
+
+    out_attended = pltpu.make_async_copy(attended, attended_hbm, out_sem.at[0])
+    out_attended.start()
+
     for j, copies in enumerate(arriving):
         for copy in copies:
             copy.wait()
+        term = None
         for c in range(per):
-            term = lax.dot_general(
+            part = lax.dot_general(
                 held[j, :, c * block : (c + 1) * block], weight[j, c], NT, preferred_element_type=F32
             )
-            grad_rows = term if grad_rows is None else grad_rows + term
+            term = part if term is None else term + part
+        grad_rows = term if j == 0 else grad_rows + term
     grads[...] = grad_rows.astype(BF16)
 
+    @pl.loop(0, docs * heads, unroll=8)
+    def _(step):
+        doc, at, query_rows, key, value = place(step)
+        grad = grads[query_rows, at]
+        prob = probs[step]
+        grad_prob = lax.dot_general(value, grad, NT, preferred_element_type=F32)
+        delta = jnp.sum(prob * grad_prob, axis=0, keepdims=True)
+        grad_score = (prob * (grad_prob - delta)).astype(BF16)
+        grad_value = jnp.dot(prob.astype(BF16), grad, preferred_element_type=F32)
+        grad_key = jnp.dot(grad_score, queries[doc, :, at], preferred_element_type=F32) * scale
+        grad_query[doc, :, at] = (lax.dot_general(grad_score, key, TN, preferred_element_type=F32) * scale).astype(BF16)
+        for m in range(own):
+            here = slice(m * rows, (m + 1) * rows)
+            own_rows[0, doc * own + m, :, at] = grad_key[here]
+            own_rows[1, doc * own + m, :, at] = grad_value[here]
+        for m in range(neg):
+            here = slice((own + m) * rows, (own + m + 1) * rows)
+            slots[doc * neg + m, :rows, at] = grad_key[here].astype(BF16)
+            slots[doc * neg + m, rows:, at] = grad_value[here].astype(BF16)
+
+        @pl.when(lax.rem(step, heads) == heads - 1)
+        def _():
+            for m in range(neg):
+                entry = doc * neg + m
+                pltpu.make_async_copy(slots.at[entry], slots_hbm.at[holder[doc, m]], slot_sem.at[entry]).start()
+            span = pl.ds(doc * own, own)
+            pltpu.make_async_copy(own_rows.at[:, span], own_rows_hbm.at[:, span], own_sem.at[doc]).start()
+
+    out_query = pltpu.make_async_copy(grad_query, grad_query_hbm, out_sem.at[1])
+    out_query.start()
     for doc in range(docs):
-        for head in range(heads):
-            at, query_rows, key, value = listed(doc, head)
-            grad = grads[query_rows, at]
-            prob = probs[doc * heads + head]
-            grad_prob = lax.dot_general(value, grad, NT, preferred_element_type=F32)
-            delta = jnp.sum(prob * grad_prob, axis=0, keepdims=True)
-            grad_score = (prob * (grad_prob - delta)).astype(BF16)
-            grad_value = jnp.dot(prob.astype(BF16), grad, preferred_element_type=F32)
-            grad_key = jnp.dot(grad_score, queries[doc, :, at], preferred_element_type=F32) * scale
-            grad_query[doc, :, at] = (
-                lax.dot_general(grad_score, key, TN, preferred_element_type=F32) * scale
-            ).astype(BF16)
-            for m in range(own):
-                here = slice(m * rows, (m + 1) * rows)
-                own_rows[0, doc * own + m, :, at] = grad_key[here]
-                own_rows[1, doc * own + m, :, at] = grad_value[here]
-            for m in range(neg):
-                here = slice((own + m) * rows, (own + m + 1) * rows)
-                slots[doc * neg + m, :rows, at] = grad_key[here].astype(BF16)
-                slots[doc * neg + m, rows:, at] = grad_value[here].astype(BF16)
         for m in range(neg):
             entry = doc * neg + m
-            outgoing.append(pltpu.make_async_copy(slots.at[entry], slots_hbm.at[holder[doc, m]], slot_sem.at[entry]))
+            pltpu.make_async_copy(slots.at[entry], slots_hbm.at[holder[doc, m]], slot_sem.at[entry]).wait()
         span = pl.ds(doc * own, own)
-        outgoing.append(pltpu.make_async_copy(own_rows.at[:, span], own_rows_hbm.at[:, span], own_sem.at[doc]))
-        for copy in outgoing[-(neg + 1) :]:
-            copy.start()
-    for copy in outgoing:
-        copy.wait()
+        pltpu.make_async_copy(own_rows.at[:, span], own_rows_hbm.at[:, span], own_sem.at[doc]).wait()
+    out_attended.wait()
+    out_query.wait()
 
 
 def layer(counts, holder, spot, queries, keys, values, recv, weight, held):
@@ -173,23 +192,24 @@
         layer_kernel,
         out_shape=[
             pltpu.HBM((rows, features), BF16),
-            jax.ShapeDtypeStruct(queries.shape, BF16),
+            pltpu.HBM(queries.shape, BF16),
             pltpu.HBM((2, *keys.shape), F32),
             pltpu.HBM(recv.shape, BF16),
         ],
         in_specs=[SMEM] * 3 + [VMEM] * 4 + [HBM] * (1 + groups),
-        out_specs=[HBM, VMEM, HBM, HBM],
+        out_specs=[HBM] * 4,
         scratch_shapes=[
             pltpu.VMEM((groups, weight.shape[0] // groups, *weight.shape[1:]), BF16),
             pltpu.VMEM((groups, rows, columns), BF16),
             pltpu.VMEM((rows, features), BF16),
             pltpu.VMEM((docs * features // HD, (keys.shape[0] // docs + holder.shape[1]) * keys.shape[1], query_count), F32),
             pltpu.VMEM((rows, features), BF16),
+            pltpu.VMEM(queries.shape, BF16),
             pltpu.VMEM((2, *keys.shape), F32),
             pltpu.VMEM((entries, *recv.shape[1:]), BF16),
             dma((groups,)),
             dma((groups,)),
-            dma,
+            dma((2,)),
             dma((docs,)),
             dma((entries,)),
         ],
@@ -242,19 +262,28 @@
     arriving = [pltpu.make_async_copy(own_rows_hbm.at[i], own_rows.at[i], in_sem.at[i]) for i in range(2)]
     for copy in arriving:
         copy.start()
-    total[...] = jnp.zeros_like(total)
-    for slot in range(back.shape[0]):
+
+    @pl.loop(0, total.shape[1])
+    def _(block):
+        total[:, block] = jnp.zeros_like(total[:, block])
+
+    @pl.loop(0, back.shape[0])
+    def _(slot):
         spot = asked[slot, 0]
 
         @pl.when(spot >= 0)
-        def _(slot=slot, spot=spot):
+        def _():
             total[0, spot] += back[slot, :rows, :].astype(F32)
             total[1, spot] += back[slot, rows:, :].astype(F32)
 
     outgoing = []
     for i, target in enumerate((key_grads_hbm, value_grads_hbm)):
         arriving[i].wait()
-        grads[i] = (own_rows[i] + total[i]).astype(BF16)
+
+        @pl.loop(0, total.shape[1])
+        def _(block, i=i):
+            grads[i, block] = (own_rows[i, block] + total[i, block]).astype(BF16)
+
         outgoing.append(pltpu.make_async_copy(grads.at[i], target, out_sem.at[i]))
         outgoing[i].start()
     for copy in outgoing:

time: 174 us -> 172 us (0.989)
  Pallas kernels: 19.7 us -> 17.9 us
where the time goes in v6:
time: 172 us; the launch traced here: 171 us
  waiting for transfers between devices  79.5 us (46%)
  starting transfers between devices  41.5 us (24%)
  Pallas kernels  17.9 us (10%)
  blocking collectives  16.3 us (9%)
  between operations  14.2 us (8%)
  other arithmetic  1.95 us (1%)
    ppermute x8, waiting for transfers between devices, passed_along(): lax.ppermute(block, axis, [(i, (i + distance) % count) for i in range(cou...  48.5 us
    ppermute x8, starting transfers between devices, passed_along(): lax.ppermute(block, axis, [(i, (i + distance) % count) for i in range(cou...  32.6 us
    all_to_all x2, waiting for transfers between devices, exchanged(): return lax.all_to_all(slots, 'dp', split_axis=0, concat_axis=0, tiled=True)  27.9 us
    all_to_all x1, blocking collectives, exchanged(): return lax.all_to_all(slots, 'dp', split_axis=0, concat_axis=0, tiled=True)  16.3 us
    all_to_all x2, starting transfers between devices, exchanged(): return lax.all_to_all(slots, 'dp', split_axis=0, concat_axis=0, tiled=True)  8.87 us
    pallas_call x1, Pallas kernels, layer(): pl.pallas_call(layer_kernel, out_shape=[pltpu.HBM((rows, features), BF16)...  8.04 us
    pallas_call x1, Pallas kernels, projected(): pl.pallas_call(project_kernel, out_shape=[shape] * groups, in_specs=[SMEM...  3.71 us
  transfers between devices with their start and end apart: 11, of which 10 were waited for; matrix products, arithmetic and copies ran while one was open for 1% of the time, Pallas kernels for 4%

profile of v6, /device:TPU:1, one launch (start us, length us, event | category | flops | bytes accessed | tf_op | source)
XLA Modules:
  0.0 171.4 jit_solution(18147621871976197413)
XLA Ops:
  8.8 16.3 %all_to_all.18 = s32[16,1,1]{2,1,0:T(1,128)S(1)} all-to-all(s32[16,1,1]{2,1,0:T(1,128)S(1)} %copy.19), channel_id=1, replica_groups=mesh['dp'=16,'section'=8,'tensor'=4] {'dp'}, dimensions={0} | all-to-all | bytes 128 | tf_op jit(solution)/shard_map/all_to_all | solution.py:26
  25.1 3.0 %pick_blocks.1 = bf16[16,128,512]{2,1,0:T(8,128)(2,1)} custom-call(s32[16,1]{1,0:T(8,128)S(1)} %bitcast.16, bf16[8,64,512]{2,1,0:T(8,128)(2,1)} %bitcast.12, bf16[8,64,512]{2,1,0:T(8,128)(2,1)} %bitcast.14), custom_call_target="tpu_custom_call" | custom-call | bytes 4194304 | tf_op jit(solution)/shard_map/pick_blocks/pallas_call | solution.py:65
  28.1 4.4 %all-to-all-start.1 = ((bf16[16,128,512]{2,1,0:T(8,128)(2,1)}), bf16[16,128,512]{2,1,0:T(8,128)(2,1)S(1)}, u32[]{:S(2)}, u32[]{:S(2)}) async-start(bf16[16,128,512]{2,1,0:T(8,128)(2,1)} %pick_blocks.1), calls=%async_computation.1 | async-start | bytes 4194304 | tf_op jit(solution)/shard_map/all_to_all | solution.py:26
  32.5 9.7 %collective-permute-start.1 = (bf16[1,2,128,1024]{3,2,1,0:T(8,128)(2,1)}, bf16[1,2,128,1024]{3,2,1,0:T(8,128)(2,1)}, u32[]{:S(2)}, u32[]{:S(2)}) collective-permute-start(bf16[1,2,128,1024]{3,2,1,0:T(8,128)(2,1)} %param.11), channel_id=1, source_target_pairs={{0,28},{4,0},{8,4},{12,8},{16,12},{20,16},{24,20},{28,24},{1,29},{... | collective-permute-start | bytes 1572872 | tf_op jit(solution)/shard_map/ppermute | solution.py:22
  42.3 11.4 %collective-permute-done.1 = bf16[1,2,128,1024]{3,2,1,0:T(8,128)(2,1)} collective-permute-done((bf16[1,2,128,1024]{3,2,1,0:T(8,128)(2,1)}, bf16[1,2,128,1024]{3,2,1,0:T(8,128)(2,1)}, u32[]{:S(2)}, u32[]{:S(2)}) %collective-permute-start.1) | collective-permute-done | bytes 524320 | tf_op jit(solution)/shard_map/ppermute | solution.py:22
  53.7 3.1 %collective-permute-start.4 = (bf16[256,1024]{1,0:T(8,128)(2,1)}, bf16[256,1024]{1,0:T(8,128)(2,1)}, u32[]{:S(2)}, u32[]{:S(2)}) collective-permute-start(bf16[256,1024]{1,0:T(8,128)(2,1)} %bitcast.6.grad0), channel_id=1, source_target_pairs={{0,1},{1,2},{2,3},{3,0},{4,5},{5,6},{6,7},{7,4},{8,9},{9,10},{10,1... | collective-permute-start | bytes 1572872 | tf_op jit(solution)/shard_map/ppermute | solution.py:22
  56.8 4.4 %collective-permute-start.3 = (bf16[256,1024]{1,0:T(8,128)(2,1)}, bf16[256,1024]{1,0:T(8,128)(2,1)}, u32[]{:S(2)}, u32[]{:S(2)}) collective-permute-start(bf16[256,1024]{1,0:T(8,128)(2,1)} %bitcast.6.grad0), channel_id=1, source_target_pairs={{0,2},{1,3},{2,0},{3,1},{4,6},{5,7},{6,4},{7,5},{8,10},{9,11},{10,... | collective-permute-start | bytes 1572872 | tf_op jit(solution)/shard_map/ppermute | solution.py:22
  61.1 3.1 %collective-permute-start.2 = (bf16[256,1024]{1,0:T(8,128)(2,1)}, bf16[256,1024]{1,0:T(8,128)(2,1)}, u32[]{:S(2)}, u32[]{:S(2)}) collective-permute-start(bf16[256,1024]{1,0:T(8,128)(2,1)} %bitcast.6.grad0), channel_id=1, source_target_pairs={{0,3},{1,0},{2,1},{3,2},{4,7},{5,4},{6,5},{7,6},{8,11},{9,8},{10,9... | collective-permute-start | bytes 1572872 | tf_op jit(solution)/shard_map/ppermute | solution.py:22
  64.2 1.9 %collective-permute-start = (bf16[1,2,128,512]{3,2,1,0:T(8,128)(2,1)}, bf16[1,2,128,512]{3,2,1,0:T(8,128)(2,1)S(1)}, u32[]{:S(2)}, u32[]{:S(2)}) collective-permute-start(bf16[1,2,128,512]{3,2,1,0:T(8,128)(2,1)} %param.7), channel_id=1, source_target_pairs={{0,4},{4,8},{8,12},{12,16},{16,20},{20,24},{24,28},{28,0},{1,5},{5... | collective-permute-start | bytes 786440 | tf_op jit(solution)/shard_map/ppermute | solution.py:22
  66.1 8.4 %collective-permute-done = bf16[1,2,128,512]{3,2,1,0:T(8,128)(2,1)S(1)} collective-permute-done((bf16[1,2,128,512]{3,2,1,0:T(8,128)(2,1)}, bf16[1,2,128,512]{3,2,1,0:T(8,128)(2,1)S(1)}, u32[]{:S(2)}, u32[]{:S(2)}) %collective-permute-start) | collective-permute-done | bytes 262176 | tf_op jit(solution)/shard_map/ppermute | solution.py:22
  74.6 7.1 %collective-permute-done.3.grad2 = bf16[256,1024]{1,0:T(8,128)(2,1)} collective-permute-done((bf16[256,1024]{1,0:T(8,128)(2,1)}, bf16[256,1024]{1,0:T(8,128)(2,1)}, u32[]{:S(2)}, u32[]{:S(2)}) %collective-permute-start.3) | collective-permute-done | bytes 524320 | tf_op jit(solution)/shard_map/ppermute | solution.py:22
  81.7 2.0 %collective-permute-done.2.grad1 = bf16[256,1024]{1,0:T(8,128)(2,1)} collective-permute-done((bf16[256,1024]{1,0:T(8,128)(2,1)}, bf16[256,1024]{1,0:T(8,128)(2,1)}, u32[]{:S(2)}, u32[]{:S(2)}) %collective-permute-start.2) | collective-permute-done | bytes 524320 | tf_op jit(solution)/shard_map/ppermute | solution.py:22
  83.6 13.9 %all-to-all-done.1.recv = bf16[16,128,512]{2,1,0:T(8,128)(2,1)S(1)} async-done(((bf16[16,128,512]{2,1,0:T(8,128)(2,1)}), bf16[16,128,512]{2,1,0:T(8,128)(2,1)S(1)}, u32[]{:S(2)}, u32[]{:S(2)}) %all-to-all-start.1) | async-done | bytes 2097184 | tf_op jit(solution)/shard_map/all_to_all | solution.py:26
  97.5 2.4 %all-gather.2.cloned.1.call-done.weight_hbm = bf16[16,512,256]{2,1,0:T(8,128)(2,1)} async-done(((bf16[1,512,256]{2,1,0:T(8,128)(2,1)}), bf16[16,512,256]{2,1,0:T(8,128)(2,1)}) %all-gather.2.cloned.1.call-update) | async-done | bytes 4194320 | tf_op jit(solution)/shard_map/all_gather | solution.py:329
  99.9 8.0 %layer.1 = (bf16[256,512]{1,0:T(8,128)(2,1)}, bf16[2,128,512]{2,1,0:T(8,128)(2,1)}, f32[2,8,64,512]{3,2,1,0:T(8,128)}, bf16[16,128,512]{2,1,0:T(8,128)(2,1)}) custom-call(s32[2]{0:T(128)S(1)} %copy-done.2, s32[2,4]{1,0:T(2,128)S(1)} %get-tuple-element.25.holder, s32[1]{0:T(128)} %bitcast.spot, bf16[2,128,512]{2,1,0:T(8,128)(2,1)S(1)} %bitcast.18, ...), custom_call_target="tpu_custom_call" | custom-call | flops 5368709120 | bytes 16777216 | tf_op jit(solution)/shard_map/layer/pallas_call | solution.py:191
  107.9 4.5 %all-to-all-start.2 = ((bf16[16,128,512]{2,1,0:T(8,128)(2,1)}), bf16[16,128,512]{2,1,0:T(8,128)(2,1)S(1)}, u32[]{:S(2)}, u32[]{:S(2)}) async-start(bf16[16,128,512]{2,1,0:T(8,128)(2,1)} %get-tuple-element.21), calls=%async_computation.2 | async-start | bytes 4194304 | tf_op jit(solution)/shard_map/all_to_all | solution.py:26
  112.4 3.7 %projection.1 = (bf16[256,1024]{1,0:T(8,128)(2,1)S(1)}, bf16[256,1024]{1,0:T(8,128)(2,1)S(1)}, bf16[256,1024]{1,0:T(8,128)(2,1)S(1)}, bf16[256,1024]{1,0:T(8,128)(2,1)S(1)}) custom-call(s32[1]{0:T(128)} %bitcast.spot, bf16[16,512,256]{2,1,0:T(8,128)(2,1)} %all-gather.2.cloned.1.call-done.weight_hbm, bf16[256,512]{1,0:T(8,128)(2,1)} %get-tuple-element.14.attended_hbm), custom_call_target="tpu_custom_call" | custom-call | flops 2147483648 | bytes 8388608 | tf_op jit(solution)/shard_map/projection/pallas_call | solution.py:243
  116.1 3.0 %collective-permute-start.5 = (bf16[256,1024]{1,0:T(8,128)(2,1)S(1)}, bf16[256,1024]{1,0:T(8,128)(2,1)S(1)}, u32[]{:S(2)}, u32[]{:S(2)}) collective-permute-start(bf16[256,1024]{1,0:T(8,128)(2,1)S(1)} %get-tuple-element.16), channel_id=1, source_target_pairs={{0,1},{1,2},{2,3},{3,0},{4,5},{5,6},{6,7},{7,4},{8,9},{9,10},{10,1... | collective-permute-start | bytes 1572872 | tf_op jit(solution)/shard_map/ppermute | solution.py:22
  119.1 4.3 %collective-permute-start.6 = (bf16[256,1024]{1,0:T(8,128)(2,1)S(1)}, bf16[256,1024]{1,0:T(8,128)(2,1)S(1)}, u32[]{:S(2)}, u32[]{:S(2)}) collective-permute-start(bf16[256,1024]{1,0:T(8,128)(2,1)S(1)} %get-tuple-element.17), channel_id=1, source_target_pairs={{0,2},{1,3},{2,0},{3,1},{4,6},{5,7},{6,4},{7,5},{8,10},{9,11},{10,... | collective-permute-start | bytes 1572872 | tf_op jit(solution)/shard_map/ppermute | solution.py:22
  123.4 3.1 %collective-permute-start.7 = (bf16[256,1024]{1,0:T(8,128)(2,1)S(1)}, bf16[256,1024]{1,0:T(8,128)(2,1)S(1)}, u32[]{:S(2)}, u32[]{:S(2)}) collective-permute-start(bf16[256,1024]{1,0:T(8,128)(2,1)S(1)} %get-tuple-element.18), channel_id=1, source_target_pairs={{0,3},{1,0},{2,1},{3,2},{4,7},{5,4},{6,5},{7,6},{8,11},{9,8},{10,9... | collective-permute-start | bytes 1572872 | tf_op jit(solution)/shard_map/ppermute | solution.py:22
  126.5 6.2 %collective-permute-done.5 = bf16[256,1024]{1,0:T(8,128)(2,1)S(1)} collective-permute-done((bf16[256,1024]{1,0:T(8,128)(2,1)S(1)}, bf16[256,1024]{1,0:T(8,128)(2,1)S(1)}, u32[]{:S(2)}, u32[]{:S(2)}) %collective-permute-start.5) | collective-permute-done | bytes 524320 | tf_op jit(solution)/shard_map/ppermute | solution.py:22
  132.7 12.0 %collective-permute-done.6 = bf16[256,1024]{1,0:T(8,128)(2,1)S(1)} collective-permute-done((bf16[256,1024]{1,0:T(8,128)(2,1)S(1)}, bf16[256,1024]{1,0:T(8,128)(2,1)S(1)}, u32[]{:S(2)}, u32[]{:S(2)}) %collective-permute-start.6) | collective-permute-done | bytes 524320 | tf_op jit(solution)/shard_map/ppermute | solution.py:22
  147.3 14.0 %all-to-all-done.2.back = bf16[16,128,512]{2,1,0:T(8,128)(2,1)S(1)} async-done(((bf16[16,128,512]{2,1,0:T(8,128)(2,1)}), bf16[16,128,512]{2,1,0:T(8,128)(2,1)S(1)}, u32[]{:S(2)}, u32[]{:S(2)}) %all-to-all-start.2) | async-done | bytes 2097184 | tf_op jit(solution)/shard_map/all_to_all | solution.py:26
  161.4 3.2 %combine.1 = (bf16[8,64,512]{2,1,0:T(8,128)(2,1)}, bf16[8,64,512]{2,1,0:T(8,128)(2,1)}) custom-call(s32[16,1]{1,0:T(8,128)S(1)} %bitcast.17, f32[2,8,64,512]{3,2,1,0:T(8,128)} %get-tuple-element.20.own_rows_hbm, bf16[16,128,512]{2,1,0:T(8,128)(2,1)S(1)} %all-to-all-done.2.back), custom_call_target="tpu_custom_call" | custom-call | bytes 4194304 | tf_op jit(solution)/shard_map/combine/pallas_call | solution.py:295
  (15 shorter events, 4.2 us)
Async XLA Ops:
  7.2 92.7 %all-gather.2.cloned.1.call-start = ((), (), s32[]{:S(2)}) async-start(), calls=%async_computation.3 | async-start | bytes 4456448 | tf_op jit(solution)/shard_map/all_gather | solution.py:329
  28.1 71.8 %copy-start = (bf16[1,8,64,512]{3,2,1,0:T(8,128)(2,1)S(1)}, bf16[1,8,64,512]{3,2,1,0:T(8,128)(2,1)}, u32[]{:S(2)}) copy-start(bf16[1,8,64,512]{3,2,1,0:T(8,128)(2,1)} %param.8) | copy-start | bytes 1572868
  28.1 71.8 %copy-start.1 = (bf16[1,8,64,512]{3,2,1,0:T(8,128)(2,1)S(1)}, bf16[1,8,64,512]{3,2,1,0:T(8,128)(2,1)}, u32[]{:S(2)}) copy-start(bf16[1,8,64,512]{3,2,1,0:T(8,128)(2,1)} %param.9) | copy-start | bytes 1572868
  28.1 71.8 %copy-start.2 = (s32[2]{0:T(128)S(1)}, s32[2]{0:T(128)}, u32[]{:S(2)}) copy-start(s32[2]{0:T(128)} %counts.1) | copy-start | bytes 28
  28.1 69.4 %all-to-all-start.1 = ((bf16[16,128,512]{2,1,0:T(8,128)(2,1)}), bf16[16,128,512]{2,1,0:T(8,128)(2,1)S(1)}, u32[]{:S(2)}, u32[]{:S(2)}) async-start(bf16[16,128,512]{2,1,0:T(8,128)(2,1)} %pick_blocks.1), calls=%async_computation.1 | async-start | bytes 4194304 | tf_op jit(solution)/shard_map/all_to_all | solution.py:26
  32.5 21.1 %collective-permute-start.1 = (bf16[1,2,128,1024]{3,2,1,0:T(8,128)(2,1)}, bf16[1,2,128,1024]{3,2,1,0:T(8,128)(2,1)}, u32[]{:S(2)}, u32[]{:S(2)}) collective-permute-start(bf16[1,2,128,1024]{3,2,1,0:T(8,128)(2,1)} %param.11), channel_id=1, source_target_pairs={{0,28},{4,0},{8,4},{12,8},{16,12},{20,16},{24,20},{28,24},{1,29},{... | collective-permute-start | bytes 1572872 | tf_op jit(solution)/shard_map/ppermute | solution.py:22
  53.7 20.9 %collective-permute-start.4 = (bf16[256,1024]{1,0:T(8,128)(2,1)}, bf16[256,1024]{1,0:T(8,128)(2,1)}, u32[]{:S(2)}, u32[]{:S(2)}) collective-permute-start(bf16[256,1024]{1,0:T(8,128)(2,1)} %bitcast.6.grad0), channel_id=1, source_target_pairs={{0,1},{1,2},{2,3},{3,0},{4,5},{5,6},{6,7},{7,4},{8,9},{9,10},{10,1... | collective-permute-start | bytes 1572872 | tf_op jit(solution)/shard_map/ppermute | solution.py:22
  56.8 24.9 %collective-permute-start.3 = (bf16[256,1024]{1,0:T(8,128)(2,1)}, bf16[256,1024]{1,0:T(8,128)(2,1)}, u32[]{:S(2)}, u32[]{:S(2)}) collective-permute-start(bf16[256,1024]{1,0:T(8,128)(2,1)} %bitcast.6.grad0), channel_id=1, source_target_pairs={{0,2},{1,3},{2,0},{3,1},{4,6},{5,7},{6,4},{7,5},{8,10},{9,11},{10,... | collective-permute-start | bytes 1572872 | tf_op jit(solution)/shard_map/ppermute | solution.py:22
  61.1 22.5 %collective-permute-start.2 = (bf16[256,1024]{1,0:T(8,128)(2,1)}, bf16[256,1024]{1,0:T(8,128)(2,1)}, u32[]{:S(2)}, u32[]{:S(2)}) collective-permute-start(bf16[256,1024]{1,0:T(8,128)(2,1)} %bitcast.6.grad0), channel_id=1, source_target_pairs={{0,3},{1,0},{2,1},{3,2},{4,7},{5,4},{6,5},{7,6},{8,11},{9,8},{10,9... | collective-permute-start | bytes 1572872 | tf_op jit(solution)/shard_map/ppermute | solution.py:22
  64.2 10.4 %collective-permute-start = (bf16[1,2,128,512]{3,2,1,0:T(8,128)(2,1)}, bf16[1,2,128,512]{3,2,1,0:T(8,128)(2,1)S(1)}, u32[]{:S(2)}, u32[]{:S(2)}) collective-permute-start(bf16[1,2,128,512]{3,2,1,0:T(8,128)(2,1)} %param.7), channel_id=1, source_target_pairs={{0,4},{4,8},{8,12},{12,16},{16,20},{20,24},{24,28},{28,0},{1,5},{5... | collective-permute-start | bytes 786440 | tf_op jit(solution)/shard_map/ppermute | solution.py:22
  107.9 53.4 %all-to-all-start.2 = ((bf16[16,128,512]{2,1,0:T(8,128)(2,1)}), bf16[16,128,512]{2,1,0:T(8,128)(2,1)S(1)}, u32[]{:S(2)}, u32[]{:S(2)}) async-start(bf16[16,128,512]{2,1,0:T(8,128)(2,1)} %get-tuple-element.21), calls=%async_computation.2 | async-start | bytes 4194304 | tf_op jit(solution)/shard_map/all_to_all | solution.py:26
  116.1 16.6 %collective-permute-start.5 = (bf16[256,1024]{1,0:T(8,128)(2,1)S(1)}, bf16[256,1024]{1,0:T(8,128)(2,1)S(1)}, u32[]{:S(2)}, u32[]{:S(2)}) collective-permute-start(bf16[256,1024]{1,0:T(8,128)(2,1)S(1)} %get-tuple-element.16), channel_id=1, source_target_pairs={{0,1},{1,2},{2,3},{3,0},{4,5},{5,6},{6,7},{7,4},{8,9},{9,10},{10,1... | collective-permute-start | bytes 1572872 | tf_op jit(solution)/shard_map/ppermute | solution.py:22
  119.1 25.6 %collective-permute-start.6 = (bf16[256,1024]{1,0:T(8,128)(2,1)S(1)}, bf16[256,1024]{1,0:T(8,128)(2,1)S(1)}, u32[]{:S(2)}, u32[]{:S(2)}) collective-permute-start(bf16[256,1024]{1,0:T(8,128)(2,1)S(1)} %get-tuple-element.17), channel_id=1, source_target_pairs={{0,2},{1,3},{2,0},{3,1},{4,6},{5,7},{6,4},{7,5},{8,10},{9,11},{10,... | collective-permute-start | bytes 1572872 | tf_op jit(solution)/shard_map/ppermute | solution.py:22
  123.4 22.7 %collective-permute-start.7 = (bf16[256,1024]{1,0:T(8,128)(2,1)S(1)}, bf16[256,1024]{1,0:T(8,128)(2,1)S(1)}, u32[]{:S(2)}, u32[]{:S(2)}) collective-permute-start(bf16[256,1024]{1,0:T(8,128)(2,1)S(1)} %get-tuple-element.18), channel_id=1, source_target_pairs={{0,3},{1,0},{2,1},{3,2},{4,7},{5,4},{6,5},{7,6},{8,11},{9,8},{10,9... | collective-permute-start | bytes 1572872 | tf_op jit(solution)/shard_map/ppermute | solution.py:22
Sparse Core Ops, SparseCore 0:
  10.1 89.7 all-gather.1

commit v7 on v6

--- a/solution.py
+++ b/solution.py
@@ -6,6 +6,7 @@
 from jax.sharding import PartitionSpec as P
 
 HD = 128
+OFFSETS = (0, -1, 1, -2, 2, -3, 3, 4)
 F32 = jnp.float32
 BF16 = jnp.bfloat16
 NT = (((1,), (1,)), ((), ()))
@@ -14,7 +15,7 @@
 HBM = pl.BlockSpec(memory_space=pltpu.HBM)
 ANY = pl.BlockSpec(memory_space=pl.ANY)
 SMEM = pl.BlockSpec(memory_space=pltpu.SMEM)
-PARAMS = pltpu.CompilerParams(vmem_limit_bytes=16 * 1024 * 1024)
+PARAMS = pltpu.CompilerParams(vmem_limit_bytes=20 * 1024 * 1024)
 
 
 def passed_along(block, axis, distance):
@@ -80,27 +81,17 @@
 
 
 def layer_kernel(
-    counts, holder, spot, queries, keys, values, recv, weight_hbm, grad0, grad1, grad2, grad3,
+    counts, holder, queries, keys, values, recv, grads,
     attended_hbm, grad_query_hbm, own_rows_hbm, slots_hbm,
-    weight, held, grads, probs, attended, grad_query, own_rows, slots, weight_sem, held_sem, out_sem, own_sem, slot_sem,
+    attended, grad_query, own_rows, slots, out_sem, own_sem, slot_sem,
 ):
     docs, query_count, _ = queries.shape
     mem_count, rows, features = keys.shape
     own = mem_count // docs
     neg = holder.shape[1]
-    groups, per, _, block = weight.shape
     heads = features // HD
     scale = HD**-0.5
     total = (own + neg) * rows
-
-    arriving = []
-    for j, grad in enumerate((grad0, grad1, grad2, grad3)):
-        first = lax.rem(spot[0] + j, groups) * per
-        in_weight = pltpu.make_async_copy(weight_hbm.at[pl.ds(first, per)], weight.at[j], weight_sem.at[j])
-        in_held = pltpu.make_async_copy(grad, held.at[j], held_sem.at[j])
-        in_held.start()
-        in_weight.start()
-        arriving.append((in_held, in_weight))
 
     def place(step):
         doc, head = step // heads, lax.rem(step, heads)
@@ -125,29 +116,8 @@
         scores = jnp.where(valid, scores, -jnp.inf)
         expo = jnp.exp(scores - jnp.max(scores, axis=0, keepdims=True))
         prob = expo * (1.0 / jnp.sum(expo, axis=0, keepdims=True))
-        probs[step] = prob
         attended[query_rows, at] = lax.dot_general(prob.astype(BF16), value, TN, preferred_element_type=F32).astype(BF16)
-
-    out_attended = pltpu.make_async_copy(attended, attended_hbm, out_sem.at[0])
-    out_attended.start()
-
-    for j, copies in enumerate(arriving):
-        for copy in copies:
-            copy.wait()
-        term = None
-        for c in range(per):
-            part = lax.dot_general(
-                held[j, :, c * block : (c + 1) * block], weight[j, c], NT, preferred_element_type=F32
-            )
-            term = part if term is None else term + part
-        grad_rows = term if j == 0 else grad_rows + term
-    grads[...] = grad_rows.astype(BF16)
-
-    @pl.loop(0, docs * heads, unroll=8)
-    def _(step):
-        doc, at, query_rows, key, value = place(step)
         grad = grads[query_rows, at]
-        prob = probs[step]
         grad_prob = lax.dot_general(value, grad, NT, preferred_element_type=F32)
         delta = jnp.sum(prob * grad_prob, axis=0, keepdims=True)
         grad_score = (prob * (grad_prob - delta)).astype(BF16)
@@ -171,6 +141,8 @@
             span = pl.ds(doc * own, own)
             pltpu.make_async_copy(own_rows.at[:, span], own_rows_hbm.at[:, span], own_sem.at[doc]).start()
 
+    out_attended = pltpu.make_async_copy(attended, attended_hbm, out_sem.at[0])
+    out_attended.start()
     out_query = pltpu.make_async_copy(grad_query, grad_query_hbm, out_sem.at[1])
     out_query.start()
     for doc in range(docs):
@@ -183,10 +155,10 @@
     out_query.wait()
 
 
-def layer(counts, holder, spot, queries, keys, values, recv, weight, held):
-    docs, query_count, features = queries.shape
-    entries, groups = holder.shape[0] * holder.shape[1], len(held)
-    rows, columns = held[0].shape
+def layer(counts, holder, queries, keys, values, recv, grads):
+    docs, _, features = queries.shape
+    entries = holder.shape[0] * holder.shape[1]
+    rows = grads.shape[0]
     dma = pltpu.SemaphoreType.DMA
     return pl.pallas_call(
         layer_kernel,
@@ -196,65 +168,123 @@
             pltpu.HBM((2, *keys.shape), F32),
             pltpu.HBM(recv.shape, BF16),
         ],
-        in_specs=[SMEM] * 3 + [VMEM] * 4 + [HBM] * (1 + groups),
+        in_specs=[SMEM] * 2 + [VMEM] * 5,
         out_specs=[HBM] * 4,
         scratch_shapes=[
-            pltpu.VMEM((groups, weight.shape[0] // groups, *weight.shape[1:]), BF16),
-            pltpu.VMEM((groups, rows, columns), BF16),
-            pltpu.VMEM((rows, features), BF16),
-            pltpu.VMEM((docs * features // HD, (keys.shape[0] // docs + holder.shape[1]) * keys.shape[1], query_count), F32),
             pltpu.VMEM((rows, features), BF16),
             pltpu.VMEM(queries.shape, BF16),
             pltpu.VMEM((2, *keys.shape), F32),
             pltpu.VMEM((entries, *recv.shape[1:]), BF16),
-            dma((groups,)),
-            dma((groups,)),
             dma((2,)),
             dma((docs,)),
             dma((entries,)),
         ],
         compiler_params=PARAMS,
-        cost_estimate=cost(5 * 2**30, 16 * 2**20),
+        cost_estimate=cost(4 * 2**30, 12 * 2**20),
         name="layer",
-    )(counts, holder, spot, queries, keys, values, recv, in_hbm(weight), *map(in_hbm, held))
-
-
-def project_kernel(spot, weight_hbm, attended_hbm, out0, out1, out2, out3, weight, attended, sem, in_sem):
-    groups, per, _, block = weight.shape
-    outs = (out0, out1, out2, out3)
-    in_attended = pltpu.make_async_copy(attended_hbm, attended, in_sem)
-    in_attended.start()
-    copies = []
-    for j in range(groups):
-        first = lax.rem(spot[0] + j, groups) * per
-        copies.append(pltpu.make_async_copy(weight_hbm.at[pl.ds(first, per)], weight.at[j], sem.at[j]))
-        copies[j].start()
-    in_attended.wait()
-    for j, out in enumerate(outs):
-        copies[j].wait()
-        for c in range(per):
-            term = jnp.dot(attended[...], weight[j, c], preferred_element_type=F32)
-            out[:, c * block : (c + 1) * block] = term.astype(BF16)
-
-
-def projected(spot, weight, attended, groups):
-    per = weight.shape[0] // groups
-    shape = jax.ShapeDtypeStruct((attended.shape[0], per * weight.shape[2]), BF16)
+    )(counts, holder, queries, keys, values, recv, grads)
+
+
+def copies_in(pairs, sem):
+    copies = [pltpu.make_async_copy(source, target, sem.at[i]) for i, (source, target) in enumerate(pairs)]
+    for copy in copies:
+        copy.start()
+    return copies
+
+
+def placed(spots, step, per, groups):
+    chips = len(OFFSETS)
+    kind, k = step // chips, lax.rem(step, chips)
+    offset = jnp.int32(0)
+    for i, value in enumerate(OFFSETS):
+        offset = jnp.where(k == i, value, offset)
+    own = spots[0] + kind * (1 - 2 * lax.rem(spots[0], 2))
+    block = lax.rem(own + 2 * offset + 2 * chips, 2 * chips)
+    return lax.rem(block // per + groups - spots[1], groups), lax.rem(block, per)
+
+
+def back_kernel(spots, own_hbm, other_hbm, grad0, grad1, grad2, grad3, out_hbm, weight, held, total, out, weight_sem, held_sem):
+    groups, rows, columns = held.shape
+    chips, _, block = own_hbm.shape
+    per = columns // block
+    waiting = copies_in([(ref, held.at[j]) for j, ref in enumerate((grad0, grad1, grad2, grad3))], held_sem)
+    waiting += copies_in([(ref, weight.at[pl.ds(i * chips, chips)]) for i, ref in enumerate((own_hbm, other_hbm))], weight_sem)
+    for copy in waiting:
+        copy.wait()
+    total[...] = jnp.zeros_like(total)
+
+    @pl.loop(0, 2 * chips)
+    def _(step):
+        group, place = placed(spots, step, per, groups)
+        at = pl.ds(pl.multiple_of(place * block, block), block)
+        total[...] += lax.dot_general(held[group, :, at], weight[step], NT, preferred_element_type=F32)
+
+    out[...] = total[...].astype(BF16)
+    pltpu.sync_copy(out, out_hbm)
+
+
+def back_projected(spots, own, other, held):
+    groups = len(held)
+    rows, columns = held[0].shape
+    _, features, block = own.shape
+    return pl.pallas_call(
+        back_kernel,
+        out_shape=pltpu.HBM((rows, features), BF16),
+        in_specs=[SMEM] + [HBM] * (2 + groups),
+        out_specs=HBM,
+        scratch_shapes=[
+            pltpu.VMEM((2 * own.shape[0], features, block), BF16),
+            pltpu.VMEM((groups, rows, columns), BF16),
+            pltpu.VMEM((rows, features), F32),
+            pltpu.VMEM((rows, features), BF16),
+            pltpu.SemaphoreType.DMA((2,)),
+            pltpu.SemaphoreType.DMA((groups,)),
+        ],
+        compiler_params=PARAMS,
+        cost_estimate=cost(2 * 2**30, 8 * 2**20),
+        name="back_projection",
+    )(spots, in_hbm(own), in_hbm(other), *map(in_hbm, held))
+
+
+def project_kernel(spots, own_hbm, other_hbm, attended_hbm, out0, out1, out2, out3, weight, attended, terms, weight_sem, in_sem):
+    groups, _, columns = terms.shape
+    chips, _, block = own_hbm.shape
+    per = columns // block
+    waiting = copies_in([(attended_hbm, attended)], in_sem)
+    waiting += copies_in([(ref, weight.at[pl.ds(i * chips, chips)]) for i, ref in enumerate((own_hbm, other_hbm))], weight_sem)
+    for copy in waiting:
+        copy.wait()
+
+    @pl.loop(0, 2 * chips)
+    def _(step):
+        group, place = placed(spots, step, per, groups)
+        at = pl.ds(pl.multiple_of(place * block, block), block)
+        terms[group, :, at] = jnp.dot(attended[...], weight[step], preferred_element_type=F32).astype(BF16)
+
+    for j, out in enumerate((out0, out1, out2, out3)):
+        out[...] = terms[j]
+
+
+def projected(spots, own, other, attended, groups):
+    chips, features, block = own.shape
+    rows, columns = attended.shape[0], 2 * chips * block // groups
+    shape = jax.ShapeDtypeStruct((rows, columns), BF16)
     return pl.pallas_call(
         project_kernel,
         out_shape=[shape] * groups,
-        in_specs=[SMEM, HBM, HBM],
+        in_specs=[SMEM] + [HBM] * 3,
         out_specs=[VMEM] * groups,
         scratch_shapes=[
-            pltpu.VMEM((groups, per, *weight.shape[1:]), BF16),
+            pltpu.VMEM((2 * chips, features, block), BF16),
             pltpu.VMEM(attended.shape, BF16),
-            pltpu.SemaphoreType.DMA((groups,)),
-            pltpu.SemaphoreType.DMA,
+            pltpu.VMEM((groups, rows, columns), BF16),
+            pltpu.SemaphoreType.DMA((2,)),
+            pltpu.SemaphoreType.DMA((1,)),
         ],
         compiler_params=PARAMS,
         cost_estimate=cost(2 * 2**30, 8 * 2**20),
         name="projection",
-    )(spot, in_hbm(weight), in_hbm(attended))
+    )(spots, in_hbm(own), in_hbm(other), in_hbm(attended))
 
 
 def combine_kernel(asked, own_rows_hbm, back, key_grads_hbm, value_grads_hbm, own_rows, total, grads, in_sem, out_sem):
@@ -315,7 +345,7 @@
     mem_count = keys.shape[0]
     groups = lax.axis_size("dp")
     tensor = lax.axis_size("tensor")
-    tensor_spot = lax.axis_index("tensor").astype(jnp.int32).reshape(1)
+    spots = jnp.stack([lax.axis_index("dp"), lax.axis_index("tensor")]).astype(jnp.int32)
 
     holder = neg_ids // mem_count
     spot = neg_ids - holder * mem_count
@@ -323,20 +353,30 @@
     request = jnp.sum(jnp.where(named, spot[None] + 1, 0), axis=(1, 2)) - 1
     asked = exchanged(request.reshape(groups, 1))
 
+    weight = out_weight[0]
+    half = weight.shape[0] // 2
+    below, above = passed_along(weight, "dp", 2), passed_along(weight, "dp", -2)
+    below2, above2 = passed_along(weight, "dp", 4), passed_along(weight, "dp", -4)
+    below2, above2, asked = lax.optimization_barrier((below2, above2, asked))
+    below3, above3 = passed_along(below2, "dp", 2), passed_along(above2, "dp", -2)
+    far_low, far_high = passed_along(below2[:half], "dp", 4), passed_along(above2[half:], "dp", -4)
+    slots = picked_slots(asked, keys, values)
+    slots, below3, above3, far_low, far_high = lax.optimization_barrier((slots, below3, above3, far_low, far_high))
+    recv = exchanged(slots)
+
+    own_kind = jnp.stack([weight, below, above, below2, above2, below3, above3, jnp.concatenate([far_low, far_high])])
+    other_kind = lax.ppermute(own_kind, "dp", [(i, i ^ 1) for i in range(groups)])
+
     queries = passed_along(sent_queries, "section", 1)[0]
     grads = passed_along(sent_grads, "section", -1)[0]
     docs, query_count, features = queries.shape
-    weight = lax.all_gather(out_weight[0], "dp")
-
-    recv = exchanged(picked_slots(asked, keys, values))
-
     grad_rows = grads.reshape(docs * query_count, grads.shape[2])
     held = [grad_rows] + [passed_along(grad_rows, "tensor", -j) for j in range(1, tensor)]
-    attended, query_grads, own_rows, slots = layer(
-        counts, holder, tensor_spot, queries, keys, values, recv, weight, held
-    )
+    grad_attended = back_projected(spots, own_kind, other_kind, held)
+
+    attended, query_grads, own_rows, slots = layer(counts, holder, queries, keys, values, recv, grad_attended)
     back = exchanged(slots)
-    terms = projected(tensor_spot, weight, attended, tensor)
+    terms = projected(spots, own_kind, other_kind, attended, tensor)
     arrived = [terms[0]] + [passed_along(terms[j], "tensor", j) for j in range(1, tensor)]
     mixed = sum(term.astype(F32) for term in arrived).astype(BF16).reshape(1, docs, query_count, -1)
 

time: 172 us -> 195 us (1.13)
  starting transfers between devices: 41.5 us -> 79.9 us
  waiting for transfers between devices: 79.5 us -> 58.8 us
  between operations: 14.2 us -> 0.97 us
  Pallas kernels: 17.9 us -> 27.8 us
  local copies, waits for them, and re-layouts: 0.11 us -> 8.76 us
    ppermute x8 -> x16, starting transfers between devices: 32.6 us -> 63.2 us  [passed_along(): lax.ppermute(block, axis, [(i, (i + distance) % count) for i in range(cou...]
    all_to_all x2, waiting for transfers between devices: 27.9 us -> 11 us  [exchanged(): return lax.all_to_all(slots, 'dp', split_axis=0, concat_axis=0, tiled=True)]
    unnamed x6 -> x23, local copies, waits for them, and re-layouts: 0.02 us -> 8.57 us
    pallas_call x0 -> x1, Pallas kernels: none -> 8.41 us  [back_projected(): pl.pallas_call(back_kernel, out_shape=pltpu.HBM((rows, features), BF16),...]
    all_to_all x2, starting transfers between devices: 8.87 us -> 14.7 us  [exchanged(): return lax.all_to_all(slots, 'dp', split_axis=0, concat_axis=0, tiled=True)]
    pallas_call x1, Pallas kernels: 3.71 us -> 6.71 us  [projected(): pl.pallas_call(project_kernel, out_shape=[shape] * groups, in_specs=[SMEM...]
    all_gather x1 -> x0, waiting for transfers between devices: 2.35 us -> none  [on_device(): weight = lax.all_gather(out_weight[0], 'dp')]
    ppermute x0 -> x1, starting transfers between devices: none -> 2 us  [on_device(): lax.ppermute(own_kind, 'dp', [(i, i ^ 1) for i in range(groups)])]
  transfers between devices with their start and end apart: 11 -> 19, of which waited for: 10 -> 8; matrix products, arithmetic and copies ran while one was open for 1% -> 5% of each run, Pallas kernels for 4% -> 9%
where the time goes in v7:
time: 195 us; the launch traced here: 194 us
  starting transfers between devices  79.9 us (41%)
  waiting for transfers between devices  58.8 us (30%)
  Pallas kernels  27.8 us (14%)
  blocking collectives  14.8 us (8%)
  local copies, waits for them, and re-layouts  8.76 us (4%)
  other arithmetic  3.13 us (2%)
    ppermute x16, starting transfers between devices, passed_along(): lax.ppermute(block, axis, [(i, (i + distance) % count) for i in range(cou...  63.2 us
    ppermute x16, waiting for transfers between devices, passed_along(): lax.ppermute(block, axis, [(i, (i + distance) % count) for i in range(cou...  47.8 us
    all_to_all x1, blocking collectives, exchanged(): return lax.all_to_all(slots, 'dp', split_axis=0, concat_axis=0, tiled=True)  14.8 us
    all_to_all x2, starting transfers between devices, exchanged(): return lax.all_to_all(slots, 'dp', split_axis=0, concat_axis=0, tiled=True)  14.7 us
    all_to_all x2, waiting for transfers between devices, exchanged(): return lax.all_to_all(slots, 'dp', split_axis=0, concat_axis=0, tiled=True)  11 us
    unnamed x23, local copies, waits for them, and re-layouts  8.57 us
    pallas_call x1, Pallas kernels, back_projected(): pl.pallas_call(back_kernel, out_shape=pltpu.HBM((rows, features), BF16),...  8.41 us
    pallas_call x1, Pallas kernels, projected(): pl.pallas_call(project_kernel, out_shape=[shape] * groups, in_specs=[SMEM...  6.71 us
  transfers between devices with their start and end apart: 19, of which 8 were waited for; matrix products, arithmetic and copies ran while one was open for 5% of the time, Pallas kernels for 9%

profile of v7, /device:TPU:1, one launch (start us, length us, event | category | flops | bytes accessed | tf_op | source)
XLA Modules:
  0.0 194.2 jit_solution(4706196541093514539)
XLA Ops:
  0.6 6.8 %collective-permute-start.3 = (bf16[512,256]{1,0:T(8,128)(2,1)}, bf16[512,256]{1,0:T(8,128)(2,1)S(1)}, u32[]{:S(2)}, u32[]{:S(2)}) collective-permute-start(bf16[512,256]{1,0:T(8,128)(2,1)} %bitcast.36), channel_id=1, source_target_pairs={{0,384},{32,416},{64,448},{96,480},{128,0},{160,32},{192,64},{224,... | collective-permute-start | bytes 786440 | tf_op jit(solution)/shard_map/ppermute | solution.py:23
  10.3 14.8 %all_to_all.19 = s32[16,1,1]{2,1,0:T(1,128)S(1)} all-to-all(s32[16,1,1]{2,1,0:T(1,128)S(1)} %copy.19), channel_id=1, replica_groups=mesh['dp'=16,'section'=8,'tensor'=4] {'dp'}, dimensions={0} | all-to-all | bytes 128 | tf_op jit(solution)/shard_map/all_to_all | solution.py:27
  25.5 3.1 %collective-permute-start.4 = (bf16[512,256]{1,0:T(8,128)(2,1)S(1)}, bf16[512,256]{1,0:T(8,128)(2,1)S(1)}, u32[]{:S(2)}, u32[]{:S(2)}) collective-permute-start(bf16[512,256]{1,0:T(8,128)(2,1)S(1)} %collective-permute-done.2), channel_id=1, source_target_pairs={{0,64},{32,96},{64,128},{96,160},{128,192},{160,224},{192,256},{22... | collective-permute-start | bytes 786440 | tf_op jit(solution)/shard_map/ppermute | solution.py:23
  28.6 3.4 %collective-permute-start.5 = (bf16[512,256]{1,0:T(8,128)(2,1)S(1)}, bf16[512,256]{1,0:T(8,128)(2,1)S(1)}, u32[]{:S(2)}, u32[]{:S(2)}) collective-permute-start(bf16[512,256]{1,0:T(8,128)(2,1)S(1)} %collective-permute-done.3), channel_id=1, source_target_pairs={{0,448},{32,480},{64,0},{96,32},{128,64},{160,96},{192,128},{224,1... | collective-permute-start | bytes 786440 | tf_op jit(solution)/shard_map/ppermute | solution.py:23
  34.0 3.1 %collective-permute-start.7 = (bf16[256,256]{1,0:T(8,128)(2,1)S(1)}, bf16[256,256]{1,0:T(8,128)(2,1)S(1)}, u32[]{:S(2)}, u32[]{:S(2)}) collective-permute-start(bf16[256,256]{1,0:T(8,128)(2,1)S(1)} %slice.7), channel_id=1, source_target_pairs={{0,384},{32,416},{64,448},{96,480},{128,0},{160,32},{192,64},{224,... | collective-permute-start | bytes 393224 | tf_op jit(solution)/shard_map/ppermute | solution.py:23
  37.1 3.1 %collective-permute-start.6 = (bf16[256,256]{1,0:T(8,128)(2,1)S(1)}, bf16[256,256]{1,0:T(8,128)(2,1)S(1)}, u32[]{:S(2)}, u32[]{:S(2)}) collective-permute-start(bf16[256,256]{1,0:T(8,128)(2,1)S(1)} %slice.6), channel_id=1, source_target_pairs={{0,128},{32,160},{64,192},{96,224},{128,256},{160,288},{192,320},{... | collective-permute-start | bytes 393224 | tf_op jit(solution)/shard_map/ppermute | solution.py:23
  43.3 6.2 %collective-permute-start.1 = (bf16[512,256]{1,0:T(8,128)(2,1)S(1)}, bf16[512,256]{1,0:T(8,128)(2,1)}, u32[]{:S(2)}, u32[]{:S(2)}) collective-permute-start(bf16[512,256]{1,0:T(8,128)(2,1)S(1)} %bitcast.39), channel_id=1, source_target_pairs={{0,448},{32,480},{64,0},{96,32},{128,64},{160,96},{192,128},{224,1... | collective-permute-start | bytes 786440 | tf_op jit(solution)/shard_map/ppermute | solution.py:23
  50.1 5.7 %all-to-all-start.1 = ((bf16[16,128,512]{2,1,0:T(8,128)(2,1)}), bf16[16,128,512]{2,1,0:T(8,128)(2,1)S(1)}, u32[]{:S(2)}, u32[]{:S(2)}) async-start(bf16[16,128,512]{2,1,0:T(8,128)(2,1)} %pick_blocks.1), calls=%async_computation.1 | async-start | bytes 4194304 | tf_op jit(solution)/shard_map/all_to_all | solution.py:27
  65.6 10.7 %collective-permute-start.10 = (bf16[1,2,128,1024]{3,2,1,0:T(8,128)(2,1)S(1)}, bf16[1,2,128,1024]{3,2,1,0:T(8,128)(2,1)}, u32[]{:S(2)}, u32[]{:S(2)}) collective-permute-start(bf16[1,2,128,1024]{3,2,1,0:T(8,128)(2,1)S(1)} %copy-done.7), channel_id=1, source_target_pairs={{0,28},{4,0},{8,4},{12,8},{16,12},{20,16},{24,20},{28,24},{1,29},{... | collective-permute-start | bytes 1572872 | tf_op jit(solution)/shard_map/ppermute | solution.py:23
  76.3 10.9 %collective-permute-done.10 = bf16[1,2,128,1024]{3,2,1,0:T(8,128)(2,1)} collective-permute-done((bf16[1,2,128,1024]{3,2,1,0:T(8,128)(2,1)S(1)}, bf16[1,2,128,1024]{3,2,1,0:T(8,128)(2,1)}, u32[]{:S(2)}, u32[]{:S(2)}) %collective-permute-start.10) | collective-permute-done | bytes 524320 | tf_op jit(solution)/shard_map/ppermute | solution.py:23
  87.2 3.1 %collective-permute-start.13 = (bf16[256,1024]{1,0:T(8,128)(2,1)}, bf16[256,1024]{1,0:T(8,128)(2,1)}, u32[]{:S(2)}, u32[]{:S(2)}) collective-permute-start(bf16[256,1024]{1,0:T(8,128)(2,1)} %bitcast.14.grad0), channel_id=1, source_target_pairs={{0,1},{1,2},{2,3},{3,0},{4,5},{5,6},{6,7},{7,4},{8,9},{9,10},{10,1... | collective-permute-start | bytes 1572872 | tf_op jit(solution)/shard_map/ppermute | solution.py:23
  90.3 4.4 %collective-permute-start.12 = (bf16[256,1024]{1,0:T(8,128)(2,1)}, bf16[256,1024]{1,0:T(8,128)(2,1)}, u32[]{:S(2)}, u32[]{:S(2)}) collective-permute-start(bf16[256,1024]{1,0:T(8,128)(2,1)} %bitcast.14.grad0), channel_id=1, source_target_pairs={{0,2},{1,3},{2,0},{3,1},{4,6},{5,7},{6,4},{7,5},{8,10},{9,11},{10,... | collective-permute-start | bytes 1572872 | tf_op jit(solution)/shard_map/ppermute | solution.py:23
  102.8 12.2 %collective-permute-done.12.grad2 = bf16[256,1024]{1,0:T(8,128)(2,1)} collective-permute-done((bf16[256,1024]{1,0:T(8,128)(2,1)}, bf16[256,1024]{1,0:T(8,128)(2,1)}, u32[]{:S(2)}, u32[]{:S(2)}) %collective-permute-start.12) | collective-permute-done | bytes 524320 | tf_op jit(solution)/shard_map/ppermute | solution.py:23
  117.2 8.4 %back_projection.1.grads = bf16[256,512]{1,0:T(8,128)(2,1)} custom-call(s32[2]{0:T(128)S(1)} %pad_add_fusion.spots, bf16[8,512,256]{2,1,0:T(8,128)(2,1)} %fusion.own_hbm, bf16[8,512,256]{2,1,0:T(8,128)(2,1)} %collective-permute-done.8.other_hbm, bf16[256,1024]{1,0:T(8,128)(2,1)} %bitcast.14.grad0, bf16[256,1024]{1,0:T(8,128)(2,1)} %collective-permute-done.11.grad1, ...), custom_call_target="tpu_custom_call" | custom-call | flops 2147483648 | bytes 8388608 | tf_op jit(solution)/shard_map/back_projection/pallas_call | solution.py:230
  126.6 6.5 %layer.1 = (bf16[256,512]{1,0:T(8,128)(2,1)}, bf16[2,128,512]{2,1,0:T(8,128)(2,1)}, f32[2,8,64,512]{3,2,1,0:T(8,128)}, bf16[16,128,512]{2,1,0:T(8,128)(2,1)}) custom-call(s32[2]{0:T(128)S(1)} %copy-done.2, s32[2,4]{1,0:T(2,128)S(1)} %get-tuple-element.41.holder, bf16[2,128,512]{2,1,0:T(8,128)(2,1)S(1)} %bitcast.34, bf16[8,64,512]{2,1,0:T(8,128)(2,1)S(1)} %bitcast.31, ...), custom_call_target="tpu_custom_call" | custom-call | flops 4294967296 | bytes 12582912 | tf_op jit(solution)/shard_map/layer/pallas_call | solution.py:163
  133.1 9.0 %all-to-all-start.2 = ((bf16[16,128,512]{2,1,0:T(8,128)(2,1)}), bf16[16,128,512]{2,1,0:T(8,128)(2,1)S(1)}, u32[]{:S(2)}, u32[]{:S(2)}) async-start(bf16[16,128,512]{2,1,0:T(8,128)(2,1)} %get-tuple-element.37), calls=%async_computation.2 | async-start | bytes 4194304 | tf_op jit(solution)/shard_map/all_to_all | solution.py:27
  142.1 6.7 %projection.1 = (bf16[256,1024]{1,0:T(8,128)(2,1)S(1)}, bf16[256,1024]{1,0:T(8,128)(2,1)S(1)}, bf16[256,1024]{1,0:T(8,128)(2,1)S(1)}, bf16[256,1024]{1,0:T(8,128)(2,1)S(1)}) custom-call(s32[2]{0:T(128)S(1)} %pad_add_fusion.spots, bf16[8,512,256]{2,1,0:T(8,128)(2,1)} %fusion.own_hbm, bf16[8,512,256]{2,1,0:T(8,128)(2,1)} %collective-permute-done.8.other_hbm, ...), custom_call_target="tpu_custom_call" | custom-call | flops 2147483648 | bytes 8388608 | tf_op jit(solution)/shard_map/projection/pallas_call | solution.py:272
  148.8 4.0 %collective-permute-start.14 = (bf16[256,1024]{1,0:T(8,128)(2,1)S(1)}, bf16[256,1024]{1,0:T(8,128)(2,1)S(1)}, u32[]{:S(2)}, u32[]{:S(2)}) collective-permute-start(bf16[256,1024]{1,0:T(8,128)(2,1)S(1)} %get-tuple-element.32), channel_id=1, source_target_pairs={{0,1},{1,2},{2,3},{3,0},{4,5},{5,6},{6,7},{7,4},{8,9},{9,10},{10,1... | collective-permute-start | bytes 1572872 | tf_op jit(solution)/shard_map/ppermute | solution.py:23
  152.8 3.3 %collective-permute-start.15 = (bf16[256,1024]{1,0:T(8,128)(2,1)S(1)}, bf16[256,1024]{1,0:T(8,128)(2,1)S(1)}, u32[]{:S(2)}, u32[]{:S(2)}) collective-permute-start(bf16[256,1024]{1,0:T(8,128)(2,1)S(1)} %get-tuple-element.33), channel_id=1, source_target_pairs={{0,2},{1,3},{2,0},{3,1},{4,6},{5,7},{6,4},{7,5},{8,10},{9,11},{10,... | collective-permute-start | bytes 1572872 | tf_op jit(solution)/shard_map/ppermute | solution.py:23
  156.2 3.2 %collective-permute-start.16 = (bf16[256,1024]{1,0:T(8,128)(2,1)S(1)}, bf16[256,1024]{1,0:T(8,128)(2,1)S(1)}, u32[]{:S(2)}, u32[]{:S(2)}) collective-permute-start(bf16[256,1024]{1,0:T(8,128)(2,1)S(1)} %get-tuple-element.34), channel_id=1, source_target_pairs={{0,3},{1,0},{2,1},{3,2},{4,7},{5,4},{6,5},{7,6},{8,11},{9,8},{10,9... | collective-permute-start | bytes 1572872 | tf_op jit(solution)/shard_map/ppermute | solution.py:23
  159.4 6.1 %collective-permute-done.14 = bf16[256,1024]{1,0:T(8,128)(2,1)S(1)} collective-permute-done((bf16[256,1024]{1,0:T(8,128)(2,1)S(1)}, bf16[256,1024]{1,0:T(8,128)(2,1)S(1)}, u32[]{:S(2)}, u32[]{:S(2)}) %collective-permute-start.14) | collective-permute-done | bytes 524320 | tf_op jit(solution)/shard_map/ppermute | solution.py:23
  165.4 12.1 %collective-permute-done.15 = bf16[256,1024]{1,0:T(8,128)(2,1)S(1)} collective-permute-done((bf16[256,1024]{1,0:T(8,128)(2,1)S(1)}, bf16[256,1024]{1,0:T(8,128)(2,1)S(1)}, u32[]{:S(2)}, u32[]{:S(2)}) %collective-permute-start.15) | collective-permute-done | bytes 524320 | tf_op jit(solution)/shard_map/ppermute | solution.py:23
  180.0 11.0 %all-to-all-done.2.back = bf16[16,128,512]{2,1,0:T(8,128)(2,1)S(1)} async-done(((bf16[16,128,512]{2,1,0:T(8,128)(2,1)}), bf16[16,128,512]{2,1,0:T(8,128)(2,1)S(1)}, u32[]{:S(2)}, u32[]{:S(2)}) %all-to-all-start.2) | async-done | bytes 2097184 | tf_op jit(solution)/shard_map/all_to_all | solution.py:27
  191.1 3.2 %combine.1 = (bf16[8,64,512]{2,1,0:T(8,128)(2,1)}, bf16[8,64,512]{2,1,0:T(8,128)(2,1)}) custom-call(s32[16,1]{1,0:T(8,128)S(1)} %copy.20.asked, f32[2,8,64,512]{3,2,1,0:T(8,128)} %get-tuple-element.36.own_rows_hbm, bf16[16,128,512]{2,1,0:T(8,128)(2,1)S(1)} %all-to-all-done.2.back), custom_call_target="tpu_custom_call" | custom-call | bytes 4194304 | tf_op jit(solution)/shard_map/combine/pallas_call | solution.py:325
  (54 shorter events, 32.3 us)
Async XLA Ops:
  0.6 42.7 %copy-start.4 = (bf16[1,512,256]{2,1,0:T(8,128)(2,1)S(1)}, bf16[1,512,256]{2,1,0:T(8,128)(2,1)}, u32[]{:S(2)}) copy-start(bf16[1,512,256]{2,1,0:T(8,128)(2,1)} %param.10) | copy-start | bytes 786436
  0.6 24.8 %collective-permute-start.3 = (bf16[512,256]{1,0:T(8,128)(2,1)}, bf16[512,256]{1,0:T(8,128)(2,1)S(1)}, u32[]{:S(2)}, u32[]{:S(2)}) collective-permute-start(bf16[512,256]{1,0:T(8,128)(2,1)} %bitcast.36), channel_id=1, source_target_pairs={{0,384},{32,416},{64,448},{96,480},{128,0},{160,32},{192,64},{224,... | collective-permute-start | bytes 786440 | tf_op jit(solution)/shard_map/ppermute | solution.py:23
  7.5 18.0 %collective-permute-start.2 = (bf16[512,256]{1,0:T(8,128)(2,1)}, bf16[512,256]{1,0:T(8,128)(2,1)S(1)}, u32[]{:S(2)}, u32[]{:S(2)}) collective-permute-start(bf16[512,256]{1,0:T(8,128)(2,1)} %bitcast.37), channel_id=1, source_target_pairs={{0,128},{32,160},{64,192},{96,224},{128,256},{160,288},{192,320},{... | collective-permute-start | bytes 786440 | tf_op jit(solution)/shard_map/ppermute | solution.py:23
  25.5 24.0 %collective-permute-start.4 = (bf16[512,256]{1,0:T(8,128)(2,1)S(1)}, bf16[512,256]{1,0:T(8,128)(2,1)S(1)}, u32[]{:S(2)}, u32[]{:S(2)}) collective-permute-start(bf16[512,256]{1,0:T(8,128)(2,1)S(1)} %collective-permute-done.2), channel_id=1, source_target_pairs={{0,64},{32,96},{64,128},{96,160},{128,192},{160,224},{192,256},{22... | collective-permute-start | bytes 786440 | tf_op jit(solution)/shard_map/ppermute | solution.py:23
  28.6 20.9 %collective-permute-start.5 = (bf16[512,256]{1,0:T(8,128)(2,1)S(1)}, bf16[512,256]{1,0:T(8,128)(2,1)S(1)}, u32[]{:S(2)}, u32[]{:S(2)}) collective-permute-start(bf16[512,256]{1,0:T(8,128)(2,1)S(1)} %collective-permute-done.3), channel_id=1, source_target_pairs={{0,448},{32,480},{64,0},{96,32},{128,64},{160,96},{192,128},{224,1... | collective-permute-start | bytes 786440 | tf_op jit(solution)/shard_map/ppermute | solution.py:23
  32.0 24.6 %collective-permute-start = (bf16[512,256]{1,0:T(8,128)(2,1)}, bf16[512,256]{1,0:T(8,128)(2,1)}, u32[]{:S(2)}, u32[]{:S(2)}) collective-permute-start(bf16[512,256]{1,0:T(8,128)(2,1)} %bitcast.38), channel_id=1, source_target_pairs={{0,64},{32,96},{64,128},{96,160},{128,192},{160,224},{192,256},{22... | collective-permute-start | bytes 786440 | tf_op jit(solution)/shard_map/ppermute | solution.py:23
  34.0 9.3 %collective-permute-start.7 = (bf16[256,256]{1,0:T(8,128)(2,1)S(1)}, bf16[256,256]{1,0:T(8,128)(2,1)S(1)}, u32[]{:S(2)}, u32[]{:S(2)}) collective-permute-start(bf16[256,256]{1,0:T(8,128)(2,1)S(1)} %slice.7), channel_id=1, source_target_pairs={{0,384},{32,416},{64,448},{96,480},{128,0},{160,32},{192,64},{224,... | collective-permute-start | bytes 393224 | tf_op jit(solution)/shard_map/ppermute | solution.py:23
  37.1 12.4 %collective-permute-start.6 = (bf16[256,256]{1,0:T(8,128)(2,1)S(1)}, bf16[256,256]{1,0:T(8,128)(2,1)S(1)}, u32[]{:S(2)}, u32[]{:S(2)}) collective-permute-start(bf16[256,256]{1,0:T(8,128)(2,1)S(1)} %slice.6), channel_id=1, source_target_pairs={{0,128},{32,160},{64,192},{96,224},{128,256},{160,288},{192,320},{... | collective-permute-start | bytes 393224 | tf_op jit(solution)/shard_map/ppermute | solution.py:23
  43.3 15.0 %collective-permute-start.1 = (bf16[512,256]{1,0:T(8,128)(2,1)S(1)}, bf16[512,256]{1,0:T(8,128)(2,1)}, u32[]{:S(2)}, u32[]{:S(2)}) collective-permute-start(bf16[512,256]{1,0:T(8,128)(2,1)S(1)} %bitcast.39), channel_id=1, source_target_pairs={{0,448},{32,480},{64,0},{96,32},{128,64},{160,96},{192,128},{224,1... | collective-permute-start | bytes 786440 | tf_op jit(solution)/shard_map/ppermute | solution.py:23
  50.1 75.4 %all-to-all-start.1 = ((bf16[16,128,512]{2,1,0:T(8,128)(2,1)}), bf16[16,128,512]{2,1,0:T(8,128)(2,1)S(1)}, u32[]{:S(2)}, u32[]{:S(2)}) async-start(bf16[16,128,512]{2,1,0:T(8,128)(2,1)} %pick_blocks.1), calls=%async_computation.1 | async-start | bytes 4194304 | tf_op jit(solution)/shard_map/all_to_all | solution.py:27
  55.9 9.7 %copy-start.7 = (bf16[1,2,128,1024]{3,2,1,0:T(8,128)(2,1)S(1)}, bf16[1,2,128,1024]{3,2,1,0:T(8,128)(2,1)}, u32[]{:S(2)}) copy-start(bf16[1,2,128,1024]{3,2,1,0:T(8,128)(2,1)} %param.11) | copy-start | bytes 1572868
  63.6 53.5 %collective-permute-start.8 = (bf16[8,512,256]{2,1,0:T(8,128)(2,1)}, bf16[8,512,256]{2,1,0:T(8,128)(2,1)}, u32[]{:S(2)}, u32[]{:S(2)}) collective-permute-start(bf16[8,512,256]{2,1,0:T(8,128)(2,1)} %fusion.own_hbm), channel_id=1, source_target_pairs={{0,32},{32,0},{64,96},{96,64},{128,160},{160,128},{192,224},{224,1... | collective-permute-start | bytes 6291464 | tf_op jit(solution)/shard_map/ppermute | solution.py:368
  65.6 21.6 %collective-permute-start.10 = (bf16[1,2,128,1024]{3,2,1,0:T(8,128)(2,1)S(1)}, bf16[1,2,128,1024]{3,2,1,0:T(8,128)(2,1)}, u32[]{:S(2)}, u32[]{:S(2)}) collective-permute-start(bf16[1,2,128,1024]{3,2,1,0:T(8,128)(2,1)S(1)} %copy-done.7), channel_id=1, source_target_pairs={{0,28},{4,0},{8,4},{12,8},{16,12},{20,16},{24,20},{28,24},{1,29},{... | collective-permute-start | bytes 1572872 | tf_op jit(solution)/shard_map/ppermute | solution.py:23
  87.2 15.6 %collective-permute-start.13 = (bf16[256,1024]{1,0:T(8,128)(2,1)}, bf16[256,1024]{1,0:T(8,128)(2,1)}, u32[]{:S(2)}, u32[]{:S(2)}) collective-permute-start(bf16[256,1024]{1,0:T(8,128)(2,1)} %bitcast.14.grad0), channel_id=1, source_target_pairs={{0,1},{1,2},{2,3},{3,0},{4,5},{5,6},{6,7},{7,4},{8,9},{9,10},{10,1... | collective-permute-start | bytes 1572872 | tf_op jit(solution)/shard_map/ppermute | solution.py:23
  90.3 24.7 %collective-permute-start.12 = (bf16[256,1024]{1,0:T(8,128)(2,1)}, bf16[256,1024]{1,0:T(8,128)(2,1)}, u32[]{:S(2)}, u32[]{:S(2)}) collective-permute-start(bf16[256,1024]{1,0:T(8,128)(2,1)} %bitcast.14.grad0), channel_id=1, source_target_pairs={{0,2},{1,3},{2,0},{3,1},{4,6},{5,7},{6,4},{7,5},{8,10},{9,11},{10,... | collective-permute-start | bytes 1572872 | tf_op jit(solution)/shard_map/ppermute | solution.py:23
  94.7 22.5 %collective-permute-start.11 = (bf16[256,1024]{1,0:T(8,128)(2,1)}, bf16[256,1024]{1,0:T(8,128)(2,1)}, u32[]{:S(2)}, u32[]{:S(2)}) collective-permute-start(bf16[256,1024]{1,0:T(8,128)(2,1)} %bitcast.14.grad0), channel_id=1, source_target_pairs={{0,3},{1,0},{2,1},{3,2},{4,7},{5,4},{6,5},{7,6},{8,11},{9,8},{10,9... | collective-permute-start | bytes 1572872 | tf_op jit(solution)/shard_map/ppermute | solution.py:23
  97.7 27.8 %collective-permute-start.9 = (bf16[1,2,128,512]{3,2,1,0:T(8,128)(2,1)}, bf16[1,2,128,512]{3,2,1,0:T(8,128)(2,1)S(1)}, u32[]{:S(2)}, u32[]{:S(2)}) collective-permute-start(bf16[1,2,128,512]{3,2,1,0:T(8,128)(2,1)} %param.7), channel_id=1, source_target_pairs={{0,4},{4,8},{8,12},{12,16},{16,20},{20,24},{24,28},{28,0},{1,5},{5... | collective-permute-start | bytes 786440 | tf_op jit(solution)/shard_map/ppermute | solution.py:23
  99.7 25.8 %copy-start = (bf16[1,8,64,512]{3,2,1,0:T(8,128)(2,1)S(1)}, bf16[1,8,64,512]{3,2,1,0:T(8,128)(2,1)}, u32[]{:S(2)}) copy-start(bf16[1,8,64,512]{3,2,1,0:T(8,128)(2,1)} %param.8) | copy-start | bytes 1572868
  99.7 25.9 %copy-start.1 = (bf16[1,8,64,512]{3,2,1,0:T(8,128)(2,1)S(1)}, bf16[1,8,64,512]{3,2,1,0:T(8,128)(2,1)}, u32[]{:S(2)}) copy-start(bf16[1,8,64,512]{3,2,1,0:T(8,128)(2,1)} %param.9) | copy-start | bytes 1572868
  99.8 25.9 %copy-start.2 = (s32[2]{0:T(128)S(1)}, s32[2]{0:T(128)}, u32[]{:S(2)}) copy-start(s32[2]{0:T(128)} %counts.1) | copy-start | bytes 28
  133.1 57.9 %all-to-all-start.2 = ((bf16[16,128,512]{2,1,0:T(8,128)(2,1)}), bf16[16,128,512]{2,1,0:T(8,128)(2,1)S(1)}, u32[]{:S(2)}, u32[]{:S(2)}) async-start(bf16[16,128,512]{2,1,0:T(8,128)(2,1)} %get-tuple-element.37), calls=%async_computation.2 | async-start | bytes 4194304 | tf_op jit(solution)/shard_map/all_to_all | solution.py:27
  148.8 16.6 %collective-permute-start.14 = (bf16[256,1024]{1,0:T(8,128)(2,1)S(1)}, bf16[256,1024]{1,0:T(8,128)(2,1)S(1)}, u32[]{:S(2)}, u32[]{:S(2)}) collective-permute-start(bf16[256,1024]{1,0:T(8,128)(2,1)S(1)} %get-tuple-element.32), channel_id=1, source_target_pairs={{0,1},{1,2},{2,3},{3,0},{4,5},{5,6},{6,7},{7,4},{8,9},{9,10},{10,1... | collective-permute-start | bytes 1572872 | tf_op jit(solution)/shard_map/ppermute | solution.py:23
  152.8 24.7 %collective-permute-start.15 = (bf16[256,1024]{1,0:T(8,128)(2,1)S(1)}, bf16[256,1024]{1,0:T(8,128)(2,1)S(1)}, u32[]{:S(2)}, u32[]{:S(2)}) collective-permute-start(bf16[256,1024]{1,0:T(8,128)(2,1)S(1)} %get-tuple-element.33), channel_id=1, source_target_pairs={{0,2},{1,3},{2,0},{3,1},{4,6},{5,7},{6,4},{7,5},{8,10},{9,11},{10,... | collective-permute-start | bytes 1572872 | tf_op jit(solution)/shard_map/ppermute | solution.py:23
  156.2 22.7 %collective-permute-start.16 = (bf16[256,1024]{1,0:T(8,128)(2,1)S(1)}, bf16[256,1024]{1,0:T(8,128)(2,1)S(1)}, u32[]{:S(2)}, u32[]{:S(2)}) collective-permute-start(bf16[256,1024]{1,0:T(8,128)(2,1)S(1)} %get-tuple-element.34), channel_id=1, source_target_pairs={{0,3},{1,0},{2,1},{3,2},{4,7},{5,4},{6,5},{7,6},{8,11},{9,8},{10,9... | collective-permute-start | bytes 1572872 | tf_op jit(solution)/shard_map/ppermute | solution.py:23
  (3 other events, 8.6 us)

commit v8 on v7

--- a/solution.py
+++ b/solution.py
@@ -6,7 +6,7 @@
 from jax.sharding import PartitionSpec as P
 
 HD = 128
-OFFSETS = (0, -1, 1, -2, 2, -3, 3, 4)
+DELTAS = (0, 1, -2, -1, -4, -3, -6, -5, -8, 3, 2, 5, 4, 7, 6, 9)
 F32 = jnp.float32
 BF16 = jnp.bfloat16
 NT = (((1,), (1,)), ((), ()))
@@ -21,6 +21,15 @@
 def passed_along(block, axis, distance):
     count = lax.axis_size(axis)
     return lax.ppermute(block, axis, [(i, (i + distance) % count) for i in range(count)])
+
+
+def swapped(block):
+    return lax.ppermute(block, "dp", [(i, i ^ 1) for i in range(lax.axis_size("dp"))])
+
+
+def along_ring(block, chips):
+    count = lax.axis_size("dp")
+    return lax.ppermute(block, "dp", [(i, (i + (1 - i % 2 * 2) * 2 * chips) % count) for i in range(count)])
 
 
 def exchanged(slots):
@@ -192,99 +201,94 @@
     return copies
 
 
-def placed(spots, step, per, groups):
-    chips = len(OFFSETS)
-    kind, k = step // chips, lax.rem(step, chips)
-    offset = jnp.int32(0)
-    for i, value in enumerate(OFFSETS):
-        offset = jnp.where(k == i, value, offset)
-    own = spots[0] + kind * (1 - 2 * lax.rem(spots[0], 2))
-    block = lax.rem(own + 2 * offset + 2 * chips, 2 * chips)
-    return lax.rem(block // per + groups - spots[1], groups), lax.rem(block, per)
-
-
-def back_kernel(spots, own_hbm, other_hbm, grad0, grad1, grad2, grad3, out_hbm, weight, held, total, out, weight_sem, held_sem):
-    groups, rows, columns = held.shape
-    chips, _, block = own_hbm.shape
-    per = columns // block
+def weight_copies(refs, weight, sem):
+    first, pairs = 0, []
+    for ref in refs:
+        count = ref.shape[0] // weight.shape[1]
+        for i in range(count):
+            pairs.append((ref.at[pl.ds(i * weight.shape[1], weight.shape[1])], weight.at[first + i]))
+        first += count
+    return copies_in(pairs, sem)
+
+
+def back_kernel(table, grad0, grad1, grad2, grad3, *refs):
+    *blocks, out_hbm, weight, held, total, out, weight_sem, held_sem = refs
+    block = weight.shape[2]
     waiting = copies_in([(ref, held.at[j]) for j, ref in enumerate((grad0, grad1, grad2, grad3))], held_sem)
-    waiting += copies_in([(ref, weight.at[pl.ds(i * chips, chips)]) for i, ref in enumerate((own_hbm, other_hbm))], weight_sem)
+    waiting += weight_copies(blocks, weight, weight_sem)
     for copy in waiting:
         copy.wait()
     total[...] = jnp.zeros_like(total)
 
-    @pl.loop(0, 2 * chips)
+    @pl.loop(0, weight.shape[0], unroll=4)
     def _(step):
-        group, place = placed(spots, step, per, groups)
-        at = pl.ds(pl.multiple_of(place * block, block), block)
-        total[...] += lax.dot_general(held[group, :, at], weight[step], NT, preferred_element_type=F32)
+        at = pl.ds(pl.multiple_of(table[1, step] * block, block), block)
+        total[...] += lax.dot_general(held[table[0, step], :, at], weight[step], NT, preferred_element_type=F32)
 
     out[...] = total[...].astype(BF16)
     pltpu.sync_copy(out, out_hbm)
 
 
-def back_projected(spots, own, other, held):
+def back_projected(table, held, blocks):
     groups = len(held)
     rows, columns = held[0].shape
-    _, features, block = own.shape
+    features, block = blocks[0].shape
+    count = table.shape[1]
     return pl.pallas_call(
         back_kernel,
         out_shape=pltpu.HBM((rows, features), BF16),
-        in_specs=[SMEM] + [HBM] * (2 + groups),
+        in_specs=[SMEM] + [HBM] * (len(blocks) + groups),
         out_specs=HBM,
         scratch_shapes=[
-            pltpu.VMEM((2 * own.shape[0], features, block), BF16),
+            pltpu.VMEM((count, features, block), BF16),
             pltpu.VMEM((groups, rows, columns), BF16),
             pltpu.VMEM((rows, features), F32),
             pltpu.VMEM((rows, features), BF16),
-            pltpu.SemaphoreType.DMA((2,)),
+            pltpu.SemaphoreType.DMA((count,)),
             pltpu.SemaphoreType.DMA((groups,)),
         ],
         compiler_params=PARAMS,
         cost_estimate=cost(2 * 2**30, 8 * 2**20),
         name="back_projection",
-    )(spots, in_hbm(own), in_hbm(other), *map(in_hbm, held))
-
-
-def project_kernel(spots, own_hbm, other_hbm, attended_hbm, out0, out1, out2, out3, weight, attended, terms, weight_sem, in_sem):
-    groups, _, columns = terms.shape
-    chips, _, block = own_hbm.shape
-    per = columns // block
-    waiting = copies_in([(attended_hbm, attended)], in_sem)
-    waiting += copies_in([(ref, weight.at[pl.ds(i * chips, chips)]) for i, ref in enumerate((own_hbm, other_hbm))], weight_sem)
+    )(table, *map(in_hbm, held), *map(in_hbm, blocks))
+
+
+def project_kernel(table, attended_hbm, *refs):
+    *blocks, out0, out1, out2, out3, weight, attended, terms, weight_sem, in_sem = refs
+    block = weight.shape[2]
+    waiting = copies_in([(attended_hbm, attended)], in_sem) + weight_copies(blocks, weight, weight_sem)
     for copy in waiting:
         copy.wait()
 
-    @pl.loop(0, 2 * chips)
+    @pl.loop(0, weight.shape[0], unroll=4)
     def _(step):
-        group, place = placed(spots, step, per, groups)
-        at = pl.ds(pl.multiple_of(place * block, block), block)
-        terms[group, :, at] = jnp.dot(attended[...], weight[step], preferred_element_type=F32).astype(BF16)
+        at = pl.ds(pl.multiple_of(table[1, step] * block, block), block)
+        terms[table[0, step], :, at] = jnp.dot(attended[...], weight[step], preferred_element_type=F32).astype(BF16)
 
     for j, out in enumerate((out0, out1, out2, out3)):
         out[...] = terms[j]
 
 
-def projected(spots, own, other, attended, groups):
-    chips, features, block = own.shape
-    rows, columns = attended.shape[0], 2 * chips * block // groups
-    shape = jax.ShapeDtypeStruct((rows, columns), BF16)
+def projected(table, attended, blocks, groups):
+    features, block = blocks[0].shape
+    rows, count = attended.shape[0], table.shape[1]
+    columns = count * block // groups
     return pl.pallas_call(
         project_kernel,
-        out_shape=[shape] * groups,
-        in_specs=[SMEM] + [HBM] * 3,
+        out_shape=[jax.ShapeDtypeStruct((rows, columns), BF16)] * groups,
+        in_specs=[SMEM] + [HBM] * (1 + len(blocks)),
         out_specs=[VMEM] * groups,
         scratch_shapes=[
-            pltpu.VMEM((2 * chips, features, block), BF16),
+            pltpu.VMEM((count, features, block), BF16),
             pltpu.VMEM(attended.shape, BF16),
             pltpu.VMEM((groups, rows, columns), BF16),
-            pltpu.SemaphoreType.DMA((2,)),
+            pltpu.SemaphoreType.DMA((count,)),
             pltpu.SemaphoreType.DMA((1,)),
         ],
         compiler_params=PARAMS,
         cost_estimate=cost(2 * 2**30, 8 * 2**20),
         name="projection",
-    )(spots, in_hbm(own), in_hbm(other), in_hbm(attended))
+    )(table, in_hbm(attended), *map(in_hbm, blocks))
 
 
 def combine_kernel(asked, own_rows_hbm, back, key_grads_hbm, value_grads_hbm, own_rows, total, grads, in_sem, out_sem):
@@ -345,7 +349,11 @@
     mem_count = keys.shape[0]
     groups = lax.axis_size("dp")
     tensor = lax.axis_size("tensor")
-    spots = jnp.stack([lax.axis_index("dp"), lax.axis_index("tensor")]).astype(jnp.int32)
+    me = lax.axis_index("dp")
+    sign = 1 - 2 * lax.rem(me, 2)
+    block_of = (me + sign * jnp.array(DELTAS, jnp.int32) + 2 * groups) % groups
+    per = groups // tensor
+    table = jnp.stack([(block_of // per + tensor - lax.axis_index("tensor")) % tensor, block_of % per]).astype(jnp.int32)
 
     holder = neg_ids // mem_count
     spot = neg_ids - holder * mem_count
@@ -354,29 +362,27 @@
     asked = exchanged(request.reshape(groups, 1))
 
     weight = out_weight[0]
-    half = weight.shape[0] // 2
-    below, above = passed_along(weight, "dp", 2), passed_along(weight, "dp", -2)
-    below2, above2 = passed_along(weight, "dp", 4), passed_along(weight, "dp", -4)
-    below2, above2, asked = lax.optimization_barrier((below2, above2, asked))
-    below3, above3 = passed_along(below2, "dp", 2), passed_along(above2, "dp", -2)
-    far_low, far_high = passed_along(below2[:half], "dp", 4), passed_along(above2[half:], "dp", -4)
+    other = swapped(weight)
+    pair = jnp.concatenate([weight, other])
+    near, next_near = along_ring(pair, 1), along_ring(pair, 2)
+    grads = passed_along(sent_grads, "section", -1)[0]
+    next_near, asked, grads = lax.optimization_barrier((next_near, asked, grads))
+    third, far = along_ring(next_near, 1), along_ring(next_near[: weight.shape[0]], 2)
     slots = picked_slots(asked, keys, values)
-    slots, below3, above3, far_low, far_high = lax.optimization_barrier((slots, below3, above3, far_low, far_high))
+    slots, near, third, far = lax.optimization_barrier((slots, near, third, far))
     recv = exchanged(slots)
-
-    own_kind = jnp.stack([weight, below, above, below2, above2, below3, above3, jnp.concatenate([far_low, far_high])])
-    other_kind = lax.ppermute(own_kind, "dp", [(i, i ^ 1) for i in range(groups)])
+    blocks = [weight, other, near, next_near, third, far]
+    blocks += [swapped(block) for block in blocks[2:]]
 
     queries = passed_along(sent_queries, "section", 1)[0]
-    grads = passed_along(sent_grads, "section", -1)[0]
     docs, query_count, features = queries.shape
     grad_rows = grads.reshape(docs * query_count, grads.shape[2])
     held = [grad_rows] + [passed_along(grad_rows, "tensor", -j) for j in range(1, tensor)]
-    grad_attended = back_projected(spots, own_kind, other_kind, held)
+    grad_attended = back_projected(table, held, blocks)
 
     attended, query_grads, own_rows, slots = layer(counts, holder, queries, keys, values, recv, grad_attended)
     back = exchanged(slots)
-    terms = projected(spots, own_kind, other_kind, attended, tensor)
+    terms = projected(table, attended, blocks, tensor)
     arrived = [terms[0]] + [passed_along(terms[j], "tensor", j) for j in range(1, tensor)]
     mixed = sum(term.astype(F32) for term in arrived).astype(BF16).reshape(1, docs, query_count, -1)
 

time: 195 us -> 181 us (0.928)
  local copies, waits for them, and re-layouts: 8.76 us -> 3.95 us
  Pallas kernels: 27.8 us -> 23.7 us
  starting transfers between devices: 79.9 us -> 77.2 us
    ppermute x16 -> x8, starting transfers between devices: 63.2 us -> 28.3 us  [passed_along(): lax.ppermute(block, axis, [(i, (i + distance) % count) for i in range(cou...]
    ppermute x1 -> x9, starting transfers between devices: 2 us -> 35.4 us  [the longest x5 19.1 us: swapped(): lax.ppermute(block, 'dp', [(i, i ^ 1) for i in range(lax.axis_size('dp'))])]
    ppermute x16 -> x8, waiting for transfers between devices: 47.8 us -> 31.4 us  [passed_along(): lax.ppermute(block, axis, [(i, (i + distance) % count) for i in range(cou...]
    all_to_all x2, waiting for transfers between devices: 11 us -> 18.8 us  [exchanged(): return lax.all_to_all(slots, 'dp', split_axis=0, concat_axis=0, tiled=True)]
    ppermute x1 -> x9, waiting for transfers between devices: 0.01 us -> 6.7 us  [the longest x4 6.68 us: along_ring(): lax.ppermute(block, 'dp', [(i, (i + (1 - i % 2 * 2) * 2 * chips) % count)...]
    unnamed x23 -> x24, local copies, waits for them, and re-layouts: 8.57 us -> 2.8 us
    pallas_call x1, Pallas kernels: 8.41 us -> 6.12 us  [back_projected(): pl.pallas_call(back_kernel, out_shape=pltpu.HBM((rows, features), BF16),...]
  transfers between devices with their start and end apart: 19 -> 19, of which waited for: 8 -> 9; matrix products, arithmetic and copies ran while one was open for 5% -> 3% of each run, Pallas kernels for 9% -> 8%
where the time goes in v8:
time: 181 us; the launch traced here: 180 us
  starting transfers between devices  77.2 us (43%)
  waiting for transfers between devices  57 us (31%)
  Pallas kernels  23.7 us (13%)
  blocking collectives  13.5 us (7%)
  local copies, waits for them, and re-layouts  3.95 us (2%)
  other arithmetic  3.45 us (2%)
    ppermute x8, waiting for transfers between devices, passed_along(): lax.ppermute(block, axis, [(i, (i + distance) % count) for i in range(cou...  31.4 us
    ppermute x8, starting transfers between devices, passed_along(): lax.ppermute(block, axis, [(i, (i + distance) % count) for i in range(cou...  28.3 us
    ppermute x5, starting transfers between devices, swapped(): lax.ppermute(block, 'dp', [(i, i ^ 1) for i in range(lax.axis_size('dp'))])  19.1 us
    all_to_all x2, waiting for transfers between devices, exchanged(): return lax.all_to_all(slots, 'dp', split_axis=0, concat_axis=0, tiled=True)  18.8 us
    ppermute x4, starting transfers between devices, along_ring(): lax.ppermute(block, 'dp', [(i, (i + (1 - i % 2 * 2) * 2 * chips) % count)...  16.4 us
    all_to_all x1, blocking collectives, exchanged(): return lax.all_to_all(slots, 'dp', split_axis=0, concat_axis=0, tiled=True)  13.5 us
    all_to_all x2, starting transfers between devices, exchanged(): return lax.all_to_all(slots, 'dp', split_axis=0, concat_axis=0, tiled=True)  13.4 us
    ppermute x4, waiting for transfers between devices, along_ring(): lax.ppermute(block, 'dp', [(i, (i + (1 - i % 2 * 2) * 2 * chips) % count)...  6.68 us
  transfers between devices with their start and end apart: 19, of which 9 were waited for; matrix products, arithmetic and copies ran while one was open for 3% of the time, Pallas kernels for 8%

profile of v8, /device:TPU:1, one launch (start us, length us, event | category | flops | bytes accessed | tf_op | source)
XLA Modules:
  0.0 179.8 jit_solution(4970757480011285338)
XLA Ops:
  0.6 8.8 %collective-permute-start.1 = (bf16[512,256]{1,0:T(8,128)(2,1)}, bf16[512,256]{1,0:T(8,128)(2,1)S(1)}, u32[]{:S(2)}, u32[]{:S(2)}) collective-permute-start(bf16[512,256]{1,0:T(8,128)(2,1)} %bitcast.23), channel_id=1, source_target_pairs={{0,32},{32,0},{64,96},{96,64},{128,160},{160,128},{192,224},{224,1... | collective-permute-start | bytes 786440 | tf_op jit(solution)/shard_map/ppermute | solution.py:27
  9.4 5.3 %collective-permute-start.3 = (bf16[1,2,128,1024]{3,2,1,0:T(8,128)(2,1)}, bf16[1,2,128,1024]{3,2,1,0:T(8,128)(2,1)S(1)}, u32[]{:S(2)}, u32[]{:S(2)}) collective-permute-start(bf16[1,2,128,1024]{3,2,1,0:T(8,128)(2,1)} %param.12), channel_id=1, source_target_pairs={{0,28},{4,0},{8,4},{12,8},{16,12},{20,16},{24,20},{28,24},{1,29},{... | collective-permute-start | bytes 1572872 | tf_op jit(solution)/shard_map/ppermute | solution.py:23
  15.8 5.9 %collective-permute-start.2 = (bf16[1024,256]{1,0:T(8,128)(2,1)S(1)}, bf16[1024,256]{1,0:T(8,128)(2,1)}, u32[]{:S(2)}, u32[]{:S(2)}) collective-permute-start(bf16[1024,256]{1,0:T(8,128)(2,1)S(1)} %pad_maximum_fusion), channel_id=1, source_target_pairs={{0,128},{32,416},{64,192},{96,480},{128,256},{160,32},{192,320},{2... | collective-permute-start | bytes 1572872 | tf_op jit(solution)/shard_map/ppermute | solution.py:32
  22.6 13.5 %all_to_all.19 = s32[16,1,1]{2,1,0:T(1,128)S(1)} all-to-all(s32[16,1,1]{2,1,0:T(1,128)S(1)} %copy.20), channel_id=1, replica_groups=mesh['dp'=16,'section'=8,'tensor'=4] {'dp'}, dimensions={0} | all-to-all | bytes 128 | tf_op jit(solution)/shard_map/all_to_all | solution.py:36
  39.1 5.3 %collective-permute-start.5 = (bf16[1024,256]{1,0:T(8,128)(2,1)}, bf16[1024,256]{1,0:T(8,128)(2,1)}, u32[]{:S(2)}, u32[]{:S(2)}) collective-permute-start(bf16[1024,256]{1,0:T(8,128)(2,1)} %collective-permute-done.2.refs_3_), channel_id=1, source_target_pairs={{0,64},{32,480},{64,128},{96,32},{128,192},{160,96},{192,256},{224... | collective-permute-start | bytes 1572872 | tf_op jit(solution)/shard_map/ppermute | solution.py:32
  48.0 3.0 %pick_blocks.1 = bf16[16,128,512]{2,1,0:T(8,128)(2,1)} custom-call(s32[16,1]{1,0:T(8,128)S(1)} %copy.21.asked, bf16[8,64,512]{2,1,0:T(8,128)(2,1)} %bitcast.17, bf16[8,64,512]{2,1,0:T(8,128)(2,1)} %bitcast.19), custom_call_target="tpu_custom_call" | custom-call | bytes 4194304 | tf_op jit(solution)/shard_map/pick_blocks/pallas_call | solution.py:75
  51.1 6.7 %collective-permute-done.6.refs_5_ = bf16[512,256]{1,0:T(8,128)(2,1)} collective-permute-done((bf16[512,256]{1,0:T(8,128)(2,1)S(1)}, bf16[512,256]{1,0:T(8,128)(2,1)}, u32[]{:S(2)}, u32[]{:S(2)}) %collective-permute-start.6) | collective-permute-done | bytes 262176 | tf_op jit(solution)/shard_map/ppermute | solution.py:32
  57.8 8.4 %all-to-all-start.1 = ((bf16[16,128,512]{2,1,0:T(8,128)(2,1)}), bf16[16,128,512]{2,1,0:T(8,128)(2,1)S(1)}, u32[]{:S(2)}, u32[]{:S(2)}) async-start(bf16[16,128,512]{2,1,0:T(8,128)(2,1)} %pick_blocks.1), calls=%async_computation.1 | async-start | bytes 4194304 | tf_op jit(solution)/shard_map/all_to_all | solution.py:36
  66.2 3.1 %collective-permute-start.9 = (bf16[256,1024]{1,0:T(8,128)(2,1)S(1)}, bf16[256,1024]{1,0:T(8,128)(2,1)S(1)}, u32[]{:S(2)}, u32[]{:S(2)}) collective-permute-start(bf16[256,1024]{1,0:T(8,128)(2,1)S(1)} %bitcast.28), channel_id=1, source_target_pairs={{0,1},{1,2},{2,3},{3,0},{4,5},{5,6},{6,7},{7,4},{8,9},{9,10},{10,1... | collective-permute-start | bytes 1572872 | tf_op jit(solution)/shard_map/ppermute | solution.py:23
  69.4 4.4 %collective-permute-start.8 = (bf16[256,1024]{1,0:T(8,128)(2,1)S(1)}, bf16[256,1024]{1,0:T(8,128)(2,1)}, u32[]{:S(2)}, u32[]{:S(2)}) collective-permute-start(bf16[256,1024]{1,0:T(8,128)(2,1)S(1)} %bitcast.29), channel_id=1, source_target_pairs={{0,2},{1,3},{2,0},{3,1},{4,6},{5,7},{6,4},{7,5},{8,10},{9,11},{10,... | collective-permute-start | bytes 1572872 | tf_op jit(solution)/shard_map/ppermute | solution.py:23
  73.7 3.1 %collective-permute-start.7 = (bf16[256,1024]{1,0:T(8,128)(2,1)S(1)}, bf16[256,1024]{1,0:T(8,128)(2,1)}, u32[]{:S(2)}, u32[]{:S(2)}) collective-permute-start(bf16[256,1024]{1,0:T(8,128)(2,1)S(1)} %bitcast.30), channel_id=1, source_target_pairs={{0,3},{1,0},{2,1},{3,2},{4,7},{5,4},{6,5},{7,6},{8,11},{9,8},{10,9... | collective-permute-start | bytes 1572872 | tf_op jit(solution)/shard_map/ppermute | solution.py:23
  85.6 9.5 %collective-permute-done.8.grad2 = bf16[256,1024]{1,0:T(8,128)(2,1)} collective-permute-done((bf16[256,1024]{1,0:T(8,128)(2,1)S(1)}, bf16[256,1024]{1,0:T(8,128)(2,1)}, u32[]{:S(2)}, u32[]{:S(2)}) %collective-permute-start.8) | collective-permute-done | bytes 524320 | tf_op jit(solution)/shard_map/ppermute | solution.py:23
  101.8 6.1 %back_projection.1.grads = bf16[256,512]{1,0:T(8,128)(2,1)} custom-call(s32[2,16]{1,0:T(2,128)S(1)} %pad_add_fusion.table, bf16[256,1024]{1,0:T(8,128)(2,1)} %bitcast.31, bf16[256,1024]{1,0:T(8,128)(2,1)} %collective-permute-done.7.grad1, bf16[256,1024]{1,0:T(8,128)(2,1)} %collective-permute-done.8.grad2, bf16[256,1024]{1,0:T(8,128)(2,1)} %copy-done.7, ...), custom_call_target="tpu_custom_call" | custom-call | flops 2147483648 | bytes 8388608 | tf_op jit(solution)/shard_map/back_projection/pallas_call | solution.py:237
  109.2 6.0 %all-to-all-done.1.recv = bf16[16,128,512]{2,1,0:T(8,128)(2,1)S(1)} async-done(((bf16[16,128,512]{2,1,0:T(8,128)(2,1)}), bf16[16,128,512]{2,1,0:T(8,128)(2,1)S(1)}, u32[]{:S(2)}, u32[]{:S(2)}) %all-to-all-start.1) | async-done | bytes 2097184 | tf_op jit(solution)/shard_map/all_to_all | solution.py:36
  116.1 6.6 %layer.1 = (bf16[256,512]{1,0:T(8,128)(2,1)}, bf16[2,128,512]{2,1,0:T(8,128)(2,1)}, f32[2,8,64,512]{3,2,1,0:T(8,128)}, bf16[16,128,512]{2,1,0:T(8,128)(2,1)}) custom-call(s32[2]{0:T(128)S(1)} %copy-done.2, s32[2,4]{1,0:T(2,128)S(1)} %get-tuple-element.39.holder, bf16[2,128,512]{2,1,0:T(8,128)(2,1)S(1)} %bitcast.21, bf16[8,64,512]{2,1,0:T(8,128)(2,1)S(1)} %bitcast.18, ...), custom_call_target="tpu_custom_call" | custom-call | flops 4294967296 | bytes 12582912 | tf_op jit(solution)/shard_map/layer/pallas_call | solution.py:172
  122.7 5.0 %all-to-all-start.2 = ((bf16[16,128,512]{2,1,0:T(8,128)(2,1)}), bf16[16,128,512]{2,1,0:T(8,128)(2,1)S(1)}, u32[]{:S(2)}, u32[]{:S(2)}) async-start(bf16[16,128,512]{2,1,0:T(8,128)(2,1)} %get-tuple-element.35), calls=%async_computation.2 | async-start | bytes 4194304 | tf_op jit(solution)/shard_map/all_to_all | solution.py:36
  127.7 4.9 %projection.1 = (bf16[256,1024]{1,0:T(8,128)(2,1)S(1)}, bf16[256,1024]{1,0:T(8,128)(2,1)S(1)}, bf16[256,1024]{1,0:T(8,128)(2,1)S(1)}, bf16[256,1024]{1,0:T(8,128)(2,1)S(1)}) custom-call(s32[2,16]{1,0:T(2,128)S(1)} %pad_add_fusion.table, bf16[256,512]{1,0:T(8,128)(2,1)} %get-tuple-element.28.attended_hbm, bf16[512,256]{1,0:T(8,128)(2,1)} %bitcast.26, ...), custom_call_target="tpu_custom_call" | custom-call | flops 2147483648 | bytes 8388608 | tf_op jit(solution)/shard_map/projection/pallas_call | solution.py:276
  132.6 3.1 %collective-permute-start.14 = (bf16[256,1024]{1,0:T(8,128)(2,1)S(1)}, bf16[256,1024]{1,0:T(8,128)(2,1)S(1)}, u32[]{:S(2)}, u32[]{:S(2)}) collective-permute-start(bf16[256,1024]{1,0:T(8,128)(2,1)S(1)} %get-tuple-element.30), channel_id=1, source_target_pairs={{0,1},{1,2},{2,3},{3,0},{4,5},{5,6},{6,7},{7,4},{8,9},{9,10},{10,1... | collective-permute-start | bytes 1572872 | tf_op jit(solution)/shard_map/ppermute | solution.py:23
  135.7 4.4 %collective-permute-start.15 = (bf16[256,1024]{1,0:T(8,128)(2,1)S(1)}, bf16[256,1024]{1,0:T(8,128)(2,1)S(1)}, u32[]{:S(2)}, u32[]{:S(2)}) collective-permute-start(bf16[256,1024]{1,0:T(8,128)(2,1)S(1)} %get-tuple-element.31), channel_id=1, source_target_pairs={{0,2},{1,3},{2,0},{3,1},{4,6},{5,7},{6,4},{7,5},{8,10},{9,11},{10,... | collective-permute-start | bytes 1572872 | tf_op jit(solution)/shard_map/ppermute | solution.py:23
  140.1 3.1 %collective-permute-start.16 = (bf16[256,1024]{1,0:T(8,128)(2,1)S(1)}, bf16[256,1024]{1,0:T(8,128)(2,1)S(1)}, u32[]{:S(2)}, u32[]{:S(2)}) collective-permute-start(bf16[256,1024]{1,0:T(8,128)(2,1)S(1)} %get-tuple-element.32), channel_id=1, source_target_pairs={{0,3},{1,0},{2,1},{3,2},{4,7},{5,4},{6,5},{7,6},{8,11},{9,8},{10,9... | collective-permute-start | bytes 1572872 | tf_op jit(solution)/shard_map/ppermute | solution.py:23
  143.2 6.0 %collective-permute-done.14 = bf16[256,1024]{1,0:T(8,128)(2,1)S(1)} collective-permute-done((bf16[256,1024]{1,0:T(8,128)(2,1)S(1)}, bf16[256,1024]{1,0:T(8,128)(2,1)S(1)}, u32[]{:S(2)}, u32[]{:S(2)}) %collective-permute-start.14) | collective-permute-done | bytes 524320 | tf_op jit(solution)/shard_map/ppermute | solution.py:23
  149.2 12.2 %collective-permute-done.15 = bf16[256,1024]{1,0:T(8,128)(2,1)S(1)} collective-permute-done((bf16[256,1024]{1,0:T(8,128)(2,1)S(1)}, bf16[256,1024]{1,0:T(8,128)(2,1)S(1)}, u32[]{:S(2)}, u32[]{:S(2)}) %collective-permute-start.15) | collective-permute-done | bytes 524320 | tf_op jit(solution)/shard_map/ppermute | solution.py:23
  163.8 12.8 %all-to-all-done.2.back = bf16[16,128,512]{2,1,0:T(8,128)(2,1)S(1)} async-done(((bf16[16,128,512]{2,1,0:T(8,128)(2,1)}), bf16[16,128,512]{2,1,0:T(8,128)(2,1)S(1)}, u32[]{:S(2)}, u32[]{:S(2)}) %all-to-all-start.2) | async-done | bytes 2097184 | tf_op jit(solution)/shard_map/all_to_all | solution.py:36
  176.6 3.2 %combine.1 = (bf16[8,64,512]{2,1,0:T(8,128)(2,1)}, bf16[8,64,512]{2,1,0:T(8,128)(2,1)}) custom-call(s32[16,1]{1,0:T(8,128)S(1)} %copy.21.asked, f32[2,8,64,512]{3,2,1,0:T(8,128)} %get-tuple-element.34.own_rows_hbm, bf16[16,128,512]{2,1,0:T(8,128)(2,1)S(1)} %all-to-all-done.2.back), custom_call_target="tpu_custom_call" | custom-call | bytes 4194304 | tf_op jit(solution)/shard_map/combine/pallas_call | solution.py:329
  (56 shorter events, 28.5 us)
Async XLA Ops:
  0.6 14.1 %collective-permute-start.1 = (bf16[512,256]{1,0:T(8,128)(2,1)}, bf16[512,256]{1,0:T(8,128)(2,1)S(1)}, u32[]{:S(2)}, u32[]{:S(2)}) collective-permute-start(bf16[512,256]{1,0:T(8,128)(2,1)} %bitcast.23), channel_id=1, source_target_pairs={{0,32},{32,0},{64,96},{96,64},{128,160},{160,128},{192,224},{224,1... | collective-permute-start | bytes 786440 | tf_op jit(solution)/shard_map/ppermute | solution.py:27
  9.4 29.6 %collective-permute-start.3 = (bf16[1,2,128,1024]{3,2,1,0:T(8,128)(2,1)}, bf16[1,2,128,1024]{3,2,1,0:T(8,128)(2,1)S(1)}, u32[]{:S(2)}, u32[]{:S(2)}) collective-permute-start(bf16[1,2,128,1024]{3,2,1,0:T(8,128)(2,1)} %param.12), channel_id=1, source_target_pairs={{0,28},{4,0},{8,4},{12,8},{16,12},{20,16},{24,20},{28,24},{1,29},{... | collective-permute-start | bytes 1572872 | tf_op jit(solution)/shard_map/ppermute | solution.py:23
  15.8 23.2 %collective-permute-start.2 = (bf16[1024,256]{1,0:T(8,128)(2,1)S(1)}, bf16[1024,256]{1,0:T(8,128)(2,1)}, u32[]{:S(2)}, u32[]{:S(2)}) collective-permute-start(bf16[1024,256]{1,0:T(8,128)(2,1)S(1)} %pad_maximum_fusion), channel_id=1, source_target_pairs={{0,128},{32,416},{64,192},{96,480},{128,256},{160,32},{192,320},{2... | collective-permute-start | bytes 1572872 | tf_op jit(solution)/shard_map/ppermute | solution.py:32
  36.4 14.6 %collective-permute-start.4 = (bf16[1024,256]{1,0:T(8,128)(2,1)S(1)}, bf16[1024,256]{1,0:T(8,128)(2,1)}, u32[]{:S(2)}, u32[]{:S(2)}) collective-permute-start(bf16[1024,256]{1,0:T(8,128)(2,1)S(1)} %pad_maximum_fusion), channel_id=1, source_target_pairs={{0,64},{32,480},{64,128},{96,32},{128,192},{160,96},{192,256},{224... | collective-permute-start | bytes 1572872 | tf_op jit(solution)/shard_map/ppermute | solution.py:32
  39.0 34.7 %copy-start.6 = (bf16[1,2,128,1024]{3,2,1,0:T(8,128)(2,1)}, bf16[1,2,128,1024]{3,2,1,0:T(8,128)(2,1)S(1)}, u32[]{:S(2)}) copy-start(bf16[1,2,128,1024]{3,2,1,0:T(8,128)(2,1)S(1)} %collective-permute-done.3) | copy-start | bytes 1572868
  39.1 18.7 %collective-permute-start.5 = (bf16[1024,256]{1,0:T(8,128)(2,1)}, bf16[1024,256]{1,0:T(8,128)(2,1)}, u32[]{:S(2)}, u32[]{:S(2)}) collective-permute-start(bf16[1024,256]{1,0:T(8,128)(2,1)} %collective-permute-done.2.refs_3_), channel_id=1, source_target_pairs={{0,64},{32,480},{64,128},{96,32},{128,192},{160,96},{192,256},{224... | collective-permute-start | bytes 1572872 | tf_op jit(solution)/shard_map/ppermute | solution.py:32
  45.4 12.4 %collective-permute-start.6 = (bf16[512,256]{1,0:T(8,128)(2,1)S(1)}, bf16[512,256]{1,0:T(8,128)(2,1)}, u32[]{:S(2)}, u32[]{:S(2)}) collective-permute-start(bf16[512,256]{1,0:T(8,128)(2,1)S(1)} %slice.3), channel_id=1, source_target_pairs={{0,128},{32,416},{64,192},{96,480},{128,256},{160,32},{192,320},{2... | collective-permute-start | bytes 786440 | tf_op jit(solution)/shard_map/ppermute | solution.py:32
  51.1 34.5 %copy-start.5 = (s32[16]{0:T(128)S(1)}, s32[16]{0:T(128)}, u32[]{:S(2)}) copy-start(s32[16]{0:T(128)} %constant.81.clone) | copy-start | bytes 196
  57.8 57.4 %all-to-all-start.1 = ((bf16[16,128,512]{2,1,0:T(8,128)(2,1)}), bf16[16,128,512]{2,1,0:T(8,128)(2,1)S(1)}, u32[]{:S(2)}, u32[]{:S(2)}) async-start(bf16[16,128,512]{2,1,0:T(8,128)(2,1)} %pick_blocks.1), calls=%async_computation.1 | async-start | bytes 4194304 | tf_op jit(solution)/shard_map/all_to_all | solution.py:36
  66.2 16.6 %collective-permute-start.9 = (bf16[256,1024]{1,0:T(8,128)(2,1)S(1)}, bf16[256,1024]{1,0:T(8,128)(2,1)S(1)}, u32[]{:S(2)}, u32[]{:S(2)}) collective-permute-start(bf16[256,1024]{1,0:T(8,128)(2,1)S(1)} %bitcast.28), channel_id=1, source_target_pairs={{0,1},{1,2},{2,3},{3,0},{4,5},{5,6},{6,7},{7,4},{8,9},{9,10},{10,1... | collective-permute-start | bytes 1572872 | tf_op jit(solution)/shard_map/ppermute | solution.py:23
  69.4 25.8 %collective-permute-start.8 = (bf16[256,1024]{1,0:T(8,128)(2,1)S(1)}, bf16[256,1024]{1,0:T(8,128)(2,1)}, u32[]{:S(2)}, u32[]{:S(2)}) collective-permute-start(bf16[256,1024]{1,0:T(8,128)(2,1)S(1)} %bitcast.29), channel_id=1, source_target_pairs={{0,2},{1,3},{2,0},{3,1},{4,6},{5,7},{6,4},{7,5},{8,10},{9,11},{10,... | collective-permute-start | bytes 1572872 | tf_op jit(solution)/shard_map/ppermute | solution.py:23
  73.7 24.2 %collective-permute-start.7 = (bf16[256,1024]{1,0:T(8,128)(2,1)S(1)}, bf16[256,1024]{1,0:T(8,128)(2,1)}, u32[]{:S(2)}, u32[]{:S(2)}) collective-permute-start(bf16[256,1024]{1,0:T(8,128)(2,1)S(1)} %bitcast.30), channel_id=1, source_target_pairs={{0,3},{1,0},{2,1},{3,2},{4,7},{5,4},{6,5},{7,6},{8,11},{9,8},{10,9... | collective-permute-start | bytes 1572872 | tf_op jit(solution)/shard_map/ppermute | solution.py:23
  76.8 23.1 %collective-permute-start.11 = (bf16[1024,256]{1,0:T(8,128)(2,1)}, bf16[1024,256]{1,0:T(8,128)(2,1)S(1)}, u32[]{:S(2)}, u32[]{:S(2)}) collective-permute-start(bf16[1024,256]{1,0:T(8,128)(2,1)} %collective-permute-done.2.refs_3_), channel_id=1, source_target_pairs={{0,32},{32,0},{64,96},{96,64},{128,160},{160,128},{192,224},{224,1... | collective-permute-start | bytes 1572872 | tf_op jit(solution)/shard_map/ppermute | solution.py:27
  79.7 20.3 %collective-permute-start.10 = (bf16[1024,256]{1,0:T(8,128)(2,1)}, bf16[1024,256]{1,0:T(8,128)(2,1)S(1)}, u32[]{:S(2)}, u32[]{:S(2)}) collective-permute-start(bf16[1024,256]{1,0:T(8,128)(2,1)} %collective-permute-done.4.refs_2_), channel_id=1, source_target_pairs={{0,32},{32,0},{64,96},{96,64},{128,160},{160,128},{192,224},{224,1... | collective-permute-start | bytes 1572872 | tf_op jit(solution)/shard_map/ppermute | solution.py:27
  82.8 17.1 %copy-start.7 = (bf16[256,1024]{1,0:T(8,128)(2,1)}, bf16[256,1024]{1,0:T(8,128)(2,1)S(1)}, u32[]{:S(2)}) copy-start(bf16[256,1024]{1,0:T(8,128)(2,1)S(1)} %collective-permute-done.9.grad3) | copy-start | bytes 1572868
  82.8 17.2 %collective-permute-start.12 = (bf16[1024,256]{1,0:T(8,128)(2,1)}, bf16[1024,256]{1,0:T(8,128)(2,1)S(1)}, u32[]{:S(2)}, u32[]{:S(2)}) collective-permute-start(bf16[1024,256]{1,0:T(8,128)(2,1)} %collective-permute-done.5.refs_4_), channel_id=1, source_target_pairs={{0,32},{32,0},{64,96},{96,64},{128,160},{160,128},{192,224},{224,1... | collective-permute-start | bytes 1572872 | tf_op jit(solution)/shard_map/ppermute | solution.py:27
  95.1 4.8 %collective-permute-start.13 = (bf16[512,256]{1,0:T(8,128)(2,1)}, bf16[512,256]{1,0:T(8,128)(2,1)S(1)}, u32[]{:S(2)}, u32[]{:S(2)}) collective-permute-start(bf16[512,256]{1,0:T(8,128)(2,1)} %collective-permute-done.6.refs_5_), channel_id=1, source_target_pairs={{0,32},{32,0},{64,96},{96,64},{128,160},{160,128},{192,224},{224,1... | collective-permute-start | bytes 786440 | tf_op jit(solution)/shard_map/ppermute | solution.py:27
  97.9 11.2 %collective-permute-start = (bf16[1,2,128,512]{3,2,1,0:T(8,128)(2,1)}, bf16[1,2,128,512]{3,2,1,0:T(8,128)(2,1)S(1)}, u32[]{:S(2)}, u32[]{:S(2)}) collective-permute-start(bf16[1,2,128,512]{3,2,1,0:T(8,128)(2,1)} %param.8), channel_id=1, source_target_pairs={{0,4},{4,8},{8,12},{12,16},{16,20},{20,24},{24,28},{28,0},{1,5},{5... | collective-permute-start | bytes 786440 | tf_op jit(solution)/shard_map/ppermute | solution.py:23
  99.9 15.3 %copy-start = (bf16[1,8,64,512]{3,2,1,0:T(8,128)(2,1)S(1)}, bf16[1,8,64,512]{3,2,1,0:T(8,128)(2,1)}, u32[]{:S(2)}) copy-start(bf16[1,8,64,512]{3,2,1,0:T(8,128)(2,1)} %param.9) | copy-start | bytes 1572868
  99.9 15.3 %copy-start.1 = (bf16[1,8,64,512]{3,2,1,0:T(8,128)(2,1)S(1)}, bf16[1,8,64,512]{3,2,1,0:T(8,128)(2,1)}, u32[]{:S(2)}) copy-start(bf16[1,8,64,512]{3,2,1,0:T(8,128)(2,1)} %param.10) | copy-start | bytes 1572868
  122.7 53.9 %all-to-all-start.2 = ((bf16[16,128,512]{2,1,0:T(8,128)(2,1)}), bf16[16,128,512]{2,1,0:T(8,128)(2,1)S(1)}, u32[]{:S(2)}, u32[]{:S(2)}) async-start(bf16[16,128,512]{2,1,0:T(8,128)(2,1)} %get-tuple-element.35), calls=%async_computation.2 | async-start | bytes 4194304 | tf_op jit(solution)/shard_map/all_to_all | solution.py:36
  132.6 16.6 %collective-permute-start.14 = (bf16[256,1024]{1,0:T(8,128)(2,1)S(1)}, bf16[256,1024]{1,0:T(8,128)(2,1)S(1)}, u32[]{:S(2)}, u32[]{:S(2)}) collective-permute-start(bf16[256,1024]{1,0:T(8,128)(2,1)S(1)} %get-tuple-element.30), channel_id=1, source_target_pairs={{0,1},{1,2},{2,3},{3,0},{4,5},{5,6},{6,7},{7,4},{8,9},{9,10},{10,1... | collective-permute-start | bytes 1572872 | tf_op jit(solution)/shard_map/ppermute | solution.py:23
  135.7 25.7 %collective-permute-start.15 = (bf16[256,1024]{1,0:T(8,128)(2,1)S(1)}, bf16[256,1024]{1,0:T(8,128)(2,1)S(1)}, u32[]{:S(2)}, u32[]{:S(2)}) collective-permute-start(bf16[256,1024]{1,0:T(8,128)(2,1)S(1)} %get-tuple-element.31), channel_id=1, source_target_pairs={{0,2},{1,3},{2,0},{3,1},{4,6},{5,7},{6,4},{7,5},{8,10},{9,11},{10,... | collective-permute-start | bytes 1572872 | tf_op jit(solution)/shard_map/ppermute | solution.py:23
  140.1 22.5 %collective-permute-start.16 = (bf16[256,1024]{1,0:T(8,128)(2,1)S(1)}, bf16[256,1024]{1,0:T(8,128)(2,1)S(1)}, u32[]{:S(2)}, u32[]{:S(2)}) collective-permute-start(bf16[256,1024]{1,0:T(8,128)(2,1)S(1)} %get-tuple-element.32), channel_id=1, source_target_pairs={{0,3},{1,0},{2,1},{3,2},{4,7},{5,4},{6,5},{7,6},{8,11},{9,8},{10,9... | collective-permute-start | bytes 1572872 | tf_op jit(solution)/shard_map/ppermute | solution.py:23
  (7 other events, 20.8 us)

commit v9 on v8

--- a/solution.py
+++ b/solution.py
@@ -363,10 +363,10 @@
 
     weight = out_weight[0]
     other = swapped(weight)
-    pair = jnp.concatenate([weight, other])
+    pair, asked = lax.optimization_barrier((jnp.concatenate([weight, other]), asked))
     near, next_near = along_ring(pair, 1), along_ring(pair, 2)
     grads = passed_along(sent_grads, "section", -1)[0]
-    next_near, asked, grads = lax.optimization_barrier((next_near, asked, grads))
+    next_near, grads = lax.optimization_barrier((next_near, grads))
     third, far = along_ring(next_near, 1), along_ring(next_near[: weight.shape[0]], 2)
     slots = picked_slots(asked, keys, values)
     slots, near, third, far = lax.optimization_barrier((slots, near, third, far))

time: 181 us -> 184 us (1.017)
  blocking collectives: 13.5 us -> 0 us
  starting transfers between devices: 77.2 us -> 85.9 us
  waiting for transfers between devices: 57 us -> 64.6 us
    all_to_all x1 -> x0, blocking collectives: 13.5 us -> none  [exchanged(): return lax.all_to_all(slots, 'dp', split_axis=0, concat_axis=0, tiled=True)]
    ppermute x4, waiting for transfers between devices: 6.68 us -> 12.7 us  [along_ring(): lax.ppermute(block, 'dp', [(i, (i + (1 - i % 2 * 2) * 2 * chips) % count)...]
    all_to_all x2 -> x3, starting transfers between devices: 13.4 us -> 18.1 us  [exchanged(): return lax.all_to_all(slots, 'dp', split_axis=0, concat_axis=0, tiled=True)]
    ppermute x8, starting transfers between devices: 28.3 us -> 32.2 us  [passed_along(): lax.ppermute(block, axis, [(i, (i + distance) % count) for i in range(cou...]
    all_to_all x2 -> x3, waiting for transfers between devices: 18.8 us -> 18.8 us  [exchanged(): return lax.all_to_all(slots, 'dp', split_axis=0, concat_axis=0, tiled=True)]
  transfers between devices with their start and end apart: 19 -> 20, of which waited for: 9 -> 11; matrix products, arithmetic and copies ran while one was open for 3% -> 3% of each run, Pallas kernels for 8% -> 8%
where the time goes in v9:
time: 184 us; the launch traced here: 183 us
  starting transfers between devices  85.9 us (47%)
  waiting for transfers between devices  64.6 us (35%)
  Pallas kernels  23.8 us (13%)
  local copies, waits for them, and re-layouts  4.53 us (2%)
  other arithmetic  3.45 us (2%)
    ppermute x8, waiting for transfers between devices, passed_along(): lax.ppermute(block, axis, [(i, (i + distance) % count) for i in range(cou...  33 us
    ppermute x8, starting transfers between devices, passed_along(): lax.ppermute(block, axis, [(i, (i + distance) % count) for i in range(cou...  32.2 us
    ppermute x5, starting transfers between devices, swapped(): lax.ppermute(block, 'dp', [(i, i ^ 1) for i in range(lax.axis_size('dp'))])  19.1 us
    all_to_all x3, waiting for transfers between devices, exchanged(): return lax.all_to_all(slots, 'dp', split_axis=0, concat_axis=0, tiled=True)  18.8 us
    all_to_all x3, starting transfers between devices, exchanged(): return lax.all_to_all(slots, 'dp', split_axis=0, concat_axis=0, tiled=True)  18.1 us
    ppermute x4, starting transfers between devices, along_ring(): lax.ppermute(block, 'dp', [(i, (i + (1 - i % 2 * 2) * 2 * chips) % count)...  16.5 us
    ppermute x4, waiting for transfers between devices, along_ring(): lax.ppermute(block, 'dp', [(i, (i + (1 - i % 2 * 2) * 2 * chips) % count)...  12.7 us
    pallas_call x1, Pallas kernels, layer(): pl.pallas_call(layer_kernel, out_shape=[pltpu.HBM((rows, features), BF16)...  6.55 us
  transfers between devices with their start and end apart: 20, of which 11 were waited for; matrix products, arithmetic and copies ran while one was open for 3% of the time, Pallas kernels for 8%

profile of v9, /device:TPU:1, one launch (start us, length us, event | category | flops | bytes accessed | tf_op | source)
XLA Modules:
  0.0 183.2 jit_solution(10176179445449746304)
XLA Ops:
  0.6 8.8 %collective-permute-start.1 = (bf16[512,256]{1,0:T(8,128)(2,1)}, bf16[512,256]{1,0:T(8,128)(2,1)S(1)}, u32[]{:S(2)}, u32[]{:S(2)}) collective-permute-start(bf16[512,256]{1,0:T(8,128)(2,1)} %bitcast.23), channel_id=1, source_target_pairs={{0,32},{32,0},{64,96},{96,64},{128,160},{160,128},{192,224},{224,1... | collective-permute-start | bytes 786440 | tf_op jit(solution)/shard_map/ppermute | solution.py:27
  10.9 3.4 %all-to-all-start = ((s32[16,1,1]{2,1,0:T(1,128)}), s32[16,1,1]{2,1,0:T(1,128)S(1)}, u32[]{:S(2)}, u32[]{:S(2)}) async-start(s32[16,1,1]{2,1,0:T(1,128)} %copy.20), calls=%async_computation | async-start | bytes 16384 | tf_op jit(solution)/shard_map/all_to_all | solution.py:36
  14.3 9.2 %collective-permute-start.4 = (bf16[1,2,128,1024]{3,2,1,0:T(8,128)(2,1)}, bf16[1,2,128,1024]{3,2,1,0:T(8,128)(2,1)S(1)}, u32[]{:S(2)}, u32[]{:S(2)}) collective-permute-start(bf16[1,2,128,1024]{3,2,1,0:T(8,128)(2,1)} %param.12), channel_id=1, source_target_pairs={{0,28},{4,0},{8,4},{12,8},{16,12},{20,16},{24,20},{28,24},{1,29},{... | collective-permute-start | bytes 1572872 | tf_op jit(solution)/shard_map/ppermute | solution.py:23
  24.9 5.4 %collective-permute-start.3 = (bf16[1024,256]{1,0:T(8,128)(2,1)S(1)}, bf16[1024,256]{1,0:T(8,128)(2,1)}, u32[]{:S(2)}, u32[]{:S(2)}) collective-permute-start(bf16[1024,256]{1,0:T(8,128)(2,1)S(1)} %pad_maximum_fusion), channel_id=1, source_target_pairs={{0,128},{32,416},{64,192},{96,480},{128,256},{160,32},{192,320},{2... | collective-permute-start | bytes 1572872 | tf_op jit(solution)/shard_map/ppermute | solution.py:32
  30.3 3.1 %collective-permute-start.2 = (bf16[1024,256]{1,0:T(8,128)(2,1)S(1)}, bf16[1024,256]{1,0:T(8,128)(2,1)}, u32[]{:S(2)}, u32[]{:S(2)}) collective-permute-start(bf16[1024,256]{1,0:T(8,128)(2,1)S(1)} %pad_maximum_fusion), channel_id=1, source_target_pairs={{0,64},{32,480},{64,128},{96,32},{128,192},{160,96},{192,256},{224... | collective-permute-start | bytes 1572872 | tf_op jit(solution)/shard_map/ppermute | solution.py:32
  35.0 7.0 %collective-permute-done.3.refs_3_ = bf16[1024,256]{1,0:T(8,128)(2,1)} collective-permute-done((bf16[1024,256]{1,0:T(8,128)(2,1)S(1)}, bf16[1024,256]{1,0:T(8,128)(2,1)}, u32[]{:S(2)}, u32[]{:S(2)}) %collective-permute-start.3) | collective-permute-done | bytes 524320 | tf_op jit(solution)/shard_map/ppermute | solution.py:32
  42.1 4.1 %collective-permute-start.5 = (bf16[1024,256]{1,0:T(8,128)(2,1)}, bf16[1024,256]{1,0:T(8,128)(2,1)}, u32[]{:S(2)}, u32[]{:S(2)}) collective-permute-start(bf16[1024,256]{1,0:T(8,128)(2,1)} %collective-permute-done.3.refs_3_), channel_id=1, source_target_pairs={{0,64},{32,480},{64,128},{96,32},{128,192},{160,96},{192,256},{224... | collective-permute-start | bytes 1572872 | tf_op jit(solution)/shard_map/ppermute | solution.py:32
  47.1 3.9 %collective-permute-start.6 = (bf16[512,256]{1,0:T(8,128)(2,1)S(1)}, bf16[512,256]{1,0:T(8,128)(2,1)}, u32[]{:S(2)}, u32[]{:S(2)}) collective-permute-start(bf16[512,256]{1,0:T(8,128)(2,1)S(1)} %slice.3), channel_id=1, source_target_pairs={{0,128},{32,416},{64,192},{96,480},{128,256},{160,32},{192,320},{2... | collective-permute-start | bytes 786440 | tf_op jit(solution)/shard_map/ppermute | solution.py:32
  54.2 5.6 %collective-permute-done.6.refs_5_ = bf16[512,256]{1,0:T(8,128)(2,1)} collective-permute-done((bf16[512,256]{1,0:T(8,128)(2,1)S(1)}, bf16[512,256]{1,0:T(8,128)(2,1)}, u32[]{:S(2)}, u32[]{:S(2)}) %collective-permute-start.6) | collective-permute-done | bytes 262176 | tf_op jit(solution)/shard_map/ppermute | solution.py:32
  59.8 9.8 %all-to-all-start.1 = ((bf16[16,128,512]{2,1,0:T(8,128)(2,1)}), bf16[16,128,512]{2,1,0:T(8,128)(2,1)S(1)}, u32[]{:S(2)}, u32[]{:S(2)}) async-start(bf16[16,128,512]{2,1,0:T(8,128)(2,1)} %pick_blocks.1), calls=%async_computation.1 | async-start | bytes 4194304 | tf_op jit(solution)/shard_map/all_to_all | solution.py:36
  69.6 3.1 %collective-permute-start.9 = (bf16[256,1024]{1,0:T(8,128)(2,1)S(1)}, bf16[256,1024]{1,0:T(8,128)(2,1)S(1)}, u32[]{:S(2)}, u32[]{:S(2)}) collective-permute-start(bf16[256,1024]{1,0:T(8,128)(2,1)S(1)} %bitcast.28), channel_id=1, source_target_pairs={{0,1},{1,2},{2,3},{3,0},{4,5},{5,6},{6,7},{7,4},{8,9},{9,10},{10,1... | collective-permute-start | bytes 1572872 | tf_op jit(solution)/shard_map/ppermute | solution.py:23
  72.8 4.4 %collective-permute-start.8 = (bf16[256,1024]{1,0:T(8,128)(2,1)S(1)}, bf16[256,1024]{1,0:T(8,128)(2,1)}, u32[]{:S(2)}, u32[]{:S(2)}) collective-permute-start(bf16[256,1024]{1,0:T(8,128)(2,1)S(1)} %bitcast.29), channel_id=1, source_target_pairs={{0,2},{1,3},{2,0},{3,1},{4,6},{5,7},{6,4},{7,5},{8,10},{9,11},{10,... | collective-permute-start | bytes 1572872 | tf_op jit(solution)/shard_map/ppermute | solution.py:23
  89.0 9.5 %collective-permute-done.8.grad2 = bf16[256,1024]{1,0:T(8,128)(2,1)} collective-permute-done((bf16[256,1024]{1,0:T(8,128)(2,1)S(1)}, bf16[256,1024]{1,0:T(8,128)(2,1)}, u32[]{:S(2)}, u32[]{:S(2)}) %collective-permute-start.8) | collective-permute-done | bytes 524320 | tf_op jit(solution)/shard_map/ppermute | solution.py:23
  105.2 6.1 %back_projection.1.grads = bf16[256,512]{1,0:T(8,128)(2,1)} custom-call(s32[2,16]{1,0:T(2,128)S(1)} %pad_add_fusion.table, bf16[256,1024]{1,0:T(8,128)(2,1)} %bitcast.31, bf16[256,1024]{1,0:T(8,128)(2,1)} %collective-permute-done.7.grad1, bf16[256,1024]{1,0:T(8,128)(2,1)} %collective-permute-done.8.grad2, bf16[256,1024]{1,0:T(8,128)(2,1)} %copy-done.7, ...), custom_call_target="tpu_custom_call" | custom-call | flops 2147483648 | bytes 8388608 | tf_op jit(solution)/shard_map/back_projection/pallas_call | solution.py:237
  112.6 6.0 %all-to-all-done.1.recv = bf16[16,128,512]{2,1,0:T(8,128)(2,1)S(1)} async-done(((bf16[16,128,512]{2,1,0:T(8,128)(2,1)}), bf16[16,128,512]{2,1,0:T(8,128)(2,1)S(1)}, u32[]{:S(2)}, u32[]{:S(2)}) %all-to-all-start.1) | async-done | bytes 2097184 | tf_op jit(solution)/shard_map/all_to_all | solution.py:36
  119.5 6.6 %layer.1 = (bf16[256,512]{1,0:T(8,128)(2,1)}, bf16[2,128,512]{2,1,0:T(8,128)(2,1)}, f32[2,8,64,512]{3,2,1,0:T(8,128)}, bf16[16,128,512]{2,1,0:T(8,128)(2,1)}) custom-call(s32[2]{0:T(128)S(1)} %copy-done.2, s32[2,4]{1,0:T(2,128)S(1)} %get-tuple-element.41.holder, bf16[2,128,512]{2,1,0:T(8,128)(2,1)S(1)} %bitcast.21, bf16[8,64,512]{2,1,0:T(8,128)(2,1)S(1)} %bitcast.18, ...), custom_call_target="tpu_custom_call" | custom-call | flops 4294967296 | bytes 12582912 | tf_op jit(solution)/shard_map/layer/pallas_call | solution.py:172
  126.1 5.0 %all-to-all-start.2 = ((bf16[16,128,512]{2,1,0:T(8,128)(2,1)}), bf16[16,128,512]{2,1,0:T(8,128)(2,1)S(1)}, u32[]{:S(2)}, u32[]{:S(2)}) async-start(bf16[16,128,512]{2,1,0:T(8,128)(2,1)} %get-tuple-element.37), calls=%async_computation.2 | async-start | bytes 4194304 | tf_op jit(solution)/shard_map/all_to_all | solution.py:36
  131.1 4.9 %projection.1 = (bf16[256,1024]{1,0:T(8,128)(2,1)S(1)}, bf16[256,1024]{1,0:T(8,128)(2,1)S(1)}, bf16[256,1024]{1,0:T(8,128)(2,1)S(1)}, bf16[256,1024]{1,0:T(8,128)(2,1)S(1)}) custom-call(s32[2,16]{1,0:T(2,128)S(1)} %pad_add_fusion.table, bf16[256,512]{1,0:T(8,128)(2,1)} %get-tuple-element.30.attended_hbm, bf16[512,256]{1,0:T(8,128)(2,1)} %bitcast.26, ...), custom_call_target="tpu_custom_call" | custom-call | flops 2147483648 | bytes 8388608 | tf_op jit(solution)/shard_map/projection/pallas_call | solution.py:276
  136.0 3.1 %collective-permute-start.14 = (bf16[256,1024]{1,0:T(8,128)(2,1)S(1)}, bf16[256,1024]{1,0:T(8,128)(2,1)S(1)}, u32[]{:S(2)}, u32[]{:S(2)}) collective-permute-start(bf16[256,1024]{1,0:T(8,128)(2,1)S(1)} %get-tuple-element.32), channel_id=1, source_target_pairs={{0,1},{1,2},{2,3},{3,0},{4,5},{5,6},{6,7},{7,4},{8,9},{9,10},{10,1... | collective-permute-start | bytes 1572872 | tf_op jit(solution)/shard_map/ppermute | solution.py:23
  139.2 4.4 %collective-permute-start.15 = (bf16[256,1024]{1,0:T(8,128)(2,1)S(1)}, bf16[256,1024]{1,0:T(8,128)(2,1)S(1)}, u32[]{:S(2)}, u32[]{:S(2)}) collective-permute-start(bf16[256,1024]{1,0:T(8,128)(2,1)S(1)} %get-tuple-element.33), channel_id=1, source_target_pairs={{0,2},{1,3},{2,0},{3,1},{4,6},{5,7},{6,4},{7,5},{8,10},{9,11},{10,... | collective-permute-start | bytes 1572872 | tf_op jit(solution)/shard_map/ppermute | solution.py:23
  146.6 6.0 %collective-permute-done.14 = bf16[256,1024]{1,0:T(8,128)(2,1)S(1)} collective-permute-done((bf16[256,1024]{1,0:T(8,128)(2,1)S(1)}, bf16[256,1024]{1,0:T(8,128)(2,1)S(1)}, u32[]{:S(2)}, u32[]{:S(2)}) %collective-permute-start.14) | collective-permute-done | bytes 524320 | tf_op jit(solution)/shard_map/ppermute | solution.py:23
  152.6 12.2 %collective-permute-done.15 = bf16[256,1024]{1,0:T(8,128)(2,1)S(1)} collective-permute-done((bf16[256,1024]{1,0:T(8,128)(2,1)S(1)}, bf16[256,1024]{1,0:T(8,128)(2,1)S(1)}, u32[]{:S(2)}, u32[]{:S(2)}) %collective-permute-start.15) | collective-permute-done | bytes 524320 | tf_op jit(solution)/shard_map/ppermute | solution.py:23
  167.2 12.8 %all-to-all-done.2.back = bf16[16,128,512]{2,1,0:T(8,128)(2,1)S(1)} async-done(((bf16[16,128,512]{2,1,0:T(8,128)(2,1)}), bf16[16,128,512]{2,1,0:T(8,128)(2,1)S(1)}, u32[]{:S(2)}, u32[]{:S(2)}) %all-to-all-start.2) | async-done | bytes 2097184 | tf_op jit(solution)/shard_map/all_to_all | solution.py:36
  180.0 3.2 %combine.1 = (bf16[8,64,512]{2,1,0:T(8,128)(2,1)}, bf16[8,64,512]{2,1,0:T(8,128)(2,1)}) custom-call(s32[16,1]{1,0:T(8,128)S(1)} %copy.21.asked, f32[2,8,64,512]{3,2,1,0:T(8,128)} %get-tuple-element.36.own_rows_hbm, bf16[16,128,512]{2,1,0:T(8,128)(2,1)S(1)} %all-to-all-done.2.back), custom_call_target="tpu_custom_call" | custom-call | bytes 4194304 | tf_op jit(solution)/shard_map/combine/pallas_call | solution.py:329
  (57 shorter events, 34.7 us)
Async XLA Ops:
  0.6 23.2 %collective-permute-start.1 = (bf16[512,256]{1,0:T(8,128)(2,1)}, bf16[512,256]{1,0:T(8,128)(2,1)S(1)}, u32[]{:S(2)}, u32[]{:S(2)}) collective-permute-start(bf16[512,256]{1,0:T(8,128)(2,1)} %bitcast.23), channel_id=1, source_target_pairs={{0,32},{32,0},{64,96},{96,64},{128,160},{160,128},{192,224},{224,1... | collective-permute-start | bytes 786440 | tf_op jit(solution)/shard_map/ppermute | solution.py:27
  10.9 12.6 %all-to-all-start = ((s32[16,1,1]{2,1,0:T(1,128)}), s32[16,1,1]{2,1,0:T(1,128)S(1)}, u32[]{:S(2)}, u32[]{:S(2)}) async-start(s32[16,1,1]{2,1,0:T(1,128)} %copy.20), calls=%async_computation | async-start | bytes 16384 | tf_op jit(solution)/shard_map/all_to_all | solution.py:36
  14.3 20.7 %collective-permute-start.4 = (bf16[1,2,128,1024]{3,2,1,0:T(8,128)(2,1)}, bf16[1,2,128,1024]{3,2,1,0:T(8,128)(2,1)S(1)}, u32[]{:S(2)}, u32[]{:S(2)}) collective-permute-start(bf16[1,2,128,1024]{3,2,1,0:T(8,128)(2,1)} %param.12), channel_id=1, source_target_pairs={{0,28},{4,0},{8,4},{12,8},{16,12},{20,16},{24,20},{28,24},{1,29},{... | collective-permute-start | bytes 1572872 | tf_op jit(solution)/shard_map/ppermute | solution.py:23
  23.8 18.2 %copy-start.4 = (bf16[512,256]{1,0:T(8,128)(2,1)}, bf16[512,256]{1,0:T(8,128)(2,1)S(1)}, u32[]{:S(2)}) copy-start(bf16[512,256]{1,0:T(8,128)(2,1)S(1)} %collective-permute-done.1.refs_1_) | copy-start | bytes 786436
  24.9 17.1 %collective-permute-start.3 = (bf16[1024,256]{1,0:T(8,128)(2,1)S(1)}, bf16[1024,256]{1,0:T(8,128)(2,1)}, u32[]{:S(2)}, u32[]{:S(2)}) collective-permute-start(bf16[1024,256]{1,0:T(8,128)(2,1)S(1)} %pad_maximum_fusion), channel_id=1, source_target_pairs={{0,128},{32,416},{64,192},{96,480},{128,256},{160,32},{192,320},{2... | collective-permute-start | bytes 1572872 | tf_op jit(solution)/shard_map/ppermute | solution.py:32
  30.3 23.9 %collective-permute-start.2 = (bf16[1024,256]{1,0:T(8,128)(2,1)S(1)}, bf16[1024,256]{1,0:T(8,128)(2,1)}, u32[]{:S(2)}, u32[]{:S(2)}) collective-permute-start(bf16[1024,256]{1,0:T(8,128)(2,1)S(1)} %pad_maximum_fusion), channel_id=1, source_target_pairs={{0,64},{32,480},{64,128},{96,32},{128,192},{160,96},{192,256},{224... | collective-permute-start | bytes 1572872 | tf_op jit(solution)/shard_map/ppermute | solution.py:32
  35.0 42.1 %copy-start.6 = (bf16[1,2,128,1024]{3,2,1,0:T(8,128)(2,1)}, bf16[1,2,128,1024]{3,2,1,0:T(8,128)(2,1)S(1)}, u32[]{:S(2)}) copy-start(bf16[1,2,128,1024]{3,2,1,0:T(8,128)(2,1)S(1)} %collective-permute-done.4) | copy-start | bytes 1572868
  42.1 17.8 %collective-permute-start.5 = (bf16[1024,256]{1,0:T(8,128)(2,1)}, bf16[1024,256]{1,0:T(8,128)(2,1)}, u32[]{:S(2)}, u32[]{:S(2)}) collective-permute-start(bf16[1024,256]{1,0:T(8,128)(2,1)} %collective-permute-done.3.refs_3_), channel_id=1, source_target_pairs={{0,64},{32,480},{64,128},{96,32},{128,192},{160,96},{192,256},{224... | collective-permute-start | bytes 1572872 | tf_op jit(solution)/shard_map/ppermute | solution.py:32
  47.1 12.7 %collective-permute-start.6 = (bf16[512,256]{1,0:T(8,128)(2,1)S(1)}, bf16[512,256]{1,0:T(8,128)(2,1)}, u32[]{:S(2)}, u32[]{:S(2)}) collective-permute-start(bf16[512,256]{1,0:T(8,128)(2,1)S(1)} %slice.3), channel_id=1, source_target_pairs={{0,128},{32,416},{64,192},{96,480},{128,256},{160,32},{192,320},{2... | collective-permute-start | bytes 786440 | tf_op jit(solution)/shard_map/ppermute | solution.py:32
  54.2 34.8 %copy-start.5 = (s32[16]{0:T(128)S(1)}, s32[16]{0:T(128)}, u32[]{:S(2)}) copy-start(s32[16]{0:T(128)} %constant.81.clone) | copy-start | bytes 196
  59.8 58.7 %all-to-all-start.1 = ((bf16[16,128,512]{2,1,0:T(8,128)(2,1)}), bf16[16,128,512]{2,1,0:T(8,128)(2,1)S(1)}, u32[]{:S(2)}, u32[]{:S(2)}) async-start(bf16[16,128,512]{2,1,0:T(8,128)(2,1)} %pick_blocks.1), calls=%async_computation.1 | async-start | bytes 4194304 | tf_op jit(solution)/shard_map/all_to_all | solution.py:36
  69.6 16.6 %collective-permute-start.9 = (bf16[256,1024]{1,0:T(8,128)(2,1)S(1)}, bf16[256,1024]{1,0:T(8,128)(2,1)S(1)}, u32[]{:S(2)}, u32[]{:S(2)}) collective-permute-start(bf16[256,1024]{1,0:T(8,128)(2,1)S(1)} %bitcast.28), channel_id=1, source_target_pairs={{0,1},{1,2},{2,3},{3,0},{4,5},{5,6},{6,7},{7,4},{8,9},{9,10},{10,1... | collective-permute-start | bytes 1572872 | tf_op jit(solution)/shard_map/ppermute | solution.py:23
  72.8 25.8 %collective-permute-start.8 = (bf16[256,1024]{1,0:T(8,128)(2,1)S(1)}, bf16[256,1024]{1,0:T(8,128)(2,1)}, u32[]{:S(2)}, u32[]{:S(2)}) collective-permute-start(bf16[256,1024]{1,0:T(8,128)(2,1)S(1)} %bitcast.29), channel_id=1, source_target_pairs={{0,2},{1,3},{2,0},{3,1},{4,6},{5,7},{6,4},{7,5},{8,10},{9,11},{10,... | collective-permute-start | bytes 1572872 | tf_op jit(solution)/shard_map/ppermute | solution.py:23
  77.2 24.2 %collective-permute-start.7 = (bf16[256,1024]{1,0:T(8,128)(2,1)S(1)}, bf16[256,1024]{1,0:T(8,128)(2,1)}, u32[]{:S(2)}, u32[]{:S(2)}) collective-permute-start(bf16[256,1024]{1,0:T(8,128)(2,1)S(1)} %bitcast.30), channel_id=1, source_target_pairs={{0,3},{1,0},{2,1},{3,2},{4,7},{5,4},{6,5},{7,6},{8,11},{9,8},{10,9... | collective-permute-start | bytes 1572872 | tf_op jit(solution)/shard_map/ppermute | solution.py:23
  80.2 23.1 %collective-permute-start.11 = (bf16[1024,256]{1,0:T(8,128)(2,1)}, bf16[1024,256]{1,0:T(8,128)(2,1)S(1)}, u32[]{:S(2)}, u32[]{:S(2)}) collective-permute-start(bf16[1024,256]{1,0:T(8,128)(2,1)} %collective-permute-done.3.refs_3_), channel_id=1, source_target_pairs={{0,32},{32,0},{64,96},{96,64},{128,160},{160,128},{192,224},{224,1... | collective-permute-start | bytes 1572872 | tf_op jit(solution)/shard_map/ppermute | solution.py:27
  83.1 20.3 %collective-permute-start.10 = (bf16[1024,256]{1,0:T(8,128)(2,1)}, bf16[1024,256]{1,0:T(8,128)(2,1)S(1)}, u32[]{:S(2)}, u32[]{:S(2)}) collective-permute-start(bf16[1024,256]{1,0:T(8,128)(2,1)} %collective-permute-done.2.refs_2_), channel_id=1, source_target_pairs={{0,32},{32,0},{64,96},{96,64},{128,160},{160,128},{192,224},{224,1... | collective-permute-start | bytes 1572872 | tf_op jit(solution)/shard_map/ppermute | solution.py:27
  86.2 17.1 %copy-start.7 = (bf16[256,1024]{1,0:T(8,128)(2,1)}, bf16[256,1024]{1,0:T(8,128)(2,1)S(1)}, u32[]{:S(2)}) copy-start(bf16[256,1024]{1,0:T(8,128)(2,1)S(1)} %collective-permute-done.9.grad3) | copy-start | bytes 1572868
  86.2 17.2 %collective-permute-start.12 = (bf16[1024,256]{1,0:T(8,128)(2,1)}, bf16[1024,256]{1,0:T(8,128)(2,1)S(1)}, u32[]{:S(2)}, u32[]{:S(2)}) collective-permute-start(bf16[1024,256]{1,0:T(8,128)(2,1)} %collective-permute-done.5.refs_4_), channel_id=1, source_target_pairs={{0,32},{32,0},{64,96},{96,64},{128,160},{160,128},{192,224},{224,1... | collective-permute-start | bytes 1572872 | tf_op jit(solution)/shard_map/ppermute | solution.py:27
  98.5 4.8 %collective-permute-start.13 = (bf16[512,256]{1,0:T(8,128)(2,1)}, bf16[512,256]{1,0:T(8,128)(2,1)S(1)}, u32[]{:S(2)}, u32[]{:S(2)}) collective-permute-start(bf16[512,256]{1,0:T(8,128)(2,1)} %collective-permute-done.6.refs_5_), channel_id=1, source_target_pairs={{0,32},{32,0},{64,96},{96,64},{128,160},{160,128},{192,224},{224,1... | collective-permute-start | bytes 786440 | tf_op jit(solution)/shard_map/ppermute | solution.py:27
  101.3 11.2 %collective-permute-start = (bf16[1,2,128,512]{3,2,1,0:T(8,128)(2,1)}, bf16[1,2,128,512]{3,2,1,0:T(8,128)(2,1)S(1)}, u32[]{:S(2)}, u32[]{:S(2)}) collective-permute-start(bf16[1,2,128,512]{3,2,1,0:T(8,128)(2,1)} %param.8), channel_id=1, source_target_pairs={{0,4},{4,8},{8,12},{12,16},{16,20},{20,24},{24,28},{28,0},{1,5},{5... | collective-permute-start | bytes 786440 | tf_op jit(solution)/shard_map/ppermute | solution.py:23
  126.1 53.9 %all-to-all-start.2 = ((bf16[16,128,512]{2,1,0:T(8,128)(2,1)}), bf16[16,128,512]{2,1,0:T(8,128)(2,1)S(1)}, u32[]{:S(2)}, u32[]{:S(2)}) async-start(bf16[16,128,512]{2,1,0:T(8,128)(2,1)} %get-tuple-element.37), calls=%async_computation.2 | async-start | bytes 4194304 | tf_op jit(solution)/shard_map/all_to_all | solution.py:36
  136.0 16.6 %collective-permute-start.14 = (bf16[256,1024]{1,0:T(8,128)(2,1)S(1)}, bf16[256,1024]{1,0:T(8,128)(2,1)S(1)}, u32[]{:S(2)}, u32[]{:S(2)}) collective-permute-start(bf16[256,1024]{1,0:T(8,128)(2,1)S(1)} %get-tuple-element.32), channel_id=1, source_target_pairs={{0,1},{1,2},{2,3},{3,0},{4,5},{5,6},{6,7},{7,4},{8,9},{9,10},{10,1... | collective-permute-start | bytes 1572872 | tf_op jit(solution)/shard_map/ppermute | solution.py:23
  139.2 25.7 %collective-permute-start.15 = (bf16[256,1024]{1,0:T(8,128)(2,1)S(1)}, bf16[256,1024]{1,0:T(8,128)(2,1)S(1)}, u32[]{:S(2)}, u32[]{:S(2)}) collective-permute-start(bf16[256,1024]{1,0:T(8,128)(2,1)S(1)} %get-tuple-element.33), channel_id=1, source_target_pairs={{0,2},{1,3},{2,0},{3,1},{4,6},{5,7},{6,4},{7,5},{8,10},{9,11},{10,... | collective-permute-start | bytes 1572872 | tf_op jit(solution)/shard_map/ppermute | solution.py:23
  143.5 22.5 %collective-permute-start.16 = (bf16[256,1024]{1,0:T(8,128)(2,1)S(1)}, bf16[256,1024]{1,0:T(8,128)(2,1)S(1)}, u32[]{:S(2)}, u32[]{:S(2)}) collective-permute-start(bf16[256,1024]{1,0:T(8,128)(2,1)S(1)} %get-tuple-element.34), channel_id=1, source_target_pairs={{0,3},{1,0},{2,1},{3,2},{4,7},{5,4},{6,5},{7,6},{8,11},{9,8},{10,9... | collective-permute-start | bytes 1572872 | tf_op jit(solution)/shard_map/ppermute | solution.py:23
  (8 other events, 50.3 us)

commit v10 on v9

--- a/solution.py
+++ b/solution.py
@@ -44,39 +44,31 @@
     return pl.CostEstimate(flops=int(flops), bytes_accessed=int(nbytes), transcendentals=0)
 
 
-def pick_kernel(asked, keys_hbm, values_hbm, slots, keys, values, in_sem, out_sem):
-    rows = keys.shape[1]
+def pick_kernel(asked, keys_hbm, values_hbm, key_slots, value_slots, keys, values, in_sem, out_sem):
     in_key = pltpu.make_async_copy(keys_hbm, keys, in_sem.at[0])
     in_value = pltpu.make_async_copy(values_hbm, values, in_sem.at[1])
     in_key.start()
     in_value.start()
-
-    def sent(slot, which, source):
-        target = slots.at[slot, pl.ds(which * rows, rows)]
-        return pltpu.make_async_copy(source.at[jnp.maximum(asked[slot, 0], 0)], target, out_sem.at[slot, which])
-
-    for which, (arriving, source) in enumerate(((in_key, keys), (in_value, values))):
+    outgoing = []
+    for which, (arriving, source, slots) in enumerate(((in_key, keys, key_slots), (in_value, values, value_slots))):
         arriving.wait()
-
-        @pl.loop(0, slots.shape[0])
-        def _(slot, which=which, source=source):
-            copy = sent(slot, which, source)
-            pl.when(asked[slot, 0] >= 0)(copy.start)
-
-    @pl.loop(0, slots.shape[0])
-    def _(slot):
-        for which, source in enumerate((keys, values)):
-            pl.when(asked[slot, 0] >= 0)(sent(slot, which, source).wait)
+        for slot in range(slots.shape[0]):
+            spot = asked[slot, 0]
+            copy = pltpu.make_async_copy(source.at[jnp.maximum(spot, 0)], slots.at[slot], out_sem.at[slot, which])
+            pl.when(spot >= 0)(copy.start)
+            outgoing.append((spot, copy))
+    for spot, copy in outgoing:
+        pl.when(spot >= 0)(copy.wait)
 
 
 def picked_slots(asked, keys, values):
     slot_count = asked.shape[0]
-    _, rows, features = keys.shape
+    shape = pltpu.HBM((slot_count, *keys.shape[1:]), BF16)
     return pl.pallas_call(
         pick_kernel,
-        out_shape=pltpu.HBM((slot_count, 2 * rows, features), BF16),
+        out_shape=[shape, shape],
         in_specs=[SMEM, HBM, HBM],
-        out_specs=HBM,
+        out_specs=[HBM, HBM],
         scratch_shapes=[
             pltpu.VMEM(keys.shape, BF16),
             pltpu.VMEM(values.shape, BF16),
@@ -90,7 +82,7 @@
 
 
 def layer_kernel(
-    counts, holder, queries, keys, values, recv, grads,
+    counts, holder, queries, keys, values, recv_keys, recv_values, grads,
     attended_hbm, grad_query_hbm, own_rows_hbm, slots_hbm,
     attended, grad_query, own_rows, slots, out_sem, own_sem, slot_sem,
 ):
@@ -108,10 +100,10 @@
         query_rows = pl.ds(pl.multiple_of(doc * query_count, query_count), query_count)
         senders = [holder[doc, m] for m in range(neg)]
         key = jnp.concatenate(
-            [keys[doc * own + m, :, at] for m in range(own)] + [recv[e, :rows, at] for e in senders], axis=0
+            [keys[doc * own + m, :, at] for m in range(own)] + [recv_keys[e, :, at] for e in senders], axis=0
         )
         value = jnp.concatenate(
-            [values[doc * own + m, :, at] for m in range(own)] + [recv[e, rows:, at] for e in senders], axis=0
+            [values[doc * own + m, :, at] for m in range(own)] + [recv_values[e, :, at] for e in senders], axis=0
         )
         return doc, at, query_rows, key, value
 
@@ -164,10 +156,12 @@
     out_query.wait()
 
 
-def layer(counts, holder, queries, keys, values, recv, grads):
+def layer(counts, holder, queries, keys, values, recv_keys, recv_values, grads):
     docs, _, features = queries.shape
     entries = holder.shape[0] * holder.shape[1]
     rows = grads.shape[0]
+    slot_count, block_rows, _ = recv_keys.shape
+    slot_shape = (2 * block_rows, features)
     dma = pltpu.SemaphoreType.DMA
     return pl.pallas_call(
         layer_kernel,
@@ -175,15 +169,15 @@
             pltpu.HBM((rows, features), BF16),
             pltpu.HBM(queries.shape, BF16),
             pltpu.HBM((2, *keys.shape), F32),
-            pltpu.HBM(recv.shape, BF16),
-        ],
-        in_specs=[SMEM] * 2 + [VMEM] * 5,
+            pltpu.HBM((slot_count, *slot_shape), BF16),
+        ],
+        in_specs=[SMEM] * 2 + [VMEM] * 6,
         out_specs=[HBM] * 4,
         scratch_shapes=[
             pltpu.VMEM((rows, features), BF16),
             pltpu.VMEM(queries.shape, BF16),
             pltpu.VMEM((2, *keys.shape), F32),
-            pltpu.VMEM((entries, *recv.shape[1:]), BF16),
+            pltpu.VMEM((entries, *slot_shape), BF16),
             dma((2,)),
             dma((docs,)),
             dma((entries,)),
@@ -191,7 +185,7 @@
         compiler_params=PARAMS,
         cost_estimate=cost(4 * 2**30, 12 * 2**20),
         name="layer",
-    )(counts, holder, queries, keys, values, recv, grads)
+    )(counts, holder, queries, keys, values, recv_keys, recv_values, grads)
 
 
 def copies_in(pairs, sem):
@@ -366,21 +360,24 @@
     pair, asked = lax.optimization_barrier((jnp.concatenate([weight, other]), asked))
     near, next_near = along_ring(pair, 1), along_ring(pair, 2)
     grads = passed_along(sent_grads, "section", -1)[0]
-    next_near, grads = lax.optimization_barrier((next_near, grads))
+    key_slots, value_slots = picked_slots(asked, keys, values)
+    key_slots, near, next_near, grads = lax.optimization_barrier((key_slots, near, next_near, grads))
+    recv_keys = exchanged(key_slots)
     third, far = along_ring(next_near, 1), along_ring(next_near[: weight.shape[0]], 2)
-    slots = picked_slots(asked, keys, values)
-    slots, near, third, far = lax.optimization_barrier((slots, near, third, far))
-    recv = exchanged(slots)
+    docs, query_count = sent_queries.shape[1:3]
+    grad_rows = grads.reshape(docs * query_count, grads.shape[2])
+    held = [grad_rows] + [passed_along(grad_rows, "tensor", -j) for j in range(1, tensor)]
+    value_slots, third, far, *held = lax.optimization_barrier((value_slots, third, far, *held))
+    recv_values = exchanged(value_slots)
     blocks = [weight, other, near, next_near, third, far]
     blocks += [swapped(block) for block in blocks[2:]]
 
     queries = passed_along(sent_queries, "section", 1)[0]
-    docs, query_count, features = queries.shape
-    grad_rows = grads.reshape(docs * query_count, grads.shape[2])
-    held = [grad_rows] + [passed_along(grad_rows, "tensor", -j) for j in range(1, tensor)]
     grad_attended = back_projected(table, held, blocks)
 
-    attended, query_grads, own_rows, slots = layer(counts, holder, queries, keys, values, recv, grad_attended)
+    attended, query_grads, own_rows, slots = layer(
+        counts, holder, queries, keys, values, recv_keys, recv_values, grad_attended
+    )
     back = exchanged(slots)
     terms = projected(table, attended, blocks, tensor)
     arrived = [terms[0]] + [passed_along(terms[j], "tensor", j) for j in range(1, tensor)]

time: 184 us -> 192 us (1.043)
  waiting for transfers between devices: 64.6 us -> 70.2 us
    ppermute x4, waiting for transfers between devices: 12.7 us -> 28.4 us  [along_ring(): lax.ppermute(block, 'dp', [(i, (i + (1 - i % 2 * 2) * 2 * chips) % count)...]
    ppermute x8, waiting for transfers between devices: 33 us -> 19.6 us  [passed_along(): lax.ppermute(block, axis, [(i, (i + distance) % count) for i in range(cou...]
    all_to_all x3 -> x4, starting transfers between devices: 18.1 us -> 21 us  [exchanged(): return lax.all_to_all(slots, 'dp', split_axis=0, concat_axis=0, tiled=True)]
    all_to_all x3 -> x4, waiting for transfers between devices: 18.8 us -> 21 us  [exchanged(): return lax.all_to_all(slots, 'dp', split_axis=0, concat_axis=0, tiled=True)]
  transfers between devices with their start and end apart: 20 -> 21, of which waited for: 11 -> 9; matrix products, arithmetic and copies ran while one was open for 3% -> 3% of each run, Pallas kernels for 8% -> 7%
where the time goes in v10:
time: 192 us; the launch traced here: 191 us
  starting transfers between devices  87.6 us (46%)
  waiting for transfers between devices  70.2 us (37%)
  Pallas kernels  23.8 us (12%)
  local copies, waits for them, and re-layouts  5.32 us (3%)
  other arithmetic  3.45 us (2%)
    ppermute x8, starting transfers between devices, passed_along(): lax.ppermute(block, axis, [(i, (i + distance) % count) for i in range(cou...  32.2 us
    ppermute x4, waiting for transfers between devices, along_ring(): lax.ppermute(block, 'dp', [(i, (i + (1 - i % 2 * 2) * 2 * chips) % count)...  28.4 us
    all_to_all x4, starting transfers between devices, exchanged(): return lax.all_to_all(slots, 'dp', split_axis=0, concat_axis=0, tiled=True)  21 us
    all_to_all x4, waiting for transfers between devices, exchanged(): return lax.all_to_all(slots, 'dp', split_axis=0, concat_axis=0, tiled=True)  21 us
    ppermute x8, waiting for transfers between devices, passed_along(): lax.ppermute(block, axis, [(i, (i + distance) % count) for i in range(cou...  19.6 us
    ppermute x5, starting transfers between devices, swapped(): lax.ppermute(block, 'dp', [(i, i ^ 1) for i in range(lax.axis_size('dp'))])  17.4 us
    ppermute x4, starting transfers between devices, along_ring(): lax.ppermute(block, 'dp', [(i, (i + (1 - i % 2 * 2) * 2 * chips) % count)...  16.9 us
    pallas_call x1, Pallas kernels, layer(): pl.pallas_call(layer_kernel, out_shape=[pltpu.HBM((rows, features), BF16)...  6.56 us
  transfers between devices with their start and end apart: 21, of which 9 were waited for; matrix products, arithmetic and copies ran while one was open for 3% of the time, Pallas kernels for 7%

profile of v10, /device:TPU:1, one launch (start us, length us, event | category | flops | bytes accessed | tf_op | source)
XLA Modules:
  0.0 191.3 jit_solution(7452454152173747232)
XLA Ops:
  0.6 8.8 %collective-permute-start.1 = (bf16[512,256]{1,0:T(8,128)(2,1)}, bf16[512,256]{1,0:T(8,128)(2,1)S(1)}, u32[]{:S(2)}, u32[]{:S(2)}) collective-permute-start(bf16[512,256]{1,0:T(8,128)(2,1)} %bitcast.23), channel_id=1, source_target_pairs={{0,32},{32,0},{64,96},{96,64},{128,160},{160,128},{192,224},{224,1... | collective-permute-start | bytes 786440 | tf_op jit(solution)/shard_map/ppermute | solution.py:27
  10.9 3.4 %all-to-all-start = ((s32[16,1,1]{2,1,0:T(1,128)}), s32[16,1,1]{2,1,0:T(1,128)S(1)}, u32[]{:S(2)}, u32[]{:S(2)}) async-start(s32[16,1,1]{2,1,0:T(1,128)} %copy.20), calls=%async_computation | async-start | bytes 16384 | tf_op jit(solution)/shard_map/all_to_all | solution.py:36
  14.3 9.2 %collective-permute-start.4 = (bf16[1,2,128,1024]{3,2,1,0:T(8,128)(2,1)}, bf16[1,2,128,1024]{3,2,1,0:T(8,128)(2,1)S(1)}, u32[]{:S(2)}, u32[]{:S(2)}) collective-permute-start(bf16[1,2,128,1024]{3,2,1,0:T(8,128)(2,1)} %param.12), channel_id=1, source_target_pairs={{0,28},{4,0},{8,4},{12,8},{16,12},{20,16},{24,20},{28,24},{1,29},{... | collective-permute-start | bytes 1572872 | tf_op jit(solution)/shard_map/ppermute | solution.py:23
  24.9 5.4 %collective-permute-start.3 = (bf16[1024,256]{1,0:T(8,128)(2,1)S(1)}, bf16[1024,256]{1,0:T(8,128)(2,1)}, u32[]{:S(2)}, u32[]{:S(2)}) collective-permute-start(bf16[1024,256]{1,0:T(8,128)(2,1)S(1)} %pad_maximum_fusion), channel_id=1, source_target_pairs={{0,128},{32,416},{64,192},{96,480},{128,256},{160,32},{192,320},{2... | collective-permute-start | bytes 1572872 | tf_op jit(solution)/shard_map/ppermute | solution.py:32
  36.6 5.5 %collective-permute-done.3.refs_3_ = bf16[1024,256]{1,0:T(8,128)(2,1)} collective-permute-done((bf16[1024,256]{1,0:T(8,128)(2,1)S(1)}, bf16[1024,256]{1,0:T(8,128)(2,1)}, u32[]{:S(2)}, u32[]{:S(2)}) %collective-permute-start.3) | collective-permute-done | bytes 524320 | tf_op jit(solution)/shard_map/ppermute | solution.py:32
  42.0 5.6 %collective-permute-done.2.refs_2_ = bf16[1024,256]{1,0:T(8,128)(2,1)} collective-permute-done((bf16[1024,256]{1,0:T(8,128)(2,1)S(1)}, bf16[1024,256]{1,0:T(8,128)(2,1)}, u32[]{:S(2)}, u32[]{:S(2)}) %collective-permute-start.2) | collective-permute-done | bytes 524320 | tf_op jit(solution)/shard_map/ppermute | solution.py:32
  47.7 8.5 %all-to-all-start.1 = ((bf16[16,64,512]{2,1,0:T(8,128)(2,1)}), bf16[16,64,512]{2,1,0:T(8,128)(2,1)S(1)}, u32[]{:S(2)}, u32[]{:S(2)}) async-start(bf16[16,64,512]{2,1,0:T(8,128)(2,1)} %get-tuple-element.32), calls=%async_computation.1 | async-start | bytes 2097152 | tf_op jit(solution)/shard_map/all_to_all | solution.py:36
  56.2 3.1 %collective-permute-start.9 = (bf16[256,1024]{1,0:T(8,128)(2,1)S(1)}, bf16[256,1024]{1,0:T(8,128)(2,1)S(1)}, u32[]{:S(2)}, u32[]{:S(2)}) collective-permute-start(bf16[256,1024]{1,0:T(8,128)(2,1)S(1)} %bitcast.28), channel_id=1, source_target_pairs={{0,1},{1,2},{2,3},{3,0},{4,5},{5,6},{6,7},{7,4},{8,9},{9,10},{10,1... | collective-permute-start | bytes 1572872 | tf_op jit(solution)/shard_map/ppermute | solution.py:23
  59.3 4.4 %collective-permute-start.8 = (bf16[256,1024]{1,0:T(8,128)(2,1)S(1)}, bf16[256,1024]{1,0:T(8,128)(2,1)S(1)}, u32[]{:S(2)}, u32[]{:S(2)}) collective-permute-start(bf16[256,1024]{1,0:T(8,128)(2,1)S(1)} %bitcast.29), channel_id=1, source_target_pairs={{0,2},{1,3},{2,0},{3,1},{4,6},{5,7},{6,4},{7,5},{8,10},{9,11},{10,... | collective-permute-start | bytes 1572872 | tf_op jit(solution)/shard_map/ppermute | solution.py:23
  66.8 4.5 %collective-permute-start.5 = (bf16[1024,256]{1,0:T(8,128)(2,1)}, bf16[1024,256]{1,0:T(8,128)(2,1)}, u32[]{:S(2)}, u32[]{:S(2)}) collective-permute-start(bf16[1024,256]{1,0:T(8,128)(2,1)} %collective-permute-done.3.refs_3_), channel_id=1, source_target_pairs={{0,64},{32,480},{64,128},{96,32},{128,192},{160,96},{192,256},{224... | collective-permute-start | bytes 1572872 | tf_op jit(solution)/shard_map/ppermute | solution.py:32
  72.2 4.0 %collective-permute-start.6 = (bf16[512,256]{1,0:T(8,128)(2,1)S(1)}, bf16[512,256]{1,0:T(8,128)(2,1)}, u32[]{:S(2)}, u32[]{:S(2)}) collective-permute-start(bf16[512,256]{1,0:T(8,128)(2,1)S(1)} %slice.3), channel_id=1, source_target_pairs={{0,128},{32,416},{64,192},{96,480},{128,256},{160,32},{192,320},{2... | collective-permute-start | bytes 786440 | tf_op jit(solution)/shard_map/ppermute | solution.py:32
  76.2 17.3 %collective-permute-done.6.refs_5_ = bf16[512,256]{1,0:T(8,128)(2,1)} collective-permute-done((bf16[512,256]{1,0:T(8,128)(2,1)S(1)}, bf16[512,256]{1,0:T(8,128)(2,1)}, u32[]{:S(2)}, u32[]{:S(2)}) %collective-permute-start.6) | collective-permute-done | bytes 262176 | tf_op jit(solution)/shard_map/ppermute | solution.py:32
  94.7 5.5 %all-to-all-start.2 = ((bf16[16,64,512]{2,1,0:T(8,128)(2,1)}), bf16[16,64,512]{2,1,0:T(8,128)(2,1)S(1)}, u32[]{:S(2)}, u32[]{:S(2)}) async-start(bf16[16,64,512]{2,1,0:T(8,128)(2,1)} %get-tuple-element.36), calls=%async_computation.2 | async-start | bytes 2097152 | tf_op jit(solution)/shard_map/all_to_all | solution.py:36
  113.7 6.1 %back_projection.1.grads = bf16[256,512]{1,0:T(8,128)(2,1)} custom-call(s32[2,16]{1,0:T(2,128)S(1)} %pad_add_fusion.table, bf16[256,1024]{1,0:T(8,128)(2,1)} %bitcast.31, bf16[256,1024]{1,0:T(8,128)(2,1)} %copy-done.9, bf16[256,1024]{1,0:T(8,128)(2,1)} %copy-done.8, bf16[256,1024]{1,0:T(8,128)(2,1)} %copy-done.7, bf16[512,256]{1,0:T(8,128)(2,1)} %bitcast.25, ...), custom_call_target="tpu_custom_call" | custom-call | flops 2147483648 | bytes 8388608 | tf_op jit(solution)/shard_map/back_projection/pallas_call | solution.py:231
  119.8 8.3 %all-to-all-done.2.recv_values = bf16[16,64,512]{2,1,0:T(8,128)(2,1)S(1)} async-done(((bf16[16,64,512]{2,1,0:T(8,128)(2,1)}), bf16[16,64,512]{2,1,0:T(8,128)(2,1)S(1)}, u32[]{:S(2)}, u32[]{:S(2)}) %all-to-all-start.2) | async-done | bytes 1048608 | tf_op jit(solution)/shard_map/all_to_all | solution.py:36
  129.1 6.6 %layer.1 = (bf16[256,512]{1,0:T(8,128)(2,1)}, bf16[2,128,512]{2,1,0:T(8,128)(2,1)}, f32[2,8,64,512]{3,2,1,0:T(8,128)}, bf16[16,128,512]{2,1,0:T(8,128)(2,1)}) custom-call(s32[2]{0:T(128)S(1)} %copy-done.2, s32[2,4]{1,0:T(2,128)S(1)} %get-tuple-element.55.holder, bf16[2,128,512]{2,1,0:T(8,128)(2,1)S(1)} %bitcast.21, bf16[8,64,512]{2,1,0:T(8,128)(2,1)S(1)} %bitcast.18, ...), custom_call_target="tpu_custom_call" | custom-call | flops 4294967296 | bytes 12582912 | tf_op jit(solution)/shard_map/layer/pallas_call | solution.py:166
  135.6 3.6 %all-to-all-start.3 = ((bf16[16,128,512]{2,1,0:T(8,128)(2,1)}), bf16[16,128,512]{2,1,0:T(8,128)(2,1)S(1)}, u32[]{:S(2)}, u32[]{:S(2)}) async-start(bf16[16,128,512]{2,1,0:T(8,128)(2,1)} %get-tuple-element.51), calls=%async_computation.3 | async-start | bytes 4194304 | tf_op jit(solution)/shard_map/all_to_all | solution.py:36
  139.3 4.9 %projection.1 = (bf16[256,1024]{1,0:T(8,128)(2,1)S(1)}, bf16[256,1024]{1,0:T(8,128)(2,1)S(1)}, bf16[256,1024]{1,0:T(8,128)(2,1)S(1)}, bf16[256,1024]{1,0:T(8,128)(2,1)S(1)}) custom-call(s32[2,16]{1,0:T(2,128)S(1)} %pad_add_fusion.table, bf16[256,512]{1,0:T(8,128)(2,1)} %get-tuple-element.44.attended_hbm, bf16[512,256]{1,0:T(8,128)(2,1)} %bitcast.26, ...), custom_call_target="tpu_custom_call" | custom-call | flops 2147483648 | bytes 8388608 | tf_op jit(solution)/shard_map/projection/pallas_call | solution.py:270
  144.2 3.1 %collective-permute-start.14 = (bf16[256,1024]{1,0:T(8,128)(2,1)S(1)}, bf16[256,1024]{1,0:T(8,128)(2,1)S(1)}, u32[]{:S(2)}, u32[]{:S(2)}) collective-permute-start(bf16[256,1024]{1,0:T(8,128)(2,1)S(1)} %get-tuple-element.46), channel_id=1, source_target_pairs={{0,1},{1,2},{2,3},{3,0},{4,5},{5,6},{6,7},{7,4},{8,9},{9,10},{10,1... | collective-permute-start | bytes 1572872 | tf_op jit(solution)/shard_map/ppermute | solution.py:23
  147.3 4.4 %collective-permute-start.15 = (bf16[256,1024]{1,0:T(8,128)(2,1)S(1)}, bf16[256,1024]{1,0:T(8,128)(2,1)S(1)}, u32[]{:S(2)}, u32[]{:S(2)}) collective-permute-start(bf16[256,1024]{1,0:T(8,128)(2,1)S(1)} %get-tuple-element.47), channel_id=1, source_target_pairs={{0,2},{1,3},{2,0},{3,1},{4,6},{5,7},{6,4},{7,5},{8,10},{9,11},{10,... | collective-permute-start | bytes 1572872 | tf_op jit(solution)/shard_map/ppermute | solution.py:23
  154.7 6.1 %collective-permute-done.14 = bf16[256,1024]{1,0:T(8,128)(2,1)S(1)} collective-permute-done((bf16[256,1024]{1,0:T(8,128)(2,1)S(1)}, bf16[256,1024]{1,0:T(8,128)(2,1)S(1)}, u32[]{:S(2)}, u32[]{:S(2)}) %collective-permute-start.14) | collective-permute-done | bytes 524320 | tf_op jit(solution)/shard_map/ppermute | solution.py:23
  160.8 12.2 %collective-permute-done.15 = bf16[256,1024]{1,0:T(8,128)(2,1)S(1)} collective-permute-done((bf16[256,1024]{1,0:T(8,128)(2,1)S(1)}, bf16[256,1024]{1,0:T(8,128)(2,1)S(1)}, u32[]{:S(2)}, u32[]{:S(2)}) %collective-permute-start.15) | collective-permute-done | bytes 524320 | tf_op jit(solution)/shard_map/ppermute | solution.py:23
  175.4 12.7 %all-to-all-done.3.back = bf16[16,128,512]{2,1,0:T(8,128)(2,1)S(1)} async-done(((bf16[16,128,512]{2,1,0:T(8,128)(2,1)}), bf16[16,128,512]{2,1,0:T(8,128)(2,1)S(1)}, u32[]{:S(2)}, u32[]{:S(2)}) %all-to-all-start.3) | async-done | bytes 2097184 | tf_op jit(solution)/shard_map/all_to_all | solution.py:36
  188.1 3.2 %combine.1 = (bf16[8,64,512]{2,1,0:T(8,128)(2,1)}, bf16[8,64,512]{2,1,0:T(8,128)(2,1)}) custom-call(s32[16,1]{1,0:T(8,128)S(1)} %copy.21.asked, f32[2,8,64,512]{3,2,1,0:T(8,128)} %get-tuple-element.50.own_rows_hbm, bf16[16,128,512]{2,1,0:T(8,128)(2,1)S(1)} %all-to-all-done.3.back), custom_call_target="tpu_custom_call" | custom-call | bytes 4194304 | tf_op jit(solution)/shard_map/combine/pallas_call | solution.py:323
  (63 shorter events, 34.1 us)
Async XLA Ops:
  0.6 23.2 %collective-permute-start.1 = (bf16[512,256]{1,0:T(8,128)(2,1)}, bf16[512,256]{1,0:T(8,128)(2,1)S(1)}, u32[]{:S(2)}, u32[]{:S(2)}) collective-permute-start(bf16[512,256]{1,0:T(8,128)(2,1)} %bitcast.23), channel_id=1, source_target_pairs={{0,32},{32,0},{64,96},{96,64},{128,160},{160,128},{192,224},{224,1... | collective-permute-start | bytes 786440 | tf_op jit(solution)/shard_map/ppermute | solution.py:27
  10.9 12.6 %all-to-all-start = ((s32[16,1,1]{2,1,0:T(1,128)}), s32[16,1,1]{2,1,0:T(1,128)S(1)}, u32[]{:S(2)}, u32[]{:S(2)}) async-start(s32[16,1,1]{2,1,0:T(1,128)} %copy.20), calls=%async_computation | async-start | bytes 16384 | tf_op jit(solution)/shard_map/all_to_all | solution.py:36
  14.3 22.3 %collective-permute-start.4 = (bf16[1,2,128,1024]{3,2,1,0:T(8,128)(2,1)}, bf16[1,2,128,1024]{3,2,1,0:T(8,128)(2,1)S(1)}, u32[]{:S(2)}, u32[]{:S(2)}) collective-permute-start(bf16[1,2,128,1024]{3,2,1,0:T(8,128)(2,1)} %param.12), channel_id=1, source_target_pairs={{0,28},{4,0},{8,4},{12,8},{16,12},{20,16},{24,20},{28,24},{1,29},{... | collective-permute-start | bytes 1572872 | tf_op jit(solution)/shard_map/ppermute | solution.py:23
  23.8 23.8 %copy-start.4 = (bf16[512,256]{1,0:T(8,128)(2,1)}, bf16[512,256]{1,0:T(8,128)(2,1)S(1)}, u32[]{:S(2)}) copy-start(bf16[512,256]{1,0:T(8,128)(2,1)S(1)} %collective-permute-done.1.refs_1_) | copy-start | bytes 786436
  24.9 17.1 %collective-permute-start.3 = (bf16[1024,256]{1,0:T(8,128)(2,1)S(1)}, bf16[1024,256]{1,0:T(8,128)(2,1)}, u32[]{:S(2)}, u32[]{:S(2)}) collective-permute-start(bf16[1024,256]{1,0:T(8,128)(2,1)S(1)} %pad_maximum_fusion), channel_id=1, source_target_pairs={{0,128},{32,416},{64,192},{96,480},{128,256},{160,32},{192,320},{2... | collective-permute-start | bytes 1572872 | tf_op jit(solution)/shard_map/ppermute | solution.py:32
  30.3 17.3 %collective-permute-start.2 = (bf16[1024,256]{1,0:T(8,128)(2,1)S(1)}, bf16[1024,256]{1,0:T(8,128)(2,1)}, u32[]{:S(2)}, u32[]{:S(2)}) collective-permute-start(bf16[1024,256]{1,0:T(8,128)(2,1)S(1)} %pad_maximum_fusion), channel_id=1, source_target_pairs={{0,64},{32,480},{64,128},{96,32},{128,192},{160,96},{192,256},{224... | collective-permute-start | bytes 1572872 | tf_op jit(solution)/shard_map/ppermute | solution.py:32
  36.6 58.0 %copy-start.6 = (bf16[1,2,128,1024]{3,2,1,0:T(8,128)(2,1)}, bf16[1,2,128,1024]{3,2,1,0:T(8,128)(2,1)S(1)}, u32[]{:S(2)}) copy-start(bf16[1,2,128,1024]{3,2,1,0:T(8,128)(2,1)S(1)} %collective-permute-done.4) | copy-start | bytes 1572868
  47.7 60.8 %copy-start.5 = (s32[16]{0:T(128)S(1)}, s32[16]{0:T(128)}, u32[]{:S(2)}) copy-start(s32[16]{0:T(128)} %constant.81.clone) | copy-start | bytes 196
  47.7 46.9 %all-to-all-start.1 = ((bf16[16,64,512]{2,1,0:T(8,128)(2,1)}), bf16[16,64,512]{2,1,0:T(8,128)(2,1)S(1)}, u32[]{:S(2)}, u32[]{:S(2)}) async-start(bf16[16,64,512]{2,1,0:T(8,128)(2,1)} %get-tuple-element.32), calls=%async_computation.1 | async-start | bytes 2097152 | tf_op jit(solution)/shard_map/all_to_all | solution.py:36
  56.2 37.3 %collective-permute-start.9 = (bf16[256,1024]{1,0:T(8,128)(2,1)S(1)}, bf16[256,1024]{1,0:T(8,128)(2,1)S(1)}, u32[]{:S(2)}, u32[]{:S(2)}) collective-permute-start(bf16[256,1024]{1,0:T(8,128)(2,1)S(1)} %bitcast.28), channel_id=1, source_target_pairs={{0,1},{1,2},{2,3},{3,0},{4,5},{5,6},{6,7},{7,4},{8,9},{9,10},{10,1... | collective-permute-start | bytes 1572872 | tf_op jit(solution)/shard_map/ppermute | solution.py:23
  59.3 34.2 %collective-permute-start.8 = (bf16[256,1024]{1,0:T(8,128)(2,1)S(1)}, bf16[256,1024]{1,0:T(8,128)(2,1)S(1)}, u32[]{:S(2)}, u32[]{:S(2)}) collective-permute-start(bf16[256,1024]{1,0:T(8,128)(2,1)S(1)} %bitcast.29), channel_id=1, source_target_pairs={{0,2},{1,3},{2,0},{3,1},{4,6},{5,7},{6,4},{7,5},{8,10},{9,11},{10,... | collective-permute-start | bytes 1572872 | tf_op jit(solution)/shard_map/ppermute | solution.py:23
  63.7 29.9 %collective-permute-start.7 = (bf16[256,1024]{1,0:T(8,128)(2,1)S(1)}, bf16[256,1024]{1,0:T(8,128)(2,1)S(1)}, u32[]{:S(2)}, u32[]{:S(2)}) collective-permute-start(bf16[256,1024]{1,0:T(8,128)(2,1)S(1)} %bitcast.30), channel_id=1, source_target_pairs={{0,3},{1,0},{2,1},{3,2},{4,7},{5,4},{6,5},{7,6},{8,11},{9,8},{10,9... | collective-permute-start | bytes 1572872 | tf_op jit(solution)/shard_map/ppermute | solution.py:23
  66.8 26.8 %collective-permute-start.5 = (bf16[1024,256]{1,0:T(8,128)(2,1)}, bf16[1024,256]{1,0:T(8,128)(2,1)}, u32[]{:S(2)}, u32[]{:S(2)}) collective-permute-start(bf16[1024,256]{1,0:T(8,128)(2,1)} %collective-permute-done.3.refs_3_), channel_id=1, source_target_pairs={{0,64},{32,480},{64,128},{96,32},{128,192},{160,96},{192,256},{224... | collective-permute-start | bytes 1572872 | tf_op jit(solution)/shard_map/ppermute | solution.py:32
  72.2 21.3 %collective-permute-start.6 = (bf16[512,256]{1,0:T(8,128)(2,1)S(1)}, bf16[512,256]{1,0:T(8,128)(2,1)}, u32[]{:S(2)}, u32[]{:S(2)}) collective-permute-start(bf16[512,256]{1,0:T(8,128)(2,1)S(1)} %slice.3), channel_id=1, source_target_pairs={{0,128},{32,416},{64,192},{96,480},{128,256},{160,32},{192,320},{2... | collective-permute-start | bytes 786440 | tf_op jit(solution)/shard_map/ppermute | solution.py:32
  94.7 33.4 %all-to-all-start.2 = ((bf16[16,64,512]{2,1,0:T(8,128)(2,1)}), bf16[16,64,512]{2,1,0:T(8,128)(2,1)S(1)}, u32[]{:S(2)}, u32[]{:S(2)}) async-start(bf16[16,64,512]{2,1,0:T(8,128)(2,1)} %get-tuple-element.36), calls=%async_computation.2 | async-start | bytes 2097152 | tf_op jit(solution)/shard_map/all_to_all | solution.py:36
  100.2 19.6 %collective-permute-start = (bf16[1,2,128,512]{3,2,1,0:T(8,128)(2,1)}, bf16[1,2,128,512]{3,2,1,0:T(8,128)(2,1)S(1)}, u32[]{:S(2)}, u32[]{:S(2)}) collective-permute-start(bf16[1,2,128,512]{3,2,1,0:T(8,128)(2,1)} %param.8), channel_id=1, source_target_pairs={{0,4},{4,8},{8,12},{12,16},{16,20},{20,24},{24,28},{28,0},{1,5},{5... | collective-permute-start | bytes 786440 | tf_op jit(solution)/shard_map/ppermute | solution.py:23
  102.1 8.8 %collective-permute-start.11 = (bf16[1024,256]{1,0:T(8,128)(2,1)}, bf16[1024,256]{1,0:T(8,128)(2,1)S(1)}, u32[]{:S(2)}, u32[]{:S(2)}) collective-permute-start(bf16[1024,256]{1,0:T(8,128)(2,1)} %collective-permute-done.3.refs_3_), channel_id=1, source_target_pairs={{0,32},{32,0},{64,96},{96,64},{128,160},{160,128},{192,224},{224,1... | collective-permute-start | bytes 1572872 | tf_op jit(solution)/shard_map/ppermute | solution.py:27
  104.1 6.8 %collective-permute-start.10 = (bf16[1024,256]{1,0:T(8,128)(2,1)}, bf16[1024,256]{1,0:T(8,128)(2,1)S(1)}, u32[]{:S(2)}, u32[]{:S(2)}) collective-permute-start(bf16[1024,256]{1,0:T(8,128)(2,1)} %collective-permute-done.2.refs_2_), channel_id=1, source_target_pairs={{0,32},{32,0},{64,96},{96,64},{128,160},{160,128},{192,224},{224,1... | collective-permute-start | bytes 1572872 | tf_op jit(solution)/shard_map/ppermute | solution.py:27
  106.4 5.7 %collective-permute-start.12 = (bf16[1024,256]{1,0:T(8,128)(2,1)}, bf16[1024,256]{1,0:T(8,128)(2,1)S(1)}, u32[]{:S(2)}, u32[]{:S(2)}) collective-permute-start(bf16[1024,256]{1,0:T(8,128)(2,1)} %collective-permute-done.5.refs_4_), channel_id=1, source_target_pairs={{0,32},{32,0},{64,96},{96,64},{128,160},{160,128},{192,224},{224,1... | collective-permute-start | bytes 1572872 | tf_op jit(solution)/shard_map/ppermute | solution.py:27
  108.5 3.7 %collective-permute-start.13 = (bf16[512,256]{1,0:T(8,128)(2,1)}, bf16[512,256]{1,0:T(8,128)(2,1)S(1)}, u32[]{:S(2)}, u32[]{:S(2)}) collective-permute-start(bf16[512,256]{1,0:T(8,128)(2,1)} %collective-permute-done.6.refs_5_), channel_id=1, source_target_pairs={{0,32},{32,0},{64,96},{96,64},{128,160},{160,128},{192,224},{224,1... | collective-permute-start | bytes 786440 | tf_op jit(solution)/shard_map/ppermute | solution.py:27
  135.6 52.5 %all-to-all-start.3 = ((bf16[16,128,512]{2,1,0:T(8,128)(2,1)}), bf16[16,128,512]{2,1,0:T(8,128)(2,1)S(1)}, u32[]{:S(2)}, u32[]{:S(2)}) async-start(bf16[16,128,512]{2,1,0:T(8,128)(2,1)} %get-tuple-element.51), calls=%async_computation.3 | async-start | bytes 4194304 | tf_op jit(solution)/shard_map/all_to_all | solution.py:36
  144.2 16.7 %collective-permute-start.14 = (bf16[256,1024]{1,0:T(8,128)(2,1)S(1)}, bf16[256,1024]{1,0:T(8,128)(2,1)S(1)}, u32[]{:S(2)}, u32[]{:S(2)}) collective-permute-start(bf16[256,1024]{1,0:T(8,128)(2,1)S(1)} %get-tuple-element.46), channel_id=1, source_target_pairs={{0,1},{1,2},{2,3},{3,0},{4,5},{5,6},{6,7},{7,4},{8,9},{9,10},{10,1... | collective-permute-start | bytes 1572872 | tf_op jit(solution)/shard_map/ppermute | solution.py:23
  147.3 25.7 %collective-permute-start.15 = (bf16[256,1024]{1,0:T(8,128)(2,1)S(1)}, bf16[256,1024]{1,0:T(8,128)(2,1)S(1)}, u32[]{:S(2)}, u32[]{:S(2)}) collective-permute-start(bf16[256,1024]{1,0:T(8,128)(2,1)S(1)} %get-tuple-element.47), channel_id=1, source_target_pairs={{0,2},{1,3},{2,0},{3,1},{4,6},{5,7},{6,4},{7,5},{8,10},{9,11},{10,... | collective-permute-start | bytes 1572872 | tf_op jit(solution)/shard_map/ppermute | solution.py:23
  151.7 22.6 %collective-permute-start.16 = (bf16[256,1024]{1,0:T(8,128)(2,1)S(1)}, bf16[256,1024]{1,0:T(8,128)(2,1)S(1)}, u32[]{:S(2)}, u32[]{:S(2)}) collective-permute-start(bf16[256,1024]{1,0:T(8,128)(2,1)S(1)} %get-tuple-element.48), channel_id=1, source_target_pairs={{0,3},{1,0},{2,1},{3,2},{4,7},{5,4},{6,5},{7,6},{8,11},{9,8},{10,9... | collective-permute-start | bytes 1572872 | tf_op jit(solution)/shard_map/ppermute | solution.py:23
  (11 other events, 59.7 us)

commit v11 on v6

--- a/solution.py
+++ b/solution.py
@@ -91,7 +91,6 @@
     groups, per, _, block = weight.shape
     heads = features // HD
     scale = HD**-0.5
-    total = (own + neg) * rows
 
     arriving = []
     for j, grad in enumerate((grad0, grad1, grad2, grad3)):
@@ -115,14 +114,14 @@
         )
         return doc, at, query_rows, key, value
 
-    position = lax.broadcasted_iota(jnp.int32, (total, 1), 0)
+    position = lax.broadcasted_iota(jnp.int32, (own * rows, 1), 0)
 
     @pl.loop(0, docs * heads, unroll=4)
     def _(step):
         doc, at, query_rows, key, value = place(step)
-        valid = (position < counts[doc] * rows) | (position >= own * rows)
+        valid = position < counts[doc] * rows
         scores = lax.dot_general(key, queries[doc, :, at], NT, preferred_element_type=F32) * scale
-        scores = jnp.where(valid, scores, -jnp.inf)
+        scores = jnp.concatenate([jnp.where(valid, scores[: own * rows], -jnp.inf), scores[own * rows :]], axis=0)
         expo = jnp.exp(scores - jnp.max(scores, axis=0, keepdims=True))
         prob = expo * (1.0 / jnp.sum(expo, axis=0, keepdims=True))
         probs[step] = prob
@@ -156,8 +155,8 @@
         grad_query[doc, :, at] = (lax.dot_general(grad_score, key, TN, preferred_element_type=F32) * scale).astype(BF16)
         for m in range(own):
             here = slice(m * rows, (m + 1) * rows)
-            own_rows[0, doc * own + m, :, at] = grad_key[here]
-            own_rows[1, doc * own + m, :, at] = grad_value[here]
+            own_rows[0, doc * own + m, :, at] = grad_key[here].astype(BF16)
+            own_rows[1, doc * own + m, :, at] = grad_value[here].astype(BF16)
         for m in range(neg):
             here = slice((own + m) * rows, (own + m + 1) * rows)
             slots[doc * neg + m, :rows, at] = grad_key[here].astype(BF16)
@@ -193,7 +192,7 @@
         out_shape=[
             pltpu.HBM((rows, features), BF16),
             pltpu.HBM(queries.shape, BF16),
-            pltpu.HBM((2, *keys.shape), F32),
+            pltpu.HBM((2, *keys.shape), BF16),
             pltpu.HBM(recv.shape, BF16),
         ],
         in_specs=[SMEM] * 3 + [VMEM] * 4 + [HBM] * (1 + groups),
@@ -205,7 +204,7 @@
             pltpu.VMEM((docs * features // HD, (keys.shape[0] // docs + holder.shape[1]) * keys.shape[1], query_count), F32),
             pltpu.VMEM((rows, features), BF16),
             pltpu.VMEM(queries.shape, BF16),
-            pltpu.VMEM((2, *keys.shape), F32),
+            pltpu.VMEM((2, *keys.shape), BF16),
             pltpu.VMEM((entries, *recv.shape[1:]), BF16),
             dma((groups,)),
             dma((groups,)),
@@ -298,7 +297,7 @@
         in_specs=[SMEM, HBM, VMEM],
         out_specs=[HBM, HBM],
         scratch_shapes=[
-            pltpu.VMEM(own_rows.shape, F32),
+            pltpu.VMEM(own_rows.shape, BF16),
             pltpu.VMEM(own_rows.shape, F32),
             pltpu.VMEM(own_rows.shape, BF16),
             pltpu.SemaphoreType.DMA((2,)),
@@ -318,9 +317,8 @@
     tensor_spot = lax.axis_index("tensor").astype(jnp.int32).reshape(1)
 
     holder = neg_ids // mem_count
-    spot = neg_ids - holder * mem_count
-    named = holder[None] == jnp.arange(groups, dtype=jnp.int32)[:, None, None]
-    request = jnp.sum(jnp.where(named, spot[None] + 1, 0), axis=(1, 2)) - 1
+    spot = neg_ids[None] - mem_count * jnp.arange(groups, dtype=jnp.int32)[:, None, None]
+    request = jnp.max(jnp.where((spot >= 0) & (spot < mem_count), spot, -1), axis=(1, 2))
     asked = exchanged(request.reshape(groups, 1))
 
     queries = passed_along(sent_queries, "section", 1)[0]

time: 172 us -> 171 us (level)
  no operation moved by 1% of the time
where the time goes in v11:
time: 171 us
  waiting for transfers between devices  79.5 us (46%)
  starting transfers between devices  41.3 us (24%)
  Pallas kernels  17.5 us (10%)
  blocking collectives  16.3 us (10%)
  between operations  14.2 us (8%)
  other arithmetic  1.94 us (1%)
    ppermute x8, waiting for transfers between devices, passed_along(): lax.ppermute(block, axis, [(i, (i + distance) % count) for i in range(cou...  48.5 us
    ppermute x8, starting transfers between devices, passed_along(): lax.ppermute(block, axis, [(i, (i + distance) % count) for i in range(cou...  32.6 us
    all_to_all x2, waiting for transfers between devices, exchanged(): return lax.all_to_all(slots, 'dp', split_axis=0, concat_axis=0, tiled=True)  28 us
    all_to_all x1, blocking collectives, exchanged(): return lax.all_to_all(slots, 'dp', split_axis=0, concat_axis=0, tiled=True)  16.3 us
    all_to_all x2, starting transfers between devices, exchanged(): return lax.all_to_all(slots, 'dp', split_axis=0, concat_axis=0, tiled=True)  8.72 us
    pallas_call x1, Pallas kernels, layer(): pl.pallas_call(layer_kernel, out_shape=[pltpu.HBM((rows, features), BF16)...  7.85 us
    pallas_call x1, Pallas kernels, projected(): pl.pallas_call(project_kernel, out_shape=[shape] * groups, in_specs=[SMEM...  3.7 us
  transfers between devices with their start and end apart: 11, of which 10 were waited for; matrix products, arithmetic and copies ran while one was open for 1% of the time, Pallas kernels for 4%

profile of v11, /device:TPU:1, one launch (start us, length us, event | category | flops | bytes accessed | tf_op | source)
XLA Modules:
  0.0 170.9 jit_solution(17558652601146046150)
XLA Ops:
  8.8 16.3 %all_to_all.21 = s32[16,1,1]{2,1,0:T(1,128)S(1)} all-to-all(s32[16,1,1]{2,1,0:T(1,128)S(1)} %copy.19), channel_id=1, replica_groups=mesh['dp'=16,'section'=8,'tensor'=4] {'dp'}, dimensions={0} | all-to-all | bytes 128 | tf_op jit(solution)/shard_map/all_to_all | solution.py:26
  25.1 3.1 %pick_blocks.1 = bf16[16,128,512]{2,1,0:T(8,128)(2,1)} custom-call(s32[16,1]{1,0:T(8,128)S(1)} %bitcast.15, bf16[8,64,512]{2,1,0:T(8,128)(2,1)} %bitcast.11, bf16[8,64,512]{2,1,0:T(8,128)(2,1)} %bitcast.13), custom_call_target="tpu_custom_call" | custom-call | bytes 4194304 | tf_op jit(solution)/shard_map/pick_blocks/pallas_call | solution.py:65
  28.3 4.3 %all-to-all-start.1 = ((bf16[16,128,512]{2,1,0:T(8,128)(2,1)}), bf16[16,128,512]{2,1,0:T(8,128)(2,1)S(1)}, u32[]{:S(2)}, u32[]{:S(2)}) async-start(bf16[16,128,512]{2,1,0:T(8,128)(2,1)} %pick_blocks.1), calls=%async_computation.1 | async-start | bytes 4194304 | tf_op jit(solution)/shard_map/all_to_all | solution.py:26
  32.5 9.7 %collective-permute-start.1 = (bf16[1,2,128,1024]{3,2,1,0:T(8,128)(2,1)}, bf16[1,2,128,1024]{3,2,1,0:T(8,128)(2,1)}, u32[]{:S(2)}, u32[]{:S(2)}) collective-permute-start(bf16[1,2,128,1024]{3,2,1,0:T(8,128)(2,1)} %param.11), channel_id=1, source_target_pairs={{0,28},{4,0},{8,4},{12,8},{16,12},{20,16},{24,20},{28,24},{1,29},{... | collective-permute-start | bytes 1572872 | tf_op jit(solution)/shard_map/ppermute | solution.py:22
  42.3 11.4 %collective-permute-done.1 = bf16[1,2,128,1024]{3,2,1,0:T(8,128)(2,1)} collective-permute-done((bf16[1,2,128,1024]{3,2,1,0:T(8,128)(2,1)}, bf16[1,2,128,1024]{3,2,1,0:T(8,128)(2,1)}, u32[]{:S(2)}, u32[]{:S(2)}) %collective-permute-start.1) | collective-permute-done | bytes 524320 | tf_op jit(solution)/shard_map/ppermute | solution.py:22
  53.7 3.1 %collective-permute-start.4 = (bf16[256,1024]{1,0:T(8,128)(2,1)}, bf16[256,1024]{1,0:T(8,128)(2,1)}, u32[]{:S(2)}, u32[]{:S(2)}) collective-permute-start(bf16[256,1024]{1,0:T(8,128)(2,1)} %bitcast.6.grad0), channel_id=1, source_target_pairs={{0,1},{1,2},{2,3},{3,0},{4,5},{5,6},{6,7},{7,4},{8,9},{9,10},{10,1... | collective-permute-start | bytes 1572872 | tf_op jit(solution)/shard_map/ppermute | solution.py:22
  56.8 4.4 %collective-permute-start.3 = (bf16[256,1024]{1,0:T(8,128)(2,1)}, bf16[256,1024]{1,0:T(8,128)(2,1)}, u32[]{:S(2)}, u32[]{:S(2)}) collective-permute-start(bf16[256,1024]{1,0:T(8,128)(2,1)} %bitcast.6.grad0), channel_id=1, source_target_pairs={{0,2},{1,3},{2,0},{3,1},{4,6},{5,7},{6,4},{7,5},{8,10},{9,11},{10,... | collective-permute-start | bytes 1572872 | tf_op jit(solution)/shard_map/ppermute | solution.py:22
  61.2 3.1 %collective-permute-start.2 = (bf16[256,1024]{1,0:T(8,128)(2,1)}, bf16[256,1024]{1,0:T(8,128)(2,1)}, u32[]{:S(2)}, u32[]{:S(2)}) collective-permute-start(bf16[256,1024]{1,0:T(8,128)(2,1)} %bitcast.6.grad0), channel_id=1, source_target_pairs={{0,3},{1,0},{2,1},{3,2},{4,7},{5,4},{6,5},{7,6},{8,11},{9,8},{10,9... | collective-permute-start | bytes 1572872 | tf_op jit(solution)/shard_map/ppermute | solution.py:22
  64.2 1.9 %collective-permute-start = (bf16[1,2,128,512]{3,2,1,0:T(8,128)(2,1)}, bf16[1,2,128,512]{3,2,1,0:T(8,128)(2,1)S(1)}, u32[]{:S(2)}, u32[]{:S(2)}) collective-permute-start(bf16[1,2,128,512]{3,2,1,0:T(8,128)(2,1)} %param.7), channel_id=1, source_target_pairs={{0,4},{4,8},{8,12},{12,16},{16,20},{20,24},{24,28},{28,0},{1,5},{5... | collective-permute-start | bytes 786440 | tf_op jit(solution)/shard_map/ppermute | solution.py:22
  66.2 8.4 %collective-permute-done = bf16[1,2,128,512]{3,2,1,0:T(8,128)(2,1)S(1)} collective-permute-done((bf16[1,2,128,512]{3,2,1,0:T(8,128)(2,1)}, bf16[1,2,128,512]{3,2,1,0:T(8,128)(2,1)S(1)}, u32[]{:S(2)}, u32[]{:S(2)}) %collective-permute-start) | collective-permute-done | bytes 262176 | tf_op jit(solution)/shard_map/ppermute | solution.py:22
  74.6 7.1 %collective-permute-done.3.grad2 = bf16[256,1024]{1,0:T(8,128)(2,1)} collective-permute-done((bf16[256,1024]{1,0:T(8,128)(2,1)}, bf16[256,1024]{1,0:T(8,128)(2,1)}, u32[]{:S(2)}, u32[]{:S(2)}) %collective-permute-start.3) | collective-permute-done | bytes 524320 | tf_op jit(solution)/shard_map/ppermute | solution.py:22
  81.7 2.0 %collective-permute-done.2.grad1 = bf16[256,1024]{1,0:T(8,128)(2,1)} collective-permute-done((bf16[256,1024]{1,0:T(8,128)(2,1)}, bf16[256,1024]{1,0:T(8,128)(2,1)}, u32[]{:S(2)}, u32[]{:S(2)}) %collective-permute-start.2) | collective-permute-done | bytes 524320 | tf_op jit(solution)/shard_map/ppermute | solution.py:22
  83.6 13.9 %all-to-all-done.1.recv = bf16[16,128,512]{2,1,0:T(8,128)(2,1)S(1)} async-done(((bf16[16,128,512]{2,1,0:T(8,128)(2,1)}), bf16[16,128,512]{2,1,0:T(8,128)(2,1)S(1)}, u32[]{:S(2)}, u32[]{:S(2)}) %all-to-all-start.1) | async-done | bytes 2097184 | tf_op jit(solution)/shard_map/all_to_all | solution.py:26
  97.6 2.3 %all-gather.2.cloned.1.call-done.weight_hbm = bf16[16,512,256]{2,1,0:T(8,128)(2,1)} async-done(((bf16[1,512,256]{2,1,0:T(8,128)(2,1)}), bf16[16,512,256]{2,1,0:T(8,128)(2,1)}) %all-gather.2.cloned.1.call-update) | async-done | bytes 4194320 | tf_op jit(solution)/shard_map/all_gather | solution.py:327
  99.9 7.8 %layer.1 = (bf16[256,512]{1,0:T(8,128)(2,1)}, bf16[2,128,512]{2,1,0:T(8,128)(2,1)}, bf16[2,8,64,512]{3,2,1,0:T(8,128)(2,1)}, bf16[16,128,512]{2,1,0:T(8,128)(2,1)}) custom-call(s32[2]{0:T(128)S(1)} %copy-done.2, s32[2,4]{1,0:T(2,128)S(1)} %and_select_fusion.holder, s32[1]{0:T(128)} %bitcast.spot, bf16[2,128,512]{2,1,0:T(8,128)(2,1)S(1)} %bitcast.17, ...), custom_call_target="tpu_custom_call" | custom-call | flops 5368709120 | bytes 16777216 | tf_op jit(solution)/shard_map/layer/pallas_call | solution.py:190
  107.8 4.5 %all-to-all-start.2 = ((bf16[16,128,512]{2,1,0:T(8,128)(2,1)}), bf16[16,128,512]{2,1,0:T(8,128)(2,1)S(1)}, u32[]{:S(2)}, u32[]{:S(2)}) async-start(bf16[16,128,512]{2,1,0:T(8,128)(2,1)} %get-tuple-element.21), calls=%async_computation.2 | async-start | bytes 4194304 | tf_op jit(solution)/shard_map/all_to_all | solution.py:26
  112.2 3.7 %projection.1 = (bf16[256,1024]{1,0:T(8,128)(2,1)S(1)}, bf16[256,1024]{1,0:T(8,128)(2,1)S(1)}, bf16[256,1024]{1,0:T(8,128)(2,1)S(1)}, bf16[256,1024]{1,0:T(8,128)(2,1)S(1)}) custom-call(s32[1]{0:T(128)} %bitcast.spot, bf16[16,512,256]{2,1,0:T(8,128)(2,1)} %all-gather.2.cloned.1.call-done.weight_hbm, bf16[256,512]{1,0:T(8,128)(2,1)} %get-tuple-element.14.attended_hbm), custom_call_target="tpu_custom_call" | custom-call | flops 2147483648 | bytes 8388608 | tf_op jit(solution)/shard_map/projection/pallas_call | solution.py:242
  115.9 3.0 %collective-permute-start.5 = (bf16[256,1024]{1,0:T(8,128)(2,1)S(1)}, bf16[256,1024]{1,0:T(8,128)(2,1)S(1)}, u32[]{:S(2)}, u32[]{:S(2)}) collective-permute-start(bf16[256,1024]{1,0:T(8,128)(2,1)S(1)} %get-tuple-element.16), channel_id=1, source_target_pairs={{0,1},{1,2},{2,3},{3,0},{4,5},{5,6},{6,7},{7,4},{8,9},{9,10},{10,1... | collective-permute-start | bytes 1572872 | tf_op jit(solution)/shard_map/ppermute | solution.py:22
  118.9 4.3 %collective-permute-start.6 = (bf16[256,1024]{1,0:T(8,128)(2,1)S(1)}, bf16[256,1024]{1,0:T(8,128)(2,1)S(1)}, u32[]{:S(2)}, u32[]{:S(2)}) collective-permute-start(bf16[256,1024]{1,0:T(8,128)(2,1)S(1)} %get-tuple-element.17), channel_id=1, source_target_pairs={{0,2},{1,3},{2,0},{3,1},{4,6},{5,7},{6,4},{7,5},{8,10},{9,11},{10,... | collective-permute-start | bytes 1572872 | tf_op jit(solution)/shard_map/ppermute | solution.py:22
  123.2 3.1 %collective-permute-start.7 = (bf16[256,1024]{1,0:T(8,128)(2,1)S(1)}, bf16[256,1024]{1,0:T(8,128)(2,1)S(1)}, u32[]{:S(2)}, u32[]{:S(2)}) collective-permute-start(bf16[256,1024]{1,0:T(8,128)(2,1)S(1)} %get-tuple-element.18), channel_id=1, source_target_pairs={{0,3},{1,0},{2,1},{3,2},{4,7},{5,4},{6,5},{7,6},{8,11},{9,8},{10,9... | collective-permute-start | bytes 1572872 | tf_op jit(solution)/shard_map/ppermute | solution.py:22
  126.3 6.2 %collective-permute-done.5 = bf16[256,1024]{1,0:T(8,128)(2,1)S(1)} collective-permute-done((bf16[256,1024]{1,0:T(8,128)(2,1)S(1)}, bf16[256,1024]{1,0:T(8,128)(2,1)S(1)}, u32[]{:S(2)}, u32[]{:S(2)}) %collective-permute-start.5) | collective-permute-done | bytes 524320 | tf_op jit(solution)/shard_map/ppermute | solution.py:22
  132.5 12.0 %collective-permute-done.6 = bf16[256,1024]{1,0:T(8,128)(2,1)S(1)} collective-permute-done((bf16[256,1024]{1,0:T(8,128)(2,1)S(1)}, bf16[256,1024]{1,0:T(8,128)(2,1)S(1)}, u32[]{:S(2)}, u32[]{:S(2)}) %collective-permute-start.6) | collective-permute-done | bytes 524320 | tf_op jit(solution)/shard_map/ppermute | solution.py:22
  147.1 14.0 %all-to-all-done.2.back = bf16[16,128,512]{2,1,0:T(8,128)(2,1)S(1)} async-done(((bf16[16,128,512]{2,1,0:T(8,128)(2,1)}), bf16[16,128,512]{2,1,0:T(8,128)(2,1)S(1)}, u32[]{:S(2)}, u32[]{:S(2)}) %all-to-all-start.2) | async-done | bytes 2097184 | tf_op jit(solution)/shard_map/all_to_all | solution.py:26
  161.2 2.8 %combine.1 = (bf16[8,64,512]{2,1,0:T(8,128)(2,1)}, bf16[8,64,512]{2,1,0:T(8,128)(2,1)}) custom-call(s32[16,1]{1,0:T(8,128)S(1)} %bitcast.16, bf16[2,8,64,512]{3,2,1,0:T(8,128)(2,1)} %get-tuple-element.20.own_rows_hbm, bf16[16,128,512]{2,1,0:T(8,128)(2,1)S(1)} %all-to-all-done.2.back), custom_call_target="tpu_custom_call" | custom-call | bytes 4194304 | tf_op jit(solution)/shard_map/combine/pallas_call | solution.py:294
  (17 shorter events, 4.2 us)
Async XLA Ops:
  7.2 92.7 %all-gather.2.cloned.1.call-start = ((), (), s32[]{:S(2)}) async-start(), calls=%async_computation.3 | async-start | bytes 4456448 | tf_op jit(solution)/shard_map/all_gather | solution.py:327
  28.2 37.9 %copy-start.3 = (s32[2,4]{1,0:T(2,128)S(1)}, s32[2,4]{1,0:T(2,128)}, u32[]{:S(2)}) copy-start(s32[2,4]{1,0:T(2,128)} %param.13) | copy-start | bytes 100
  28.2 71.6 %copy-start = (bf16[1,8,64,512]{3,2,1,0:T(8,128)(2,1)S(1)}, bf16[1,8,64,512]{3,2,1,0:T(8,128)(2,1)}, u32[]{:S(2)}) copy-start(bf16[1,8,64,512]{3,2,1,0:T(8,128)(2,1)} %param.8) | copy-start | bytes 1572868
  28.3 71.6 %copy-start.1 = (bf16[1,8,64,512]{3,2,1,0:T(8,128)(2,1)S(1)}, bf16[1,8,64,512]{3,2,1,0:T(8,128)(2,1)}, u32[]{:S(2)}) copy-start(bf16[1,8,64,512]{3,2,1,0:T(8,128)(2,1)} %param.9) | copy-start | bytes 1572868
  28.3 71.6 %copy-start.2 = (s32[2]{0:T(128)S(1)}, s32[2]{0:T(128)}, u32[]{:S(2)}) copy-start(s32[2]{0:T(128)} %counts.1) | copy-start | bytes 28
  28.3 69.3 %all-to-all-start.1 = ((bf16[16,128,512]{2,1,0:T(8,128)(2,1)}), bf16[16,128,512]{2,1,0:T(8,128)(2,1)S(1)}, u32[]{:S(2)}, u32[]{:S(2)}) async-start(bf16[16,128,512]{2,1,0:T(8,128)(2,1)} %pick_blocks.1), calls=%async_computation.1 | async-start | bytes 4194304 | tf_op jit(solution)/shard_map/all_to_all | solution.py:26
  32.5 21.1 %collective-permute-start.1 = (bf16[1,2,128,1024]{3,2,1,0:T(8,128)(2,1)}, bf16[1,2,128,1024]{3,2,1,0:T(8,128)(2,1)}, u32[]{:S(2)}, u32[]{:S(2)}) collective-permute-start(bf16[1,2,128,1024]{3,2,1,0:T(8,128)(2,1)} %param.11), channel_id=1, source_target_pairs={{0,28},{4,0},{8,4},{12,8},{16,12},{20,16},{24,20},{28,24},{1,29},{... | collective-permute-start | bytes 1572872 | tf_op jit(solution)/shard_map/ppermute | solution.py:22
  53.7 20.9 %collective-permute-start.4 = (bf16[256,1024]{1,0:T(8,128)(2,1)}, bf16[256,1024]{1,0:T(8,128)(2,1)}, u32[]{:S(2)}, u32[]{:S(2)}) collective-permute-start(bf16[256,1024]{1,0:T(8,128)(2,1)} %bitcast.6.grad0), channel_id=1, source_target_pairs={{0,1},{1,2},{2,3},{3,0},{4,5},{5,6},{6,7},{7,4},{8,9},{9,10},{10,1... | collective-permute-start | bytes 1572872 | tf_op jit(solution)/shard_map/ppermute | solution.py:22
  56.8 24.9 %collective-permute-start.3 = (bf16[256,1024]{1,0:T(8,128)(2,1)}, bf16[256,1024]{1,0:T(8,128)(2,1)}, u32[]{:S(2)}, u32[]{:S(2)}) collective-permute-start(bf16[256,1024]{1,0:T(8,128)(2,1)} %bitcast.6.grad0), channel_id=1, source_target_pairs={{0,2},{1,3},{2,0},{3,1},{4,6},{5,7},{6,4},{7,5},{8,10},{9,11},{10,... | collective-permute-start | bytes 1572872 | tf_op jit(solution)/shard_map/ppermute | solution.py:22
  61.2 22.5 %collective-permute-start.2 = (bf16[256,1024]{1,0:T(8,128)(2,1)}, bf16[256,1024]{1,0:T(8,128)(2,1)}, u32[]{:S(2)}, u32[]{:S(2)}) collective-permute-start(bf16[256,1024]{1,0:T(8,128)(2,1)} %bitcast.6.grad0), channel_id=1, source_target_pairs={{0,3},{1,0},{2,1},{3,2},{4,7},{5,4},{6,5},{7,6},{8,11},{9,8},{10,9... | collective-permute-start | bytes 1572872 | tf_op jit(solution)/shard_map/ppermute | solution.py:22
  64.2 10.4 %collective-permute-start = (bf16[1,2,128,512]{3,2,1,0:T(8,128)(2,1)}, bf16[1,2,128,512]{3,2,1,0:T(8,128)(2,1)S(1)}, u32[]{:S(2)}, u32[]{:S(2)}) collective-permute-start(bf16[1,2,128,512]{3,2,1,0:T(8,128)(2,1)} %param.7), channel_id=1, source_target_pairs={{0,4},{4,8},{8,12},{12,16},{16,20},{20,24},{24,28},{28,0},{1,5},{5... | collective-permute-start | bytes 786440 | tf_op jit(solution)/shard_map/ppermute | solution.py:22
  107.8 53.4 %all-to-all-start.2 = ((bf16[16,128,512]{2,1,0:T(8,128)(2,1)}), bf16[16,128,512]{2,1,0:T(8,128)(2,1)S(1)}, u32[]{:S(2)}, u32[]{:S(2)}) async-start(bf16[16,128,512]{2,1,0:T(8,128)(2,1)} %get-tuple-element.21), calls=%async_computation.2 | async-start | bytes 4194304 | tf_op jit(solution)/shard_map/all_to_all | solution.py:26
  115.9 16.6 %collective-permute-start.5 = (bf16[256,1024]{1,0:T(8,128)(2,1)S(1)}, bf16[256,1024]{1,0:T(8,128)(2,1)S(1)}, u32[]{:S(2)}, u32[]{:S(2)}) collective-permute-start(bf16[256,1024]{1,0:T(8,128)(2,1)S(1)} %get-tuple-element.16), channel_id=1, source_target_pairs={{0,1},{1,2},{2,3},{3,0},{4,5},{5,6},{6,7},{7,4},{8,9},{9,10},{10,1... | collective-permute-start | bytes 1572872 | tf_op jit(solution)/shard_map/ppermute | solution.py:22
  118.9 25.6 %collective-permute-start.6 = (bf16[256,1024]{1,0:T(8,128)(2,1)S(1)}, bf16[256,1024]{1,0:T(8,128)(2,1)S(1)}, u32[]{:S(2)}, u32[]{:S(2)}) collective-permute-start(bf16[256,1024]{1,0:T(8,128)(2,1)S(1)} %get-tuple-element.17), channel_id=1, source_target_pairs={{0,2},{1,3},{2,0},{3,1},{4,6},{5,7},{6,4},{7,5},{8,10},{9,11},{10,... | collective-permute-start | bytes 1572872 | tf_op jit(solution)/shard_map/ppermute | solution.py:22
  123.2 22.7 %collective-permute-start.7 = (bf16[256,1024]{1,0:T(8,128)(2,1)S(1)}, bf16[256,1024]{1,0:T(8,128)(2,1)S(1)}, u32[]{:S(2)}, u32[]{:S(2)}) collective-permute-start(bf16[256,1024]{1,0:T(8,128)(2,1)S(1)} %get-tuple-element.18), channel_id=1, source_target_pairs={{0,3},{1,0},{2,1},{3,2},{4,7},{5,4},{6,5},{7,6},{8,11},{9,8},{10,9... | collective-permute-start | bytes 1572872 | tf_op jit(solution)/shard_map/ppermute | solution.py:22
Sparse Core Ops, SparseCore 0:
  10.1 89.7 all-gather.1

commit v12 on v11

--- a/solution.py
+++ b/solution.py
@@ -34,29 +34,18 @@
     return pl.CostEstimate(flops=int(flops), bytes_accessed=int(nbytes), transcendentals=0)
 
 
-def pick_kernel(asked, keys_hbm, values_hbm, slots, keys, values, in_sem, out_sem):
-    rows = keys.shape[1]
-    in_key = pltpu.make_async_copy(keys_hbm, keys, in_sem.at[0])
-    in_value = pltpu.make_async_copy(values_hbm, values, in_sem.at[1])
-    in_key.start()
-    in_value.start()
-
-    def sent(slot, which, source):
-        target = slots.at[slot, pl.ds(which * rows, rows)]
-        return pltpu.make_async_copy(source.at[jnp.maximum(asked[slot, 0], 0)], target, out_sem.at[slot, which])
-
-    for which, (arriving, source) in enumerate(((in_key, keys), (in_value, values))):
-        arriving.wait()
-
-        @pl.loop(0, slots.shape[0])
-        def _(slot, which=which, source=source):
-            copy = sent(slot, which, source)
-            pl.when(asked[slot, 0] >= 0)(copy.start)
-
-    @pl.loop(0, slots.shape[0])
-    def _(slot):
-        for which, source in enumerate((keys, values)):
-            pl.when(asked[slot, 0] >= 0)(sent(slot, which, source).wait)
+def pick_kernel(asked, keys_hbm, values_hbm, slots, sem):
+    rows = keys_hbm.shape[1]
+    copies = []
+    for slot in range(slots.shape[0]):
+        spot = asked[slot, 0]
+        for which, source in enumerate((keys_hbm, values_hbm)):
+            target = slots.at[slot, pl.ds(which * rows, rows)]
+            copy = pltpu.make_async_copy(source.at[jnp.maximum(spot, 0)], target, sem.at[slot, which])
+            pl.when(spot >= 0)(copy.start)
+            copies.append((spot, copy))
+    for spot, copy in copies:
+        pl.when(spot >= 0)(copy.wait)
 
 
 def picked_slots(asked, keys, values):
@@ -64,17 +53,12 @@
     _, rows, features = keys.shape
     return pl.pallas_call(
         pick_kernel,
-        out_shape=pltpu.HBM((slot_count, 2 * rows, features), BF16),
+        out_shape=pltpu.VMEM((slot_count, 2 * rows, features), BF16),
         in_specs=[SMEM, HBM, HBM],
-        out_specs=HBM,
-        scratch_shapes=[
-            pltpu.VMEM(keys.shape, BF16),
-            pltpu.VMEM(values.shape, BF16),
-            pltpu.SemaphoreType.DMA((2,)),
-            pltpu.SemaphoreType.DMA((slot_count, 2)),
-        ],
+        out_specs=VMEM,
+        scratch_shapes=[pltpu.SemaphoreType.DMA((slot_count, 2))],
         compiler_params=PARAMS,
-        cost_estimate=cost(0, 4 * 2**20),
+        cost_estimate=cost(0, 2 * 2**20),
         name="pick_blocks",
     )(asked, in_hbm(keys), in_hbm(values))
 
@@ -256,11 +240,8 @@
     )(spot, in_hbm(weight), in_hbm(attended))
 
 
-def combine_kernel(asked, own_rows_hbm, back, key_grads_hbm, value_grads_hbm, own_rows, total, grads, in_sem, out_sem):
+def combine_kernel(asked, own_rows, back, key_grads_hbm, value_grads_hbm, total, grads, out_sem):
     rows = own_rows.shape[2]
-    arriving = [pltpu.make_async_copy(own_rows_hbm.at[i], own_rows.at[i], in_sem.at[i]) for i in range(2)]
-    for copy in arriving:
-        copy.start()
 
     @pl.loop(0, total.shape[1])
     def _(block):
@@ -277,7 +258,6 @@
 
     outgoing = []
     for i, target in enumerate((key_grads_hbm, value_grads_hbm)):
-        arriving[i].wait()
 
         @pl.loop(0, total.shape[1])
         def _(block, i=i):
@@ -294,19 +274,17 @@
     return pl.pallas_call(
         combine_kernel,
         out_shape=[shape, shape],
-        in_specs=[SMEM, HBM, VMEM],
+        in_specs=[SMEM, VMEM, VMEM],
         out_specs=[HBM, HBM],
         scratch_shapes=[
-            pltpu.VMEM(own_rows.shape, BF16),
             pltpu.VMEM(own_rows.shape, F32),
             pltpu.VMEM(own_rows.shape, BF16),
-            pltpu.SemaphoreType.DMA((2,)),
             pltpu.SemaphoreType.DMA((2,)),
         ],
         compiler_params=PARAMS,
         cost_estimate=cost(0, 4 * 2**20),
         name="combine",
-    )(asked, in_hbm(own_rows), back)
+    )(asked, own_rows, back)
 
 
 def on_device(sent_queries, mem_keys, mem_values, out_weight, sent_grads, counts, neg_ids):

time: 171 us -> 171 us (level)
  no operation moved by 1% of the time
where the time goes in v12:
time: 171 us
  waiting for transfers between devices  79.5 us (46%)
  starting transfers between devices  40.9 us (24%)
  Pallas kernels  17.7 us (10%)
  blocking collectives  16.3 us (10%)
  between operations  14.2 us (8%)
  other arithmetic  1.94 us (1%)
    ppermute x8, waiting for transfers between devices, passed_along(): lax.ppermute(block, axis, [(i, (i + distance) % count) for i in range(cou...  48.7 us
    ppermute x8, starting transfers between devices, passed_along(): lax.ppermute(block, axis, [(i, (i + distance) % count) for i in range(cou...  32.5 us
    all_to_all x2, waiting for transfers between devices, exchanged(): return lax.all_to_all(slots, 'dp', split_axis=0, concat_axis=0, tiled=True)  28.1 us
    all_to_all x1, blocking collectives, exchanged(): return lax.all_to_all(slots, 'dp', split_axis=0, concat_axis=0, tiled=True)  16.3 us
    all_to_all x2, starting transfers between devices, exchanged(): return lax.all_to_all(slots, 'dp', split_axis=0, concat_axis=0, tiled=True)  8.36 us
    pallas_call x1, Pallas kernels, layer(): pl.pallas_call(layer_kernel, out_shape=[pltpu.HBM((rows, features), BF16)...  7.85 us
    pallas_call x1, Pallas kernels, picked_slots(): pl.pallas_call(pick_kernel, out_shape=pltpu.VMEM((slot_count, 2 * rows, f...  3.74 us
    pallas_call x1, Pallas kernels, projected(): pl.pallas_call(project_kernel, out_shape=[shape] * groups, in_specs=[SMEM...  3.7 us
  transfers between devices with their start and end apart: 11, of which 10 were waited for; matrix products, arithmetic and copies ran while one was open for 1% of the time, Pallas kernels for 4%

profile of v12, /device:TPU:1, one launch (start us, length us, event | category | flops | bytes accessed | tf_op | source)
XLA Modules:
  0.0 170.7 jit_solution(7709137649213124167)
XLA Ops:
  8.8 16.3 %all_to_all.21 = s32[16,1,1]{2,1,0:T(1,128)S(1)} all-to-all(s32[16,1,1]{2,1,0:T(1,128)S(1)} %copy.19), channel_id=1, replica_groups=mesh['dp'=16,'section'=8,'tensor'=4] {'dp'}, dimensions={0} | all-to-all | bytes 128 | tf_op jit(solution)/shard_map/all_to_all | solution.py:26
  25.1 3.7 %pick_blocks.1 = bf16[16,128,512]{2,1,0:T(8,128)(2,1)} custom-call(s32[16,1]{1,0:T(8,128)S(1)} %bitcast.15, bf16[8,64,512]{2,1,0:T(8,128)(2,1)} %bitcast.11, bf16[8,64,512]{2,1,0:T(8,128)(2,1)} %bitcast.13), custom_call_target="tpu_custom_call" | custom-call | bytes 2097152 | tf_op jit(solution)/shard_map/pick_blocks/pallas_call | solution.py:54
  28.9 4.0 %all-to-all-start.1 = ((bf16[16,128,512]{2,1,0:T(8,128)(2,1)}), bf16[16,128,512]{2,1,0:T(8,128)(2,1)S(1)}, u32[]{:S(2)}, u32[]{:S(2)}) async-start(bf16[16,128,512]{2,1,0:T(8,128)(2,1)} %pick_blocks.1), calls=%async_computation.1 | async-start | bytes 4194304 | tf_op jit(solution)/shard_map/all_to_all | solution.py:26
  32.8 9.8 %collective-permute-start.1 = (bf16[1,2,128,1024]{3,2,1,0:T(8,128)(2,1)}, bf16[1,2,128,1024]{3,2,1,0:T(8,128)(2,1)}, u32[]{:S(2)}, u32[]{:S(2)}) collective-permute-start(bf16[1,2,128,1024]{3,2,1,0:T(8,128)(2,1)} %param.11), channel_id=1, source_target_pairs={{0,28},{4,0},{8,4},{12,8},{16,12},{20,16},{24,20},{28,24},{1,29},{... | collective-permute-start | bytes 1572872 | tf_op jit(solution)/shard_map/ppermute | solution.py:22
  42.6 11.4 %collective-permute-done.1 = bf16[1,2,128,1024]{3,2,1,0:T(8,128)(2,1)} collective-permute-done((bf16[1,2,128,1024]{3,2,1,0:T(8,128)(2,1)}, bf16[1,2,128,1024]{3,2,1,0:T(8,128)(2,1)}, u32[]{:S(2)}, u32[]{:S(2)}) %collective-permute-start.1) | collective-permute-done | bytes 524320 | tf_op jit(solution)/shard_map/ppermute | solution.py:22
  54.0 3.1 %collective-permute-start.4 = (bf16[256,1024]{1,0:T(8,128)(2,1)}, bf16[256,1024]{1,0:T(8,128)(2,1)}, u32[]{:S(2)}, u32[]{:S(2)}) collective-permute-start(bf16[256,1024]{1,0:T(8,128)(2,1)} %bitcast.6.grad0), channel_id=1, source_target_pairs={{0,1},{1,2},{2,3},{3,0},{4,5},{5,6},{6,7},{7,4},{8,9},{9,10},{10,1... | collective-permute-start | bytes 1572872 | tf_op jit(solution)/shard_map/ppermute | solution.py:22
  57.1 4.4 %collective-permute-start.3 = (bf16[256,1024]{1,0:T(8,128)(2,1)}, bf16[256,1024]{1,0:T(8,128)(2,1)}, u32[]{:S(2)}, u32[]{:S(2)}) collective-permute-start(bf16[256,1024]{1,0:T(8,128)(2,1)} %bitcast.6.grad0), channel_id=1, source_target_pairs={{0,2},{1,3},{2,0},{3,1},{4,6},{5,7},{6,4},{7,5},{8,10},{9,11},{10,... | collective-permute-start | bytes 1572872 | tf_op jit(solution)/shard_map/ppermute | solution.py:22
  61.5 3.1 %collective-permute-start.2 = (bf16[256,1024]{1,0:T(8,128)(2,1)}, bf16[256,1024]{1,0:T(8,128)(2,1)}, u32[]{:S(2)}, u32[]{:S(2)}) collective-permute-start(bf16[256,1024]{1,0:T(8,128)(2,1)} %bitcast.6.grad0), channel_id=1, source_target_pairs={{0,3},{1,0},{2,1},{3,2},{4,7},{5,4},{6,5},{7,6},{8,11},{9,8},{10,9... | collective-permute-start | bytes 1572872 | tf_op jit(solution)/shard_map/ppermute | solution.py:22
  64.5 1.9 %collective-permute-start = (bf16[1,2,128,512]{3,2,1,0:T(8,128)(2,1)}, bf16[1,2,128,512]{3,2,1,0:T(8,128)(2,1)S(1)}, u32[]{:S(2)}, u32[]{:S(2)}) collective-permute-start(bf16[1,2,128,512]{3,2,1,0:T(8,128)(2,1)} %param.7), channel_id=1, source_target_pairs={{0,4},{4,8},{8,12},{12,16},{16,20},{20,24},{24,28},{28,0},{1,5},{5... | collective-permute-start | bytes 786440 | tf_op jit(solution)/shard_map/ppermute | solution.py:22
  66.5 8.4 %collective-permute-done = bf16[1,2,128,512]{3,2,1,0:T(8,128)(2,1)S(1)} collective-permute-done((bf16[1,2,128,512]{3,2,1,0:T(8,128)(2,1)}, bf16[1,2,128,512]{3,2,1,0:T(8,128)(2,1)S(1)}, u32[]{:S(2)}, u32[]{:S(2)}) %collective-permute-start) | collective-permute-done | bytes 262176 | tf_op jit(solution)/shard_map/ppermute | solution.py:22
  74.9 7.1 %collective-permute-done.3.grad2 = bf16[256,1024]{1,0:T(8,128)(2,1)} collective-permute-done((bf16[256,1024]{1,0:T(8,128)(2,1)}, bf16[256,1024]{1,0:T(8,128)(2,1)}, u32[]{:S(2)}, u32[]{:S(2)}) %collective-permute-start.3) | collective-permute-done | bytes 524320 | tf_op jit(solution)/shard_map/ppermute | solution.py:22
  82.0 2.0 %collective-permute-done.2.grad1 = bf16[256,1024]{1,0:T(8,128)(2,1)} collective-permute-done((bf16[256,1024]{1,0:T(8,128)(2,1)}, bf16[256,1024]{1,0:T(8,128)(2,1)}, u32[]{:S(2)}, u32[]{:S(2)}) %collective-permute-start.2) | collective-permute-done | bytes 524320 | tf_op jit(solution)/shard_map/ppermute | solution.py:22
  83.9 14.2 %all-to-all-done.1.recv = bf16[16,128,512]{2,1,0:T(8,128)(2,1)S(1)} async-done(((bf16[16,128,512]{2,1,0:T(8,128)(2,1)}), bf16[16,128,512]{2,1,0:T(8,128)(2,1)S(1)}, u32[]{:S(2)}, u32[]{:S(2)}) %all-to-all-start.1) | async-done | bytes 2097184 | tf_op jit(solution)/shard_map/all_to_all | solution.py:26
  98.1 2.0 %all-gather.2.cloned.1.call-done.weight_hbm = bf16[16,512,256]{2,1,0:T(8,128)(2,1)} async-done(((bf16[1,512,256]{2,1,0:T(8,128)(2,1)}), bf16[16,512,256]{2,1,0:T(8,128)(2,1)}) %all-gather.2.cloned.1.call-update) | async-done | bytes 4194320 | tf_op jit(solution)/shard_map/all_gather | solution.py:305
  100.2 7.8 %layer.1 = (bf16[256,512]{1,0:T(8,128)(2,1)}, bf16[2,128,512]{2,1,0:T(8,128)(2,1)}, bf16[2,8,64,512]{3,2,1,0:T(8,128)(2,1)}, bf16[16,128,512]{2,1,0:T(8,128)(2,1)}) custom-call(s32[2]{0:T(128)S(1)} %copy-done.3, s32[2,4]{1,0:T(2,128)S(1)} %and_select_fusion.holder, s32[1]{0:T(128)} %bitcast.spot, bf16[2,128,512]{2,1,0:T(8,128)(2,1)S(1)} %bitcast.17, ...), custom_call_target="tpu_custom_call" | custom-call | flops 5368709120 | bytes 16777216 | tf_op jit(solution)/shard_map/layer/pallas_call | solution.py:174
  108.0 4.4 %all-to-all-start.2 = ((bf16[16,128,512]{2,1,0:T(8,128)(2,1)}), bf16[16,128,512]{2,1,0:T(8,128)(2,1)S(1)}, u32[]{:S(2)}, u32[]{:S(2)}) async-start(bf16[16,128,512]{2,1,0:T(8,128)(2,1)} %get-tuple-element.21), calls=%async_computation.2 | async-start | bytes 4194304 | tf_op jit(solution)/shard_map/all_to_all | solution.py:26
  112.4 3.7 %projection.1 = (bf16[256,1024]{1,0:T(8,128)(2,1)S(1)}, bf16[256,1024]{1,0:T(8,128)(2,1)S(1)}, bf16[256,1024]{1,0:T(8,128)(2,1)S(1)}, bf16[256,1024]{1,0:T(8,128)(2,1)S(1)}) custom-call(s32[1]{0:T(128)} %bitcast.spot, bf16[16,512,256]{2,1,0:T(8,128)(2,1)} %all-gather.2.cloned.1.call-done.weight_hbm, bf16[256,512]{1,0:T(8,128)(2,1)} %get-tuple-element.14.attended_hbm), custom_call_target="tpu_custom_call" | custom-call | flops 2147483648 | bytes 8388608 | tf_op jit(solution)/shard_map/projection/pallas_call | solution.py:226
  116.2 2.9 %collective-permute-start.5 = (bf16[256,1024]{1,0:T(8,128)(2,1)S(1)}, bf16[256,1024]{1,0:T(8,128)(2,1)S(1)}, u32[]{:S(2)}, u32[]{:S(2)}) collective-permute-start(bf16[256,1024]{1,0:T(8,128)(2,1)S(1)} %get-tuple-element.16), channel_id=1, source_target_pairs={{0,1},{1,2},{2,3},{3,0},{4,5},{5,6},{6,7},{7,4},{8,9},{9,10},{10,1... | collective-permute-start | bytes 1572872 | tf_op jit(solution)/shard_map/ppermute | solution.py:22
  119.1 4.3 %collective-permute-start.6 = (bf16[256,1024]{1,0:T(8,128)(2,1)S(1)}, bf16[256,1024]{1,0:T(8,128)(2,1)S(1)}, u32[]{:S(2)}, u32[]{:S(2)}) collective-permute-start(bf16[256,1024]{1,0:T(8,128)(2,1)S(1)} %get-tuple-element.17), channel_id=1, source_target_pairs={{0,2},{1,3},{2,0},{3,1},{4,6},{5,7},{6,4},{7,5},{8,10},{9,11},{10,... | collective-permute-start | bytes 1572872 | tf_op jit(solution)/shard_map/ppermute | solution.py:22
  123.4 3.1 %collective-permute-start.7 = (bf16[256,1024]{1,0:T(8,128)(2,1)S(1)}, bf16[256,1024]{1,0:T(8,128)(2,1)S(1)}, u32[]{:S(2)}, u32[]{:S(2)}) collective-permute-start(bf16[256,1024]{1,0:T(8,128)(2,1)S(1)} %get-tuple-element.18), channel_id=1, source_target_pairs={{0,3},{1,0},{2,1},{3,2},{4,7},{5,4},{6,5},{7,6},{8,11},{9,8},{10,9... | collective-permute-start | bytes 1572872 | tf_op jit(solution)/shard_map/ppermute | solution.py:22
  126.5 6.4 %collective-permute-done.5 = bf16[256,1024]{1,0:T(8,128)(2,1)S(1)} collective-permute-done((bf16[256,1024]{1,0:T(8,128)(2,1)S(1)}, bf16[256,1024]{1,0:T(8,128)(2,1)S(1)}, u32[]{:S(2)}, u32[]{:S(2)}) %collective-permute-start.5) | collective-permute-done | bytes 524320 | tf_op jit(solution)/shard_map/ppermute | solution.py:22
  132.9 11.8 %collective-permute-done.6 = bf16[256,1024]{1,0:T(8,128)(2,1)S(1)} collective-permute-done((bf16[256,1024]{1,0:T(8,128)(2,1)S(1)}, bf16[256,1024]{1,0:T(8,128)(2,1)S(1)}, u32[]{:S(2)}, u32[]{:S(2)}) %collective-permute-start.6) | collective-permute-done | bytes 524320 | tf_op jit(solution)/shard_map/ppermute | solution.py:22
  147.5 13.9 %all-to-all-done.2.back = bf16[16,128,512]{2,1,0:T(8,128)(2,1)S(1)} async-done(((bf16[16,128,512]{2,1,0:T(8,128)(2,1)}), bf16[16,128,512]{2,1,0:T(8,128)(2,1)S(1)}, u32[]{:S(2)}, u32[]{:S(2)}) %all-to-all-start.2) | async-done | bytes 2097184 | tf_op jit(solution)/shard_map/all_to_all | solution.py:26
  161.4 2.4 %combine.1 = (bf16[8,64,512]{2,1,0:T(8,128)(2,1)}, bf16[8,64,512]{2,1,0:T(8,128)(2,1)}) custom-call(s32[16,1]{1,0:T(8,128)S(1)} %bitcast.16, bf16[2,8,64,512]{3,2,1,0:T(8,128)(2,1)S(1)} %copy-done, bf16[16,128,512]{2,1,0:T(8,128)(2,1)S(1)} %all-to-all-done.2.back), custom_call_target="tpu_custom_call" | custom-call | bytes 4194304 | tf_op jit(solution)/shard_map/combine/pallas_call | solution.py:274
  (19 shorter events, 4.4 us)
Async XLA Ops:
  7.2 93.0 %all-gather.2.cloned.1.call-start = ((), (), s32[]{:S(2)}) async-start(), calls=%async_computation.3 | async-start | bytes 4456448 | tf_op jit(solution)/shard_map/all_gather | solution.py:305
  28.8 37.6 %copy-start.4 = (s32[2,4]{1,0:T(2,128)S(1)}, s32[2,4]{1,0:T(2,128)}, u32[]{:S(2)}) copy-start(s32[2,4]{1,0:T(2,128)} %param.13) | copy-start | bytes 100
  28.8 71.3 %copy-start.1 = (bf16[1,8,64,512]{3,2,1,0:T(8,128)(2,1)S(1)}, bf16[1,8,64,512]{3,2,1,0:T(8,128)(2,1)}, u32[]{:S(2)}) copy-start(bf16[1,8,64,512]{3,2,1,0:T(8,128)(2,1)} %param.8) | copy-start | bytes 1572868
  28.8 71.3 %copy-start.2 = (bf16[1,8,64,512]{3,2,1,0:T(8,128)(2,1)S(1)}, bf16[1,8,64,512]{3,2,1,0:T(8,128)(2,1)}, u32[]{:S(2)}) copy-start(bf16[1,8,64,512]{3,2,1,0:T(8,128)(2,1)} %param.9) | copy-start | bytes 1572868
  28.9 71.3 %copy-start.3 = (s32[2]{0:T(128)S(1)}, s32[2]{0:T(128)}, u32[]{:S(2)}) copy-start(s32[2]{0:T(128)} %counts.1) | copy-start | bytes 28
  28.9 69.3 %all-to-all-start.1 = ((bf16[16,128,512]{2,1,0:T(8,128)(2,1)}), bf16[16,128,512]{2,1,0:T(8,128)(2,1)S(1)}, u32[]{:S(2)}, u32[]{:S(2)}) async-start(bf16[16,128,512]{2,1,0:T(8,128)(2,1)} %pick_blocks.1), calls=%async_computation.1 | async-start | bytes 4194304 | tf_op jit(solution)/shard_map/all_to_all | solution.py:26
  32.8 21.1 %collective-permute-start.1 = (bf16[1,2,128,1024]{3,2,1,0:T(8,128)(2,1)}, bf16[1,2,128,1024]{3,2,1,0:T(8,128)(2,1)}, u32[]{:S(2)}, u32[]{:S(2)}) collective-permute-start(bf16[1,2,128,1024]{3,2,1,0:T(8,128)(2,1)} %param.11), channel_id=1, source_target_pairs={{0,28},{4,0},{8,4},{12,8},{16,12},{20,16},{24,20},{28,24},{1,29},{... | collective-permute-start | bytes 1572872 | tf_op jit(solution)/shard_map/ppermute | solution.py:22
  54.0 20.9 %collective-permute-start.4 = (bf16[256,1024]{1,0:T(8,128)(2,1)}, bf16[256,1024]{1,0:T(8,128)(2,1)}, u32[]{:S(2)}, u32[]{:S(2)}) collective-permute-start(bf16[256,1024]{1,0:T(8,128)(2,1)} %bitcast.6.grad0), channel_id=1, source_target_pairs={{0,1},{1,2},{2,3},{3,0},{4,5},{5,6},{6,7},{7,4},{8,9},{9,10},{10,1... | collective-permute-start | bytes 1572872 | tf_op jit(solution)/shard_map/ppermute | solution.py:22
  57.1 24.9 %collective-permute-start.3 = (bf16[256,1024]{1,0:T(8,128)(2,1)}, bf16[256,1024]{1,0:T(8,128)(2,1)}, u32[]{:S(2)}, u32[]{:S(2)}) collective-permute-start(bf16[256,1024]{1,0:T(8,128)(2,1)} %bitcast.6.grad0), channel_id=1, source_target_pairs={{0,2},{1,3},{2,0},{3,1},{4,6},{5,7},{6,4},{7,5},{8,10},{9,11},{10,... | collective-permute-start | bytes 1572872 | tf_op jit(solution)/shard_map/ppermute | solution.py:22
  61.5 22.5 %collective-permute-start.2 = (bf16[256,1024]{1,0:T(8,128)(2,1)}, bf16[256,1024]{1,0:T(8,128)(2,1)}, u32[]{:S(2)}, u32[]{:S(2)}) collective-permute-start(bf16[256,1024]{1,0:T(8,128)(2,1)} %bitcast.6.grad0), channel_id=1, source_target_pairs={{0,3},{1,0},{2,1},{3,2},{4,7},{5,4},{6,5},{7,6},{8,11},{9,8},{10,9... | collective-permute-start | bytes 1572872 | tf_op jit(solution)/shard_map/ppermute | solution.py:22
  64.5 10.4 %collective-permute-start = (bf16[1,2,128,512]{3,2,1,0:T(8,128)(2,1)}, bf16[1,2,128,512]{3,2,1,0:T(8,128)(2,1)S(1)}, u32[]{:S(2)}, u32[]{:S(2)}) collective-permute-start(bf16[1,2,128,512]{3,2,1,0:T(8,128)(2,1)} %param.7), channel_id=1, source_target_pairs={{0,4},{4,8},{8,12},{12,16},{16,20},{20,24},{24,28},{28,0},{1,5},{5... | collective-permute-start | bytes 786440 | tf_op jit(solution)/shard_map/ppermute | solution.py:22
  108.0 53.4 %all-to-all-start.2 = ((bf16[16,128,512]{2,1,0:T(8,128)(2,1)}), bf16[16,128,512]{2,1,0:T(8,128)(2,1)S(1)}, u32[]{:S(2)}, u32[]{:S(2)}) async-start(bf16[16,128,512]{2,1,0:T(8,128)(2,1)} %get-tuple-element.21), calls=%async_computation.2 | async-start | bytes 4194304 | tf_op jit(solution)/shard_map/all_to_all | solution.py:26
  116.2 45.2 %copy-start = (bf16[2,8,64,512]{3,2,1,0:T(8,128)(2,1)S(1)}, bf16[2,8,64,512]{3,2,1,0:T(8,128)(2,1)}, u32[]{:S(2)}) copy-start(bf16[2,8,64,512]{3,2,1,0:T(8,128)(2,1)} %get-tuple-element.20.own_rows) | copy-start | bytes 3145732
  116.2 16.7 %collective-permute-start.5 = (bf16[256,1024]{1,0:T(8,128)(2,1)S(1)}, bf16[256,1024]{1,0:T(8,128)(2,1)S(1)}, u32[]{:S(2)}, u32[]{:S(2)}) collective-permute-start(bf16[256,1024]{1,0:T(8,128)(2,1)S(1)} %get-tuple-element.16), channel_id=1, source_target_pairs={{0,1},{1,2},{2,3},{3,0},{4,5},{5,6},{6,7},{7,4},{8,9},{9,10},{10,1... | collective-permute-start | bytes 1572872 | tf_op jit(solution)/shard_map/ppermute | solution.py:22
  119.1 25.6 %collective-permute-start.6 = (bf16[256,1024]{1,0:T(8,128)(2,1)S(1)}, bf16[256,1024]{1,0:T(8,128)(2,1)S(1)}, u32[]{:S(2)}, u32[]{:S(2)}) collective-permute-start(bf16[256,1024]{1,0:T(8,128)(2,1)S(1)} %get-tuple-element.17), channel_id=1, source_target_pairs={{0,2},{1,3},{2,0},{3,1},{4,6},{5,7},{6,4},{7,5},{8,10},{9,11},{10,... | collective-permute-start | bytes 1572872 | tf_op jit(solution)/shard_map/ppermute | solution.py:22
  123.4 23.0 %collective-permute-start.7 = (bf16[256,1024]{1,0:T(8,128)(2,1)S(1)}, bf16[256,1024]{1,0:T(8,128)(2,1)S(1)}, u32[]{:S(2)}, u32[]{:S(2)}) collective-permute-start(bf16[256,1024]{1,0:T(8,128)(2,1)S(1)} %get-tuple-element.18), channel_id=1, source_target_pairs={{0,3},{1,0},{2,1},{3,2},{4,7},{5,4},{6,5},{7,6},{8,11},{9,8},{10,9... | collective-permute-start | bytes 1572872 | tf_op jit(solution)/shard_map/ppermute | solution.py:22
Sparse Core Ops, SparseCore 0:
  10.1 90.0 all-gather.1

commit v13 on v11

--- a/solution.py
+++ b/solution.py
@@ -256,11 +256,8 @@
     )(spot, in_hbm(weight), in_hbm(attended))
 
 
-def combine_kernel(asked, own_rows_hbm, back, key_grads_hbm, value_grads_hbm, own_rows, total, grads, in_sem, out_sem):
+def combine_kernel(asked, own_rows, back, key_grads_hbm, value_grads_hbm, total, grads, out_sem):
     rows = own_rows.shape[2]
-    arriving = [pltpu.make_async_copy(own_rows_hbm.at[i], own_rows.at[i], in_sem.at[i]) for i in range(2)]
-    for copy in arriving:
-        copy.start()
 
     @pl.loop(0, total.shape[1])
     def _(block):
@@ -277,7 +274,6 @@
 
     outgoing = []
     for i, target in enumerate((key_grads_hbm, value_grads_hbm)):
-        arriving[i].wait()
 
         @pl.loop(0, total.shape[1])
         def _(block, i=i):
@@ -294,19 +290,17 @@
     return pl.pallas_call(
         combine_kernel,
         out_shape=[shape, shape],
-        in_specs=[SMEM, HBM, VMEM],
+        in_specs=[SMEM, VMEM, VMEM],
         out_specs=[HBM, HBM],
         scratch_shapes=[
-            pltpu.VMEM(own_rows.shape, BF16),
             pltpu.VMEM(own_rows.shape, F32),
             pltpu.VMEM(own_rows.shape, BF16),
             pltpu.SemaphoreType.DMA((2,)),
-            pltpu.SemaphoreType.DMA((2,)),
         ],
         compiler_params=PARAMS,
         cost_estimate=cost(0, 4 * 2**20),
         name="combine",
-    )(asked, in_hbm(own_rows), back)
+    )(asked, own_rows, back)
 
 
 def on_device(sent_queries, mem_keys, mem_values, out_weight, sent_grads, counts, neg_ids):

time: 171 us -> 171 us (level)
  no operation moved by 1% of the time
where the time goes in v13:
time: 171 us; the launch traced here: 170 us
  waiting for transfers between devices  79.3 us (46%)
  starting transfers between devices  41.5 us (24%)
  Pallas kernels  17 us (10%)
  blocking collectives  16.3 us (10%)
  between operations  14.2 us (8%)
  other arithmetic  1.94 us (1%)
    ppermute x8, waiting for transfers between devices, passed_along(): lax.ppermute(block, axis, [(i, (i + distance) % count) for i in range(cou...  48.5 us
    ppermute x8, starting transfers between devices, passed_along(): lax.ppermute(block, axis, [(i, (i + distance) % count) for i in range(cou...  32.7 us
    all_to_all x2, waiting for transfers between devices, exchanged(): return lax.all_to_all(slots, 'dp', split_axis=0, concat_axis=0, tiled=True)  27.8 us
    all_to_all x1, blocking collectives, exchanged(): return lax.all_to_all(slots, 'dp', split_axis=0, concat_axis=0, tiled=True)  16.3 us
    all_to_all x2, starting transfers between devices, exchanged(): return lax.all_to_all(slots, 'dp', split_axis=0, concat_axis=0, tiled=True)  8.8 us
    pallas_call x1, Pallas kernels, layer(): pl.pallas_call(layer_kernel, out_shape=[pltpu.HBM((rows, features), BF16)...  7.85 us
    pallas_call x1, Pallas kernels, projected(): pl.pallas_call(project_kernel, out_shape=[shape] * groups, in_specs=[SMEM...  3.7 us
  transfers between devices with their start and end apart: 11, of which 10 were waited for; matrix products, arithmetic and copies ran while one was open for 1% of the time, Pallas kernels for 4%

profile of v13, /device:TPU:1, one launch (start us, length us, event | category | flops | bytes accessed | tf_op | source)
XLA Modules:
  0.0 170.4 jit_solution(10736239692720605746)
XLA Ops:
  8.8 16.3 %all_to_all.21 = s32[16,1,1]{2,1,0:T(1,128)S(1)} all-to-all(s32[16,1,1]{2,1,0:T(1,128)S(1)} %copy.19), channel_id=1, replica_groups=mesh['dp'=16,'section'=8,'tensor'=4] {'dp'}, dimensions={0} | all-to-all | bytes 128 | tf_op jit(solution)/shard_map/all_to_all | solution.py:26
  25.1 3.1 %pick_blocks.1 = bf16[16,128,512]{2,1,0:T(8,128)(2,1)} custom-call(s32[16,1]{1,0:T(8,128)S(1)} %bitcast.15, bf16[8,64,512]{2,1,0:T(8,128)(2,1)} %bitcast.11, bf16[8,64,512]{2,1,0:T(8,128)(2,1)} %bitcast.13), custom_call_target="tpu_custom_call" | custom-call | bytes 4194304 | tf_op jit(solution)/shard_map/pick_blocks/pallas_call | solution.py:65
  28.2 4.4 %all-to-all-start.1 = ((bf16[16,128,512]{2,1,0:T(8,128)(2,1)}), bf16[16,128,512]{2,1,0:T(8,128)(2,1)S(1)}, u32[]{:S(2)}, u32[]{:S(2)}) async-start(bf16[16,128,512]{2,1,0:T(8,128)(2,1)} %pick_blocks.1), calls=%async_computation.1 | async-start | bytes 4194304 | tf_op jit(solution)/shard_map/all_to_all | solution.py:26
  32.6 9.8 %collective-permute-start.1 = (bf16[1,2,128,1024]{3,2,1,0:T(8,128)(2,1)}, bf16[1,2,128,1024]{3,2,1,0:T(8,128)(2,1)}, u32[]{:S(2)}, u32[]{:S(2)}) collective-permute-start(bf16[1,2,128,1024]{3,2,1,0:T(8,128)(2,1)} %param.11), channel_id=1, source_target_pairs={{0,28},{4,0},{8,4},{12,8},{16,12},{20,16},{24,20},{28,24},{1,29},{... | collective-permute-start | bytes 1572872 | tf_op jit(solution)/shard_map/ppermute | solution.py:22
  42.4 11.4 %collective-permute-done.1 = bf16[1,2,128,1024]{3,2,1,0:T(8,128)(2,1)} collective-permute-done((bf16[1,2,128,1024]{3,2,1,0:T(8,128)(2,1)}, bf16[1,2,128,1024]{3,2,1,0:T(8,128)(2,1)}, u32[]{:S(2)}, u32[]{:S(2)}) %collective-permute-start.1) | collective-permute-done | bytes 524320 | tf_op jit(solution)/shard_map/ppermute | solution.py:22
  53.8 3.1 %collective-permute-start.4 = (bf16[256,1024]{1,0:T(8,128)(2,1)}, bf16[256,1024]{1,0:T(8,128)(2,1)}, u32[]{:S(2)}, u32[]{:S(2)}) collective-permute-start(bf16[256,1024]{1,0:T(8,128)(2,1)} %bitcast.6.grad0), channel_id=1, source_target_pairs={{0,1},{1,2},{2,3},{3,0},{4,5},{5,6},{6,7},{7,4},{8,9},{9,10},{10,1... | collective-permute-start | bytes 1572872 | tf_op jit(solution)/shard_map/ppermute | solution.py:22
  56.9 4.4 %collective-permute-start.3 = (bf16[256,1024]{1,0:T(8,128)(2,1)}, bf16[256,1024]{1,0:T(8,128)(2,1)}, u32[]{:S(2)}, u32[]{:S(2)}) collective-permute-start(bf16[256,1024]{1,0:T(8,128)(2,1)} %bitcast.6.grad0), channel_id=1, source_target_pairs={{0,2},{1,3},{2,0},{3,1},{4,6},{5,7},{6,4},{7,5},{8,10},{9,11},{10,... | collective-permute-start | bytes 1572872 | tf_op jit(solution)/shard_map/ppermute | solution.py:22
  61.3 3.1 %collective-permute-start.2 = (bf16[256,1024]{1,0:T(8,128)(2,1)}, bf16[256,1024]{1,0:T(8,128)(2,1)}, u32[]{:S(2)}, u32[]{:S(2)}) collective-permute-start(bf16[256,1024]{1,0:T(8,128)(2,1)} %bitcast.6.grad0), channel_id=1, source_target_pairs={{0,3},{1,0},{2,1},{3,2},{4,7},{5,4},{6,5},{7,6},{8,11},{9,8},{10,9... | collective-permute-start | bytes 1572872 | tf_op jit(solution)/shard_map/ppermute | solution.py:22
  64.3 1.9 %collective-permute-start = (bf16[1,2,128,512]{3,2,1,0:T(8,128)(2,1)}, bf16[1,2,128,512]{3,2,1,0:T(8,128)(2,1)S(1)}, u32[]{:S(2)}, u32[]{:S(2)}) collective-permute-start(bf16[1,2,128,512]{3,2,1,0:T(8,128)(2,1)} %param.7), channel_id=1, source_target_pairs={{0,4},{4,8},{8,12},{12,16},{16,20},{20,24},{24,28},{28,0},{1,5},{5... | collective-permute-start | bytes 786440 | tf_op jit(solution)/shard_map/ppermute | solution.py:22
  66.3 8.4 %collective-permute-done = bf16[1,2,128,512]{3,2,1,0:T(8,128)(2,1)S(1)} collective-permute-done((bf16[1,2,128,512]{3,2,1,0:T(8,128)(2,1)}, bf16[1,2,128,512]{3,2,1,0:T(8,128)(2,1)S(1)}, u32[]{:S(2)}, u32[]{:S(2)}) %collective-permute-start) | collective-permute-done | bytes 262176 | tf_op jit(solution)/shard_map/ppermute | solution.py:22
  74.7 7.1 %collective-permute-done.3.grad2 = bf16[256,1024]{1,0:T(8,128)(2,1)} collective-permute-done((bf16[256,1024]{1,0:T(8,128)(2,1)}, bf16[256,1024]{1,0:T(8,128)(2,1)}, u32[]{:S(2)}, u32[]{:S(2)}) %collective-permute-start.3) | collective-permute-done | bytes 524320 | tf_op jit(solution)/shard_map/ppermute | solution.py:22
  81.8 2.0 %collective-permute-done.2.grad1 = bf16[256,1024]{1,0:T(8,128)(2,1)} collective-permute-done((bf16[256,1024]{1,0:T(8,128)(2,1)}, bf16[256,1024]{1,0:T(8,128)(2,1)}, u32[]{:S(2)}, u32[]{:S(2)}) %collective-permute-start.2) | collective-permute-done | bytes 524320 | tf_op jit(solution)/shard_map/ppermute | solution.py:22
  83.7 13.9 %all-to-all-done.1.recv = bf16[16,128,512]{2,1,0:T(8,128)(2,1)S(1)} async-done(((bf16[16,128,512]{2,1,0:T(8,128)(2,1)}), bf16[16,128,512]{2,1,0:T(8,128)(2,1)S(1)}, u32[]{:S(2)}, u32[]{:S(2)}) %all-to-all-start.1) | async-done | bytes 2097184 | tf_op jit(solution)/shard_map/all_to_all | solution.py:26
  97.7 2.3 %all-gather.2.cloned.1.call-done.weight_hbm = bf16[16,512,256]{2,1,0:T(8,128)(2,1)} async-done(((bf16[1,512,256]{2,1,0:T(8,128)(2,1)}), bf16[16,512,256]{2,1,0:T(8,128)(2,1)}) %all-gather.2.cloned.1.call-update) | async-done | bytes 4194320 | tf_op jit(solution)/shard_map/all_gather | solution.py:321
  100.0 7.8 %layer.1 = (bf16[256,512]{1,0:T(8,128)(2,1)}, bf16[2,128,512]{2,1,0:T(8,128)(2,1)}, bf16[2,8,64,512]{3,2,1,0:T(8,128)(2,1)}, bf16[16,128,512]{2,1,0:T(8,128)(2,1)}) custom-call(s32[2]{0:T(128)S(1)} %copy-done.3, s32[2,4]{1,0:T(2,128)S(1)} %and_select_fusion.holder, s32[1]{0:T(128)} %bitcast.spot, bf16[2,128,512]{2,1,0:T(8,128)(2,1)S(1)} %bitcast.17, ...), custom_call_target="tpu_custom_call" | custom-call | flops 5368709120 | bytes 16777216 | tf_op jit(solution)/shard_map/layer/pallas_call | solution.py:190
  107.8 4.4 %all-to-all-start.2 = ((bf16[16,128,512]{2,1,0:T(8,128)(2,1)}), bf16[16,128,512]{2,1,0:T(8,128)(2,1)S(1)}, u32[]{:S(2)}, u32[]{:S(2)}) async-start(bf16[16,128,512]{2,1,0:T(8,128)(2,1)} %get-tuple-element.21), calls=%async_computation.2 | async-start | bytes 4194304 | tf_op jit(solution)/shard_map/all_to_all | solution.py:26
  112.2 3.7 %projection.1 = (bf16[256,1024]{1,0:T(8,128)(2,1)S(1)}, bf16[256,1024]{1,0:T(8,128)(2,1)S(1)}, bf16[256,1024]{1,0:T(8,128)(2,1)S(1)}, bf16[256,1024]{1,0:T(8,128)(2,1)S(1)}) custom-call(s32[1]{0:T(128)} %bitcast.spot, bf16[16,512,256]{2,1,0:T(8,128)(2,1)} %all-gather.2.cloned.1.call-done.weight_hbm, bf16[256,512]{1,0:T(8,128)(2,1)} %get-tuple-element.14.attended_hbm), custom_call_target="tpu_custom_call" | custom-call | flops 2147483648 | bytes 8388608 | tf_op jit(solution)/shard_map/projection/pallas_call | solution.py:242
  116.0 3.1 %collective-permute-start.5 = (bf16[256,1024]{1,0:T(8,128)(2,1)S(1)}, bf16[256,1024]{1,0:T(8,128)(2,1)S(1)}, u32[]{:S(2)}, u32[]{:S(2)}) collective-permute-start(bf16[256,1024]{1,0:T(8,128)(2,1)S(1)} %get-tuple-element.16), channel_id=1, source_target_pairs={{0,1},{1,2},{2,3},{3,0},{4,5},{5,6},{6,7},{7,4},{8,9},{9,10},{10,1... | collective-permute-start | bytes 1572872 | tf_op jit(solution)/shard_map/ppermute | solution.py:22
  119.1 4.3 %collective-permute-start.6 = (bf16[256,1024]{1,0:T(8,128)(2,1)S(1)}, bf16[256,1024]{1,0:T(8,128)(2,1)S(1)}, u32[]{:S(2)}, u32[]{:S(2)}) collective-permute-start(bf16[256,1024]{1,0:T(8,128)(2,1)S(1)} %get-tuple-element.17), channel_id=1, source_target_pairs={{0,2},{1,3},{2,0},{3,1},{4,6},{5,7},{6,4},{7,5},{8,10},{9,11},{10,... | collective-permute-start | bytes 1572872 | tf_op jit(solution)/shard_map/ppermute | solution.py:22
  123.4 3.1 %collective-permute-start.7 = (bf16[256,1024]{1,0:T(8,128)(2,1)S(1)}, bf16[256,1024]{1,0:T(8,128)(2,1)S(1)}, u32[]{:S(2)}, u32[]{:S(2)}) collective-permute-start(bf16[256,1024]{1,0:T(8,128)(2,1)S(1)} %get-tuple-element.18), channel_id=1, source_target_pairs={{0,3},{1,0},{2,1},{3,2},{4,7},{5,4},{6,5},{7,6},{8,11},{9,8},{10,9... | collective-permute-start | bytes 1572872 | tf_op jit(solution)/shard_map/ppermute | solution.py:22
  126.5 6.2 %collective-permute-done.5 = bf16[256,1024]{1,0:T(8,128)(2,1)S(1)} collective-permute-done((bf16[256,1024]{1,0:T(8,128)(2,1)S(1)}, bf16[256,1024]{1,0:T(8,128)(2,1)S(1)}, u32[]{:S(2)}, u32[]{:S(2)}) %collective-permute-start.5) | collective-permute-done | bytes 524320 | tf_op jit(solution)/shard_map/ppermute | solution.py:22
  132.7 12.0 %collective-permute-done.6 = bf16[256,1024]{1,0:T(8,128)(2,1)S(1)} collective-permute-done((bf16[256,1024]{1,0:T(8,128)(2,1)S(1)}, bf16[256,1024]{1,0:T(8,128)(2,1)S(1)}, u32[]{:S(2)}, u32[]{:S(2)}) %collective-permute-start.6) | collective-permute-done | bytes 524320 | tf_op jit(solution)/shard_map/ppermute | solution.py:22
  147.3 13.9 %all-to-all-done.2.back = bf16[16,128,512]{2,1,0:T(8,128)(2,1)S(1)} async-done(((bf16[16,128,512]{2,1,0:T(8,128)(2,1)}), bf16[16,128,512]{2,1,0:T(8,128)(2,1)S(1)}, u32[]{:S(2)}, u32[]{:S(2)}) %all-to-all-start.2) | async-done | bytes 2097184 | tf_op jit(solution)/shard_map/all_to_all | solution.py:26
  161.2 2.4 %combine.1 = (bf16[8,64,512]{2,1,0:T(8,128)(2,1)}, bf16[8,64,512]{2,1,0:T(8,128)(2,1)}) custom-call(s32[16,1]{1,0:T(8,128)S(1)} %bitcast.16, bf16[2,8,64,512]{3,2,1,0:T(8,128)(2,1)S(1)} %copy-done, bf16[16,128,512]{2,1,0:T(8,128)(2,1)S(1)} %all-to-all-done.2.back), custom_call_target="tpu_custom_call" | custom-call | bytes 4194304 | tf_op jit(solution)/shard_map/combine/pallas_call | solution.py:290
  (19 shorter events, 4.3 us)
Async XLA Ops:
  7.2 92.8 %all-gather.2.cloned.1.call-start = ((), (), s32[]{:S(2)}) async-start(), calls=%async_computation.3 | async-start | bytes 4456448 | tf_op jit(solution)/shard_map/all_gather | solution.py:321
  28.2 38.1 %copy-start.4 = (s32[2,4]{1,0:T(2,128)S(1)}, s32[2,4]{1,0:T(2,128)}, u32[]{:S(2)}) copy-start(s32[2,4]{1,0:T(2,128)} %param.13) | copy-start | bytes 100
  28.2 71.8 %copy-start.1 = (bf16[1,8,64,512]{3,2,1,0:T(8,128)(2,1)S(1)}, bf16[1,8,64,512]{3,2,1,0:T(8,128)(2,1)}, u32[]{:S(2)}) copy-start(bf16[1,8,64,512]{3,2,1,0:T(8,128)(2,1)} %param.8) | copy-start | bytes 1572868
  28.2 71.8 %copy-start.2 = (bf16[1,8,64,512]{3,2,1,0:T(8,128)(2,1)S(1)}, bf16[1,8,64,512]{3,2,1,0:T(8,128)(2,1)}, u32[]{:S(2)}) copy-start(bf16[1,8,64,512]{3,2,1,0:T(8,128)(2,1)} %param.9) | copy-start | bytes 1572868
  28.2 71.8 %copy-start.3 = (s32[2]{0:T(128)S(1)}, s32[2]{0:T(128)}, u32[]{:S(2)}) copy-start(s32[2]{0:T(128)} %counts.1) | copy-start | bytes 28
  28.2 69.4 %all-to-all-start.1 = ((bf16[16,128,512]{2,1,0:T(8,128)(2,1)}), bf16[16,128,512]{2,1,0:T(8,128)(2,1)S(1)}, u32[]{:S(2)}, u32[]{:S(2)}) async-start(bf16[16,128,512]{2,1,0:T(8,128)(2,1)} %pick_blocks.1), calls=%async_computation.1 | async-start | bytes 4194304 | tf_op jit(solution)/shard_map/all_to_all | solution.py:26
  32.6 21.1 %collective-permute-start.1 = (bf16[1,2,128,1024]{3,2,1,0:T(8,128)(2,1)}, bf16[1,2,128,1024]{3,2,1,0:T(8,128)(2,1)}, u32[]{:S(2)}, u32[]{:S(2)}) collective-permute-start(bf16[1,2,128,1024]{3,2,1,0:T(8,128)(2,1)} %param.11), channel_id=1, source_target_pairs={{0,28},{4,0},{8,4},{12,8},{16,12},{20,16},{24,20},{28,24},{1,29},{... | collective-permute-start | bytes 1572872 | tf_op jit(solution)/shard_map/ppermute | solution.py:22
  53.8 20.9 %collective-permute-start.4 = (bf16[256,1024]{1,0:T(8,128)(2,1)}, bf16[256,1024]{1,0:T(8,128)(2,1)}, u32[]{:S(2)}, u32[]{:S(2)}) collective-permute-start(bf16[256,1024]{1,0:T(8,128)(2,1)} %bitcast.6.grad0), channel_id=1, source_target_pairs={{0,1},{1,2},{2,3},{3,0},{4,5},{5,6},{6,7},{7,4},{8,9},{9,10},{10,1... | collective-permute-start | bytes 1572872 | tf_op jit(solution)/shard_map/ppermute | solution.py:22
  56.9 24.9 %collective-permute-start.3 = (bf16[256,1024]{1,0:T(8,128)(2,1)}, bf16[256,1024]{1,0:T(8,128)(2,1)}, u32[]{:S(2)}, u32[]{:S(2)}) collective-permute-start(bf16[256,1024]{1,0:T(8,128)(2,1)} %bitcast.6.grad0), channel_id=1, source_target_pairs={{0,2},{1,3},{2,0},{3,1},{4,6},{5,7},{6,4},{7,5},{8,10},{9,11},{10,... | collective-permute-start | bytes 1572872 | tf_op jit(solution)/shard_map/ppermute | solution.py:22
  61.3 22.5 %collective-permute-start.2 = (bf16[256,1024]{1,0:T(8,128)(2,1)}, bf16[256,1024]{1,0:T(8,128)(2,1)}, u32[]{:S(2)}, u32[]{:S(2)}) collective-permute-start(bf16[256,1024]{1,0:T(8,128)(2,1)} %bitcast.6.grad0), channel_id=1, source_target_pairs={{0,3},{1,0},{2,1},{3,2},{4,7},{5,4},{6,5},{7,6},{8,11},{9,8},{10,9... | collective-permute-start | bytes 1572872 | tf_op jit(solution)/shard_map/ppermute | solution.py:22
  64.3 10.4 %collective-permute-start = (bf16[1,2,128,512]{3,2,1,0:T(8,128)(2,1)}, bf16[1,2,128,512]{3,2,1,0:T(8,128)(2,1)S(1)}, u32[]{:S(2)}, u32[]{:S(2)}) collective-permute-start(bf16[1,2,128,512]{3,2,1,0:T(8,128)(2,1)} %param.7), channel_id=1, source_target_pairs={{0,4},{4,8},{8,12},{12,16},{16,20},{20,24},{24,28},{28,0},{1,5},{5... | collective-permute-start | bytes 786440 | tf_op jit(solution)/shard_map/ppermute | solution.py:22
  107.8 53.4 %all-to-all-start.2 = ((bf16[16,128,512]{2,1,0:T(8,128)(2,1)}), bf16[16,128,512]{2,1,0:T(8,128)(2,1)S(1)}, u32[]{:S(2)}, u32[]{:S(2)}) async-start(bf16[16,128,512]{2,1,0:T(8,128)(2,1)} %get-tuple-element.21), calls=%async_computation.2 | async-start | bytes 4194304 | tf_op jit(solution)/shard_map/all_to_all | solution.py:26
  116.0 45.2 %copy-start = (bf16[2,8,64,512]{3,2,1,0:T(8,128)(2,1)S(1)}, bf16[2,8,64,512]{3,2,1,0:T(8,128)(2,1)}, u32[]{:S(2)}) copy-start(bf16[2,8,64,512]{3,2,1,0:T(8,128)(2,1)} %get-tuple-element.20.own_rows) | copy-start | bytes 3145732
  116.0 16.7 %collective-permute-start.5 = (bf16[256,1024]{1,0:T(8,128)(2,1)S(1)}, bf16[256,1024]{1,0:T(8,128)(2,1)S(1)}, u32[]{:S(2)}, u32[]{:S(2)}) collective-permute-start(bf16[256,1024]{1,0:T(8,128)(2,1)S(1)} %get-tuple-element.16), channel_id=1, source_target_pairs={{0,1},{1,2},{2,3},{3,0},{4,5},{5,6},{6,7},{7,4},{8,9},{9,10},{10,1... | collective-permute-start | bytes 1572872 | tf_op jit(solution)/shard_map/ppermute | solution.py:22
  119.1 25.6 %collective-permute-start.6 = (bf16[256,1024]{1,0:T(8,128)(2,1)S(1)}, bf16[256,1024]{1,0:T(8,128)(2,1)S(1)}, u32[]{:S(2)}, u32[]{:S(2)}) collective-permute-start(bf16[256,1024]{1,0:T(8,128)(2,1)S(1)} %get-tuple-element.17), channel_id=1, source_target_pairs={{0,2},{1,3},{2,0},{3,1},{4,6},{5,7},{6,4},{7,5},{8,10},{9,11},{10,... | collective-permute-start | bytes 1572872 | tf_op jit(solution)/shard_map/ppermute | solution.py:22
  123.4 22.8 %collective-permute-start.7 = (bf16[256,1024]{1,0:T(8,128)(2,1)S(1)}, bf16[256,1024]{1,0:T(8,128)(2,1)S(1)}, u32[]{:S(2)}, u32[]{:S(2)}) collective-permute-start(bf16[256,1024]{1,0:T(8,128)(2,1)S(1)} %get-tuple-element.18), channel_id=1, source_target_pairs={{0,3},{1,0},{2,1},{3,2},{4,7},{5,4},{6,5},{7,6},{8,11},{9,8},{10,9... | collective-permute-start | bytes 1572872 | tf_op jit(solution)/shard_map/ppermute | solution.py:22
Sparse Core Ops, SparseCore 0:
  10.1 89.8 all-gather.1
